TPU v7x, 32 devices: a whole 2x2x4 slice. The times are simulated.
32 devices in a mesh: grp: 4 (over z), ep: 8 (over y, x, core).
Axes of the slice: x: 2, y: 2, z: 4, core: 2. Of those that a mesh axis runs over, the one named last changes fastest.
Arguments:
- pol_hidden: bfloat16 [1280, 1024], P(('grp', 'ep')), may hold values from -80 to 80
- ref_hidden: bfloat16 [1280, 1024], P(('grp', 'ep')), may hold values from -80 to 80
- pol_routes: int32 [1280, 8], P(('grp', 'ep')), may hold values from 0 to 63, all different within a row; in each aligned block of 40 rows (0 to 39, 40 to 79, ...) at most 7 rows name the same one
- ref_routes: int32 [1280, 8], P(('grp', 'ep')), may hold values from 0 to 63, all different within a row; in each aligned block of 40 rows (0 to 39, 40 to 79, ...) at most 7 rows name the same one
- pol_gates: float32 [1280, 8], P(('grp', 'ep')), may hold values from 0.02 to 0.3
- ref_gates: float32 [1280, 8], P(('grp', 'ep')), may hold values from 0.02 to 0.3
- w_gate: bfloat16 [64, 1024, 384], P('ep'), may hold values from -0.1875 to 0.1875
- w_up: bfloat16 [64, 1024, 384], P('ep'), may hold values from -0.1875 to 0.1875
- w_down: bfloat16 [64, 384, 1024], P('ep'), may hold values from -0.3125 to 0.3125
- norm_gain: float32 [1024], replicated, may hold values from 0.5 to 1.5
- vocab_head: bfloat16 [77824, 1024], P(('grp', 'ep')), may hold values from -2 to 2
- targets: int32 [1280], P(('grp', 'ep')), may hold values from 0 to 77823
- seq_lengths: int32 [32], replicated, may hold values from 1 to 640, 1280 in all
- owners: int32 [32], replicated, may hold values from 0 to 31, each once
Outputs:
- token_ratio: float32 [1280], P(('grp', 'ep'))
- owned_mean: float32 [32], P(('grp', 'ep'))
Inputs may be any that keep to these rules, and one draw needn't show every extreme that they name: `pol_routes`: each row names 8 different experts; among the 40 rows of one device no expert is named by more than 7 rows, a bound that some block reaches. `ref_routes`: each row names 8 different experts; among the 40 rows of one device no expert is named by more than 7 rows, a bound that some block reaches. `seq_lengths`: the lengths sum to 1280; the longest is exactly 640. `owners`: every device index appears exactly once.
All inputs are finite; a program needn't handle non-finite values.
Results may differ from a plain program's by a relative error of at most 0.0062.
Values may be sent and summed in bfloat16 or wider, within the bound.
No kernel may reach another device: no remote copies, remote signals or barrier semaphores. Data moves between devices by JAX's collectives and lax.ppermute only.
A program may use at most 128 MiB of HBM per device.

v0:
```python
import jax
import jax.numpy as jnp
from jax import lax
from jax.sharding import PartitionSpec as P


def joined_2(value, axis, join):
    pieces = jax.tree.map(lambda part: lax.all_gather(part, axis), value)
    head = jax.tree.map(lambda part: part[0], pieces)
    tail = jax.tree.map(lambda part: part[1:], pieces)
    so_far, _ = lax.scan(lambda so_far, share: (join(so_far, share), None), head, tail)
    return so_far


def combine_stats(earlier_part, second):
    peak = jnp.maximum(earlier_part[0], second[0])
    totals = earlier_part[1] * jnp.exp(earlier_part[0] - peak) + second[1] * jnp.exp(
        second[0] - peak
    )
    return (peak, totals, earlier_part[2] + second[2])


def vocab_stats(row_block, weights, vocab_ids, wanted):
    logits = jnp.einsum("td,vd->tv", row_block, weights, preferred_element_type=jnp.float32)
    peak = jnp.max(logits, axis=1)
    totals = jnp.sum(jnp.exp(logits - peak[:, None]), axis=1)
    picked = jnp.sum(jnp.where(vocab_ids[None, :] == wanted[:, None], logits, 0.0), axis=1)
    return (peak, totals, picked)


def expert_tables(routes, gates, experts, capacity):
    route_hits = routes[:, :, None] == jnp.arange(experts, dtype=jnp.int32)[None, None, :]
    members = jnp.sum(route_hits.astype(jnp.int32), axis=1)
    earlier = jnp.cumsum(members, axis=0) - members
    placed = (members[:, :, None] > 0) & (
        earlier[:, :, None] == jnp.arange(capacity, dtype=jnp.int32)[None, None, :]
    )
    weight = jnp.sum(jnp.where(route_hits, gates[:, :, None], 0.0), axis=1)
    tok_count = routes.shape[0]
    picker = placed.astype(jnp.bfloat16).reshape(tok_count, experts * capacity)
    mixing = (weight[:, :, None] * placed.astype(jnp.float32)).reshape(
        tok_count, experts * capacity
    )
    return (picker, mixing)


def local(
    pol_hidden,
    ref_hidden,
    pol_routes,
    ref_routes,
    pol_gates,
    ref_gates,
    w_gate,
    w_up,
    w_down,
    norm_gain,
    vocab_head,
    targets,
    seq_lengths,
    owners,
):
    groups = lax.axis_size("ep")
    device_index = lax.axis_index(("grp", "ep"))
    local_experts = w_gate.shape[0]
    experts = local_experts * groups
    tok_count = pol_hidden.shape[0]
    width = pol_hidden.shape[1]
    fanout = pol_routes.shape[1]
    capacity = tok_count * fanout // experts + 2
    pol_pick, pol_mixing = expert_tables(pol_routes, pol_gates, experts, capacity)
    ref_pick, ref_mixing = expert_tables(ref_routes, ref_gates, experts, capacity)
    pol_send = jnp.einsum(
        "ts,td->sd", pol_pick, pol_hidden, preferred_element_type=jnp.float32
    ).astype(jnp.bfloat16)
    ref_send = jnp.einsum(
        "ts,td->sd", ref_pick, ref_hidden, preferred_element_type=jnp.float32
    ).astype(jnp.bfloat16)
    pol_send = pol_send.reshape(groups, local_experts, capacity, width)
    ref_send = ref_send.reshape(groups, local_experts, capacity, width)
    pol_part = lax.all_to_all(pol_send, "ep", split_axis=0, concat_axis=0, tiled=True)
    ref_part = lax.all_to_all(ref_send, "ep", split_axis=0, concat_axis=0, tiled=True)
    slots = pol_part.shape[2]
    joined = jnp.concatenate((pol_part, ref_part), axis=2)
    gate_act = jnp.einsum("nesd,edf->nesf", joined, w_gate, preferred_element_type=jnp.float32)
    up_act = jnp.einsum("nesd,edf->nesf", joined, w_up, preferred_element_type=jnp.float32)
    inner = (jax.nn.silu(gate_act) * up_act).astype(jnp.bfloat16)
    outputs = jnp.einsum(
        "nesf,efd->nesd", inner, w_down, preferred_element_type=jnp.float32
    ).astype(jnp.bfloat16)
    pol_back = lax.all_to_all(outputs[:, :, :slots], "ep", split_axis=0, concat_axis=0, tiled=True)
    ref_back = lax.all_to_all(outputs[:, :, slots:], "ep", split_axis=0, concat_axis=0, tiled=True)

    def mix_back(hidden, mixing, back):
        rows_back = back.reshape(experts * capacity, width).astype(jnp.float32)
        mixed = hidden.astype(jnp.float32) + jnp.dot(
            mixing, rows_back, precision=lax.Precision.HIGHEST
        )
        scale = lax.rsqrt(jnp.mean(mixed * mixed, axis=1, keepdims=True) + 1e-06)
        return (mixed * scale * norm_gain).astype(jnp.bfloat16)

    pol_normed = mix_back(pol_hidden, pol_mixing, pol_back)
    ref_normed = mix_back(ref_hidden, ref_mixing, ref_back)
    vocab_rows = vocab_head.shape[0]
    band = lax.axis_index("grp")
    pol_col, ref_col, wanted = (
        lax.all_gather(pol_normed, "grp", axis=0, tiled=True),
        lax.all_gather(ref_normed, "grp", axis=0, tiled=True),
        lax.all_gather(targets, "grp", axis=0, tiled=True),
    )
    col_count = wanted.shape[0]
    floor_value = jnp.full((2, col_count), -1e30, jnp.float32)
    blank = jnp.zeros((2, col_count), jnp.float32)
    piece = lax.all_gather(vocab_head, "ep", axis=0, tiled=True)
    count = piece.shape[0]
    place = jnp.arange(count, dtype=jnp.int32)
    vocab_ids = band * groups * vocab_rows + place
    pol_stats = vocab_stats(pol_col, piece, vocab_ids, wanted)
    ref_stats = vocab_stats(ref_col, piece, vocab_ids, wanted)
    fresh = tuple(
        (jnp.stack((pol_part, ref_part)) for pol_part, ref_part in zip(pol_stats, ref_stats))
    )
    stats = combine_stats((floor_value, blank, blank), fresh)
    peak, totals, picked = joined_2(stats, "grp", combine_stats)
    logprob = picked - (peak + jnp.log(totals))
    mine = lax.dynamic_slice_in_dim(logprob, band * tok_count, tok_count, axis=1)
    token_ratio = mine[0] - mine[1]
    offsets = jnp.cumsum(seq_lengths) - seq_lengths
    positions = device_index * tok_count + jnp.arange(tok_count, dtype=jnp.int32)
    inside = (positions[:, None] >= offsets[None, :]) & (
        positions[:, None] < (offsets + seq_lengths)[None, :]
    )
    partial_value = jnp.dot(
        token_ratio, inside.astype(jnp.float32), precision=lax.Precision.HIGHEST
    ) / seq_lengths.astype(jnp.float32)
    sums = lax.psum(partial_value, ("grp", "ep"))
    owned = jnp.sum(jnp.where(owners == device_index, sums, 0.0)).reshape(1)
    return (token_ratio, owned)


def solution(mesh):
    return jax.shard_map(
        local,
        mesh=mesh,
        in_specs=(
            P(("grp", "ep"), None),
            P(("grp", "ep"), None),
            P(("grp", "ep"), None),
            P(("grp", "ep"), None),
            P(("grp", "ep"), None),
            P(("grp", "ep"), None),
            P("ep", None, None),
            P("ep", None, None),
            P("ep", None, None),
            P(),
            P(("grp", "ep"), None),
            P(("grp", "ep")),
            P(),
            P(),
        ),
        out_specs=(P(("grp", "ep")), P(("grp", "ep"))),
        check_vma=False,
    )
```

profile of v0, /device:TPU:0, one launch (start us, length us, event | category | flops | bytes accessed | tf_op | source)
XLA Modules:
  0.0 372.4 jit_solution(16694666369273000657)
XLA Ops:
  7.2 0.7 all-gather.4.cloned.1.call-update
  7.9 0.8 copy.53
  9.4 0.4 convolution_convert_fusion.1
  9.9 0.3 reshape.314
  10.2 1.5 copy.58
  11.7 5.2 %all-to-all-start = ((bf16[8,8,7,1024]{3,1,2,0:T(8,128)(2,1)}), bf16[8,8,7,1024]{3,1,2,0:T(8,128)(2,1)S(1)}, u32[]{:S(2)}, u32[]{:S(2)}) async-start(bf16[8,8,7,1024]{3,1,2,0:T(8,128)(2,1)} %copy.58), calls=%async_computation | async-start | bytes 1835008 | tf_op jit(solution)/shard_map/all_to_all | solution.py:81
  17.5 0.5 convolution_convert_fusion
  18.0 0.3 reshape.315
  18.3 1.6 copy.62
  19.9 12.6 %all-to-all-done = bf16[8,8,7,1024]{3,1,2,0:T(8,128)(2,1)S(1)} async-done(((bf16[8,8,7,1024]{3,1,2,0:T(8,128)(2,1)}), bf16[8,8,7,1024]{3,1,2,0:T(8,128)(2,1)S(1)}, u32[]{:S(2)}, u32[]{:S(2)}) %all-to-all-start) | async-done | bytes 917536 | tf_op jit(solution)/shard_map/all_to_all | solution.py:81
  32.5 3.6 all-to-all-start.1
  36.0 0.5 copy.63
  36.5 23.5 %all-to-all-done.1 = bf16[8,8,7,1024]{3,1,2,0:T(8,128)(2,1)S(1)} async-done(((bf16[8,8,7,1024]{3,1,2,0:T(8,128)(2,1)}), bf16[8,8,7,1024]{3,1,2,0:T(8,128)(2,1)S(1)}, u32[]{:S(2)}, u32[]{:S(2)}) %all-to-all-start.1) | async-done | bytes 917536 | tf_op jit(solution)/shard_map/all_to_all | solution.py:82
  60.0 0.5 copy.64
  60.6 5.3 %fusion.8 = f32[8,8,14,384]{3,2,1,0:T(8,128)} fusion(bf16[8,1024,384]{2,1,0:T(8,128)(2,1)} %param.22, bf16[8,8,7,1024]{3,2,0,1:T(8,128)(2,1)S(1)} %copy.64, bf16[8,8,7,1024]{3,2,0,1:T(8,128)(2,1)S(1)} %copy.63), kind=kOutput, calls=%fused_computation.16 | convolution fusion | flops 708313088 | bytes 9502720 | tf_op jit(solution)/shard_map/nesd,edf->nesf/dot_general | solution.py:85
  65.8 9.0 %convert_bitcast_fusion = bf16[8,8,14,1024]{3,2,0,1:T(8,128)(2,1)} fusion(bf16[8,384,1024]{2,1,0:T(8,128)(2,1)} %param.24, f32[8,8,14,384]{3,2,1,0:T(8,128)} %fusion.8, bf16[8,1024,384]{2,1,0:T(8,128)(2,1)} %param.23, bf16[8,8,7,1024]{3,2,0,1:T(8,128)(2,1)S(1)} %copy.64, bf16[8,8,7,1024]{3,2,0,1:T(8,128)(2,1)S(1)} %copy.63), kind=kOutput, calls=%fused_computation.19 | convolution fusion | flops 1415938048 | bytes 17629184 | tf_op jit(solution)/shard_map/nesf,efd->nesd/dot_general | solution.py:88
  74.8 2.5 fusion.43
  77.3 1.5 copy.69
  78.8 3.6 all-to-all-start.3
  82.5 0.2 select_reduce_fusion
  82.9 1.6 copy.65
  84.5 19.4 %all-to-all-done.3 = bf16[8,8,7,1024]{3,1,2,0:T(8,128)(2,1)S(1)} async-done(((bf16[8,8,7,1024]{3,1,2,0:T(8,128)(2,1)}), bf16[8,8,7,1024]{3,1,2,0:T(8,128)(2,1)S(1)}, u32[]{:S(2)}, u32[]{:S(2)}) %all-to-all-start.3) | async-done | bytes 917536 | tf_op jit(solution)/shard_map/all_to_all | solution.py:92
  103.9 3.7 %all-to-all-start.2 = ((bf16[8,8,7,1024]{3,1,2,0:T(8,128)(2,1)}), bf16[8,8,7,1024]{3,1,2,0:T(8,128)(2,1)S(1)}, u32[]{:S(2)}, u32[]{:S(2)}) async-start(bf16[8,8,7,1024]{3,1,2,0:T(8,128)(2,1)} %copy.65), calls=%async_computation.2 | async-start | bytes 1835008 | tf_op jit(solution)/shard_map/all_to_all | solution.py:91
  107.7 0.2 select_reduce_fusion.1
  108.3 0.6 dynamic-slice
  109.6 0.2 dynamic-update-slice
  109.8 8.4 %all-reduce = s32[160]{0:T(256)S(1)} all-reduce(s32[160]{0:T(256)S(1)} %dynamic-update-slice), channel_id=1, replica_groups=mesh['grp'=4,'ep'=8] {'grp'}, use_global_device_ids=true, to_apply=%add | all-reduce | flops 160 | bytes 1280
  118.3 0.6 iota_add_fusion
  118.9 0.5 copy.70
  119.5 0.3 reshape.317
  119.8 11.4 %all-to-all-done.2 = bf16[8,8,7,1024]{3,1,2,0:T(8,128)(2,1)S(1)} async-done(((bf16[8,8,7,1024]{3,1,2,0:T(8,128)(2,1)}), bf16[8,8,7,1024]{3,1,2,0:T(8,128)(2,1)S(1)}, u32[]{:S(2)}, u32[]{:S(2)}) %all-to-all-start.2) | async-done | bytes 917536 | tf_op jit(solution)/shard_map/all_to_all | solution.py:91
  131.2 0.5 copy.66
  131.7 0.3 reshape.316
  132.0 0.7 multiply_reduce_fusion
  132.8 0.7 multiply_reduce_fusion.1
  133.6 15.2 %all_gather.26 = bf16[160,1024]{1,0:T(8,128)(2,1)S(1)} all-gather(bf16[40,1024]{1,0:T(8,128)(2,1)S(1)} %get-tuple-element.69), channel_id=1, replica_groups=mesh['grp'=4,'ep'=8] {'grp'}, dimensions={0}, use_global_device_ids=true | all-gather | bytes 409600 | tf_op jit(solution)/shard_map/all_gather | solution.py:107
  148.8 14.0 %all_gather.28 = bf16[160,1024]{1,0:T(8,128)(2,1)S(1)} all-gather(bf16[40,1024]{1,0:T(8,128)(2,1)S(1)} %get-tuple-element.70), channel_id=1, replica_groups=mesh['grp'=4,'ep'=8] {'grp'}, dimensions={0}, use_global_device_ids=true | all-gather | bytes 409600 | tf_op jit(solution)/shard_map/all_gather | solution.py:108
  162.8 68.5 %all-gather.4.cloned.1.call-done = bf16[19456,1024]{1,0:T(8,128)(2,1)} async-done(((bf16[2432,1024]{1,0:T(8,128)(2,1)}), bf16[19456,1024]{1,0:T(8,128)(2,1)}) %all-gather.4.cloned.1.call-update) | async-done | bytes 39845904 | tf_op jit(solution)/shard_map/all_gather | solution.py:114
  231.3 23.7 %fusion.44 = (f32[160]{0:T(256)S(1)}, f32[160,19456]{1,0:T(8,128)}) fusion(bf16[160,1024]{1,0:T(8,128)(2,1)S(1)} %all_gather.26, bf16[19456,1024]{1,0:T(8,128)(2,1)} %all-gather.4.cloned.1.call-done), kind=kOutput, calls=%fused_computation.86 | convolution fusion | flops 6378455040 | bytes 52626048 | tf_op jit(solution)/shard_map/td,vd->tv/dot_general | solution.py:24
  255.0 23.8 %fusion.45 = (f32[160]{0:T(256)S(1)}, f32[160,19456]{1,0:T(8,128)}) fusion(bf16[160,1024]{1,0:T(8,128)(2,1)S(1)} %all_gather.28, bf16[19456,1024]{1,0:T(8,128)(2,1)} %all-gather.4.cloned.1.call-done), kind=kOutput, calls=%fused_computation.87 | convolution fusion | flops 6378455040 | bytes 52626048 | tf_op jit(solution)/shard_map/td,vd->tv/dot_general | solution.py:24
  278.8 11.5 %fusion.2 = (f32[160]{0:T(256)S(1)}, f32[160]{0:T(256)S(1)}, f32[160]{0:T(256)S(1)}, f32[160]{0:T(256)S(1)}) fusion(f32[160,19456]{1,0:T(8,128)} %get-tuple-element.78, s32[19456]{0:T(1024)S(1)} %copy-done.2, s32[160]{0:T(256)S(1)} %all-reduce, f32[160]{0:T(256)S(1)} %get-tuple-element.77, f32[160,19456]{1,0:T(8,128)} %get-tuple-element.80, ...), kind=kLoop, calls=%fused_computation.8 | loop fusion | flops 28016000 | bytes 24985984 | tf_op jit(solution)/shard_map/reduce_sum | solution.py:27
  290.3 12.1 %all-gather.1 = f32[4,2,160]{2,1,0:T(2,128)S(1)} all-gather(f32[1,2,160]{2,1,0:T(2,128)S(1)} %maximum_bitcast_fusion), channel_id=2, replica_groups=mesh['grp'=4,'ep'=8] {'grp'}, dimensions={0}, use_global_device_ids=true | all-gather | bytes 6400 | tf_op jit(solution)/shard_map/all_gather | solution.py:8
  302.5 11.9 %all_gather.30 = f32[4,2,160]{2,1,0:T(2,128)S(1)} all-gather(f32[1,2,160]{2,1,0:T(2,128)S(1)} %get-tuple-element.71), channel_id=1, replica_groups=mesh['grp'=4,'ep'=8] {'grp'}, dimensions={0}, use_global_device_ids=true | all-gather | bytes 6400 | tf_op jit(solution)/shard_map/all_gather | solution.py:8
  314.3 11.9 %all_gather.29 = f32[4,2,160]{2,1,0:T(2,128)S(1)} all-gather(f32[1,2,160]{2,1,0:T(2,128)S(1)} %get-tuple-element.72), channel_id=1, replica_groups=mesh['grp'=4,'ep'=8] {'grp'}, dimensions={0}, use_global_device_ids=true | all-gather | bytes 6400 | tf_op jit(solution)/shard_map/all_gather | solution.py:8
  326.4 0.2 fusion.18
  326.6 0.5 fusion.42
  327.2 37.8 %psum.7 = f32[32]{0:T(128)S(1)} all-reduce(f32[32]{0:T(128)S(1)} %fusion.18), channel_id=1, replica_groups=mesh['grp'=4,'ep'=8] {'grp','ep'}, use_global_device_ids=true, to_apply=%region_17.18 | all-reduce | flops 32 | bytes 256 | tf_op jit(solution)/shard_map/psum | solution.py:136
  364.9 0.6 fusion.36
  (75 shorter events, 2.6 us)
Async XLA Ops:
  7.2 2.3 copy-start.1
  7.2 9.7 %copy-start.4 = (s32[40,8]{0,1:T(8,128)S(1)}, s32[40,8]{0,1:T(8,128)}, u32[]{:S(2)}) copy-start(s32[40,8]{0,1:T(8,128)} %param.19) | copy-start | bytes 3844
  7.2 10.4 %copy-start = (bf16[40,1024]{1,0:T(8,128)(2,1)S(1)}, bf16[40,1024]{1,0:T(8,128)(2,1)}, u32[]{:S(2)}) copy-start(bf16[40,1024]{1,0:T(8,128)(2,1)} %param.17) | copy-start | bytes 245764
  7.2 224.1 %all-gather.4.cloned.1.call-start = ((), (), s32[]{:S(2)}) async-start(), calls=%async_computation.4 | async-start | bytes 44826624 | tf_op jit(solution)/shard_map/all_gather | solution.py:114
  11.7 20.7 %all-to-all-start = ((bf16[8,8,7,1024]{3,1,2,0:T(8,128)(2,1)}), bf16[8,8,7,1024]{3,1,2,0:T(8,128)(2,1)S(1)}, u32[]{:S(2)}, u32[]{:S(2)}) async-start(bf16[8,8,7,1024]{3,1,2,0:T(8,128)(2,1)} %copy.58), calls=%async_computation | async-start | bytes 1835008 | tf_op jit(solution)/shard_map/all_to_all | solution.py:81
  32.5 27.6 %all-to-all-start.1 = ((bf16[8,8,7,1024]{3,1,2,0:T(8,128)(2,1)}), bf16[8,8,7,1024]{3,1,2,0:T(8,128)(2,1)S(1)}, u32[]{:S(2)}, u32[]{:S(2)}) async-start(bf16[8,8,7,1024]{3,1,2,0:T(8,128)(2,1)} %copy.62), calls=%async_computation.1 | async-start | bytes 1835008 | tf_op jit(solution)/shard_map/all_to_all | solution.py:82
  74.8 7.6 %copy-start.5 = (f32[40,8]{0,1:T(8,128)S(1)}, f32[40,8]{0,1:T(8,128)}, u32[]{:S(2)}) copy-start(f32[40,8]{0,1:T(8,128)} %param.21) | copy-start | bytes 3844
  74.8 8.0 %copy-start.6 = (f32[40,8]{0,1:T(8,128)S(1)}, f32[40,8]{0,1:T(8,128)}, u32[]{:S(2)}) copy-start(f32[40,8]{0,1:T(8,128)} %param.20) | copy-start | bytes 3844
  74.8 33.2 %copy-start.7 = (s32[32]{0:T(128)S(1)}, s32[32]{0:T(128)}, u32[]{:S(2)}) copy-start(s32[32]{0:T(128)} %param.28) | copy-start | bytes 388
  74.8 33.5 %copy-start.10 = (u32[32]{0:T(128)S(1)}, u32[32]{0:T(128)}, u32[]{:S(2)}) copy-start(u32[32]{0:T(128)} %constant.63) | copy-start | bytes 388
  74.8 34.8 %copy-start.9 = (s32[40]{0:T(128)S(1)}, s32[40]{0:T(128)}, u32[]{:S(2)}) copy-start(s32[40]{0:T(128)} %param.27) | copy-start | bytes 484
  78.8 25.1 %all-to-all-start.3 = ((bf16[8,8,7,1024]{3,1,2,0:T(8,128)(2,1)}), bf16[8,8,7,1024]{3,1,2,0:T(8,128)(2,1)S(1)}, u32[]{:S(2)}, u32[]{:S(2)}) async-start(bf16[8,8,7,1024]{3,1,2,0:T(8,128)(2,1)} %copy.69), calls=%async_computation.3 | async-start | bytes 1835008 | tf_op jit(solution)/shard_map/all_to_all | solution.py:92
  103.9 27.3 %all-to-all-start.2 = ((bf16[8,8,7,1024]{3,1,2,0:T(8,128)(2,1)}), bf16[8,8,7,1024]{3,1,2,0:T(8,128)(2,1)S(1)}, u32[]{:S(2)}, u32[]{:S(2)}) async-start(bf16[8,8,7,1024]{3,1,2,0:T(8,128)(2,1)} %copy.65), calls=%async_computation.2 | async-start | bytes 1835008 | tf_op jit(solution)/shard_map/all_to_all | solution.py:91
  107.7 25.9 %copy-start.3 = (f32[1024]{0:T(1024)S(1)}, f32[1024]{0:T(1024)}, u32[]{:S(2)}) copy-start(f32[1024]{0:T(1024)} %param.25) | copy-start | bytes 12292
  255.0 23.8 %copy-start.2 = (s32[19456]{0:T(1024)S(1)}, s32[19456]{0:T(1024)}, u32[]{:S(2)}) copy-start(s32[19456]{0:T(1024)} %iota_add_fusion) | copy-start | bytes 233476
  278.8 86.1 %copy-start.8 = (s32[32]{0:T(128)S(1)}, s32[32]{0:T(128)}, u32[]{:S(2)}) copy-start(s32[32]{0:T(128)} %param.29) | copy-start | bytes 388
Sparse Core Ops, SparseCore 0:
  9.9 221.3 all-gather.3
where the time goes:
time: 373 us; the launch traced here: 372 us
  waiting for transfers between devices  136 us (36%)
  blocking collectives  111 us (30%)
  matrix products  64.3 us (17%)
  starting transfers between devices  16 us (4%)
  between operations  15.1 us (4%)
  local copies, waits for them, and re-layouts  14.9 us (4%)
  other arithmetic  14.6 us (4%)
    all_gather x1, waiting for transfers between devices, local(): piece = lax.all_gather(vocab_head, 'ep', axis=0, tiled=True)  68.5 us
    dot_general x2, matrix products, vocab_stats(): jnp.einsum('td,vd->tv', row_block, weights, preferred_element_type=jnp.fl...  47.5 us
    psum x1, blocking collectives, local(): sums = lax.psum(partial_value, ('grp', 'ep'))  37.8 us
    all_gather x3, blocking collectives, joined_2(): pieces = jax.tree.map(lambda part: lax.all_gather(part, axis), value)  35.8 us
    all_to_all x1, waiting for transfers between devices, local(): lax.all_to_all(ref_send, 'ep', split_axis=0, concat_axis=0, tiled=True)  23.5 us
    all_to_all x1, waiting for transfers between devices, local(): lax.all_to_all(outputs[:, :, slots:], 'ep', split_axis=0, concat_axis=0,...  19.4 us
    all_gather x1, blocking collectives, local(): lax.all_gather(pol_normed, 'grp', axis=0, tiled=True)  15.2 us
    all_gather x1, blocking collectives, local(): lax.all_gather(ref_normed, 'grp', axis=0, tiled=True)  14 us
  transfers between devices with their start and end apart: 5, of which 5 were waited for; matrix products, arithmetic and copies ran while one was open for 9% of the time, Pallas kernels for 0%

commit v1 on v0

v1 whole, which is shorter than its diff:
```python
import functools

import jax
import jax.numpy as jnp
from jax import lax
from jax.experimental import pallas as pl
from jax.experimental.pallas import tpu as pltpu
from jax.sharding import Mesh, PartitionSpec as P

MIB = 1 << 20
LOW = -1e30


def round_up(value, step):
    return -(-value // step) * step


def largest_tile(rows, limit, step):
    best = rows
    for tile in range(step, min(rows, limit) + 1, step):
        if rows % tile == 0:
            best = tile
    return best


def expert_kernel(
    block, slots, width, experts, place_ref, x_ref, gate_ref, up_ref, down_ref, keep_ref, give_ref,
    table, pick, mix_hi, mix_lo, picked, made,
):
    step = pl.program_id(0)
    last = pl.num_programs(0) - 1
    rows = x_ref.shape[0]
    local_experts = pick.shape[0] // slots

    @pl.when(step == 0)
    def _():
        gates = x_ref[:, width:].astype(jnp.float32).T
        hits = (gates > 0.0).astype(jnp.bfloat16)
        before = lax.broadcasted_iota(jnp.int32, (rows, rows), 0)
        after = lax.broadcasted_iota(jnp.int32, (rows, rows), 1)
        first = after - after % block
        order = ((before < after) & (before >= first)).astype(jnp.bfloat16)
        rank = jnp.dot(hits, order, preferred_element_type=jnp.float32)
        token = lax.broadcasted_iota(jnp.int32, rank.shape, 1)
        per_block = slots // (rows // block)
        slot = rank + ((token // block) * per_block).astype(jnp.float32)
        table[0] = jnp.where(gates > 0.0, slot, -1.0)
        table[1] = gates
        spot = lax.broadcasted_iota(jnp.int32, (slots, rows), 0).astype(jnp.float32)
        for e in range(local_experts):
            row = place_ref[0] * local_experts + e
            chosen = table[0, pl.ds(row, 1), :] == spot
            band = pl.ds(e * slots, slots)
            pick[band, :] = jnp.where(chosen, 1.0, 0.0).astype(jnp.bfloat16)
            mix_hi[band, :] = jnp.where(chosen, table[1, pl.ds(row, 1), :], 0.0).astype(
                jnp.bfloat16
            )
            mix_lo[band, :] = jnp.where(
                chosen, table[1, pl.ds(row + experts, 1), :], 0.0
            ).astype(jnp.bfloat16)
        picked[...] = jnp.dot(
            pick[...], x_ref[:, :width], preferred_element_type=jnp.float32
        ).astype(jnp.bfloat16)

    band = pl.ds(pl.multiple_of(step * slots, slots), slots)
    mine = picked[band, :]
    gate_act = jnp.dot(mine, gate_ref[0], preferred_element_type=jnp.float32)
    up_act = jnp.dot(mine, up_ref[0], preferred_element_type=jnp.float32)
    inner = (gate_act / (1.0 + jnp.exp(-gate_act)) * up_act).astype(jnp.bfloat16)
    made[band, :] = jnp.dot(inner, down_ref[0], preferred_element_type=jnp.float32).astype(
        jnp.bfloat16
    )

    @pl.when(step == last)
    def _():
        over_slots = (((0,), (0,)), ((), ()))
        total = lax.dot_general(
            mix_hi[...], made[...], over_slots, preferred_element_type=jnp.float32
        )
        total += lax.dot_general(
            mix_lo[...], made[...], over_slots, preferred_element_type=jnp.float32
        )
        core = place_ref[0] % 2
        chips, share, _ = keep_ref.shape
        for owner in range(2):
            target = [total[(2 * c + owner) * share:(2 * c + owner + 1) * share] for c in range(chips)]

            @pl.when(core == owner)
            def _():
                for c in range(chips):
                    keep_ref[c] = target[c]

            @pl.when(core != owner)
            def _():
                for c in range(chips):
                    give_ref[c] = target[c]


def expert_sums(place, rows_in, w_gate, w_up, w_down, block, capacity, width, experts):
    rows = rows_in.shape[0]
    local_experts, _, hidden = w_gate.shape
    slots = round_up(capacity, 8) * (rows // block)
    every = local_experts * slots
    half = jax.ShapeDtypeStruct((rows // (4 * block), 2 * block, width), jnp.float32)
    return pl.pallas_call(
        functools.partial(expert_kernel, block, slots, width, experts),
        out_shape=(half, half),
        grid_spec=pltpu.PrefetchScalarGridSpec(
            num_scalar_prefetch=1,
            grid=(local_experts,),
            in_specs=[
                pl.BlockSpec(rows_in.shape, lambda e, place: (0, 0)),
                pl.BlockSpec((1, width, hidden), lambda e, place: (e, 0, 0)),
                pl.BlockSpec((1, width, hidden), lambda e, place: (e, 0, 0)),
                pl.BlockSpec((1, hidden, width), lambda e, place: (e, 0, 0)),
            ],
            out_specs=(
                pl.BlockSpec(half.shape, lambda e, place: (0, 0, 0)),
                pl.BlockSpec(half.shape, lambda e, place: (0, 0, 0)),
            ),
            scratch_shapes=[
                pltpu.VMEM((2, rows_in.shape[1] - width, rows), jnp.float32),
                pltpu.VMEM((every, rows), jnp.bfloat16),
                pltpu.VMEM((every, rows), jnp.bfloat16),
                pltpu.VMEM((every, rows), jnp.bfloat16),
                pltpu.VMEM((every, width), jnp.bfloat16),
                pltpu.VMEM((every, width), jnp.bfloat16),
            ],
        ),
        compiler_params=pltpu.CompilerParams(vmem_limit_bytes=56 * MIB),
        cost_estimate=pl.CostEstimate(
            flops=2 * every * width * (3 * hidden + 3 * rows),
            bytes_accessed=w_gate.size * 6 + rows_in.size * 2 + rows * width * 2,
            transcendentals=every * hidden,
        ),
    )(place, rows_in, w_gate, w_up, w_down)


def head_kernel(
    base_ref, wanted_ref, x_ref, head_a, head_b, lse_ref, hit_ref,
    peak, total, found, logits_a, logits_b,
):
    step = pl.program_id(1)
    last = pl.num_programs(1) - 1
    tile, columns = logits_a.shape
    lane_band = 128

    def product(head_ref, logits):
        logits[...] = lax.dot_general(
            head_ref[...], x_ref[...], (((1,), (1,)), ((), ())),
            preferred_element_type=jnp.float32,
        )

    def absorb(logits, first):
        row = lax.broadcasted_iota(jnp.int32, (tile, lane_band), 0)
        for start in range(0, columns, lane_band):
            band = pl.ds(start, lane_band)
            values = logits[:, band]
            old = peak[:, band]
            new = jnp.maximum(old, jnp.max(values.reshape(tile // 8, 8, lane_band), axis=0))
            grown = jnp.exp(values.reshape(tile // 8, 8, lane_band) - new[None])
            total[:, band] = total[:, band] * jnp.exp(old - new) + jnp.sum(grown, axis=0)
            same = row == wanted_ref[:, band] - first
            kept = jnp.where(same, values, 0.0).reshape(tile // 8, 8, lane_band)
            found[:, band] += jnp.sum(kept, axis=0)
            peak[:, band] = new

    @pl.when(step == 0)
    def _():
        peak[...] = jnp.full_like(peak, LOW)
        total[...] = jnp.zeros_like(total)
        found[...] = jnp.zeros_like(found)
        logits_b[...] = jnp.full_like(logits_b, LOW)

    product(head_a, logits_a)
    absorb(logits_b, jnp.where(step == 0, -(1 << 28), base_ref[1] + (step - 1) * tile))
    product(head_b, logits_b)
    absorb(logits_a, base_ref[0] + step * tile)

    @pl.when(step == last)
    def _():
        absorb(logits_b, base_ref[1] + step * tile)
        top = jnp.max(peak[...], axis=0, keepdims=True)
        full = jnp.sum(total[...] * jnp.exp(peak[...] - top), axis=0, keepdims=True)
        lse_ref[...] = top + jnp.log(full)
        hit_ref[...] = jnp.sum(found[...], axis=0, keepdims=True)


def head_stats(base, wanted, rows_in, head_a, head_b):
    rows, width = rows_in.shape
    chunk = largest_tile(rows, 1280, 128)
    tile = largest_tile(head_a.shape[0], 608, 16)
    steps = head_a.shape[0] // tile
    line = jax.ShapeDtypeStruct((1, rows), jnp.float32)
    return pl.pallas_call(
        head_kernel,
        out_shape=(line, line),
        grid_spec=pltpu.PrefetchScalarGridSpec(
            num_scalar_prefetch=1,
            grid=(rows // chunk, steps),
            in_specs=[
                pl.BlockSpec((1, chunk), lambda c, s, base: (0, c)),
                pl.BlockSpec((chunk, width), lambda c, s, base: (c, 0)),
                pl.BlockSpec((tile, width), lambda c, s, base: (s, 0)),
                pl.BlockSpec((tile, width), lambda c, s, base: (s, 0)),
            ],
            out_specs=(
                pl.BlockSpec((1, chunk), lambda c, s, base: (0, c)),
                pl.BlockSpec((1, chunk), lambda c, s, base: (0, c)),
            ),
            scratch_shapes=[
                pltpu.VMEM((8, chunk), jnp.float32),
                pltpu.VMEM((8, chunk), jnp.float32),
                pltpu.VMEM((8, chunk), jnp.float32),
                pltpu.VMEM((tile, chunk), jnp.float32),
                pltpu.VMEM((tile, chunk), jnp.float32),
            ],
        ),
        compiler_params=pltpu.CompilerParams(vmem_limit_bytes=56 * MIB),
        cost_estimate=pl.CostEstimate(
            flops=4 * rows * width * head_a.shape[0],
            bytes_accessed=head_a.size * 4 + rows_in.size * 2,
            transcendentals=2 * rows * head_a.shape[0],
        ),
    )(base, wanted, rows_in, head_a, head_b)


def gate_table(routes, gates, experts):
    hits = routes[:, :, None] == jnp.arange(experts, dtype=jnp.int32)[None, None, :]
    dense = jnp.sum(jnp.where(hits, gates[:, :, None], 0.0), axis=1)
    high = dense.astype(jnp.bfloat16)
    low = (dense - high.astype(jnp.float32)).astype(jnp.bfloat16)
    return jnp.concatenate((high, low), axis=1)


def local(
    pol_hidden, ref_hidden, pol_routes, ref_routes, pol_gates, ref_gates,
    w_gate, w_up, w_down, norm_gain, vocab_head, targets, seq_lengths, owners,
):
    plane = ("chip", "core")
    band = ("grp", "chip")
    everyone = ("grp", "chip", "core")
    core = lax.axis_index("core")
    device = lax.axis_index(everyone)
    devices = lax.axis_size(everyone)
    peers = lax.axis_size(band)
    experts = w_gate.shape[0] * lax.axis_size(plane)
    tokens, width = pol_hidden.shape
    capacity = tokens * pol_routes.shape[1] // experts + 2
    vocab_rows = vocab_head.shape[0]

    other_head = lax.ppermute(vocab_head, "core", ((0, 1), (1, 0)))
    wanted = lax.all_gather(targets, band, axis=0)
    wanted = jnp.concatenate((wanted, wanted), axis=1).reshape(1, -1)

    hidden = jnp.concatenate((pol_hidden, ref_hidden), axis=0)
    tables = jnp.concatenate(
        (gate_table(pol_routes, pol_gates, experts), gate_table(ref_routes, ref_gates, experts)),
        axis=0,
    )
    send = jnp.concatenate((hidden, tables), axis=1)
    plane_rows = lax.all_gather(send, plane, axis=0, tiled=True)
    place = lax.axis_index(plane).reshape(1)
    keep, give = expert_sums(
        place, plane_rows, w_gate, w_up, w_down, tokens, capacity, width, experts
    )
    parts = keep + lax.ppermute(give, "core", ((0, 1), (1, 0)))
    parts = lax.all_to_all(parts, "chip", split_axis=0, concat_axis=0, tiled=True)
    mixed = hidden.astype(jnp.float32) + jnp.sum(parts, axis=0)
    scale = lax.rsqrt(jnp.mean(mixed * mixed, axis=1, keepdims=True) + 1e-06)
    normed = (mixed * scale * norm_gain).astype(jnp.bfloat16)

    rows = lax.all_gather(normed, band, axis=0, tiled=True)
    base = jnp.stack((device, device + 1 - 2 * core)).astype(jnp.int32) * vocab_rows
    lse, hit = head_stats(base, wanted, rows, vocab_head, other_head)
    stats = jnp.stack((lse.reshape(peers, -1), hit.reshape(peers, -1)), axis=1)
    stats = lax.all_to_all(stats, band, split_axis=0, concat_axis=0, tiled=True)
    top = jnp.max(stats[:, 0], axis=0)
    whole = top + jnp.log(jnp.sum(jnp.exp(stats[:, 0] - top[None]), axis=0))
    logprob = jnp.sum(stats[:, 1], axis=0) - whole
    token_ratio = logprob[:tokens] - logprob[tokens:]

    ends = jnp.cumsum(seq_lengths)
    offsets = ends - seq_lengths
    positions = device * tokens + jnp.arange(tokens, dtype=jnp.int32)
    inside = (positions[None, :] >= offsets[:, None]) & (positions[None, :] < ends[:, None])
    share = jnp.sum(jnp.where(inside, token_ratio[None, :], 0.0), axis=1)
    share = share / seq_lengths.astype(jnp.float32)
    to_owner = owners[None, :] == jnp.arange(devices, dtype=jnp.int32)[:, None]
    outgoing = jnp.sum(jnp.where(to_owner, share[None, :], 0.0), axis=1).reshape(devices, 1)
    incoming = lax.all_to_all(outgoing, everyone, split_axis=0, concat_axis=0, tiled=True)
    return (token_ratio, jnp.sum(incoming).reshape(1))


def solution(mesh):
    names = ("grp", "chip", "core")
    groups, plane = mesh.devices.shape
    fine = Mesh(mesh.devices.reshape(groups, plane // 2, 2), names)
    return jax.shard_map(
        local,
        mesh=fine,
        in_specs=(
            P(names, None), P(names, None), P(names, None), P(names, None),
            P(names, None), P(names, None),
            P(names[1:], None, None), P(names[1:], None, None), P(names[1:], None, None),
            P(), P(names, None), P(names), P(), P(),
        ),
        out_specs=(P(names), P(names)),
        check_vma=False,
    )
```

time: 373 us -> 203 us (0.54)
  blocking collectives: 111 us -> 23.3 us
  matrix products: 64.3 us -> 0 us
  Pallas kernels: 0 us -> 37.7 us
  waiting for transfers between devices: 136 us -> 102 us
  local copies, waits for them, and re-layouts: 14.9 us -> 6.79 us
  starting transfers between devices: 16 us -> 8.95 us
  other arithmetic: 14.6 us -> 8.79 us
    all_gather x5 -> x0, blocking collectives: 65 us -> none  [the longest x3 35.8 us: joined_2(): pieces = jax.tree.map(lambda part: lax.all_gather(part, axis), value)]
    dot_general x9 -> x0, matrix products: 64.3 us -> none  [the longest x2 47.5 us: vocab_stats(): jnp.einsum('td,vd->tv', row_block, weights, preferred_element_type=jnp.fl...]
    all_to_all x4 -> x2, waiting for transfers between devices: 67 us -> 23.8 us  [the longest x1 16.7 us: local(): lax.all_to_all(parts, 'chip', split_axis=0, concat_axis=0, tiled=True)]
    psum x1 -> x0, blocking collectives: 37.8 us -> none  [local(): sums = lax.psum(partial_value, ('grp', 'ep'))]
    pallas_call x0 -> x2, Pallas kernels: none -> 37.7 us  [the longest x1 19.5 us: head_stats(): pl.pallas_call(head_kernel, out_shape=(line, line), grid_spec=pltpu.Prefe...]
    reduce_sum x6 -> x8, other arithmetic: 12.7 us -> 1.52 us  [the longest x1 0.63 us: local(): return (token_ratio, jnp.sum(incoming).reshape(1))]
    all_to_all x0 -> x1, blocking collectives: none -> 8.83 us  [local(): lax.all_to_all(outgoing, everyone, split_axis=0, concat_axis=0, tiled=True)]
    all_to_all x4 -> x2, starting transfers between devices: 16 us -> 8.24 us  [the longest x1 4.57 us: local(): stats = lax.all_to_all(stats, band, split_axis=0, concat_axis=0, tiled=True)]
  transfers between devices with their start and end apart: 5 -> 6, of which waited for: 5 -> 5; matrix products, arithmetic and copies ran while one was open for 9% -> 2% of each run, Pallas kernels for 0% -> 0%
where the time goes in v1:
time: 203 us; the launch traced here: 202 us
  waiting for transfers between devices  102 us (50%)
  Pallas kernels  37.7 us (19%)
  blocking collectives  23.3 us (11%)
  between operations  14.8 us (7%)
  starting transfers between devices  8.95 us (4%)
  other arithmetic  8.79 us (4%)
  local copies, waits for them, and re-layouts  6.79 us (3%)
    all_gather x1, waiting for transfers between devices, local(): rows = lax.all_gather(normed, band, axis=0, tiled=True)  46.6 us
    all_gather x1, waiting for transfers between devices, local(): plane_rows = lax.all_gather(send, plane, axis=0, tiled=True)  28.1 us
    pallas_call x1, Pallas kernels, head_stats(): pl.pallas_call(head_kernel, out_shape=(line, line), grid_spec=pltpu.Prefe...  19.5 us
    pallas_call x1, Pallas kernels, expert_sums(): pl.pallas_call(functools.partial(expert_kernel, block, slots, width, expe...  18.2 us
    all_to_all x1, waiting for transfers between devices, local(): lax.all_to_all(parts, 'chip', split_axis=0, concat_axis=0, tiled=True)  16.7 us
    unnamed x1, blocking collectives  14.4 us
    all_to_all x1, blocking collectives, local(): lax.all_to_all(outgoing, everyone, split_axis=0, concat_axis=0, tiled=True)  8.83 us
    all_to_all x1, waiting for transfers between devices, local(): stats = lax.all_to_all(stats, band, split_axis=0, concat_axis=0, tiled=True)  7.04 us
  transfers between devices with their start and end apart: 6, of which 5 were waited for; matrix products, arithmetic and copies ran while one was open for 2% of the time, Pallas kernels for 0%

profile of v1, /device:TPU:0, one launch (start us, length us, event | category | flops | bytes accessed | tf_op | source)
XLA Modules:
  0.0 201.9 jit_solution(5145186966410798191)
XLA Ops:
  7.2 0.0 all-gather.4.cloned.1.call-start
  7.2 0.8 copy.36
  8.0 0.8 copy.37
  8.7 0.8 copy.34
  9.5 0.8 copy.35
  10.3 0.9 constant_dynamic-update-slice_fusion.1
  11.2 0.2 select_reduce_fusion
  11.3 0.2 select_reduce_fusion.1
  11.5 0.9 constant_dynamic-update-slice_fusion
  12.4 0.7 maximum_maximum_fusion
  13.2 0.0 all-gather.4.cloned.1.call-update
  13.2 28.1 %all-gather.4.cloned.1.call-done.x_ref = bf16[640,1152]{1,0:T(8,128)(2,1)} async-done(((bf16[80,1152]{1,0:T(8,128)(2,1)}), bf16[640,1152]{1,0:T(8,128)(2,1)}) %all-gather.4.cloned.1.call-update) | async-done | bytes 1474576 | tf_op jit(solution)/shard_map/all_gather | solution.py:262
  41.3 18.2 %shard_map.149 = (f32[4,80,1024]{2,1,0:T(8,128)}, f32[4,80,1024]{2,1,0:T(8,128)}) custom-call(s32[1]{0:T(128)} %bitcast.3.place_ref, bf16[640,1152]{1,0:T(8,128)(2,1)} %all-gather.4.cloned.1.call-done.x_ref, bf16[8,1024,384]{2,1,0:T(8,128)(2,1)} %gate_ref.1, bf16[8,1024,384]{2,1,0:T(8,128)(2,1)} %up_ref.1, bf16[8,384,1024]{2,1,0:T(8,128)(2,1)} %down_ref.1), custom_call_target="tpu_custom_call" | custom-call | flops 6442450944 | bytes 21659648 | tf_op jit(solution)/shard_map/pallas_call | solution.py:105
  59.5 0.3 collective-permute-start
  59.8 3.0 %collective-permute-done = f32[4,80,1024]{2,1,0:T(8,128)S(1)} collective-permute-done((f32[4,80,1024]{2,1,0:T(8,128)}, f32[4,80,1024]{2,1,0:T(8,128)S(1)}, u32[]{:S(2)}, u32[]{:S(2)}) %collective-permute-start) | collective-permute-done | bytes 1310752 | tf_op jit(solution)/shard_map/ppermute | solution.py:267
  62.7 2.7 %add.43 = f32[4,80,1024]{2,1,0:T(8,128)} add(f32[4,80,1024]{2,1,0:T(8,128)} %get-tuple-element.6, f32[4,80,1024]{2,1,0:T(8,128)S(1)} %collective-permute-done) | non-fusion elementwise | flops 327680 | bytes 3932160 | tf_op jit(solution)/shard_map/add | solution.py:267
  65.4 3.7 %all-to-all-start = ((f32[4,80,1024]{2,1,0:T(8,128)}), f32[4,80,1024]{2,1,0:T(8,128)S(1)}, u32[]{:S(2)}, u32[]{:S(2)}) async-start(f32[4,80,1024]{2,1,0:T(8,128)} %add.43), calls=%async_computation | async-start | bytes 2621440 | tf_op jit(solution)/shard_map/all_to_all | solution.py:268
  69.1 0.0 all-gather.6.cloned.1.call-start
  69.1 0.3 collective-permute-start.1
  69.5 16.7 %all-to-all-done = f32[4,80,1024]{2,1,0:T(8,128)S(1)} async-done(((f32[4,80,1024]{2,1,0:T(8,128)}), f32[4,80,1024]{2,1,0:T(8,128)S(1)}, u32[]{:S(2)}, u32[]{:S(2)}) %all-to-all-start) | async-done | bytes 1310752 | tf_op jit(solution)/shard_map/all_to_all | solution.py:268
  86.2 0.1 reduce_sum.83
  86.3 0.1 multiply_reduce_fusion
  86.5 0.8 multiply_convert_fusion
  87.3 0.6 dynamic-slice
  88.6 0.2 dynamic-update-slice
  88.8 14.4 %all-reduce = s32[640]{0:T(1024)S(1)} all-reduce(s32[640]{0:T(1024)S(1)} %dynamic-update-slice), channel_id=2, replica_groups=mesh['grp'=4,'chip'=4,'core'=2] {'grp','chip'}, use_global_device_ids=true, to_apply=%add | all-reduce | flops 640 | bytes 5120
  103.2 0.1 reshape.67
  103.3 0.1 pad_add_fusion
  103.4 0.7 reshape.62.wanted_ref
  104.1 0.6 add_multiply_fusion.base_ref
  104.7 46.6 %all-gather.6.cloned.1.call-done.x_ref = bf16[1280,1024]{1,0:T(8,128)(2,1)} async-done(((bf16[80,1024]{1,0:T(8,128)(2,1)}), bf16[1280,1024]{1,0:T(8,128)(2,1)}) %all-gather.6.cloned.1.call-update) | async-done | bytes 2621456 | tf_op jit(solution)/shard_map/all_gather | solution.py:273
  151.4 19.5 %shard_map.150 = (f32[1,1280]{1,0:T(1,128)}, f32[1,1280]{1,0:T(1,128)}) custom-call(s32[2]{0:T(128)} %add_multiply_fusion.base_ref, s32[1,1280]{1,0:T(1,128)} %reshape.62.wanted_ref, bf16[1280,1024]{1,0:T(8,128)(2,1)} %all-gather.6.cloned.1.call-done.x_ref, bf16[2432,1024]{1,0:T(8,128)(2,1)} %head_a.1, bf16[2432,1024]{1,0:T(8,128)(2,1)} %collective-permute-done.1.head_b), custom_call_target="tpu_custom_call" | custom-call | flops 12750684160 | bytes 12582912 | tf_op jit(solution)/shard_map/pallas_call | solution.py:195
  170.9 0.7 reduce.4
  171.6 0.1 stack_reshape.6
  171.7 0.7 reduce.5
  172.4 0.1 stack_reshape.7
  172.5 0.6 pad_maximum_fusion
  173.1 4.6 %all-to-all-start.1 = ((f32[16,2,80]{2,1,0:T(2,128)}), f32[16,2,80]{2,1,0:T(2,128)S(1)}, u32[]{:S(2)}, u32[]{:S(2)}) async-start(f32[16,2,80]{2,1,0:T(2,128)} %pad_maximum_fusion), calls=%async_computation.1 | async-start | bytes 32768 | tf_op jit(solution)/shard_map/all_to_all | solution.py:277
  177.7 0.1 copy.40
  177.8 0.1 reduce-window.8
  177.8 0.1 reduce.6
  177.9 7.0 %all-to-all-done.1 = f32[16,2,80]{2,1,0:T(2,128)S(1)} async-done(((f32[16,2,80]{2,1,0:T(2,128)}), f32[16,2,80]{2,1,0:T(2,128)S(1)}, u32[]{:S(2)}, u32[]{:S(2)}) %all-to-all-start.1) | async-done | bytes 10272 | tf_op jit(solution)/shard_map/all_to_all | solution.py:277
  185.1 0.1 slice_subtract_fusion
  185.1 0.2 select_reduce_fusion.3
  185.3 0.1 select_reduce_fusion.2
  185.5 0.1 copy.41
  185.6 8.8 %all_to_all.19 = f32[32,1,1]{2,1,0:T(1,128)S(1)} all-to-all(f32[32,1,1]{2,1,0:T(1,128)S(1)} %copy.41), channel_id=1, replica_groups=mesh['grp'=4,'chip'=4,'core'=2] {'grp','chip','core'}, dimensions={0} | all-to-all | bytes 256 | tf_op jit(solution)/shard_map/all_to_all | solution.py:291
  194.4 0.6 reduce_sum.89
  (23 shorter events, 0.2 us)
Async XLA Ops:
  7.2 34.1 %all-gather.4.cloned.1.call-start = ((), (), s32[]{:S(2)}) async-start(), calls=%async_computation.3 | async-start | bytes 1658880 | tf_op jit(solution)/shard_map/all_gather | solution.py:262
  59.5 3.2 %collective-permute-start = (f32[4,80,1024]{2,1,0:T(8,128)}, f32[4,80,1024]{2,1,0:T(8,128)S(1)}, u32[]{:S(2)}, u32[]{:S(2)}) collective-permute-start(f32[4,80,1024]{2,1,0:T(8,128)} %get-tuple-element.7), channel_id=1, source_target_pairs={{0,1},{1,0},{2,3},{3,2},{4,5},{5,4},{6,7},{7,6},{8,9},{9,8},{10,11... | collective-permute-start | bytes 3932168 | tf_op jit(solution)/shard_map/ppermute | solution.py:267
  65.4 21.1 %copy-start = (f32[1024]{0:T(1024)S(1)}, f32[1024]{0:T(1024)}, u32[]{:S(2)}) copy-start(f32[1024]{0:T(1024)} %param.23) | copy-start | bytes 12292
  65.4 21.9 %copy-start.5 = (u32[32]{0:T(128)S(1)}, u32[32]{0:T(128)}, u32[]{:S(2)}) copy-start(u32[32]{0:T(128)} %constant.43) | copy-start | bytes 388
  65.4 23.1 %copy-start.3 = (s32[40]{0:T(128)S(1)}, s32[40]{0:T(128)}, u32[]{:S(2)}) copy-start(s32[40]{0:T(128)} %param.25) | copy-start | bytes 484
  65.4 20.8 %all-to-all-start = ((f32[4,80,1024]{2,1,0:T(8,128)}), f32[4,80,1024]{2,1,0:T(8,128)S(1)}, u32[]{:S(2)}, u32[]{:S(2)}) async-start(f32[4,80,1024]{2,1,0:T(8,128)} %add.43), calls=%async_computation | async-start | bytes 2621440 | tf_op jit(solution)/shard_map/all_to_all | solution.py:268
  69.1 82.3 %all-gather.6.cloned.1.call-start = ((), (), s32[]{:S(2)}) async-start(), calls=%async_computation.4 | async-start | bytes 2785280 | tf_op jit(solution)/shard_map/all_gather | solution.py:273
  69.1 35.6 %collective-permute-start.1 = (bf16[2432,1024]{1,0:T(8,128)(2,1)}, bf16[2432,1024]{1,0:T(8,128)(2,1)}, u32[]{:S(2)}, u32[]{:S(2)}) collective-permute-start(bf16[2432,1024]{1,0:T(8,128)(2,1)} %head_a.1), channel_id=1, source_target_pairs={{0,1},{1,0},{2,3},{3,2},{4,5},{5,4},{6,7},{7,6},{8,9},{9,8},{10,11... | collective-permute-start | bytes 14942216 | tf_op jit(solution)/shard_map/ppermute | solution.py:252
  104.7 72.9 %copy-start.1 = (s32[32]{0:T(128)S(1)}, s32[32]{0:T(128)}, u32[]{:S(2)}) copy-start(s32[32]{0:T(128)} %param.26) | copy-start | bytes 388
  104.7 80.6 %copy-start.4 = (s32[32]{0:T(128)S(1)}, s32[32]{0:T(128)}, u32[]{:S(2)}) copy-start(s32[32]{0:T(128)} %param.27) | copy-start | bytes 388
  173.1 11.9 %all-to-all-start.1 = ((f32[16,2,80]{2,1,0:T(2,128)}), f32[16,2,80]{2,1,0:T(2,128)S(1)}, u32[]{:S(2)}, u32[]{:S(2)}) async-start(f32[16,2,80]{2,1,0:T(2,128)} %pad_maximum_fusion), calls=%async_computation.1 | async-start | bytes 32768 | tf_op jit(solution)/shard_map/all_to_all | solution.py:277
  185.1 9.9 %copy-start.2 = (f32[40]{0:T(128)}, f32[40]{0:T(128)S(1)}, u32[]{:S(2)}) copy-start(f32[40]{0:T(128)S(1)} %slice_subtract_fusion) | copy-start | bytes 484
Sparse Core Ops, SparseCore 0:
  13.3 27.9 all-gather.3
  87.4 63.9 all-gather.5

commit v2 on v1

v2 whole, which is shorter than its diff:
```python
import functools
import math

import jax
import jax.numpy as jnp
from jax import lax
from jax.experimental import pallas as pl
from jax.experimental.pallas import tpu as pltpu
from jax.sharding import Mesh, PartitionSpec as P

MIB = 1 << 20
LOW = -1e30


def round_up(value, step):
    return -(-value // step) * step


def largest_tile(rows, limit, step):
    best = rows
    for tile in range(step, min(rows, limit) + 1, step):
        if rows % tile == 0:
            best = tile
    return best


def pack_kernel(pol_ref, ref_ref, pol_routes, ref_routes, pol_gates, ref_gates, out_ref, room):
    tokens, width = pol_ref.shape
    experts = (room.shape[1] - width) // 2
    parts = ((pol_ref, pol_routes, pol_gates), (ref_ref, ref_routes, ref_gates))
    for index, (hidden, routes, gates) in enumerate(parts):
        band = pl.ds(index * tokens, tokens)
        room[band, :width] = hidden[...].astype(jnp.float32)
        expert = lax.broadcasted_iota(jnp.int32, (experts, tokens), 0)
        dense = jnp.zeros((experts, tokens), jnp.float32)
        for k in range(routes.shape[0]):
            dense = jnp.where(expert == routes[pl.ds(k, 1), :], gates[pl.ds(k, 1), :], dense)
        high = dense.astype(jnp.bfloat16).astype(jnp.float32)
        table = jnp.concatenate((high, dense - high), axis=0)
        room[band, width:] = table.T
    out_ref[...] = room[...].astype(jnp.bfloat16)


def pack_rows(pol_hidden, ref_hidden, pol_routes, ref_routes, pol_gates, ref_gates, experts):
    tokens, width = pol_hidden.shape
    shape = (2 * tokens, width + 2 * experts)
    return pl.pallas_call(
        pack_kernel,
        out_shape=jax.ShapeDtypeStruct(shape, jnp.bfloat16),
        scratch_shapes=[pltpu.VMEM(shape, jnp.float32)],
        compiler_params=pltpu.CompilerParams(vmem_limit_bytes=16 * MIB),
    )(pol_hidden, ref_hidden, pol_routes.T, ref_routes.T, pol_gates.T, ref_gates.T)


def expert_kernel(block, slots, width, experts, chips, place_ref, *refs):
    count = 2 * chips
    blocks, refs = refs[:count], refs[count:]
    gate_ref, up_ref, down_ref, keep_ref, give_ref = refs[:5]
    rows_in, table, pick, mix_hi, mix_lo, picked, made = refs[5:]
    step = pl.program_id(0)
    last = pl.num_programs(0) - 1
    rows = rows_in.shape[0]
    share = rows // count
    local_experts = pick.shape[0] // slots
    chip, core = place_ref[0], place_ref[1]

    @pl.when(step == 0)
    def _():
        for index, ref in enumerate(blocks):
            owner = 2 * (chip ^ (index % chips)) + (core ^ (index // chips))
            rows_in[pl.ds(pl.multiple_of(owner * share, 16), share), :] = ref[...]
        gates = rows_in[:, width:].astype(jnp.float32).T
        hits = (gates > 0.0).astype(jnp.bfloat16)
        span = math.gcd(rows, 16 * block)
        before = lax.broadcasted_iota(jnp.int32, (span, span), 0)
        after = lax.broadcasted_iota(jnp.int32, (1, span), 1)
        first = after - after % block
        order = ((before < after) & (before >= first)).astype(jnp.bfloat16)
        per_block = slots // (rows // block)
        for start in range(0, rows, span):
            band = slice(start, start + span)
            rank = jnp.dot(hits[:, band], order, preferred_element_type=jnp.float32)
            slot = rank + ((start + after) // block * per_block).astype(jnp.float32)
            table[0, :, band] = jnp.where(gates[:, band] > 0.0, slot, -1.0)
        table[1] = gates
        spot = lax.broadcasted_iota(jnp.int32, (slots, rows), 0).astype(jnp.float32)
        for e in range(local_experts):
            row = (2 * chip + core) * local_experts + e
            chosen = table[0, pl.ds(row, 1), :] == spot
            band = pl.ds(e * slots, slots)
            pick[band, :] = jnp.where(chosen, 1.0, 0.0).astype(jnp.bfloat16)
            mix_hi[band, :] = jnp.where(chosen, table[1, pl.ds(row, 1), :], 0.0).astype(
                jnp.bfloat16
            )
            mix_lo[band, :] = jnp.where(
                chosen, table[1, pl.ds(row + experts, 1), :], 0.0
            ).astype(jnp.bfloat16)
        picked[...] = jnp.dot(
            pick[...], rows_in[:, :width], preferred_element_type=jnp.float32
        ).astype(jnp.bfloat16)

    band = pl.ds(pl.multiple_of(step * slots, slots), slots)
    mine = picked[band, :]
    gate_act = jnp.dot(mine, gate_ref[0], preferred_element_type=jnp.float32)
    up_act = jnp.dot(mine, up_ref[0], preferred_element_type=jnp.float32)
    inner = (gate_act / (1.0 + jnp.exp(-gate_act)) * up_act).astype(jnp.bfloat16)
    made[band, :] = jnp.dot(inner, down_ref[0], preferred_element_type=jnp.float32).astype(
        jnp.bfloat16
    )

    @pl.when(step == last)
    def _():
        over_slots = (((0,), (0,)), ((), ()))
        span = math.gcd(rows, 16 * block)
        for start in range(0, rows, span):
            band = pl.ds(start, span)
            total = lax.dot_general(
                mix_hi[:, band], made[...], over_slots, preferred_element_type=jnp.float32
            )
            total += lax.dot_general(
                mix_lo[:, band], made[...], over_slots, preferred_element_type=jnp.float32
            )
            for index in range(span // share):
                c, owner = divmod(start // share + index, 2)
                target = total[index * share:(index + 1) * share]

                @pl.when(core == owner)
                def _():
                    keep_ref[c ^ chip] = target

                @pl.when(core != owner)
                def _():
                    give_ref[c ^ chip] = target


def expert_sums(place, blocks, w_gate, w_up, w_down, block, capacity, width, experts):
    count = len(blocks)
    share, wide = blocks[0].shape
    rows = count * share
    local_experts, _, hidden = w_gate.shape
    slots = round_up(capacity, 8) * (rows // block)
    every = local_experts * slots
    half = jax.ShapeDtypeStruct((count // 2, share, width), jnp.float32)
    whole = pl.BlockSpec(
        (share, wide), lambda e, place: (0, 0), pipeline_mode=pl.Buffered(1)
    )
    return pl.pallas_call(
        functools.partial(expert_kernel, block, slots, width, experts, count // 2),
        out_shape=(half, half),
        grid_spec=pltpu.PrefetchScalarGridSpec(
            num_scalar_prefetch=1,
            grid=(local_experts,),
            in_specs=[whole] * count + [
                pl.BlockSpec((1, width, hidden), lambda e, place: (e, 0, 0)),
                pl.BlockSpec((1, width, hidden), lambda e, place: (e, 0, 0)),
                pl.BlockSpec((1, hidden, width), lambda e, place: (e, 0, 0)),
            ],
            out_specs=(
                pl.BlockSpec(
                    half.shape, lambda e, place: (0, 0, 0), pipeline_mode=pl.Buffered(1)
                ),
                pl.BlockSpec(
                    half.shape, lambda e, place: (0, 0, 0), pipeline_mode=pl.Buffered(1)
                ),
            ),
            scratch_shapes=[
                pltpu.VMEM((rows, wide), jnp.bfloat16),
                pltpu.VMEM((2, wide - width, rows), jnp.float32),
                pltpu.VMEM((every, rows), jnp.bfloat16),
                pltpu.VMEM((every, rows), jnp.bfloat16),
                pltpu.VMEM((every, rows), jnp.bfloat16),
                pltpu.VMEM((every, width), jnp.bfloat16),
                pltpu.VMEM((every, width), jnp.bfloat16),
            ],
        ),
        compiler_params=pltpu.CompilerParams(vmem_limit_bytes=58 * MIB),
        cost_estimate=pl.CostEstimate(
            flops=2 * every * width * (3 * hidden + 3 * rows),
            bytes_accessed=w_gate.size * 6 + rows * wide * 2 + rows * width * 4,
            transcendentals=every * hidden,
        ),
    )(place, *blocks, w_gate, w_up, w_down)


def pair_kernel(keep_ref, came_ref, own_ref, *sends):
    own_ref[...] = keep_ref[0] + came_ref[0]
    for index, send in enumerate(sends):
        send[...] = keep_ref[index + 1] + came_ref[index + 1]


def pair_sums(keep, came):
    chips, share, width = keep.shape
    own = jax.ShapeDtypeStruct((share, width), jnp.float32)
    return pl.pallas_call(
        pair_kernel,
        out_shape=(own,) * chips,
        compiler_params=pltpu.CompilerParams(vmem_limit_bytes=32 * MIB),
    )(keep, came)


def norm_kernel(hidden_ref, gain_ref, own_ref, *refs):
    width = own_ref.shape[1]
    mixed = hidden_ref[:, :width].astype(jnp.float32) + own_ref[...]
    for ref in refs[:-1]:
        mixed += ref[...]
    scale = lax.rsqrt(jnp.mean(mixed * mixed, axis=1, keepdims=True) + 1e-06)
    refs[-1][...] = (mixed * scale * gain_ref[...]).astype(jnp.bfloat16)


def norm_rows(hidden, gain, own, others):
    return pl.pallas_call(
        norm_kernel,
        out_shape=jax.ShapeDtypeStruct(own.shape, jnp.bfloat16),
        compiler_params=pltpu.CompilerParams(vmem_limit_bytes=16 * MIB),
    )(hidden, gain.reshape(1, -1), own, *others)


def head_kernel(count, spots_ref, wanted_ref, *refs):
    blocks, refs = refs[:count], refs[count:]
    head_a, head_b, out_ref, rows_in, peak, total, found, logits_a, logits_b = refs
    step = pl.program_id(0)
    last = pl.num_programs(0) - 1
    tile, columns = logits_a.shape
    lane_band = 128
    share = columns // out_ref.shape[0]
    base_a, base_b = spots_ref[0], spots_ref[1]

    def product(head_ref, logits):
        logits[...] = lax.dot_general(
            head_ref[...], rows_in[...], (((1,), (1,)), ((), ())),
            preferred_element_type=jnp.float32,
        )

    def absorb(logits, first):
        row = lax.broadcasted_iota(jnp.int32, (tile, lane_band), 0)
        for start in range(0, columns, lane_band):
            band = pl.ds(start, lane_band)
            values = logits[:, band]
            old = peak[:, band]
            new = jnp.maximum(old, jnp.max(values.reshape(tile // 8, 8, lane_band), axis=0))
            grown = jnp.exp(values.reshape(tile // 8, 8, lane_band) - new[None])
            total[:, band] = total[:, band] * jnp.exp(old - new) + jnp.sum(grown, axis=0)
            same = row == wanted_ref[:, band] - first
            kept = jnp.where(same, values, 0.0).reshape(tile // 8, 8, lane_band)
            found[:, band] += jnp.sum(kept, axis=0)
            peak[:, band] = new

    @pl.when(step == 0)
    def _():
        start = 0
        for ref in blocks:
            rows_in[start:start + ref.shape[0], :] = ref[...]
            start += ref.shape[0]
        peak[...] = jnp.full_like(peak, LOW)
        total[...] = jnp.zeros_like(total)
        found[...] = jnp.zeros_like(found)
        logits_b[...] = jnp.full_like(logits_b, LOW)

    product(head_a, logits_a)
    absorb(logits_b, jnp.where(step == 0, -(1 << 28), base_b + (step - 1) * tile))
    product(head_b, logits_b)
    absorb(logits_a, base_a + step * tile)

    @pl.when(step == last)
    def _():
        absorb(logits_b, base_b + step * tile)
        top = jnp.max(peak[...], axis=0, keepdims=True)
        full = jnp.sum(total[...] * jnp.exp(peak[...] - top), axis=0, keepdims=True)
        lse = top + jnp.log(full)
        hit = jnp.sum(found[...], axis=0, keepdims=True)
        for index in range(out_ref.shape[0]):
            band = slice(index * share, (index + 1) * share)
            spot = spots_ref[2 + index]
            out_ref[spot, 0:1, :] = lse[:, band]
            out_ref[spot, 1:2, :] = hit[:, band]


def head_stats(spots, wanted, blocks, head_a, head_b, share):
    rows = sum(block.shape[0] for block in blocks)
    width = head_a.shape[1]
    tile = largest_tile(head_a.shape[0], 608 * 1280 // rows, 16)
    steps = head_a.shape[0] // tile
    return pl.pallas_call(
        functools.partial(head_kernel, len(blocks)),
        out_shape=jax.ShapeDtypeStruct((rows // share, 2, share), jnp.float32),
        grid_spec=pltpu.PrefetchScalarGridSpec(
            num_scalar_prefetch=1,
            grid=(steps,),
            in_specs=[pl.BlockSpec((1, rows), lambda s, spots: (0, 0))] + [
                pl.BlockSpec(block.shape, lambda s, spots: (0, 0), pipeline_mode=pl.Buffered(1))
                for block in blocks
            ] + [
                pl.BlockSpec((tile, width), lambda s, spots: (s, 0)),
                pl.BlockSpec((tile, width), lambda s, spots: (s, 0)),
            ],
            out_specs=pl.BlockSpec((rows // share, 2, share), lambda s, spots: (0, 0, 0)),
            scratch_shapes=[
                pltpu.VMEM((rows, width), jnp.bfloat16),
                pltpu.VMEM((8, rows), jnp.float32),
                pltpu.VMEM((8, rows), jnp.float32),
                pltpu.VMEM((8, rows), jnp.float32),
                pltpu.VMEM((tile, rows), jnp.float32),
                pltpu.VMEM((tile, rows), jnp.float32),
            ],
        ),
        compiler_params=pltpu.CompilerParams(vmem_limit_bytes=58 * MIB),
        cost_estimate=pl.CostEstimate(
            flops=4 * rows * width * head_a.shape[0],
            bytes_accessed=head_a.size * 4 + rows * width * 2,
            transcendentals=2 * rows * head_a.shape[0],
        ),
    )(spots, wanted, *blocks, head_a, head_b)


def combine(parts):
    top = functools.reduce(jnp.maximum, [part[:, 0] for part in parts])
    total = sum(jnp.exp(part[:, 0] - top) for part in parts)
    return top + jnp.log(total), sum(part[:, 1] for part in parts)


def across(value, offset):
    chips = lax.axis_size("chip")
    return lax.ppermute(value, "chip", [(c, c ^ offset) for c in range(chips)])


def along(value, offset):
    groups = lax.axis_size("grp")
    return lax.ppermute(value, "grp", [(g, (g + offset) % groups) for g in range(groups)])


def partner(value):
    return lax.ppermute(value, "core", ((0, 1), (1, 0)))


def local(
    pol_hidden, ref_hidden, pol_routes, ref_routes, pol_gates, ref_gates,
    w_gate, w_up, w_down, norm_gain, vocab_head, targets, seq_lengths, owners,
):
    chip, core, group = lax.axis_index("chip"), lax.axis_index("core"), lax.axis_index("grp")
    chips, groups = lax.axis_size("chip"), lax.axis_size("grp")
    device = (group * chips + chip) * 2 + core
    experts = w_gate.shape[0] * chips * 2
    tokens, width = pol_hidden.shape
    share = 2 * tokens
    capacity = tokens * pol_routes.shape[1] // experts + 2
    vocab_rows = vocab_head.shape[0]
    offsets = range(1, chips)

    send = pack_rows(
        pol_hidden, ref_hidden, pol_routes, ref_routes, pol_gates, ref_gates, experts
    )
    plane = [send] + [across(send, d) for d in offsets]
    plane = plane + [partner(rows) for rows in plane]

    goal = targets.reshape(1, tokens)
    goal = jnp.concatenate([goal] + [along(goal, k) for k in range(1, groups)], axis=0)
    goal = jnp.stack([goal] + [across(goal, d) for d in offsets])
    wanted = jnp.concatenate((goal, goal), axis=2).reshape(1, -1)
    other_head = partner(vocab_head)

    place = jnp.stack((chip, core)).astype(jnp.int32)
    keep, give = expert_sums(place, plane, w_gate, w_up, w_down, tokens, capacity, width, experts)
    own, *sends = pair_sums(keep, partner(give))
    came = [across(rows, d) for d, rows in zip(offsets, sends)]
    normed = norm_rows(send, norm_gain, own, came)

    column = [normed] + [along(normed, k) for k in range(1, groups)]
    if chips == 4:
        near = [across(rows, 1) for rows in column]
        far = [across(rows, 2) for rows in column]
        half = groups // 2
        cross = [across(rows, 2) for rows in near[:half]] + [
            across(rows, 1) for rows in far[half:]
        ]
        blocks = column + near + far + cross
    else:
        column = jnp.concatenate(column, axis=0)
        blocks = [column] + [across(column, d) for d in offsets]
    home = (group - jnp.arange(groups, dtype=jnp.int32)) % groups
    spots = home[None, :] * chips + (chip ^ jnp.arange(chips, dtype=jnp.int32))[:, None]
    base = jnp.stack((device, device + 1 - 2 * core)).astype(jnp.int32) * vocab_rows
    rows = groups * chips * share
    if rows <= 1280:
        spots = jnp.concatenate((base, spots.reshape(-1)))
        stats = head_stats(spots, wanted, blocks, vocab_head, other_head, share)
    else:
        lines = groups * share
        pieces = [
            head_stats(
                jnp.concatenate((base, jnp.arange(groups, dtype=jnp.int32))),
                wanted[:, d * lines:(d + 1) * lines], [block], vocab_head, other_head, share,
            )
            for d, block in enumerate(blocks)
        ]
        pieces = jnp.concatenate(pieces, axis=0)
        stats = jnp.zeros_like(pieces).at[spots.reshape(-1)].set(pieces)

    lse, hit = combine([stats] + [along(stats, k) for k in range(1, groups)])
    stats = jnp.stack((lse, hit), axis=1)
    lse, hit = combine([stats] + [across(stats, d) for d in offsets])
    logprob = hit - lse
    ratio = logprob[:, :tokens] - logprob[:, tokens:]
    other = partner(ratio)
    token_ratio = lax.dynamic_index_in_dim(ratio, group * chips + chip, keepdims=False)

    mine = owners == device
    ends = jnp.cumsum(seq_lengths)
    length = jnp.sum(jnp.where(mine, seq_lengths, 0))
    end = jnp.sum(jnp.where(mine, ends, 0))
    row = jnp.arange(groups * chips, dtype=jnp.int32)[:, None]
    lane = jnp.arange(tokens, dtype=jnp.int32)[None, :]
    position = (2 * row + core) * tokens + lane
    inside = (position >= end - length) & (position < end)
    position = (2 * row + 1 - core) * tokens + lane
    inside_other = (position >= end - length) & (position < end)
    mean = jnp.sum(jnp.where(inside, ratio, 0.0) + jnp.where(inside_other, other, 0.0))
    return (token_ratio, (mean / length.astype(jnp.float32)).reshape(1))


def solution(mesh):
    names = ("grp", "chip", "core")
    groups, plane = mesh.devices.shape
    fine = Mesh(mesh.devices.reshape(groups, plane // 2, 2), names)
    return jax.shard_map(
        local,
        mesh=fine,
        in_specs=(
            P(names, None), P(names, None), P(names, None), P(names, None),
            P(names, None), P(names, None),
            P(names[1:], None, None), P(names[1:], None, None), P(names[1:], None, None),
            P(), P(names, None), P(names), P(), P(),
        ),
        out_specs=(P(names), P(names)),
        check_vma=False,
    )
```

time: 203 us -> 162 us (0.80)
  waiting for transfers between devices: 102 us -> 58.8 us
  starting transfers between devices: 8.95 us -> 43.9 us
  blocking collectives: 23.3 us -> 0 us
  between operations: 14.8 us -> 4.72 us
  other arithmetic: 8.79 us -> 3.73 us
  local copies, waits for them, and re-layouts: 6.79 us -> 11.3 us
    all_gather x2 -> x0, waiting for transfers between devices: 74.8 us -> none  [the longest x1 46.6 us: local(): rows = lax.all_gather(normed, band, axis=0, tiled=True)]
    ppermute x2 -> x40, waiting for transfers between devices: 2.97 us -> 58.8 us  [the longest x24 41.8 us: across(): return lax.ppermute(value, 'chip', [(c, c ^ offset) for c in range(chips)])]
    ppermute x2 -> x40, starting transfers between devices: 0.63 us -> 43.9 us  [the longest x24 26.1 us: across(): return lax.ppermute(value, 'chip', [(c, c ^ offset) for c in range(chips)])]
    all_to_all x2 -> x0, waiting for transfers between devices: 23.8 us -> none  [the longest x1 16.7 us: local(): lax.all_to_all(parts, 'chip', split_axis=0, concat_axis=0, tiled=True)]
    unnamed x1 -> x0, blocking collectives: 14.4 us -> none
    all_to_all x1 -> x0, blocking collectives: 8.83 us -> none  [local(): lax.all_to_all(outgoing, everyone, split_axis=0, concat_axis=0, tiled=True)]
    all_to_all x2 -> x0, starting transfers between devices: 8.24 us -> none  [the longest x1 4.57 us: local(): stats = lax.all_to_all(stats, band, split_axis=0, concat_axis=0, tiled=True)]
    unnamed x20 -> x72, local copies, waits for them, and re-layouts: 4.8 us -> 8.43 us
  transfers between devices with their start and end apart: 6 -> 40, of which waited for: 5 -> 23; matrix products, arithmetic and copies ran while one was open for 2% -> 3% of each run, Pallas kernels for 0% -> 12%
where the time goes in v2:
time: 162 us; the launch traced here: 161 us
  waiting for transfers between devices  58.8 us (36%)
  starting transfers between devices  43.9 us (27%)
  Pallas kernels  39 us (24%)
  local copies, waits for them, and re-layouts  11.3 us (7%)
  between operations  4.72 us (3%)
  other arithmetic  3.73 us (2%)
    ppermute x24, waiting for transfers between devices, across(): return lax.ppermute(value, 'chip', [(c, c ^ offset) for c in range(chips)])  41.8 us
    ppermute x24, starting transfers between devices, across(): return lax.ppermute(value, 'chip', [(c, c ^ offset) for c in range(chips)])  26.1 us
    pallas_call x1, Pallas kernels, head_stats(): pl.pallas_call(functools.partial(head_kernel, len(blocks)), out_shape=jax...  19.8 us
    pallas_call x1, Pallas kernels, expert_sums(): pl.pallas_call(functools.partial(expert_kernel, block, slots, width, expe...  18.8 us
    ppermute x9, starting transfers between devices, along(): lax.ppermute(value, 'grp', [(g, (g + offset) % groups) for g in range(gro...  16.6 us
    ppermute x9, waiting for transfers between devices, along(): lax.ppermute(value, 'grp', [(g, (g + offset) % groups) for g in range(gro...  12.7 us
    unnamed x72, local copies, waits for them, and re-layouts  8.43 us
    ppermute x7, waiting for transfers between devices, partner(): return lax.ppermute(value, 'core', ((0, 1), (1, 0)))  4.27 us
  transfers between devices with their start and end apart: 40, of which 23 were waited for; matrix products, arithmetic and copies ran while one was open for 3% of the time, Pallas kernels for 12%

profile of v2, /device:TPU:0, one launch (start us, length us, event | category | flops | bytes accessed | tf_op | source)
XLA Modules:
  0.0 161.4 jit_solution(199649401379010069)
XLA Ops:
  1.2 0.9 copy-done.4
  2.0 0.9 copy-done.5
  5.8 2.6 %collective-permute-start.6 = (bf16[80,1152]{1,0:T(8,128)(2,1)S(1)}, bf16[80,1152]{1,0:T(8,128)(2,1)S(1)}, u32[]{:S(2)}, u32[]{:S(2)}) collective-permute-start(bf16[80,1152]{1,0:T(8,128)(2,1)S(1)} %shard_map.149.refs_0_.hidden_ref), channel_id=1, source_target_pairs={{0,2},{2,0},{4,6},{6,4},{1,3},{3,1},{5,7},{7,5},{8,10},{10,8},{12,... | collective-permute-start | bytes 552968 | tf_op jit(solution)/shard_map/ppermute | solution.py:323
  8.4 1.5 collective-permute-start.7
  9.9 3.9 %collective-permute-done.6.refs_1_ = bf16[80,1152]{1,0:T(8,128)(2,1)S(1)} collective-permute-done((bf16[80,1152]{1,0:T(8,128)(2,1)S(1)}, bf16[80,1152]{1,0:T(8,128)(2,1)S(1)}, u32[]{:S(2)}, u32[]{:S(2)}) %collective-permute-start.6) | collective-permute-done | bytes 184352 | tf_op jit(solution)/shard_map/ppermute | solution.py:323
  13.8 5.2 %collective-permute-done.7.refs_2_ = bf16[80,1152]{1,0:T(8,128)(2,1)S(1)} collective-permute-done((bf16[80,1152]{1,0:T(8,128)(2,1)S(1)}, bf16[80,1152]{1,0:T(8,128)(2,1)S(1)}, u32[]{:S(2)}, u32[]{:S(2)}) %collective-permute-start.7) | collective-permute-done | bytes 184352 | tf_op jit(solution)/shard_map/ppermute | solution.py:323
  21.8 18.8 %shard_map.150 = (f32[4,80,1024]{2,1,0:T(8,128)}, f32[4,80,1024]{2,1,0:T(8,128)}) custom-call(s32[2]{0:T(128)} %pad_add_fusion.2.place_ref, bf16[80,1152]{1,0:T(8,128)(2,1)} %copy-done.1, bf16[80,1152]{1,0:T(8,128)(2,1)} %copy-done.14, bf16[80,1152]{1,0:T(8,128)(2,1)} %copy-done.15, bf16[80,1152]{1,0:T(8,128)(2,1)} %copy-done.16, ...), custom_call_target="tpu_custom_call" | custom-call | flops 6442450944 | bytes 22970368 | tf_op jit(solution)/shard_map/pallas_call | solution.py:147
  40.8 3.1 %collective-permute-done.13.came_ref = f32[4,80,1024]{2,1,0:T(8,128)S(1)} collective-permute-done((f32[4,80,1024]{2,1,0:T(8,128)}, f32[4,80,1024]{2,1,0:T(8,128)S(1)}, u32[]{:S(2)}, u32[]{:S(2)}) %collective-permute-start.13) | collective-permute-done | bytes 1310752 | tf_op jit(solution)/shard_map/ppermute | solution.py:332
  43.9 1.3 copy-done
  46.1 1.3 collective-permute-start.15
  47.5 1.4 collective-permute-start.16
  48.9 7.1 %collective-permute-done.14.refs_0_ = f32[80,1024]{1,0:T(8,128)S(1)} collective-permute-done((f32[80,1024]{1,0:T(8,128)S(1)}, f32[80,1024]{1,0:T(8,128)S(1)}, u32[]{:S(2)}, u32[]{:S(2)}) %collective-permute-start.14) | collective-permute-done | bytes 327712 | tf_op jit(solution)/shard_map/ppermute | solution.py:323
  56.0 5.6 %collective-permute-done.15.refs_1_ = f32[80,1024]{1,0:T(8,128)S(1)} collective-permute-done((f32[80,1024]{1,0:T(8,128)S(1)}, f32[80,1024]{1,0:T(8,128)S(1)}, u32[]{:S(2)}, u32[]{:S(2)}) %collective-permute-start.15) | collective-permute-done | bytes 327712 | tf_op jit(solution)/shard_map/ppermute | solution.py:323
  61.5 1.6 %collective-permute-done.16.refs_2_ = f32[80,1024]{1,0:T(8,128)S(1)} collective-permute-done((f32[80,1024]{1,0:T(8,128)S(1)}, f32[80,1024]{1,0:T(8,128)S(1)}, u32[]{:S(2)}, u32[]{:S(2)}) %collective-permute-start.16) | collective-permute-done | bytes 327712 | tf_op jit(solution)/shard_map/ppermute | solution.py:323
  63.2 0.9 copy-done.2
  64.3 1.6 %collective-permute-start.17 = (bf16[80,1024]{1,0:T(8,128)(2,1)S(1)}, bf16[80,1024]{1,0:T(8,128)(2,1)S(1)}, u32[]{:S(2)}, u32[]{:S(2)}) collective-permute-start(bf16[80,1024]{1,0:T(8,128)(2,1)S(1)} %shard_map.152.refs_0_), channel_id=1, source_target_pairs={{0,8},{8,16},{16,24},{24,0},{1,9},{9,17},{17,25},{25,1},{2,10},{10... | collective-permute-start | bytes 491528 | tf_op jit(solution)/shard_map/ppermute | solution.py:328
  65.9 2.6 %collective-permute-start.18 = (bf16[80,1024]{1,0:T(8,128)(2,1)S(1)}, bf16[80,1024]{1,0:T(8,128)(2,1)S(1)}, u32[]{:S(2)}, u32[]{:S(2)}) collective-permute-start(bf16[80,1024]{1,0:T(8,128)(2,1)S(1)} %shard_map.152.refs_0_), channel_id=1, source_target_pairs={{0,16},{8,24},{16,0},{24,8},{1,17},{9,25},{17,1},{25,9},{2,18},{10... | collective-permute-start | bytes 491528 | tf_op jit(solution)/shard_map/ppermute | solution.py:328
  68.5 1.3 collective-permute-start.19
  70.5 8.1 %collective-permute-done = s32[1,40]{1,0:T(1,128)S(1)} collective-permute-done((s32[1,40]{1,0:T(1,128)S(1)}, s32[1,40]{1,0:T(1,128)S(1)}, u32[]{:S(2)}, u32[]{:S(2)}) %collective-permute-start) | collective-permute-done | bytes 192 | tf_op jit(solution)/shard_map/ppermute | solution.py:328
  78.6 4.2 %collective-permute-start.1 = (s32[1,40]{1,0:T(1,128)S(1)}, s32[1,40]{1,0:T(1,128)S(1)}, u32[]{:S(2)}, u32[]{:S(2)}) collective-permute-start(s32[1,40]{1,0:T(1,128)S(1)} %bitcast.112), channel_id=1, source_target_pairs={{0,16},{8,24},{16,0},{24,8},{1,17},{9,25},{17,1},{25,9},{2,18},{10... | collective-permute-start | bytes 488 | tf_op jit(solution)/shard_map/ppermute | solution.py:328
  82.9 1.5 collective-permute-done.1
  84.9 3.0 %collective-permute-done.2 = s32[1,40]{1,0:T(1,128)S(1)} collective-permute-done((s32[1,40]{1,0:T(1,128)S(1)}, s32[1,40]{1,0:T(1,128)S(1)}, u32[]{:S(2)}, u32[]{:S(2)}) %collective-permute-start.2) | collective-permute-done | bytes 192 | tf_op jit(solution)/shard_map/ppermute | solution.py:328
  88.6 3.0 %collective-permute-done.3 = s32[4,40]{1,0:T(4,128)S(1)} collective-permute-done((s32[4,40]{1,0:T(4,128)S(1)}, s32[4,40]{1,0:T(4,128)S(1)}, u32[]{:S(2)}, u32[]{:S(2)}) %collective-permute-start.3) | collective-permute-done | bytes 672 | tf_op jit(solution)/shard_map/ppermute | solution.py:323
  92.1 3.0 %collective-permute-done.4 = s32[4,40]{1,0:T(4,128)S(1)} collective-permute-done((s32[4,40]{1,0:T(4,128)S(1)}, s32[4,40]{1,0:T(4,128)S(1)}, u32[]{:S(2)}, u32[]{:S(2)}) %collective-permute-start.4) | collective-permute-done | bytes 672 | tf_op jit(solution)/shard_map/ppermute | solution.py:323
  95.2 1.1 collective-permute-start.5
  96.3 3.4 %collective-permute-done.5 = s32[4,40]{1,0:T(4,128)S(1)} collective-permute-done((s32[4,40]{1,0:T(4,128)S(1)}, s32[4,40]{1,0:T(4,128)S(1)}, u32[]{:S(2)}, u32[]{:S(2)}) %collective-permute-start.5) | collective-permute-done | bytes 672 | tf_op jit(solution)/shard_map/ppermute | solution.py:323
  100.3 1.0 collective-permute-start.24
  101.4 0.9 collective-permute-start.21
  102.2 1.5 collective-permute-start.26
  103.8 1.2 collective-permute-done.20.refs_4_
  105.7 1.8 %collective-permute-done.24.refs_8_ = bf16[80,1024]{1,0:T(8,128)(2,1)S(1)} collective-permute-done((bf16[80,1024]{1,0:T(8,128)(2,1)S(1)}, bf16[80,1024]{1,0:T(8,128)(2,1)S(1)}, u32[]{:S(2)}, u32[]{:S(2)}) %collective-permute-start.24) | collective-permute-done | bytes 163872 | tf_op jit(solution)/shard_map/ppermute | solution.py:323
  107.4 1.0 collective-permute-start.27
  108.4 0.9 collective-permute-start.23
  109.3 1.5 collective-permute-done.26.refs_10_
  110.8 1.1 collective-permute-start.25
  112.7 1.0 collective-permute-start.28
  113.8 1.0 collective-permute-start.29
  114.8 1.4 collective-permute-start.30
  116.2 1.4 collective-permute-start.31
  120.1 1.8 %collective-permute-done.31.refs_15_ = bf16[80,1024]{1,0:T(8,128)(2,1)S(1)} collective-permute-done((bf16[80,1024]{1,0:T(8,128)(2,1)S(1)}, bf16[80,1024]{1,0:T(8,128)(2,1)S(1)}, u32[]{:S(2)}, u32[]{:S(2)}) %collective-permute-start.31) | collective-permute-done | bytes 163872 | tf_op jit(solution)/shard_map/ppermute | solution.py:323
  122.5 19.8 %shard_map.153 = f32[16,2,80]{2,1,0:T(2,128)} custom-call(s32[18]{0:T(128)} %pad_add_fusion.1.spots_ref, s32[1,1280]{1,0:T(1,128)} %reshape.88.wanted_ref, bf16[80,1024]{1,0:T(8,128)(2,1)} %copy-done.3, bf16[80,1024]{1,0:T(8,128)(2,1)} %copy-done.21, bf16[80,1024]{1,0:T(8,128)(2,1)} %copy-done.22, bf16[80,1024]{1,0:T(8,128)(2,1)} %copy-done.23, ...), custom_call_target="tpu_custom_call" | custom-call | flops 12750684160 | bytes 12582912 | tf_op jit(solution)/shard_map/pallas_call | solution.py:283
  143.0 1.4 collective-permute-start.33
  144.4 1.4 collective-permute-start.34
  145.8 2.8 %collective-permute-start.35 = (f32[16,2,80]{2,0,1:T(8,128)S(1)}, f32[16,2,80]{2,0,1:T(8,128)S(1)}, u32[]{:S(2)}, u32[]{:S(2)}) collective-permute-start(f32[16,2,80]{2,0,1:T(8,128)S(1)} %copy.23), channel_id=1, source_target_pairs={{0,24},{8,0},{16,8},{24,16},{1,25},{9,1},{17,9},{25,17},{2,26},{10... | collective-permute-start | bytes 30728 | tf_op jit(solution)/shard_map/ppermute | solution.py:328
  150.2 1.6 %collective-permute-start.36 = (f32[16,2,80]{2,0,1:T(8,128)S(1)}, f32[16,2,80]{2,0,1:T(8,128)S(1)}, u32[]{:S(2)}, u32[]{:S(2)}) collective-permute-start(f32[16,2,80]{2,0,1:T(8,128)S(1)} %pad_maximum_fusion), channel_id=1, source_target_pairs={{0,2},{2,0},{4,6},{6,4},{1,3},{3,1},{5,7},{7,5},{8,10},{10,8},{12,... | collective-permute-start | bytes 30728 | tf_op jit(solution)/shard_map/ppermute | solution.py:323
  152.4 1.4 collective-permute-start.38
  155.8 1.2 collective-permute-done.38
  158.3 1.3 add_reduce_fusion
  (131 shorter events, 19.1 us)
Async XLA Ops:
  0.6 121.2 %collective-permute-start.32 = (bf16[2432,1024]{1,0:T(8,128)(2,1)}, bf16[2432,1024]{1,0:T(8,128)(2,1)}, u32[]{:S(2)}, u32[]{:S(2)}) collective-permute-start(bf16[2432,1024]{1,0:T(8,128)(2,1)} %refs_16_.1), channel_id=1, source_target_pairs={{0,1},{1,0},{2,3},{3,2},{4,5},{5,4},{6,7},{7,6},{8,9},{9,8},{10,11... | collective-permute-start | bytes 14942216 | tf_op jit(solution)/shard_map/ppermute | solution.py:332
  5.8 8.1 %collective-permute-start.6 = (bf16[80,1152]{1,0:T(8,128)(2,1)S(1)}, bf16[80,1152]{1,0:T(8,128)(2,1)S(1)}, u32[]{:S(2)}, u32[]{:S(2)}) collective-permute-start(bf16[80,1152]{1,0:T(8,128)(2,1)S(1)} %shard_map.149.refs_0_.hidden_ref), channel_id=1, source_target_pairs={{0,2},{2,0},{4,6},{6,4},{1,3},{3,1},{5,7},{7,5},{8,10},{10,8},{12,... | collective-permute-start | bytes 552968 | tf_op jit(solution)/shard_map/ppermute | solution.py:323
  8.4 10.7 %collective-permute-start.7 = (bf16[80,1152]{1,0:T(8,128)(2,1)S(1)}, bf16[80,1152]{1,0:T(8,128)(2,1)S(1)}, u32[]{:S(2)}, u32[]{:S(2)}) collective-permute-start(bf16[80,1152]{1,0:T(8,128)(2,1)S(1)} %shard_map.149.refs_0_.hidden_ref), channel_id=1, source_target_pairs={{0,4},{2,6},{4,0},{6,2},{1,5},{3,7},{5,1},{7,3},{8,12},{10,14},{12... | collective-permute-start | bytes 552968 | tf_op jit(solution)/shard_map/ppermute | solution.py:323
  9.9 9.2 %collective-permute-start.8 = (bf16[80,1152]{1,0:T(8,128)(2,1)S(1)}, bf16[80,1152]{1,0:T(8,128)(2,1)S(1)}, u32[]{:S(2)}, u32[]{:S(2)}) collective-permute-start(bf16[80,1152]{1,0:T(8,128)(2,1)S(1)} %shard_map.149.refs_0_.hidden_ref), channel_id=1, source_target_pairs={{0,6},{2,4},{4,2},{6,0},{1,7},{3,5},{5,3},{7,1},{8,14},{10,12},{12... | collective-permute-start | bytes 552968 | tf_op jit(solution)/shard_map/ppermute | solution.py:323
  9.9 10.3 %collective-permute-start.9 = (bf16[80,1152]{1,0:T(8,128)(2,1)S(1)}, bf16[80,1152]{1,0:T(8,128)(2,1)S(1)}, u32[]{:S(2)}, u32[]{:S(2)}) collective-permute-start(bf16[80,1152]{1,0:T(8,128)(2,1)S(1)} %shard_map.149.refs_0_.hidden_ref), channel_id=1, source_target_pairs={{0,1},{1,0},{2,3},{3,2},{4,5},{5,4},{6,7},{7,6},{8,9},{9,8},{10,11... | collective-permute-start | bytes 552968 | tf_op jit(solution)/shard_map/ppermute | solution.py:332
  13.8 6.4 %collective-permute-start.10 = (bf16[80,1152]{1,0:T(8,128)(2,1)S(1)}, bf16[80,1152]{1,0:T(8,128)(2,1)S(1)}, u32[]{:S(2)}, u32[]{:S(2)}) collective-permute-start(bf16[80,1152]{1,0:T(8,128)(2,1)S(1)} %collective-permute-done.6.refs_1_), channel_id=1, source_target_pairs={{0,1},{1,0},{2,3},{3,2},{4,5},{5,4},{6,7},{7,6},{8,9},{9,8},{10,11... | collective-permute-start | bytes 552968 | tf_op jit(solution)/shard_map/ppermute | solution.py:332
  19.1 1.4 collective-permute-start.11
  19.1 1.7 %collective-permute-start.12 = (bf16[80,1152]{1,0:T(8,128)(2,1)S(1)}, bf16[80,1152]{1,0:T(8,128)(2,1)S(1)}, u32[]{:S(2)}, u32[]{:S(2)}) collective-permute-start(bf16[80,1152]{1,0:T(8,128)(2,1)S(1)} %collective-permute-done.8.refs_3_), channel_id=1, source_target_pairs={{0,1},{1,0},{2,3},{3,2},{4,5},{5,4},{6,7},{7,6},{8,9},{9,8},{10,11... | collective-permute-start | bytes 552968 | tf_op jit(solution)/shard_map/ppermute | solution.py:332
  20.2 43.0 %copy-start.10 = (f32[1024]{0:T(1024)S(1)}, f32[1024]{0:T(1024)}, u32[]{:S(2)}) copy-start(f32[1024]{0:T(1024)} %param.23) | copy-start | bytes 12292
  20.2 49.7 %copy-start.12 = (s32[40]{0:T(128)S(1)}, s32[40]{0:T(128)}, u32[]{:S(2)}) copy-start(s32[40]{0:T(128)} %param.25) | copy-start | bytes 484
  20.2 98.0 %copy-start.11 = (s32[32]{0:T(128)S(1)}, s32[32]{0:T(128)}, u32[]{:S(2)}) copy-start(s32[32]{0:T(128)} %param.26) | copy-start | bytes 388
  40.6 3.2 %collective-permute-start.13 = (f32[4,80,1024]{2,1,0:T(8,128)}, f32[4,80,1024]{2,1,0:T(8,128)S(1)}, u32[]{:S(2)}, u32[]{:S(2)}) collective-permute-start(f32[4,80,1024]{2,1,0:T(8,128)} %get-tuple-element.9), channel_id=1, source_target_pairs={{0,1},{1,0},{2,3},{3,2},{4,5},{5,4},{6,7},{7,6},{8,9},{9,8},{10,11... | collective-permute-start | bytes 3932168 | tf_op jit(solution)/shard_map/ppermute | solution.py:332
  45.3 10.6 %collective-permute-start.14 = (f32[80,1024]{1,0:T(8,128)S(1)}, f32[80,1024]{1,0:T(8,128)S(1)}, u32[]{:S(2)}, u32[]{:S(2)}) collective-permute-start(f32[80,1024]{1,0:T(8,128)S(1)} %get-tuple-element.11), channel_id=1, source_target_pairs={{0,2},{2,0},{4,6},{6,4},{1,3},{3,1},{5,7},{7,5},{8,10},{10,8},{12,... | collective-permute-start | bytes 983048 | tf_op jit(solution)/shard_map/ppermute | solution.py:323
  46.1 15.4 %collective-permute-start.15 = (f32[80,1024]{1,0:T(8,128)S(1)}, f32[80,1024]{1,0:T(8,128)S(1)}, u32[]{:S(2)}, u32[]{:S(2)}) collective-permute-start(f32[80,1024]{1,0:T(8,128)S(1)} %get-tuple-element.12), channel_id=1, source_target_pairs={{0,4},{2,6},{4,0},{6,2},{1,5},{3,7},{5,1},{7,3},{8,12},{10,14},{12... | collective-permute-start | bytes 983048 | tf_op jit(solution)/shard_map/ppermute | solution.py:323
  47.5 15.7 %collective-permute-start.16 = (f32[80,1024]{1,0:T(8,128)S(1)}, f32[80,1024]{1,0:T(8,128)S(1)}, u32[]{:S(2)}, u32[]{:S(2)}) collective-permute-start(f32[80,1024]{1,0:T(8,128)S(1)} %get-tuple-element.13), channel_id=1, source_target_pairs={{0,6},{2,4},{4,2},{6,0},{1,7},{3,5},{5,3},{7,1},{8,14},{10,12},{12... | collective-permute-start | bytes 983048 | tf_op jit(solution)/shard_map/ppermute | solution.py:323
  64.3 57.6 %copy-start.3 = (bf16[80,1024]{1,0:T(8,128)(2,1)}, bf16[80,1024]{1,0:T(8,128)(2,1)S(1)}, u32[]{:S(2)}) copy-start(bf16[80,1024]{1,0:T(8,128)(2,1)S(1)} %shard_map.152.refs_0_) | copy-start | bytes 491524
  64.3 36.1 %collective-permute-start.17 = (bf16[80,1024]{1,0:T(8,128)(2,1)S(1)}, bf16[80,1024]{1,0:T(8,128)(2,1)S(1)}, u32[]{:S(2)}, u32[]{:S(2)}) collective-permute-start(bf16[80,1024]{1,0:T(8,128)(2,1)S(1)} %shard_map.152.refs_0_), channel_id=1, source_target_pairs={{0,8},{8,16},{16,24},{24,0},{1,9},{9,17},{17,25},{25,1},{2,10},{10... | collective-permute-start | bytes 491528 | tf_op jit(solution)/shard_map/ppermute | solution.py:328
  65.9 35.5 %collective-permute-start.18 = (bf16[80,1024]{1,0:T(8,128)(2,1)S(1)}, bf16[80,1024]{1,0:T(8,128)(2,1)S(1)}, u32[]{:S(2)}, u32[]{:S(2)}) collective-permute-start(bf16[80,1024]{1,0:T(8,128)(2,1)S(1)} %shard_map.152.refs_0_), channel_id=1, source_target_pairs={{0,16},{8,24},{16,0},{24,8},{1,17},{9,25},{17,1},{25,9},{2,18},{10... | collective-permute-start | bytes 491528 | tf_op jit(solution)/shard_map/ppermute | solution.py:328
  68.5 33.8 %collective-permute-start.19 = (bf16[80,1024]{1,0:T(8,128)(2,1)S(1)}, bf16[80,1024]{1,0:T(8,128)(2,1)S(1)}, u32[]{:S(2)}, u32[]{:S(2)}) collective-permute-start(bf16[80,1024]{1,0:T(8,128)(2,1)S(1)} %shard_map.152.refs_0_), channel_id=1, source_target_pairs={{0,24},{8,0},{16,8},{24,16},{1,25},{9,1},{17,9},{25,17},{2,26},{10... | collective-permute-start | bytes 491528 | tf_op jit(solution)/shard_map/ppermute | solution.py:328
  69.8 8.8 %collective-permute-start = (s32[1,40]{1,0:T(1,128)S(1)}, s32[1,40]{1,0:T(1,128)S(1)}, u32[]{:S(2)}, u32[]{:S(2)}) collective-permute-start(s32[1,40]{1,0:T(1,128)S(1)} %bitcast.111), channel_id=1, source_target_pairs={{0,8},{8,16},{16,24},{24,0},{1,9},{9,17},{17,25},{25,1},{2,10},{10... | collective-permute-start | bytes 488 | tf_op jit(solution)/shard_map/ppermute | solution.py:328
  78.6 5.7 %collective-permute-start.1 = (s32[1,40]{1,0:T(1,128)S(1)}, s32[1,40]{1,0:T(1,128)S(1)}, u32[]{:S(2)}, u32[]{:S(2)}) collective-permute-start(s32[1,40]{1,0:T(1,128)S(1)} %bitcast.112), channel_id=1, source_target_pairs={{0,16},{8,24},{16,0},{24,8},{1,17},{9,25},{17,1},{25,9},{2,18},{10... | collective-permute-start | bytes 488 | tf_op jit(solution)/shard_map/ppermute | solution.py:328
  84.4 3.5 %collective-permute-start.2 = (s32[1,40]{1,0:T(1,128)S(1)}, s32[1,40]{1,0:T(1,128)S(1)}, u32[]{:S(2)}, u32[]{:S(2)}) collective-permute-start(s32[1,40]{1,0:T(1,128)S(1)} %bitcast.113), channel_id=1, source_target_pairs={{0,24},{8,0},{16,8},{24,16},{1,25},{9,1},{17,9},{25,17},{2,26},{10... | collective-permute-start | bytes 488 | tf_op jit(solution)/shard_map/ppermute | solution.py:328
  87.9 3.7 %collective-permute-start.3 = (s32[4,40]{1,0:T(4,128)S(1)}, s32[4,40]{1,0:T(4,128)S(1)}, u32[]{:S(2)}, u32[]{:S(2)}) collective-permute-start(s32[4,40]{1,0:T(4,128)S(1)} %get-tuple-element.19), channel_id=1, source_target_pairs={{0,2},{2,0},{4,6},{6,4},{1,3},{3,1},{5,7},{7,5},{8,10},{10,8},{12,... | collective-permute-start | bytes 1928 | tf_op jit(solution)/shard_map/ppermute | solution.py:323
  91.6 3.6 %collective-permute-start.4 = (s32[4,40]{1,0:T(4,128)S(1)}, s32[4,40]{1,0:T(4,128)S(1)}, u32[]{:S(2)}, u32[]{:S(2)}) collective-permute-start(s32[4,40]{1,0:T(4,128)S(1)} %get-tuple-element.19), channel_id=1, source_target_pairs={{0,4},{2,6},{4,0},{6,2},{1,5},{3,7},{5,1},{7,3},{8,12},{10,14},{12... | collective-permute-start | bytes 1928 | tf_op jit(solution)/shard_map/ppermute | solution.py:323
  95.2 4.5 %collective-permute-start.5 = (s32[4,40]{1,0:T(4,128)S(1)}, s32[4,40]{1,0:T(4,128)S(1)}, u32[]{:S(2)}, u32[]{:S(2)}) collective-permute-start(s32[4,40]{1,0:T(4,128)S(1)} %get-tuple-element.19), channel_id=1, source_target_pairs={{0,6},{2,4},{4,2},{6,0},{1,7},{3,5},{5,3},{7,1},{8,14},{10,12},{12... | collective-permute-start | bytes 1928 | tf_op jit(solution)/shard_map/ppermute | solution.py:323
  99.7 5.3 %collective-permute-start.20 = (bf16[80,1024]{1,0:T(8,128)(2,1)S(1)}, bf16[80,1024]{1,0:T(8,128)(2,1)S(1)}, u32[]{:S(2)}, u32[]{:S(2)}) collective-permute-start(bf16[80,1024]{1,0:T(8,128)(2,1)S(1)} %shard_map.152.refs_0_), channel_id=1, source_target_pairs={{0,2},{2,0},{4,6},{6,4},{1,3},{3,1},{5,7},{7,5},{8,10},{10,8},{12,... | collective-permute-start | bytes 491528 | tf_op jit(solution)/shard_map/ppermute | solution.py:323
  100.3 21.5 %copy-start.21 = (bf16[80,1024]{1,0:T(8,128)(2,1)}, bf16[80,1024]{1,0:T(8,128)(2,1)S(1)}, u32[]{:S(2)}) copy-start(bf16[80,1024]{1,0:T(8,128)(2,1)S(1)} %collective-permute-done.17.refs_1_) | copy-start | bytes 491524
  100.3 7.1 %collective-permute-start.24 = (bf16[80,1024]{1,0:T(8,128)(2,1)S(1)}, bf16[80,1024]{1,0:T(8,128)(2,1)S(1)}, u32[]{:S(2)}, u32[]{:S(2)}) collective-permute-start(bf16[80,1024]{1,0:T(8,128)(2,1)S(1)} %shard_map.152.refs_0_), channel_id=1, source_target_pairs={{0,4},{2,6},{4,0},{6,2},{1,5},{3,7},{5,1},{7,3},{8,12},{10,14},{12... | collective-permute-start | bytes 491528 | tf_op jit(solution)/shard_map/ppermute | solution.py:323
  101.4 20.5 %copy-start.22 = (bf16[80,1024]{1,0:T(8,128)(2,1)}, bf16[80,1024]{1,0:T(8,128)(2,1)S(1)}, u32[]{:S(2)}) copy-start(bf16[80,1024]{1,0:T(8,128)(2,1)S(1)} %collective-permute-done.18.refs_2_) | copy-start | bytes 491524
  101.4 7.1 %collective-permute-start.21 = (bf16[80,1024]{1,0:T(8,128)(2,1)S(1)}, bf16[80,1024]{1,0:T(8,128)(2,1)S(1)}, u32[]{:S(2)}, u32[]{:S(2)}) collective-permute-start(bf16[80,1024]{1,0:T(8,128)(2,1)S(1)} %collective-permute-done.17.refs_1_), channel_id=1, source_target_pairs={{0,2},{2,0},{4,6},{6,4},{1,3},{3,1},{5,7},{7,5},{8,10},{10,8},{12,... | collective-permute-start | bytes 491528 | tf_op jit(solution)/shard_map/ppermute | solution.py:323
  102.2 19.7 %copy-start.23 = (bf16[80,1024]{1,0:T(8,128)(2,1)}, bf16[80,1024]{1,0:T(8,128)(2,1)S(1)}, u32[]{:S(2)}) copy-start(bf16[80,1024]{1,0:T(8,128)(2,1)S(1)} %collective-permute-done.19.refs_3_) | copy-start | bytes 491524
  102.2 8.6 %collective-permute-start.26 = (bf16[80,1024]{1,0:T(8,128)(2,1)S(1)}, bf16[80,1024]{1,0:T(8,128)(2,1)S(1)}, u32[]{:S(2)}, u32[]{:S(2)}) collective-permute-start(bf16[80,1024]{1,0:T(8,128)(2,1)S(1)} %collective-permute-done.18.refs_2_), channel_id=1, source_target_pairs={{0,4},{2,6},{4,0},{6,2},{1,5},{3,7},{5,1},{7,3},{8,12},{10,14},{12... | collective-permute-start | bytes 491528 | tf_op jit(solution)/shard_map/ppermute | solution.py:323
  105.0 8.8 %collective-permute-start.22 = (bf16[80,1024]{1,0:T(8,128)(2,1)S(1)}, bf16[80,1024]{1,0:T(8,128)(2,1)S(1)}, u32[]{:S(2)}, u32[]{:S(2)}) collective-permute-start(bf16[80,1024]{1,0:T(8,128)(2,1)S(1)} %collective-permute-done.18.refs_2_), channel_id=1, source_target_pairs={{0,2},{2,0},{4,6},{6,4},{1,3},{3,1},{5,7},{7,5},{8,10},{10,8},{12,... | collective-permute-start | bytes 491528 | tf_op jit(solution)/shard_map/ppermute | solution.py:323
  107.4 5.3 %collective-permute-start.27 = (bf16[80,1024]{1,0:T(8,128)(2,1)S(1)}, bf16[80,1024]{1,0:T(8,128)(2,1)S(1)}, u32[]{:S(2)}, u32[]{:S(2)}) collective-permute-start(bf16[80,1024]{1,0:T(8,128)(2,1)S(1)} %collective-permute-done.19.refs_3_), channel_id=1, source_target_pairs={{0,4},{2,6},{4,0},{6,2},{1,5},{3,7},{5,1},{7,3},{8,12},{10,14},{12... | collective-permute-start | bytes 491528 | tf_op jit(solution)/shard_map/ppermute | solution.py:323
  108.4 6.3 %collective-permute-start.23 = (bf16[80,1024]{1,0:T(8,128)(2,1)S(1)}, bf16[80,1024]{1,0:T(8,128)(2,1)S(1)}, u32[]{:S(2)}, u32[]{:S(2)}) collective-permute-start(bf16[80,1024]{1,0:T(8,128)(2,1)S(1)} %collective-permute-done.19.refs_3_), channel_id=1, source_target_pairs={{0,2},{2,0},{4,6},{6,4},{1,3},{3,1},{5,7},{7,5},{8,10},{10,8},{12,... | collective-permute-start | bytes 491528 | tf_op jit(solution)/shard_map/ppermute | solution.py:323
  110.8 5.3 %collective-permute-start.25 = (bf16[80,1024]{1,0:T(8,128)(2,1)S(1)}, bf16[80,1024]{1,0:T(8,128)(2,1)S(1)}, u32[]{:S(2)}, u32[]{:S(2)}) collective-permute-start(bf16[80,1024]{1,0:T(8,128)(2,1)S(1)} %collective-permute-done.17.refs_1_), channel_id=1, source_target_pairs={{0,4},{2,6},{4,0},{6,2},{1,5},{3,7},{5,1},{7,3},{8,12},{10,14},{12... | collective-permute-start | bytes 491528 | tf_op jit(solution)/shard_map/ppermute | solution.py:323
  112.7 6.4 %collective-permute-start.28 = (bf16[80,1024]{1,0:T(8,128)(2,1)S(1)}, bf16[80,1024]{1,0:T(8,128)(2,1)S(1)}, u32[]{:S(2)}, u32[]{:S(2)}) collective-permute-start(bf16[80,1024]{1,0:T(8,128)(2,1)S(1)} %collective-permute-done.20.refs_4_), channel_id=1, source_target_pairs={{0,4},{2,6},{4,0},{6,2},{1,5},{3,7},{5,1},{7,3},{8,12},{10,14},{12... | collective-permute-start | bytes 491528 | tf_op jit(solution)/shard_map/ppermute | solution.py:323
  113.8 6.0 %collective-permute-start.29 = (bf16[80,1024]{1,0:T(8,128)(2,1)S(1)}, bf16[80,1024]{1,0:T(8,128)(2,1)S(1)}, u32[]{:S(2)}, u32[]{:S(2)}) collective-permute-start(bf16[80,1024]{1,0:T(8,128)(2,1)S(1)} %collective-permute-done.21.refs_5_), channel_id=1, source_target_pairs={{0,4},{2,6},{4,0},{6,2},{1,5},{3,7},{5,1},{7,3},{8,12},{10,14},{12... | collective-permute-start | bytes 491528 | tf_op jit(solution)/shard_map/ppermute | solution.py:323
  114.8 5.3 %collective-permute-start.30 = (bf16[80,1024]{1,0:T(8,128)(2,1)S(1)}, bf16[80,1024]{1,0:T(8,128)(2,1)S(1)}, u32[]{:S(2)}, u32[]{:S(2)}) collective-permute-start(bf16[80,1024]{1,0:T(8,128)(2,1)S(1)} %collective-permute-done.26.refs_10_), channel_id=1, source_target_pairs={{0,2},{2,0},{4,6},{6,4},{1,3},{3,1},{5,7},{7,5},{8,10},{10,8},{12,... | collective-permute-start | bytes 491528 | tf_op jit(solution)/shard_map/ppermute | solution.py:323
  116.2 5.7 %collective-permute-start.31 = (bf16[80,1024]{1,0:T(8,128)(2,1)S(1)}, bf16[80,1024]{1,0:T(8,128)(2,1)S(1)}, u32[]{:S(2)}, u32[]{:S(2)}) collective-permute-start(bf16[80,1024]{1,0:T(8,128)(2,1)S(1)} %collective-permute-done.27.refs_11_), channel_id=1, source_target_pairs={{0,2},{2,0},{4,6},{6,4},{1,3},{3,1},{5,7},{7,5},{8,10},{10,8},{12,... | collective-permute-start | bytes 491528 | tf_op jit(solution)/shard_map/ppermute | solution.py:323
  119.2 29.5 %copy-start.13 = (s32[32]{0:T(128)S(1)}, s32[32]{0:T(128)}, u32[]{:S(2)}) copy-start(s32[32]{0:T(128)} %param.27) | copy-start | bytes 388
  143.0 7.1 %collective-permute-start.33 = (f32[16,2,80]{2,0,1:T(8,128)S(1)}, f32[16,2,80]{2,0,1:T(8,128)S(1)}, u32[]{:S(2)}, u32[]{:S(2)}) collective-permute-start(f32[16,2,80]{2,0,1:T(8,128)S(1)} %copy.23), channel_id=1, source_target_pairs={{0,8},{8,16},{16,24},{24,0},{1,9},{9,17},{17,25},{25,1},{2,10},{10... | collective-permute-start | bytes 30728 | tf_op jit(solution)/shard_map/ppermute | solution.py:328
  144.4 5.7 %collective-permute-start.34 = (f32[16,2,80]{2,0,1:T(8,128)S(1)}, f32[16,2,80]{2,0,1:T(8,128)S(1)}, u32[]{:S(2)}, u32[]{:S(2)}) collective-permute-start(f32[16,2,80]{2,0,1:T(8,128)S(1)} %copy.23), channel_id=1, source_target_pairs={{0,16},{8,24},{16,0},{24,8},{1,17},{9,25},{17,1},{25,9},{2,18},{10... | collective-permute-start | bytes 30728 | tf_op jit(solution)/shard_map/ppermute | solution.py:328
  145.8 4.3 %collective-permute-start.35 = (f32[16,2,80]{2,0,1:T(8,128)S(1)}, f32[16,2,80]{2,0,1:T(8,128)S(1)}, u32[]{:S(2)}, u32[]{:S(2)}) collective-permute-start(f32[16,2,80]{2,0,1:T(8,128)S(1)} %copy.23), channel_id=1, source_target_pairs={{0,24},{8,0},{16,8},{24,16},{1,25},{9,1},{17,9},{25,17},{2,26},{10... | collective-permute-start | bytes 30728 | tf_op jit(solution)/shard_map/ppermute | solution.py:328
  150.2 5.6 %collective-permute-start.36 = (f32[16,2,80]{2,0,1:T(8,128)S(1)}, f32[16,2,80]{2,0,1:T(8,128)S(1)}, u32[]{:S(2)}, u32[]{:S(2)}) collective-permute-start(f32[16,2,80]{2,0,1:T(8,128)S(1)} %pad_maximum_fusion), channel_id=1, source_target_pairs={{0,2},{2,0},{4,6},{6,4},{1,3},{3,1},{5,7},{7,5},{8,10},{10,8},{12,... | collective-permute-start | bytes 30728 | tf_op jit(solution)/shard_map/ppermute | solution.py:323
  151.8 3.9 %collective-permute-start.37 = (f32[16,2,80]{2,0,1:T(8,128)S(1)}, f32[16,2,80]{2,0,1:T(8,128)S(1)}, u32[]{:S(2)}, u32[]{:S(2)}) collective-permute-start(f32[16,2,80]{2,0,1:T(8,128)S(1)} %pad_maximum_fusion), channel_id=1, source_target_pairs={{0,4},{2,6},{4,0},{6,2},{1,5},{3,7},{5,1},{7,3},{8,12},{10,14},{12... | collective-permute-start | bytes 30728 | tf_op jit(solution)/shard_map/ppermute | solution.py:323
  152.4 4.6 %collective-permute-start.38 = (f32[16,2,80]{2,0,1:T(8,128)S(1)}, f32[16,2,80]{2,0,1:T(8,128)S(1)}, u32[]{:S(2)}, u32[]{:S(2)}) collective-permute-start(f32[16,2,80]{2,0,1:T(8,128)S(1)} %pad_maximum_fusion), channel_id=1, source_target_pairs={{0,6},{2,4},{4,2},{6,0},{1,7},{3,5},{5,3},{7,1},{8,14},{10,12},{12... | collective-permute-start | bytes 30728 | tf_op jit(solution)/shard_map/ppermute | solution.py:323
  157.1 1.2 collective-permute-start.39
  (28 other events, 128.7 us)

commit v3 on v2

--- a/solution.py
+++ b/solution.py
@@ -48,11 +48,12 @@
         pack_kernel,
         out_shape=jax.ShapeDtypeStruct(shape, jnp.bfloat16),
         scratch_shapes=[pltpu.VMEM(shape, jnp.float32)],
-        compiler_params=pltpu.CompilerParams(vmem_limit_bytes=16 * MIB),
+        compiler_params=pltpu.CompilerParams(vmem_limit_bytes=58 * MIB),
     )(pol_hidden, ref_hidden, pol_routes.T, ref_routes.T, pol_gates.T, ref_gates.T)
 
 
-def expert_kernel(block, slots, width, experts, chips, place_ref, *refs):
+def expert_kernel(block, slots, width, experts, chips, place_ref, early_ref, *refs):
+    del early_ref
     count = 2 * chips
     blocks, refs = refs[:count], refs[count:]
     gate_ref, up_ref, down_ref, keep_ref, give_ref = refs[:5]
@@ -133,7 +134,7 @@
                     give_ref[c ^ chip] = target
 
 
-def expert_sums(place, blocks, w_gate, w_up, w_down, block, capacity, width, experts):
+def expert_sums(place, early, blocks, w_gate, w_up, w_down, block, capacity, width, experts):
     count = len(blocks)
     share, wide = blocks[0].shape
     rows = count * share
@@ -150,7 +151,7 @@
         grid_spec=pltpu.PrefetchScalarGridSpec(
             num_scalar_prefetch=1,
             grid=(local_experts,),
-            in_specs=[whole] * count + [
+            in_specs=[pl.BlockSpec(memory_space=pl.ANY)] + [whole] * count + [
                 pl.BlockSpec((1, width, hidden), lambda e, place: (e, 0, 0)),
                 pl.BlockSpec((1, width, hidden), lambda e, place: (e, 0, 0)),
                 pl.BlockSpec((1, hidden, width), lambda e, place: (e, 0, 0)),
@@ -179,7 +180,7 @@
             bytes_accessed=w_gate.size * 6 + rows * wide * 2 + rows * width * 4,
             transcendentals=every * hidden,
         ),
-    )(place, *blocks, w_gate, w_up, w_down)
+    )(place, early, *blocks, w_gate, w_up, w_down)
 
 
 def pair_kernel(keep_ref, came_ref, own_ref, *sends):
@@ -194,7 +195,7 @@
     return pl.pallas_call(
         pair_kernel,
         out_shape=(own,) * chips,
-        compiler_params=pltpu.CompilerParams(vmem_limit_bytes=32 * MIB),
+        compiler_params=pltpu.CompilerParams(vmem_limit_bytes=58 * MIB),
     )(keep, came)
 
 
@@ -211,18 +212,18 @@
     return pl.pallas_call(
         norm_kernel,
         out_shape=jax.ShapeDtypeStruct(own.shape, jnp.bfloat16),
-        compiler_params=pltpu.CompilerParams(vmem_limit_bytes=16 * MIB),
+        compiler_params=pltpu.CompilerParams(vmem_limit_bytes=58 * MIB),
     )(hidden, gain.reshape(1, -1), own, *others)
 
 
-def head_kernel(count, spots_ref, wanted_ref, *refs):
+def head_kernel(count, before, spots_ref, wanted_ref, *refs):
     blocks, refs = refs[:count], refs[count:]
+    earlier, refs = refs[:before], refs[before:]
     head_a, head_b, out_ref, rows_in, peak, total, found, logits_a, logits_b = refs
     step = pl.program_id(0)
     last = pl.num_programs(0) - 1
     tile, columns = logits_a.shape
-    lane_band = 128
-    share = columns // out_ref.shape[0]
+    share = out_ref.shape[2]
     base_a, base_b = spots_ref[0], spots_ref[1]
 
     def product(head_ref, logits):
@@ -232,16 +233,17 @@
         )
 
     def absorb(logits, first):
-        row = lax.broadcasted_iota(jnp.int32, (tile, lane_band), 0)
-        for start in range(0, columns, lane_band):
-            band = pl.ds(start, lane_band)
+        for start in range(0, columns, 128):
+            lanes = min(128, columns - start)
+            band = pl.ds(start, lanes)
+            row = lax.broadcasted_iota(jnp.int32, (tile, lanes), 0)
             values = logits[:, band]
             old = peak[:, band]
-            new = jnp.maximum(old, jnp.max(values.reshape(tile // 8, 8, lane_band), axis=0))
-            grown = jnp.exp(values.reshape(tile // 8, 8, lane_band) - new[None])
+            new = jnp.maximum(old, jnp.max(values.reshape(tile // 8, 8, lanes), axis=0))
+            grown = jnp.exp(values.reshape(tile // 8, 8, lanes) - new[None])
             total[:, band] = total[:, band] * jnp.exp(old - new) + jnp.sum(grown, axis=0)
             same = row == wanted_ref[:, band] - first
-            kept = jnp.where(same, values, 0.0).reshape(tile // 8, 8, lane_band)
+            kept = jnp.where(same, values, 0.0).reshape(tile // 8, 8, lanes)
             found[:, band] += jnp.sum(kept, axis=0)
             peak[:, band] = new
 
@@ -268,21 +270,27 @@
         full = jnp.sum(total[...] * jnp.exp(peak[...] - top), axis=0, keepdims=True)
         lse = top + jnp.log(full)
         hit = jnp.sum(found[...], axis=0, keepdims=True)
-        for index in range(out_ref.shape[0]):
+        done = 0
+        for ref in earlier:
+            for index in range(ref.shape[0]):
+                out_ref[spots_ref[2 + done + index]] = ref[index]
+            done += ref.shape[0]
+        for index in range(columns // share):
             band = slice(index * share, (index + 1) * share)
-            spot = spots_ref[2 + index]
+            spot = spots_ref[2 + done + index]
             out_ref[spot, 0:1, :] = lse[:, band]
             out_ref[spot, 1:2, :] = hit[:, band]
 
 
-def head_stats(spots, wanted, blocks, head_a, head_b, share):
+def head_stats(spots, wanted, blocks, earlier, head_a, head_b, share):
+    places = spots.shape[0] - 2
     rows = sum(block.shape[0] for block in blocks)
     width = head_a.shape[1]
     tile = largest_tile(head_a.shape[0], 608 * 1280 // rows, 16)
     steps = head_a.shape[0] // tile
     return pl.pallas_call(
-        functools.partial(head_kernel, len(blocks)),
-        out_shape=jax.ShapeDtypeStruct((rows // share, 2, share), jnp.float32),
+        functools.partial(head_kernel, len(blocks), len(earlier)),
+        out_shape=jax.ShapeDtypeStruct((places, 2, share), jnp.float32),
         grid_spec=pltpu.PrefetchScalarGridSpec(
             num_scalar_prefetch=1,
             grid=(steps,),
@@ -290,10 +298,12 @@
                 pl.BlockSpec(block.shape, lambda s, spots: (0, 0), pipeline_mode=pl.Buffered(1))
                 for block in blocks
             ] + [
+                pl.BlockSpec(part.shape, lambda s, spots: (0, 0, 0)) for part in earlier
+            ] + [
                 pl.BlockSpec((tile, width), lambda s, spots: (s, 0)),
                 pl.BlockSpec((tile, width), lambda s, spots: (s, 0)),
             ],
-            out_specs=pl.BlockSpec((rows // share, 2, share), lambda s, spots: (0, 0, 0)),
+            out_specs=pl.BlockSpec((places, 2, share), lambda s, spots: (0, 0, 0)),
             scratch_shapes=[
                 pltpu.VMEM((rows, width), jnp.bfloat16),
                 pltpu.VMEM((8, rows), jnp.float32),
@@ -309,7 +319,7 @@
             bytes_accessed=head_a.size * 4 + rows * width * 2,
             transcendentals=2 * rows * head_a.shape[0],
         ),
-    )(spots, wanted, *blocks, head_a, head_b)
+    )(spots, wanted, *blocks, *earlier, head_a, head_b)
 
 
 def combine(parts):
@@ -352,14 +362,20 @@
     plane = [send] + [across(send, d) for d in offsets]
     plane = plane + [partner(rows) for rows in plane]
 
-    goal = targets.reshape(1, tokens)
-    goal = jnp.concatenate([goal] + [along(goal, k) for k in range(1, groups)], axis=0)
-    goal = jnp.stack([goal] + [across(goal, d) for d in offsets])
-    wanted = jnp.concatenate((goal, goal), axis=2).reshape(1, -1)
+    home = (group - jnp.arange(groups, dtype=jnp.int32)) % groups
+    spots = home[None, :] * chips + (chip ^ jnp.arange(chips, dtype=jnp.int32))[:, None]
+    spots = spots.reshape(-1)
+    goal = jnp.broadcast_to(targets[None], (groups * chips, tokens))
+    goal = lax.all_to_all(goal, ("grp", "chip"), split_axis=0, concat_axis=0, tiled=True)
+    place = spots[:, None] == jnp.arange(groups * chips, dtype=jnp.int32)[None, :]
+    goal = jnp.sum(jnp.where(place[:, :, None], goal[None], 0), axis=1)
+    wanted = jnp.concatenate((goal, goal), axis=1).reshape(1, -1)
     other_head = partner(vocab_head)
 
     place = jnp.stack((chip, core)).astype(jnp.int32)
-    keep, give = expert_sums(place, plane, w_gate, w_up, w_down, tokens, capacity, width, experts)
+    keep, give = expert_sums(
+        place, wanted, plane, w_gate, w_up, w_down, tokens, capacity, width, experts
+    )
     own, *sends = pair_sums(keep, partner(give))
     came = [across(rows, d) for d, rows in zip(offsets, sends)]
     normed = norm_rows(send, norm_gain, own, came)
@@ -372,28 +388,30 @@
         cross = [across(rows, 2) for rows in near[:half]] + [
             across(rows, 1) for rows in far[half:]
         ]
-        blocks = column + near + far + cross
     else:
         column = jnp.concatenate(column, axis=0)
         blocks = [column] + [across(column, d) for d in offsets]
-    home = (group - jnp.arange(groups, dtype=jnp.int32)) % groups
-    spots = home[None, :] * chips + (chip ^ jnp.arange(chips, dtype=jnp.int32))[:, None]
     base = jnp.stack((device, device + 1 - 2 * core)).astype(jnp.int32) * vocab_rows
-    rows = groups * chips * share
-    if rows <= 1280:
-        spots = jnp.concatenate((base, spots.reshape(-1)))
-        stats = head_stats(spots, wanted, blocks, vocab_head, other_head, share)
+    lines = groups * share
+    fixed = jnp.arange(groups * chips, dtype=jnp.int32)
+
+    def stats_of(spots, start, blocks, earlier):
+        end = start + sum(block.shape[0] for block in blocks)
+        spots = jnp.concatenate((base, spots))
+        return head_stats(
+            spots, wanted[:, start:end], blocks, earlier, vocab_head, other_head, share
+        )
+
+    if chips == 4:
+        first = stats_of(fixed[:groups], 0, column, ())
+        second = stats_of(fixed[:3 * groups], lines, near + far, (first,))
+        stats = stats_of(spots, 3 * lines, cross, (second,))
     else:
-        lines = groups * share
         pieces = [
-            head_stats(
-                jnp.concatenate((base, jnp.arange(groups, dtype=jnp.int32))),
-                wanted[:, d * lines:(d + 1) * lines], [block], vocab_head, other_head, share,
-            )
-            for d, block in enumerate(blocks)
+            stats_of(fixed[:groups], d * lines, [block], ()) for d, block in enumerate(blocks)
         ]
         pieces = jnp.concatenate(pieces, axis=0)
-        stats = jnp.zeros_like(pieces).at[spots.reshape(-1)].set(pieces)
+        stats = jnp.zeros_like(pieces).at[spots].set(pieces)
 
     lse, hit = combine([stats] + [along(stats, k) for k in range(1, groups)])
     stats = jnp.stack((lse, hit), axis=1)

time: 162 us -> 163 us (level)
  Pallas kernels: 39 us -> 66.3 us
  waiting for transfers between devices: 58.8 us -> 37.9 us
  starting transfers between devices: 43.9 us -> 37.5 us
    ppermute x24 -> x21, waiting for transfers between devices: 41.8 us -> 18.2 us  [across(): return lax.ppermute(value, 'chip', [(c, c ^ offset) for c in range(chips)])]
    pallas_call x1 -> x3, Pallas kernels: 19.8 us -> 40.7 us  [head_stats(): pl.pallas_call(functools.partial(head_kernel, len(blocks), len(earlier)),...]
    ppermute x9 -> x6, starting transfers between devices: 16.6 us -> 7.65 us  [along(): lax.ppermute(value, 'grp', [(g, (g + offset) % groups) for g in range(gro...]
    all_to_all x0 -> x1, starting transfers between devices: none -> 7.34 us  [local(): lax.all_to_all(goal, ('grp', 'chip'), split_axis=0, concat_axis=0, tiled=...]
    all_to_all x0 -> x1, waiting for transfers between devices: none -> 5.68 us  [local(): lax.all_to_all(goal, ('grp', 'chip'), split_axis=0, concat_axis=0, tiled=...]
    ppermute x24 -> x21, starting transfers between devices: 26.1 us -> 21.2 us  [across(): return lax.ppermute(value, 'chip', [(c, c ^ offset) for c in range(chips)])]
    unnamed x72 -> x58, local copies, waits for them, and re-layouts: 8.43 us -> 5.33 us
    pallas_call x1, Pallas kernels: 0.13 us -> 2.84 us  [pair_sums(): pl.pallas_call(pair_kernel, out_shape=(own,) * chips, compiler_params=plt...]
  transfers between devices with their start and end apart: 40 -> 35, of which waited for: 23 -> 12; matrix products, arithmetic and copies ran while one was open for 3% -> 5% of each run, Pallas kernels for 12% -> 33%
where the time goes in v3:
time: 163 us; the launch traced here: 162 us
  Pallas kernels  66.3 us (41%)
  waiting for transfers between devices  37.9 us (23%)
  starting transfers between devices  37.5 us (23%)
  local copies, waits for them, and re-layouts  10.7 us (7%)
  other arithmetic  5.09 us (3%)
  between operations  4.65 us (3%)
    pallas_call x3, Pallas kernels, head_stats(): pl.pallas_call(functools.partial(head_kernel, len(blocks), len(earlier)),...  40.7 us
    ppermute x21, starting transfers between devices, across(): return lax.ppermute(value, 'chip', [(c, c ^ offset) for c in range(chips)])  21.2 us
    pallas_call x1, Pallas kernels, expert_sums(): pl.pallas_call(functools.partial(expert_kernel, block, slots, width, expe...  18.8 us
    ppermute x21, waiting for transfers between devices, across(): return lax.ppermute(value, 'chip', [(c, c ^ offset) for c in range(chips)])  18.2 us
    ppermute x6, waiting for transfers between devices, along(): lax.ppermute(value, 'grp', [(g, (g + offset) % groups) for g in range(gro...  10.1 us
    ppermute x6, starting transfers between devices, along(): lax.ppermute(value, 'grp', [(g, (g + offset) % groups) for g in range(gro...  7.65 us
    all_to_all x1, starting transfers between devices, local(): lax.all_to_all(goal, ('grp', 'chip'), split_axis=0, concat_axis=0, tiled=...  7.34 us
    all_to_all x1, waiting for transfers between devices, local(): lax.all_to_all(goal, ('grp', 'chip'), split_axis=0, concat_axis=0, tiled=...  5.68 us
  transfers between devices with their start and end apart: 35, of which 12 were waited for; matrix products, arithmetic and copies ran while one was open for 5% of the time, Pallas kernels for 33%

profile of v3, /device:TPU:0, one launch (start us, length us, event | category | flops | bytes accessed | tf_op | source)
XLA Modules:
  0.0 162.2 jit_solution(13667744896059289138)
XLA Ops:
  1.1 1.8 %shard_map.149.refs_0_.hidden_ref = bf16[80,1152]{1,0:T(8,128)(2,1)} custom-call(bf16[40,1024]{1,0:T(8,128)(2,1)} %pol_ref.1, bf16[40,1024]{1,0:T(8,128)(2,1)} %ref_ref.1, s32[8,40]{1,0:T(8,128)} %bitcast.100, s32[8,40]{1,0:T(8,128)} %bitcast.101, f32[8,40]{1,0:T(8,128)} %bitcast.102, f32[8,40]{1,0:T(8,128)} %bitcast.103), custom_call_target="tpu_custom_call" | custom-call | tf_op jit(solution)/shard_map/pallas_call | solution.py:47
  2.9 2.5 %collective-permute-start = (bf16[80,1152]{1,0:T(8,128)(2,1)}, bf16[80,1152]{1,0:T(8,128)(2,1)S(1)}, u32[]{:S(2)}, u32[]{:S(2)}) collective-permute-start(bf16[80,1152]{1,0:T(8,128)(2,1)} %shard_map.149.refs_0_.hidden_ref), channel_id=1, source_target_pairs={{0,2},{2,0},{4,6},{6,4},{1,3},{3,1},{5,7},{7,5},{8,10},{10,8},{12,... | collective-permute-start | bytes 552968 | tf_op jit(solution)/shard_map/ppermute | solution.py:333
  5.4 1.5 collective-permute-start.1
  6.9 1.3 broadcast_in_dim.46
  8.2 7.3 %all-to-all-start = ((s32[16,1,40]{2,1,0:T(1,128)}), s32[16,1,40]{2,1,0:T(1,128)S(1)}, u32[]{:S(2)}, u32[]{:S(2)}) async-start(s32[16,1,40]{2,1,0:T(1,128)} %broadcast_in_dim.46), calls=%async_computation | async-start | bytes 16384 | tf_op jit(solution)/shard_map/all_to_all | solution.py:369
  17.1 5.7 %all-to-all-done = s32[16,1,40]{2,1,0:T(1,128)S(1)} async-done(((s32[16,1,40]{2,1,0:T(1,128)}), s32[16,1,40]{2,1,0:T(1,128)S(1)}, u32[]{:S(2)}, u32[]{:S(2)}) %all-to-all-start) | async-done | bytes 2592 | tf_op jit(solution)/shard_map/all_to_all | solution.py:369
  23.0 0.7 reshape.125.early_ref
  24.5 0.7 copy-done.13
  25.2 18.8 %shard_map.150 = (f32[4,80,1024]{2,1,0:T(8,128)}, f32[4,80,1024]{2,1,0:T(8,128)}) custom-call(s32[2]{0:T(128)} %pad_add_fusion.2.place_ref, s32[1,1280]{1,0:T(1,128)} %reshape.125.early_ref, bf16[80,1152]{1,0:T(8,128)(2,1)} %shard_map.149.refs_0_.hidden_ref, bf16[80,1152]{1,0:T(8,128)(2,1)} %copy-done.7, bf16[80,1152]{1,0:T(8,128)(2,1)} %copy-done.8, ...), custom_call_target="tpu_custom_call" | custom-call | flops 6442450944 | bytes 22970368 | tf_op jit(solution)/shard_map/pallas_call | solution.py:148
  44.0 3.2 %collective-permute-done.7.came_ref = f32[4,80,1024]{2,1,0:T(8,128)S(1)} collective-permute-done((f32[4,80,1024]{2,1,0:T(8,128)}, f32[4,80,1024]{2,1,0:T(8,128)S(1)}, u32[]{:S(2)}, u32[]{:S(2)}) %collective-permute-start.7) | collective-permute-done | bytes 1310752 | tf_op jit(solution)/shard_map/ppermute | solution.py:342
  47.3 1.1 copy-done
  48.4 2.8 %shard_map.151 = (f32[80,1024]{1,0:T(8,128)}, f32[80,1024]{1,0:T(8,128)}, f32[80,1024]{1,0:T(8,128)}, f32[80,1024]{1,0:T(8,128)}) custom-call(f32[4,80,1024]{2,1,0:T(8,128)} %get-tuple-element.8.keep_ref, f32[4,80,1024]{2,1,0:T(8,128)} %copy-done), custom_call_target="tpu_custom_call" | custom-call | tf_op jit(solution)/shard_map/pallas_call | solution.py:195
  51.8 1.5 collective-permute-start.8
  53.3 1.5 collective-permute-start.9
  55.4 7.6 %collective-permute-done.10.refs_2_ = f32[80,1024]{1,0:T(8,128)S(1)} collective-permute-done((f32[80,1024]{1,0:T(8,128)}, f32[80,1024]{1,0:T(8,128)S(1)}, u32[]{:S(2)}, u32[]{:S(2)}) %collective-permute-start.10) | collective-permute-done | bytes 327712 | tf_op jit(solution)/shard_map/ppermute | solution.py:333
  63.0 5.3 %collective-permute-done.8.refs_0_ = f32[80,1024]{1,0:T(8,128)S(1)} collective-permute-done((f32[80,1024]{1,0:T(8,128)}, f32[80,1024]{1,0:T(8,128)S(1)}, u32[]{:S(2)}, u32[]{:S(2)}) %collective-permute-start.8) | collective-permute-done | bytes 327712 | tf_op jit(solution)/shard_map/ppermute | solution.py:333
  68.3 0.8 collective-permute-done.9.refs_1_
  69.1 0.7 copy-done.3
  69.9 2.2 %shard_map.152.refs_0_ = bf16[80,1024]{1,0:T(8,128)(2,1)} custom-call(bf16[80,1152]{1,0:T(8,128)(2,1)} %shard_map.149.refs_0_.hidden_ref, f32[1,1024]{1,0:T(1,128)} %bitcast.104, f32[80,1024]{1,0:T(8,128)} %get-tuple-element.10.own_ref, f32[80,1024]{1,0:T(8,128)} %copy-done.2, f32[80,1024]{1,0:T(8,128)} %copy-done.3, f32[80,1024]{1,0:T(8,128)} %copy-done.1), custom_call_target="tpu_custom_call" | custom-call | tf_op jit(solution)/shard_map/pallas_call | solution.py:212
  73.2 0.6 pad_add_fusion.4.spots_ref
  74.1 0.6 pad_add_fusion.3.spots_ref
  74.7 0.7 slice.92.wanted_ref
  75.4 2.7 %collective-permute-start.19 = (bf16[80,1024]{1,0:T(8,128)(2,1)}, bf16[80,1024]{1,0:T(8,128)(2,1)S(1)}, u32[]{:S(2)}, u32[]{:S(2)}) collective-permute-start(bf16[80,1024]{1,0:T(8,128)(2,1)} %shard_map.152.refs_0_), channel_id=1, source_target_pairs={{0,24},{8,0},{16,8},{24,16},{1,25},{9,1},{17,9},{25,17},{2,26},{10... | collective-permute-start | bytes 491528 | tf_op jit(solution)/shard_map/ppermute | solution.py:338
  78.0 0.6 collective-permute-start.11
  78.6 2.6 %collective-permute-done.13.refs_1_ = bf16[80,1024]{1,0:T(8,128)(2,1)S(1)} collective-permute-done((bf16[80,1024]{1,0:T(8,128)(2,1)}, bf16[80,1024]{1,0:T(8,128)(2,1)S(1)}, u32[]{:S(2)}, u32[]{:S(2)}) %collective-permute-start.13) | collective-permute-done | bytes 163872 | tf_op jit(solution)/shard_map/ppermute | solution.py:338
  81.2 0.7 collective-permute-start.24
  82.0 5.4 %collective-permute-done.16.refs_2_ = bf16[80,1024]{1,0:T(8,128)(2,1)S(1)} collective-permute-done((bf16[80,1024]{1,0:T(8,128)(2,1)}, bf16[80,1024]{1,0:T(8,128)(2,1)S(1)}, u32[]{:S(2)}, u32[]{:S(2)}) %collective-permute-start.16) | collective-permute-done | bytes 163872 | tf_op jit(solution)/shard_map/ppermute | solution.py:338
  87.4 0.6 collective-permute-start.14
  88.0 0.7 fusion.22
  89.2 1.5 collective-permute-start.22
  90.6 1.4 collective-permute-start.20
  92.1 2.4 %collective-permute-done.14.refs_1_ = bf16[80,1024]{1,0:T(8,128)(2,1)S(1)} collective-permute-done((bf16[80,1024]{1,0:T(8,128)(2,1)S(1)}, bf16[80,1024]{1,0:T(8,128)(2,1)S(1)}, u32[]{:S(2)}, u32[]{:S(2)}) %collective-permute-start.14) | collective-permute-done | bytes 163872 | tf_op jit(solution)/shard_map/ppermute | solution.py:333
  95.1 13.0 %shard_map.153.refs_8_ = f32[4,2,80]{2,1,0:T(2,128)} custom-call(s32[6]{0:T(128)} %pad_add_fusion.4.spots_ref, s32[1,320]{1,0:T(1,128)} %get-tuple-element.18.wanted_ref, bf16[80,1024]{1,0:T(8,128)(2,1)} %shard_map.152.refs_0_, bf16[80,1024]{1,0:T(8,128)(2,1)} %copy-done.14, bf16[80,1024]{1,0:T(8,128)(2,1)} %copy-done.16, bf16[80,1024]{1,0:T(8,128)(2,1)} %copy-done.19, ...), custom_call_target="tpu_custom_call" | custom-call | flops 3187671040 | bytes 10616832 | tf_op jit(solution)/shard_map/pallas_call | solution.py:291
  108.2 2.0 %collective-permute-start.12 = (bf16[80,1024]{1,0:T(8,128)(2,1)S(1)}, bf16[80,1024]{1,0:T(8,128)(2,1)S(1)}, u32[]{:S(2)}, u32[]{:S(2)}) collective-permute-start(bf16[80,1024]{1,0:T(8,128)(2,1)S(1)} %collective-permute-done.11.refs_0_), channel_id=1, source_target_pairs={{0,4},{2,6},{4,0},{6,2},{1,5},{3,7},{5,1},{7,3},{8,12},{10,14},{12... | collective-permute-start | bytes 491528 | tf_op jit(solution)/shard_map/ppermute | solution.py:333
  110.3 2.0 %collective-permute-start.18 = (bf16[80,1024]{1,0:T(8,128)(2,1)S(1)}, bf16[80,1024]{1,0:T(8,128)(2,1)S(1)}, u32[]{:S(2)}, u32[]{:S(2)}) collective-permute-start(bf16[80,1024]{1,0:T(8,128)(2,1)S(1)} %collective-permute-done.17.refs_6_), channel_id=1, source_target_pairs={{0,2},{2,0},{4,6},{6,4},{1,3},{3,1},{5,7},{7,5},{8,10},{10,8},{12,... | collective-permute-start | bytes 491528 | tf_op jit(solution)/shard_map/ppermute | solution.py:333
  112.9 0.7 copy-done.26
  113.6 14.4 %shard_map.154.refs_4_ = f32[12,2,80]{2,1,0:T(2,128)} custom-call(s32[14]{0:T(128)} %pad_add_fusion.3.spots_ref, s32[1,640]{1,0:T(1,128)} %slice.92.wanted_ref, bf16[80,1024]{1,0:T(8,128)(2,1)} %copy-done.15, bf16[80,1024]{1,0:T(8,128)(2,1)} %copy-done.17, bf16[80,1024]{1,0:T(8,128)(2,1)} %copy-done.22, bf16[80,1024]{1,0:T(8,128)(2,1)} %copy-done.24, ...), custom_call_target="tpu_custom_call" | custom-call | flops 6375342080 | bytes 11272192 | tf_op jit(solution)/shard_map/pallas_call | solution.py:291
  128.9 13.2 %shard_map.155 = f32[16,2,80]{2,1,0:T(2,128)} custom-call(s32[18]{0:T(128)} %pad_add_fusion.1.spots_ref, s32[1,320]{1,0:T(1,128)} %get-tuple-element.19.wanted_ref, bf16[80,1024]{1,0:T(8,128)(2,1)} %copy-done.23, bf16[80,1024]{1,0:T(8,128)(2,1)} %copy-done.25, bf16[80,1024]{1,0:T(8,128)(2,1)} %copy-done.27, bf16[80,1024]{1,0:T(8,128)(2,1)} %copy-done.28, ...), custom_call_target="tpu_custom_call" | custom-call | flops 3187671040 | bytes 10616832 | tf_op jit(solution)/shard_map/pallas_call | solution.py:291
  142.1 0.7 copy.37
  142.8 3.6 %collective-permute-start.28 = (f32[16,2,80]{2,0,1:T(8,128)S(1)}, f32[16,2,80]{2,0,1:T(8,128)S(1)}, u32[]{:S(2)}, u32[]{:S(2)}) collective-permute-start(f32[16,2,80]{2,0,1:T(8,128)S(1)} %copy.37), channel_id=1, source_target_pairs={{0,16},{8,24},{16,0},{24,8},{1,17},{9,25},{17,1},{25,9},{2,18},{10... | collective-permute-start | bytes 30728 | tf_op jit(solution)/shard_map/ppermute | solution.py:338
  146.6 0.7 fusion.19
  147.3 0.7 slice.98
  148.3 1.8 %collective-permute-done.29 = f32[16,2,80]{2,0,1:T(8,128)S(1)} collective-permute-done((f32[16,2,80]{2,0,1:T(8,128)S(1)}, f32[16,2,80]{2,0,1:T(8,128)S(1)}, u32[]{:S(2)}, u32[]{:S(2)}) %collective-permute-start.29) | collective-permute-done | bytes 10272 | tf_op jit(solution)/shard_map/ppermute | solution.py:338
  150.2 1.5 collective-permute-start.30
  151.7 1.5 collective-permute-start.31
  155.8 2.1 %collective-permute-done.32 = f32[16,2,80]{2,0,1:T(8,128)S(1)} collective-permute-done((f32[16,2,80]{2,0,1:T(8,128)S(1)}, f32[16,2,80]{2,0,1:T(8,128)S(1)}, u32[]{:S(2)}, u32[]{:S(2)}) %collective-permute-start.32) | collective-permute-done | bytes 10272 | tf_op jit(solution)/shard_map/ppermute | solution.py:333
  158.5 0.6 collective-permute-done.33
  159.1 1.3 add_reduce_fusion
  (117 shorter events, 10.2 us)
Async XLA Ops:
  0.6 94.4 %collective-permute-start.26 = (bf16[2432,1024]{1,0:T(8,128)(2,1)}, bf16[2432,1024]{1,0:T(8,128)(2,1)}, u32[]{:S(2)}, u32[]{:S(2)}) collective-permute-start(bf16[2432,1024]{1,0:T(8,128)(2,1)} %refs_5_.1), channel_id=1, source_target_pairs={{0,1},{1,0},{2,3},{3,2},{4,5},{5,4},{6,7},{7,6},{8,9},{9,8},{10,11... | collective-permute-start | bytes 14942216 | tf_op jit(solution)/shard_map/ppermute | solution.py:342
  2.9 13.5 %collective-permute-start = (bf16[80,1152]{1,0:T(8,128)(2,1)}, bf16[80,1152]{1,0:T(8,128)(2,1)S(1)}, u32[]{:S(2)}, u32[]{:S(2)}) collective-permute-start(bf16[80,1152]{1,0:T(8,128)(2,1)} %shard_map.149.refs_0_.hidden_ref), channel_id=1, source_target_pairs={{0,2},{2,0},{4,6},{6,4},{1,3},{3,1},{5,7},{7,5},{8,10},{10,8},{12,... | collective-permute-start | bytes 552968 | tf_op jit(solution)/shard_map/ppermute | solution.py:333
  5.4 11.2 %collective-permute-start.1 = (bf16[80,1152]{1,0:T(8,128)(2,1)}, bf16[80,1152]{1,0:T(8,128)(2,1)S(1)}, u32[]{:S(2)}, u32[]{:S(2)}) collective-permute-start(bf16[80,1152]{1,0:T(8,128)(2,1)} %shard_map.149.refs_0_.hidden_ref), channel_id=1, source_target_pairs={{0,4},{2,6},{4,0},{6,2},{1,5},{3,7},{5,1},{7,3},{8,12},{10,14},{12... | collective-permute-start | bytes 552968 | tf_op jit(solution)/shard_map/ppermute | solution.py:333
  6.9 10.0 %collective-permute-start.2 = (bf16[80,1152]{1,0:T(8,128)(2,1)}, bf16[80,1152]{1,0:T(8,128)(2,1)S(1)}, u32[]{:S(2)}, u32[]{:S(2)}) collective-permute-start(bf16[80,1152]{1,0:T(8,128)(2,1)} %shard_map.149.refs_0_.hidden_ref), channel_id=1, source_target_pairs={{0,6},{2,4},{4,2},{6,0},{1,7},{3,5},{5,3},{7,1},{8,14},{10,12},{12... | collective-permute-start | bytes 552968 | tf_op jit(solution)/shard_map/ppermute | solution.py:333
  6.9 16.8 %collective-permute-start.3 = (bf16[80,1152]{1,0:T(8,128)(2,1)}, bf16[80,1152]{1,0:T(8,128)(2,1)S(1)}, u32[]{:S(2)}, u32[]{:S(2)}) collective-permute-start(bf16[80,1152]{1,0:T(8,128)(2,1)} %shard_map.149.refs_0_.hidden_ref), channel_id=1, source_target_pairs={{0,1},{1,0},{2,3},{3,2},{4,5},{5,4},{6,7},{7,6},{8,9},{9,8},{10,11... | collective-permute-start | bytes 552968 | tf_op jit(solution)/shard_map/ppermute | solution.py:342
  8.2 14.6 %all-to-all-start = ((s32[16,1,40]{2,1,0:T(1,128)}), s32[16,1,40]{2,1,0:T(1,128)S(1)}, u32[]{:S(2)}, u32[]{:S(2)}) async-start(s32[16,1,40]{2,1,0:T(1,128)} %broadcast_in_dim.46), calls=%async_computation | async-start | bytes 16384 | tf_op jit(solution)/shard_map/all_to_all | solution.py:369
  16.4 7.4 %copy-start.7 = (bf16[80,1152]{1,0:T(8,128)(2,1)}, bf16[80,1152]{1,0:T(8,128)(2,1)S(1)}, u32[]{:S(2)}) copy-start(bf16[80,1152]{1,0:T(8,128)(2,1)S(1)} %collective-permute-done.refs_1_) | copy-start | bytes 552964
  16.4 7.3 %collective-permute-start.4 = (bf16[80,1152]{1,0:T(8,128)(2,1)S(1)}, bf16[80,1152]{1,0:T(8,128)(2,1)S(1)}, u32[]{:S(2)}, u32[]{:S(2)}) collective-permute-start(bf16[80,1152]{1,0:T(8,128)(2,1)S(1)} %collective-permute-done.refs_1_), channel_id=1, source_target_pairs={{0,1},{1,0},{2,3},{3,2},{4,5},{5,4},{6,7},{7,6},{8,9},{9,8},{10,11... | collective-permute-start | bytes 552968 | tf_op jit(solution)/shard_map/ppermute | solution.py:342
  16.6 7.1 %copy-start.8 = (bf16[80,1152]{1,0:T(8,128)(2,1)}, bf16[80,1152]{1,0:T(8,128)(2,1)S(1)}, u32[]{:S(2)}) copy-start(bf16[80,1152]{1,0:T(8,128)(2,1)S(1)} %collective-permute-done.1.refs_2_) | copy-start | bytes 552964
  16.6 7.1 %collective-permute-start.5 = (bf16[80,1152]{1,0:T(8,128)(2,1)S(1)}, bf16[80,1152]{1,0:T(8,128)(2,1)S(1)}, u32[]{:S(2)}, u32[]{:S(2)}) collective-permute-start(bf16[80,1152]{1,0:T(8,128)(2,1)S(1)} %collective-permute-done.1.refs_2_), channel_id=1, source_target_pairs={{0,1},{1,0},{2,3},{3,2},{4,5},{5,4},{6,7},{7,6},{8,9},{9,8},{10,11... | collective-permute-start | bytes 552968 | tf_op jit(solution)/shard_map/ppermute | solution.py:342
  16.9 6.9 %copy-start.9 = (bf16[80,1152]{1,0:T(8,128)(2,1)}, bf16[80,1152]{1,0:T(8,128)(2,1)S(1)}, u32[]{:S(2)}) copy-start(bf16[80,1152]{1,0:T(8,128)(2,1)S(1)} %collective-permute-done.2.refs_3_) | copy-start | bytes 552964
  16.9 6.8 %collective-permute-start.6 = (bf16[80,1152]{1,0:T(8,128)(2,1)S(1)}, bf16[80,1152]{1,0:T(8,128)(2,1)S(1)}, u32[]{:S(2)}, u32[]{:S(2)}) collective-permute-start(bf16[80,1152]{1,0:T(8,128)(2,1)S(1)} %collective-permute-done.2.refs_3_), channel_id=1, source_target_pairs={{0,1},{1,0},{2,3},{3,2},{4,5},{5,4},{6,7},{7,6},{8,9},{9,8},{10,11... | collective-permute-start | bytes 552968 | tf_op jit(solution)/shard_map/ppermute | solution.py:342
  23.7 50.2 %copy-start.5 = (s32[32]{0:T(128)S(1)}, s32[32]{0:T(128)}, u32[]{:S(2)}) copy-start(s32[32]{0:T(128)} %param.26) | copy-start | bytes 388
  23.7 51.0 %copy-start.4 = (s32[1,1280]{1,0:T(1,128)S(1)}, s32[1,1280]{1,0:T(1,128)}, u32[]{:S(2)}) copy-start(s32[1,1280]{1,0:T(1,128)} %reshape.125.early_ref) | copy-start | bytes 15364
  44.0 3.2 %collective-permute-start.7 = (f32[4,80,1024]{2,1,0:T(8,128)}, f32[4,80,1024]{2,1,0:T(8,128)S(1)}, u32[]{:S(2)}, u32[]{:S(2)}) collective-permute-start(f32[4,80,1024]{2,1,0:T(8,128)} %get-tuple-element.9), channel_id=1, source_target_pairs={{0,1},{1,0},{2,3},{3,2},{4,5},{5,4},{6,7},{7,6},{8,9},{9,8},{10,11... | collective-permute-start | bytes 3932168 | tf_op jit(solution)/shard_map/ppermute | solution.py:342
  51.3 11.7 %collective-permute-start.10 = (f32[80,1024]{1,0:T(8,128)}, f32[80,1024]{1,0:T(8,128)S(1)}, u32[]{:S(2)}, u32[]{:S(2)}) collective-permute-start(f32[80,1024]{1,0:T(8,128)} %get-tuple-element.13), channel_id=1, source_target_pairs={{0,6},{2,4},{4,2},{6,0},{1,7},{3,5},{5,3},{7,1},{8,14},{10,12},{12... | collective-permute-start | bytes 983048 | tf_op jit(solution)/shard_map/ppermute | solution.py:333
  51.8 16.5 %collective-permute-start.8 = (f32[80,1024]{1,0:T(8,128)}, f32[80,1024]{1,0:T(8,128)S(1)}, u32[]{:S(2)}, u32[]{:S(2)}) collective-permute-start(f32[80,1024]{1,0:T(8,128)} %get-tuple-element.11), channel_id=1, source_target_pairs={{0,2},{2,0},{4,6},{6,4},{1,3},{3,1},{5,7},{7,5},{8,10},{10,8},{12,... | collective-permute-start | bytes 983048 | tf_op jit(solution)/shard_map/ppermute | solution.py:333
  53.3 15.9 %collective-permute-start.9 = (f32[80,1024]{1,0:T(8,128)}, f32[80,1024]{1,0:T(8,128)S(1)}, u32[]{:S(2)}, u32[]{:S(2)}) collective-permute-start(f32[80,1024]{1,0:T(8,128)} %get-tuple-element.12), channel_id=1, source_target_pairs={{0,4},{2,6},{4,0},{6,2},{1,5},{3,7},{5,1},{7,3},{8,12},{10,14},{12... | collective-permute-start | bytes 983048 | tf_op jit(solution)/shard_map/ppermute | solution.py:333
  63.0 6.2 %copy-start.1 = (f32[80,1024]{1,0:T(8,128)}, f32[80,1024]{1,0:T(8,128)S(1)}, u32[]{:S(2)}) copy-start(f32[80,1024]{1,0:T(8,128)S(1)} %collective-permute-done.10.refs_2_) | copy-start | bytes 983044
  72.1 9.2 %collective-permute-start.13 = (bf16[80,1024]{1,0:T(8,128)(2,1)}, bf16[80,1024]{1,0:T(8,128)(2,1)S(1)}, u32[]{:S(2)}, u32[]{:S(2)}) collective-permute-start(bf16[80,1024]{1,0:T(8,128)(2,1)} %shard_map.152.refs_0_), channel_id=1, source_target_pairs={{0,8},{8,16},{16,24},{24,0},{1,9},{9,17},{17,25},{25,1},{2,10},{10... | collective-permute-start | bytes 491528 | tf_op jit(solution)/shard_map/ppermute | solution.py:338
  72.7 14.7 %collective-permute-start.16 = (bf16[80,1024]{1,0:T(8,128)(2,1)}, bf16[80,1024]{1,0:T(8,128)(2,1)S(1)}, u32[]{:S(2)}, u32[]{:S(2)}) collective-permute-start(bf16[80,1024]{1,0:T(8,128)(2,1)} %shard_map.152.refs_0_), channel_id=1, source_target_pairs={{0,16},{8,24},{16,0},{24,8},{1,17},{9,25},{17,1},{25,9},{2,18},{10... | collective-permute-start | bytes 491528 | tf_op jit(solution)/shard_map/ppermute | solution.py:338
  75.4 13.2 %collective-permute-start.19 = (bf16[80,1024]{1,0:T(8,128)(2,1)}, bf16[80,1024]{1,0:T(8,128)(2,1)S(1)}, u32[]{:S(2)}, u32[]{:S(2)}) collective-permute-start(bf16[80,1024]{1,0:T(8,128)(2,1)} %shard_map.152.refs_0_), channel_id=1, source_target_pairs={{0,24},{8,0},{16,8},{24,16},{1,25},{9,1},{17,9},{25,17},{2,26},{10... | collective-permute-start | bytes 491528 | tf_op jit(solution)/shard_map/ppermute | solution.py:338
  78.0 11.1 %collective-permute-start.11 = (bf16[80,1024]{1,0:T(8,128)(2,1)}, bf16[80,1024]{1,0:T(8,128)(2,1)S(1)}, u32[]{:S(2)}, u32[]{:S(2)}) collective-permute-start(bf16[80,1024]{1,0:T(8,128)(2,1)} %shard_map.152.refs_0_), channel_id=1, source_target_pairs={{0,2},{2,0},{4,6},{6,4},{1,3},{3,1},{5,7},{7,5},{8,10},{10,8},{12,... | collective-permute-start | bytes 491528 | tf_op jit(solution)/shard_map/ppermute | solution.py:333
  81.2 13.9 %copy-start.14 = (bf16[80,1024]{1,0:T(8,128)(2,1)}, bf16[80,1024]{1,0:T(8,128)(2,1)S(1)}, u32[]{:S(2)}) copy-start(bf16[80,1024]{1,0:T(8,128)(2,1)S(1)} %collective-permute-done.13.refs_1_) | copy-start | bytes 491524
  81.2 9.4 %collective-permute-start.24 = (bf16[80,1024]{1,0:T(8,128)(2,1)}, bf16[80,1024]{1,0:T(8,128)(2,1)S(1)}, u32[]{:S(2)}, u32[]{:S(2)}) collective-permute-start(bf16[80,1024]{1,0:T(8,128)(2,1)} %shard_map.152.refs_0_), channel_id=1, source_target_pairs={{0,4},{2,6},{4,0},{6,2},{1,5},{3,7},{5,1},{7,3},{8,12},{10,14},{12... | collective-permute-start | bytes 491528 | tf_op jit(solution)/shard_map/ppermute | solution.py:333
  87.4 7.7 %copy-start.16 = (bf16[80,1024]{1,0:T(8,128)(2,1)}, bf16[80,1024]{1,0:T(8,128)(2,1)S(1)}, u32[]{:S(2)}) copy-start(bf16[80,1024]{1,0:T(8,128)(2,1)S(1)} %collective-permute-done.16.refs_2_) | copy-start | bytes 491524
  87.4 7.1 %collective-permute-start.14 = (bf16[80,1024]{1,0:T(8,128)(2,1)S(1)}, bf16[80,1024]{1,0:T(8,128)(2,1)S(1)}, u32[]{:S(2)}, u32[]{:S(2)}) collective-permute-start(bf16[80,1024]{1,0:T(8,128)(2,1)S(1)} %collective-permute-done.13.refs_1_), channel_id=1, source_target_pairs={{0,2},{2,0},{4,6},{6,4},{1,3},{3,1},{5,7},{7,5},{8,10},{10,8},{12,... | collective-permute-start | bytes 491528 | tf_op jit(solution)/shard_map/ppermute | solution.py:333
  88.6 6.5 %copy-start.19 = (bf16[80,1024]{1,0:T(8,128)(2,1)}, bf16[80,1024]{1,0:T(8,128)(2,1)S(1)}, u32[]{:S(2)}) copy-start(bf16[80,1024]{1,0:T(8,128)(2,1)S(1)} %collective-permute-done.19.refs_3_) | copy-start | bytes 491524
  88.6 19.5 %collective-permute-start.17 = (bf16[80,1024]{1,0:T(8,128)(2,1)S(1)}, bf16[80,1024]{1,0:T(8,128)(2,1)S(1)}, u32[]{:S(2)}, u32[]{:S(2)}) collective-permute-start(bf16[80,1024]{1,0:T(8,128)(2,1)S(1)} %collective-permute-done.16.refs_2_), channel_id=1, source_target_pairs={{0,4},{2,6},{4,0},{6,2},{1,5},{3,7},{5,1},{7,3},{8,12},{10,14},{12... | collective-permute-start | bytes 491528 | tf_op jit(solution)/shard_map/ppermute | solution.py:333
  89.2 19.0 %copy-start.15 = (bf16[80,1024]{1,0:T(8,128)(2,1)}, bf16[80,1024]{1,0:T(8,128)(2,1)S(1)}, u32[]{:S(2)}) copy-start(bf16[80,1024]{1,0:T(8,128)(2,1)S(1)} %collective-permute-done.11.refs_0_) | copy-start | bytes 491524
  89.2 21.1 %collective-permute-start.22 = (bf16[80,1024]{1,0:T(8,128)(2,1)S(1)}, bf16[80,1024]{1,0:T(8,128)(2,1)S(1)}, u32[]{:S(2)}, u32[]{:S(2)}) collective-permute-start(bf16[80,1024]{1,0:T(8,128)(2,1)S(1)} %collective-permute-done.16.refs_2_), channel_id=1, source_target_pairs={{0,2},{2,0},{4,6},{6,4},{1,3},{3,1},{5,7},{7,5},{8,10},{10,8},{12,... | collective-permute-start | bytes 491528 | tf_op jit(solution)/shard_map/ppermute | solution.py:333
  90.6 17.5 %copy-start.18 = (bf16[80,1024]{1,0:T(8,128)(2,1)}, bf16[80,1024]{1,0:T(8,128)(2,1)S(1)}, u32[]{:S(2)}) copy-start(bf16[80,1024]{1,0:T(8,128)(2,1)S(1)} %collective-permute-done.24.refs_4_) | copy-start | bytes 491524
  90.6 19.5 %collective-permute-start.20 = (bf16[80,1024]{1,0:T(8,128)(2,1)S(1)}, bf16[80,1024]{1,0:T(8,128)(2,1)S(1)}, u32[]{:S(2)}, u32[]{:S(2)}) collective-permute-start(bf16[80,1024]{1,0:T(8,128)(2,1)S(1)} %collective-permute-done.19.refs_3_), channel_id=1, source_target_pairs={{0,4},{2,6},{4,0},{6,2},{1,5},{3,7},{5,1},{7,3},{8,12},{10,14},{12... | collective-permute-start | bytes 491528 | tf_op jit(solution)/shard_map/ppermute | solution.py:333
  94.5 15.7 %copy-start.17 = (bf16[80,1024]{1,0:T(8,128)(2,1)}, bf16[80,1024]{1,0:T(8,128)(2,1)S(1)}, u32[]{:S(2)}) copy-start(bf16[80,1024]{1,0:T(8,128)(2,1)S(1)} %collective-permute-done.14.refs_1_) | copy-start | bytes 491524
  94.5 17.8 %collective-permute-start.23 = (bf16[80,1024]{1,0:T(8,128)(2,1)S(1)}, bf16[80,1024]{1,0:T(8,128)(2,1)S(1)}, u32[]{:S(2)}, u32[]{:S(2)}) collective-permute-start(bf16[80,1024]{1,0:T(8,128)(2,1)S(1)} %collective-permute-done.19.refs_3_), channel_id=1, source_target_pairs={{0,2},{2,0},{4,6},{6,4},{1,3},{3,1},{5,7},{7,5},{8,10},{10,8},{12,... | collective-permute-start | bytes 491528 | tf_op jit(solution)/shard_map/ppermute | solution.py:333
  95.0 17.4 %collective-permute-start.25 = (bf16[80,1024]{1,0:T(8,128)(2,1)S(1)}, bf16[80,1024]{1,0:T(8,128)(2,1)S(1)}, u32[]{:S(2)}, u32[]{:S(2)}) collective-permute-start(bf16[80,1024]{1,0:T(8,128)(2,1)S(1)} %collective-permute-done.13.refs_1_), channel_id=1, source_target_pairs={{0,4},{2,6},{4,0},{6,2},{1,5},{3,7},{5,1},{7,3},{8,12},{10,14},{12... | collective-permute-start | bytes 491528 | tf_op jit(solution)/shard_map/ppermute | solution.py:333
  108.2 19.9 %collective-permute-start.12 = (bf16[80,1024]{1,0:T(8,128)(2,1)S(1)}, bf16[80,1024]{1,0:T(8,128)(2,1)S(1)}, u32[]{:S(2)}, u32[]{:S(2)}) collective-permute-start(bf16[80,1024]{1,0:T(8,128)(2,1)S(1)} %collective-permute-done.11.refs_0_), channel_id=1, source_target_pairs={{0,4},{2,6},{4,0},{6,2},{1,5},{3,7},{5,1},{7,3},{8,12},{10,14},{12... | collective-permute-start | bytes 491528 | tf_op jit(solution)/shard_map/ppermute | solution.py:333
  110.2 17.8 %collective-permute-start.15 = (bf16[80,1024]{1,0:T(8,128)(2,1)S(1)}, bf16[80,1024]{1,0:T(8,128)(2,1)S(1)}, u32[]{:S(2)}, u32[]{:S(2)}) collective-permute-start(bf16[80,1024]{1,0:T(8,128)(2,1)S(1)} %collective-permute-done.14.refs_1_), channel_id=1, source_target_pairs={{0,4},{2,6},{4,0},{6,2},{1,5},{3,7},{5,1},{7,3},{8,12},{10,14},{12... | collective-permute-start | bytes 491528 | tf_op jit(solution)/shard_map/ppermute | solution.py:333
  110.3 17.7 %collective-permute-start.18 = (bf16[80,1024]{1,0:T(8,128)(2,1)S(1)}, bf16[80,1024]{1,0:T(8,128)(2,1)S(1)}, u32[]{:S(2)}, u32[]{:S(2)}) collective-permute-start(bf16[80,1024]{1,0:T(8,128)(2,1)S(1)} %collective-permute-done.17.refs_6_), channel_id=1, source_target_pairs={{0,2},{2,0},{4,6},{6,4},{1,3},{3,1},{5,7},{7,5},{8,10},{10,8},{12,... | collective-permute-start | bytes 491528 | tf_op jit(solution)/shard_map/ppermute | solution.py:333
  112.3 15.8 %collective-permute-start.21 = (bf16[80,1024]{1,0:T(8,128)(2,1)S(1)}, bf16[80,1024]{1,0:T(8,128)(2,1)S(1)}, u32[]{:S(2)}, u32[]{:S(2)}) collective-permute-start(bf16[80,1024]{1,0:T(8,128)(2,1)S(1)} %collective-permute-done.20.refs_7_), channel_id=1, source_target_pairs={{0,2},{2,0},{4,6},{6,4},{1,3},{3,1},{5,7},{7,5},{8,10},{10,8},{12,... | collective-permute-start | bytes 491528 | tf_op jit(solution)/shard_map/ppermute | solution.py:333
  128.9 17.8 %copy-start.6 = (s32[32]{0:T(128)S(1)}, s32[32]{0:T(128)}, u32[]{:S(2)}) copy-start(s32[32]{0:T(128)} %param.27) | copy-start | bytes 388
  142.8 5.5 %collective-permute-start.27 = (f32[16,2,80]{2,0,1:T(8,128)S(1)}, f32[16,2,80]{2,0,1:T(8,128)S(1)}, u32[]{:S(2)}, u32[]{:S(2)}) collective-permute-start(f32[16,2,80]{2,0,1:T(8,128)S(1)} %copy.37), channel_id=1, source_target_pairs={{0,8},{8,16},{16,24},{24,0},{1,9},{9,17},{17,25},{25,1},{2,10},{10... | collective-permute-start | bytes 30728 | tf_op jit(solution)/shard_map/ppermute | solution.py:338
  142.8 5.5 %collective-permute-start.28 = (f32[16,2,80]{2,0,1:T(8,128)S(1)}, f32[16,2,80]{2,0,1:T(8,128)S(1)}, u32[]{:S(2)}, u32[]{:S(2)}) collective-permute-start(f32[16,2,80]{2,0,1:T(8,128)S(1)} %copy.37), channel_id=1, source_target_pairs={{0,16},{8,24},{16,0},{24,8},{1,17},{9,25},{17,1},{25,9},{2,18},{10... | collective-permute-start | bytes 30728 | tf_op jit(solution)/shard_map/ppermute | solution.py:338
  146.5 3.7 %collective-permute-start.29 = (f32[16,2,80]{2,0,1:T(8,128)S(1)}, f32[16,2,80]{2,0,1:T(8,128)S(1)}, u32[]{:S(2)}, u32[]{:S(2)}) collective-permute-start(f32[16,2,80]{2,0,1:T(8,128)S(1)} %copy.37), channel_id=1, source_target_pairs={{0,24},{8,0},{16,8},{24,16},{1,25},{9,1},{17,9},{25,17},{2,26},{10... | collective-permute-start | bytes 30728 | tf_op jit(solution)/shard_map/ppermute | solution.py:338
  150.2 5.5 %collective-permute-start.30 = (f32[16,2,80]{2,0,1:T(8,128)S(1)}, f32[16,2,80]{2,0,1:T(8,128)S(1)}, u32[]{:S(2)}, u32[]{:S(2)}) collective-permute-start(f32[16,2,80]{2,0,1:T(8,128)S(1)} %pad_maximum_fusion), channel_id=1, source_target_pairs={{0,2},{2,0},{4,6},{6,4},{1,3},{3,1},{5,7},{7,5},{8,10},{10,8},{12,... | collective-permute-start | bytes 30728 | tf_op jit(solution)/shard_map/ppermute | solution.py:333
  151.7 4.1 %collective-permute-start.31 = (f32[16,2,80]{2,0,1:T(8,128)S(1)}, f32[16,2,80]{2,0,1:T(8,128)S(1)}, u32[]{:S(2)}, u32[]{:S(2)}) collective-permute-start(f32[16,2,80]{2,0,1:T(8,128)S(1)} %pad_maximum_fusion), channel_id=1, source_target_pairs={{0,4},{2,6},{4,0},{6,2},{1,5},{3,7},{5,1},{7,3},{8,12},{10,14},{12... | collective-permute-start | bytes 30728 | tf_op jit(solution)/shard_map/ppermute | solution.py:333
  153.2 4.6 %collective-permute-start.32 = (f32[16,2,80]{2,0,1:T(8,128)S(1)}, f32[16,2,80]{2,0,1:T(8,128)S(1)}, u32[]{:S(2)}, u32[]{:S(2)}) collective-permute-start(f32[16,2,80]{2,0,1:T(8,128)S(1)} %pad_maximum_fusion), channel_id=1, source_target_pairs={{0,6},{2,4},{4,2},{6,0},{1,7},{3,5},{5,3},{7,1},{8,14},{10,12},{12... | collective-permute-start | bytes 30728 | tf_op jit(solution)/shard_map/ppermute | solution.py:333
  158.0 1.2 collective-permute-start.33
  (16 other events, 18.4 us)

commit v4 on v3

--- a/solution.py
+++ b/solution.py
@@ -52,12 +52,11 @@
     )(pol_hidden, ref_hidden, pol_routes.T, ref_routes.T, pol_gates.T, ref_gates.T)
 
 
-def expert_kernel(block, slots, width, experts, chips, place_ref, early_ref, *refs):
-    del early_ref
+def expert_kernel(block, slots, width, experts, chips, place_ref, *refs):
     count = 2 * chips
     blocks, refs = refs[:count], refs[count:]
     gate_ref, up_ref, down_ref, keep_ref, give_ref = refs[:5]
-    rows_in, table, pick, mix_hi, mix_lo, picked, made = refs[5:]
+    rows_in, table, pick, weight, picked, made = refs[5:]
     step = pl.program_id(0)
     last = pl.num_programs(0) - 1
     rows = rows_in.shape[0]
@@ -90,12 +89,8 @@
             chosen = table[0, pl.ds(row, 1), :] == spot
             band = pl.ds(e * slots, slots)
             pick[band, :] = jnp.where(chosen, 1.0, 0.0).astype(jnp.bfloat16)
-            mix_hi[band, :] = jnp.where(chosen, table[1, pl.ds(row, 1), :], 0.0).astype(
-                jnp.bfloat16
-            )
-            mix_lo[band, :] = jnp.where(
-                chosen, table[1, pl.ds(row + experts, 1), :], 0.0
-            ).astype(jnp.bfloat16)
+            gate = table[1, pl.ds(row, 1), :] + table[1, pl.ds(row + experts, 1), :]
+            weight[band, :] = jnp.sum(jnp.where(chosen, gate, 0.0), axis=1, keepdims=True)
         picked[...] = jnp.dot(
             pick[...], rows_in[:, :width], preferred_element_type=jnp.float32
         ).astype(jnp.bfloat16)
@@ -105,9 +100,11 @@
     gate_act = jnp.dot(mine, gate_ref[0], preferred_element_type=jnp.float32)
     up_act = jnp.dot(mine, up_ref[0], preferred_element_type=jnp.float32)
     inner = (gate_act / (1.0 + jnp.exp(-gate_act)) * up_act).astype(jnp.bfloat16)
-    made[band, :] = jnp.dot(inner, down_ref[0], preferred_element_type=jnp.float32).astype(
-        jnp.bfloat16
-    )
+    output = jnp.dot(inner, down_ref[0], preferred_element_type=jnp.float32).astype(jnp.bfloat16)
+    scaled = output.astype(jnp.float32) * weight[band, :]
+    high = scaled.astype(jnp.bfloat16)
+    made[band, :width] = high
+    made[band, width:] = (scaled - high.astype(jnp.float32)).astype(jnp.bfloat16)
 
     @pl.when(step == last)
     def _():
@@ -116,11 +113,9 @@
         for start in range(0, rows, span):
             band = pl.ds(start, span)
             total = lax.dot_general(
-                mix_hi[:, band], made[...], over_slots, preferred_element_type=jnp.float32
+                pick[:, band], made[...], over_slots, preferred_element_type=jnp.float32
             )
-            total += lax.dot_general(
-                mix_lo[:, band], made[...], over_slots, preferred_element_type=jnp.float32
-            )
+            total = total[:, :width] + total[:, width:]
             for index in range(span // share):
                 c, owner = divmod(start // share + index, 2)
                 target = total[index * share:(index + 1) * share]
@@ -134,7 +129,7 @@
                     give_ref[c ^ chip] = target
 
 
-def expert_sums(place, early, blocks, w_gate, w_up, w_down, block, capacity, width, experts):
+def expert_sums(place, blocks, w_gate, w_up, w_down, block, capacity, width, experts):
     count = len(blocks)
     share, wide = blocks[0].shape
     rows = count * share
@@ -151,7 +146,7 @@
         grid_spec=pltpu.PrefetchScalarGridSpec(
             num_scalar_prefetch=1,
             grid=(local_experts,),
-            in_specs=[pl.BlockSpec(memory_space=pl.ANY)] + [whole] * count + [
+            in_specs=[whole] * count + [
                 pl.BlockSpec((1, width, hidden), lambda e, place: (e, 0, 0)),
                 pl.BlockSpec((1, width, hidden), lambda e, place: (e, 0, 0)),
                 pl.BlockSpec((1, hidden, width), lambda e, place: (e, 0, 0)),
@@ -168,38 +163,41 @@
                 pltpu.VMEM((rows, wide), jnp.bfloat16),
                 pltpu.VMEM((2, wide - width, rows), jnp.float32),
                 pltpu.VMEM((every, rows), jnp.bfloat16),
-                pltpu.VMEM((every, rows), jnp.bfloat16),
-                pltpu.VMEM((every, rows), jnp.bfloat16),
+                pltpu.VMEM((every, 1), jnp.float32),
                 pltpu.VMEM((every, width), jnp.bfloat16),
-                pltpu.VMEM((every, width), jnp.bfloat16),
+                pltpu.VMEM((every, 2 * width), jnp.bfloat16),
             ],
         ),
-        compiler_params=pltpu.CompilerParams(vmem_limit_bytes=58 * MIB),
+        compiler_params=pltpu.CompilerParams(
+            vmem_limit_bytes=(36 if rows <= 640 else 58) * MIB
+        ),
         cost_estimate=pl.CostEstimate(
             flops=2 * every * width * (3 * hidden + 3 * rows),
             bytes_accessed=w_gate.size * 6 + rows * wide * 2 + rows * width * 4,
             transcendentals=every * hidden,
         ),
-    )(place, early, *blocks, w_gate, w_up, w_down)
-
-
-def pair_kernel(keep_ref, came_ref, own_ref, *sends):
-    own_ref[...] = keep_ref[0] + came_ref[0]
-    for index, send in enumerate(sends):
-        send[...] = keep_ref[index + 1] + came_ref[index + 1]
-
-
-def pair_sums(keep, came):
+    )(place, *blocks, w_gate, w_up, w_down)
+
+
+def pair_kernel(keep_ref, came_ref, targets_ref, goal_ref, *sums):
+    for index, total in enumerate(sums):
+        total[...] = keep_ref[index] + came_ref[index]
+    goal_ref[...] = jnp.broadcast_to(targets_ref[...], goal_ref.shape)
+
+
+def pair_sums(keep, came, targets, peers):
     chips, share, width = keep.shape
-    own = jax.ShapeDtypeStruct((share, width), jnp.float32)
+    part = jax.ShapeDtypeStruct((share, width), jnp.float32)
+    goal = jax.ShapeDtypeStruct((peers, targets.shape[0]), jnp.int32)
     return pl.pallas_call(
         pair_kernel,
-        out_shape=(own,) * chips,
-        compiler_params=pltpu.CompilerParams(vmem_limit_bytes=58 * MIB),
-    )(keep, came)
-
-
-def norm_kernel(hidden_ref, gain_ref, own_ref, *refs):
+        out_shape=(goal,) + (part,) * chips,
+        compiler_params=pltpu.CompilerParams(vmem_limit_bytes=24 * MIB),
+    )(keep, came, targets.reshape(1, -1))
+
+
+def norm_kernel(hidden_ref, gain_ref, early_ref, own_ref, *refs):
+    del early_ref
     width = own_ref.shape[1]
     mixed = hidden_ref[:, :width].astype(jnp.float32) + own_ref[...]
     for ref in refs[:-1]:
@@ -208,12 +206,12 @@
     refs[-1][...] = (mixed * scale * gain_ref[...]).astype(jnp.bfloat16)
 
 
-def norm_rows(hidden, gain, own, others):
+def norm_rows(hidden, gain, early, own, others):
     return pl.pallas_call(
         norm_kernel,
         out_shape=jax.ShapeDtypeStruct(own.shape, jnp.bfloat16),
-        compiler_params=pltpu.CompilerParams(vmem_limit_bytes=58 * MIB),
-    )(hidden, gain.reshape(1, -1), own, *others)
+        compiler_params=pltpu.CompilerParams(vmem_limit_bytes=16 * MIB),
+    )(hidden, gain.reshape(1, -1), early, own, *others)
 
 
 def head_kernel(count, before, spots_ref, wanted_ref, *refs):
@@ -286,7 +284,7 @@
     places = spots.shape[0] - 2
     rows = sum(block.shape[0] for block in blocks)
     width = head_a.shape[1]
-    tile = largest_tile(head_a.shape[0], 608 * 1280 // rows, 16)
+    tile = largest_tile(head_a.shape[0], 608, 16)
     steps = head_a.shape[0] // tile
     return pl.pallas_call(
         functools.partial(head_kernel, len(blocks), len(earlier)),
@@ -365,20 +363,17 @@
     home = (group - jnp.arange(groups, dtype=jnp.int32)) % groups
     spots = home[None, :] * chips + (chip ^ jnp.arange(chips, dtype=jnp.int32))[:, None]
     spots = spots.reshape(-1)
-    goal = jnp.broadcast_to(targets[None], (groups * chips, tokens))
+    other_head = partner(vocab_head)
+
+    place = jnp.stack((chip, core)).astype(jnp.int32)
+    keep, give = expert_sums(place, plane, w_gate, w_up, w_down, tokens, capacity, width, experts)
+    goal, own, *sends = pair_sums(keep, partner(give), targets, groups * chips)
+    came = [across(rows, d) for d, rows in zip(offsets, sends)]
     goal = lax.all_to_all(goal, ("grp", "chip"), split_axis=0, concat_axis=0, tiled=True)
-    place = spots[:, None] == jnp.arange(groups * chips, dtype=jnp.int32)[None, :]
-    goal = jnp.sum(jnp.where(place[:, :, None], goal[None], 0), axis=1)
+    match = spots[:, None] == jnp.arange(groups * chips, dtype=jnp.int32)[None, :]
+    goal = jnp.sum(jnp.where(match[:, :, None], goal[None], 0), axis=1)
     wanted = jnp.concatenate((goal, goal), axis=1).reshape(1, -1)
-    other_head = partner(vocab_head)
-
-    place = jnp.stack((chip, core)).astype(jnp.int32)
-    keep, give = expert_sums(
-        place, wanted, plane, w_gate, w_up, w_down, tokens, capacity, width, experts
-    )
-    own, *sends = pair_sums(keep, partner(give))
-    came = [across(rows, d) for d, rows in zip(offsets, sends)]
-    normed = norm_rows(send, norm_gain, own, came)
+    normed = norm_rows(send, norm_gain, wanted, own, came)
 
     column = [normed] + [along(normed, k) for k in range(1, groups)]
     if chips == 4:

time: 163 us -> 155 us (0.951)
  Pallas kernels: 66.3 us -> 51.8 us
  starting transfers between devices: 37.5 us -> 43.9 us
  local copies, waits for them, and re-layouts: 10.7 us -> 13 us
  waiting for transfers between devices: 37.9 us -> 36 us
    pallas_call x3, Pallas kernels: 40.7 us -> 33.6 us  [head_stats(): pl.pallas_call(functools.partial(head_kernel, len(blocks), len(earlier)),...]
    ppermute x21, starting transfers between devices: 21.2 us -> 26 us  [across(): return lax.ppermute(value, 'chip', [(c, c ^ offset) for c in range(chips)])]
    unnamed x58 -> x52, local copies, waits for them, and re-layouts: 5.33 us -> 9.43 us
    pallas_call x1, Pallas kernels: 18.8 us -> 15.5 us  [expert_sums(): pl.pallas_call(functools.partial(expert_kernel, block, slots, width, expe...]
    ppermute x21, waiting for transfers between devices: 18.2 us -> 21.5 us  [across(): return lax.ppermute(value, 'chip', [(c, c ^ offset) for c in range(chips)])]
    ppermute x6, waiting for transfers between devices: 10.1 us -> 7 us  [along(): lax.ppermute(value, 'grp', [(g, (g + offset) % groups) for g in range(gro...]
    ppermute x6, starting transfers between devices: 7.65 us -> 10.7 us  [along(): lax.ppermute(value, 'grp', [(g, (g + offset) % groups) for g in range(gro...]
    all_to_all x1, waiting for transfers between devices: 5.68 us -> 3.12 us  [local(): lax.all_to_all(goal, ('grp', 'chip'), split_axis=0, concat_axis=0, tiled=...]
  transfers between devices with their start and end apart: 35 -> 35, of which waited for: 12 -> 14; matrix products, arithmetic and copies ran while one was open for 5% -> 4% of each run, Pallas kernels for 33% -> 27%
where the time goes in v4:
time: 155 us; the launch traced here: 154 us
  Pallas kernels  51.8 us (33%)
  starting transfers between devices  43.9 us (28%)
  waiting for transfers between devices  36 us (23%)
  local copies, waits for them, and re-layouts  13 us (8%)
  other arithmetic  4.68 us (3%)
  between operations  4.56 us (3%)
    pallas_call x3, Pallas kernels, head_stats(): pl.pallas_call(functools.partial(head_kernel, len(blocks), len(earlier)),...  33.6 us
    ppermute x21, starting transfers between devices, across(): return lax.ppermute(value, 'chip', [(c, c ^ offset) for c in range(chips)])  26 us
    ppermute x21, waiting for transfers between devices, across(): return lax.ppermute(value, 'chip', [(c, c ^ offset) for c in range(chips)])  21.5 us
    pallas_call x1, Pallas kernels, expert_sums(): pl.pallas_call(functools.partial(expert_kernel, block, slots, width, expe...  15.5 us
    ppermute x6, starting transfers between devices, along(): lax.ppermute(value, 'grp', [(g, (g + offset) % groups) for g in range(gro...  10.7 us
    unnamed x52, local copies, waits for them, and re-layouts  9.43 us
    ppermute x6, waiting for transfers between devices, along(): lax.ppermute(value, 'grp', [(g, (g + offset) % groups) for g in range(gro...  7 us
    all_to_all x1, starting transfers between devices, local(): lax.all_to_all(goal, ('grp', 'chip'), split_axis=0, concat_axis=0, tiled=...  5.94 us
  transfers between devices with their start and end apart: 35, of which 14 were waited for; matrix products, arithmetic and copies ran while one was open for 4% of the time, Pallas kernels for 27%

profile of v4, /device:TPU:0, one launch (start us, length us, event | category | flops | bytes accessed | tf_op | source)
XLA Modules:
  0.0 153.9 jit_solution(3096327577773744661)
XLA Ops:
  1.1 1.8 %shard_map.149.refs_0_.hidden_ref = bf16[80,1152]{1,0:T(8,128)(2,1)} custom-call(bf16[40,1024]{1,0:T(8,128)(2,1)} %pol_ref.1, bf16[40,1024]{1,0:T(8,128)(2,1)} %ref_ref.1, s32[8,40]{1,0:T(8,128)} %bitcast.106, s32[8,40]{1,0:T(8,128)} %bitcast.107, f32[8,40]{1,0:T(8,128)} %bitcast.108, f32[8,40]{1,0:T(8,128)} %bitcast.109), custom_call_target="tpu_custom_call" | custom-call | tf_op jit(solution)/shard_map/pallas_call | solution.py:47
  2.9 2.5 %collective-permute-start = (bf16[80,1152]{1,0:T(8,128)(2,1)}, bf16[80,1152]{1,0:T(8,128)(2,1)S(1)}, u32[]{:S(2)}, u32[]{:S(2)}) collective-permute-start(bf16[80,1152]{1,0:T(8,128)(2,1)} %shard_map.149.refs_0_.hidden_ref), channel_id=1, source_target_pairs={{0,2},{2,0},{4,6},{6,4},{1,3},{3,1},{5,7},{7,5},{8,10},{10,8},{12,... | collective-permute-start | bytes 552968 | tf_op jit(solution)/shard_map/ppermute | solution.py:331
  5.4 1.5 collective-permute-start.1
  6.9 4.2 %collective-permute-done.refs_1_ = bf16[80,1152]{1,0:T(8,128)(2,1)S(1)} collective-permute-done((bf16[80,1152]{1,0:T(8,128)(2,1)}, bf16[80,1152]{1,0:T(8,128)(2,1)S(1)}, u32[]{:S(2)}, u32[]{:S(2)}) %collective-permute-start) | collective-permute-done | bytes 184352 | tf_op jit(solution)/shard_map/ppermute | solution.py:331
  11.1 5.2 %collective-permute-done.1.refs_2_ = bf16[80,1152]{1,0:T(8,128)(2,1)S(1)} collective-permute-done((bf16[80,1152]{1,0:T(8,128)(2,1)}, bf16[80,1152]{1,0:T(8,128)(2,1)S(1)}, u32[]{:S(2)}, u32[]{:S(2)}) %collective-permute-start.1) | collective-permute-done | bytes 184352 | tf_op jit(solution)/shard_map/ppermute | solution.py:331
  16.9 0.8 collective-permute-done.5.refs_6_
  18.0 0.9 copy-done
  18.9 2.8 %copy-done.5 = bf16[8,1024,384]{2,1,0:T(8,128)(2,1)S(1)} copy-done((bf16[8,1024,384]{2,1,0:T(8,128)(2,1)S(1)}, bf16[8,1024,384]{2,1,0:T(8,128)(2,1)}, u32[]{:S(2)}) %copy-start.5) | copy-done | bytes 6291480
  21.7 2.8 %copy-done.6 = bf16[8,1024,384]{2,1,0:T(8,128)(2,1)S(1)} copy-done((bf16[8,1024,384]{2,1,0:T(8,128)(2,1)S(1)}, bf16[8,1024,384]{2,1,0:T(8,128)(2,1)}, u32[]{:S(2)}) %copy-start.6) | copy-done | bytes 6291480
  24.5 15.5 %shard_map.150 = (f32[4,80,1024]{2,1,0:T(8,128)S(1)}, f32[4,80,1024]{2,1,0:T(8,128)}) custom-call(s32[2]{0:T(128)S(1)} %pad_add_fusion.2.place_ref, bf16[80,1152]{1,0:T(8,128)(2,1)S(1)} %copy-done, bf16[80,1152]{1,0:T(8,128)(2,1)S(1)} %collective-permute-done.refs_1_, bf16[80,1152]{1,0:T(8,128)(2,1)S(1)} %collective-permute-done.1.refs_2_, ...), custom_call_target="tpu_custom_call" | custom-call | flops 6442450944 | bytes 22970368 | tf_op jit(solution)/shard_map/pallas_call | solution.py:143
  40.6 2.7 %collective-permute-done.7.came_ref = f32[4,80,1024]{2,1,0:T(8,128)S(1)} collective-permute-done((f32[4,80,1024]{2,1,0:T(8,128)}, f32[4,80,1024]{2,1,0:T(8,128)S(1)}, u32[]{:S(2)}, u32[]{:S(2)}) %collective-permute-start.7) | collective-permute-done | bytes 1310752 | tf_op jit(solution)/shard_map/ppermute | solution.py:340
  43.3 0.7 shard_map.151
  44.0 0.7 copy-done.7
  44.7 0.7 copy-done.8
  45.5 5.9 %all-to-all-start = ((s32[16,1,40]{2,1,0:T(1,128)}), s32[16,1,40]{2,1,0:T(1,128)S(1)}, u32[]{:S(2)}, u32[]{:S(2)}) async-start(s32[16,1,40]{2,1,0:T(1,128)} %bitcast.10), calls=%async_computation | async-start | bytes 16384 | tf_op jit(solution)/shard_map/all_to_all | solution.py:372
  51.4 2.8 %collective-permute-start.10 = (f32[80,1024]{1,0:T(8,128)}, f32[80,1024]{1,0:T(8,128)S(1)}, u32[]{:S(2)}, u32[]{:S(2)}) collective-permute-start(f32[80,1024]{1,0:T(8,128)} %copy-done.8), channel_id=1, source_target_pairs={{0,6},{2,4},{4,2},{6,0},{1,7},{3,5},{5,3},{7,1},{8,14},{10,12},{12... | collective-permute-start | bytes 983048 | tf_op jit(solution)/shard_map/ppermute | solution.py:331
  55.0 0.7 pad_add_fusion.1.spots_ref
  55.6 3.1 %all-to-all-done = s32[16,1,40]{2,1,0:T(1,128)S(1)} async-done(((s32[16,1,40]{2,1,0:T(1,128)}), s32[16,1,40]{2,1,0:T(1,128)S(1)}, u32[]{:S(2)}, u32[]{:S(2)}) %all-to-all-start) | async-done | bytes 2592 | tf_op jit(solution)/shard_map/all_to_all | solution.py:372
  59.0 4.2 %collective-permute-done.10.refs_2_ = f32[80,1024]{1,0:T(8,128)S(1)} collective-permute-done((f32[80,1024]{1,0:T(8,128)}, f32[80,1024]{1,0:T(8,128)S(1)}, u32[]{:S(2)}, u32[]{:S(2)}) %collective-permute-start.10) | collective-permute-done | bytes 327712 | tf_op jit(solution)/shard_map/ppermute | solution.py:331
  63.2 6.2 %collective-permute-done.8.refs_0_ = f32[80,1024]{1,0:T(8,128)S(1)} collective-permute-done((f32[80,1024]{1,0:T(8,128)}, f32[80,1024]{1,0:T(8,128)S(1)}, u32[]{:S(2)}, u32[]{:S(2)}) %collective-permute-start.8) | collective-permute-done | bytes 327712 | tf_op jit(solution)/shard_map/ppermute | solution.py:331
  69.6 1.5 collective-permute-start.13
  71.1 2.3 %collective-permute-start.16 = (bf16[80,1024]{1,0:T(8,128)(2,1)S(1)}, bf16[80,1024]{1,0:T(8,128)(2,1)S(1)}, u32[]{:S(2)}, u32[]{:S(2)}) collective-permute-start(bf16[80,1024]{1,0:T(8,128)(2,1)S(1)} %shard_map.152.refs_0_), channel_id=1, source_target_pairs={{0,16},{8,24},{16,0},{24,8},{1,17},{9,25},{17,1},{25,9},{2,18},{10... | collective-permute-start | bytes 491528 | tf_op jit(solution)/shard_map/ppermute | solution.py:336
  73.4 0.7 pad_add_fusion.4.spots_ref
  74.9 0.7 slice.92.wanted_ref
  75.6 1.5 collective-permute-start.19
  77.1 1.5 collective-permute-start.11
  78.6 1.4 collective-permute-start.24
  80.0 4.6 %collective-permute-done.16.refs_2_ = bf16[80,1024]{1,0:T(8,128)(2,1)S(1)} collective-permute-done((bf16[80,1024]{1,0:T(8,128)(2,1)S(1)}, bf16[80,1024]{1,0:T(8,128)(2,1)S(1)}, u32[]{:S(2)}, u32[]{:S(2)}) %collective-permute-start.16) | collective-permute-done | bytes 163872 | tf_op jit(solution)/shard_map/ppermute | solution.py:336
  84.6 1.6 %collective-permute-start.14 = (bf16[80,1024]{1,0:T(8,128)(2,1)S(1)}, bf16[80,1024]{1,0:T(8,128)(2,1)S(1)}, u32[]{:S(2)}, u32[]{:S(2)}) collective-permute-start(bf16[80,1024]{1,0:T(8,128)(2,1)S(1)} %collective-permute-done.13.refs_1_), channel_id=1, source_target_pairs={{0,2},{2,0},{4,6},{6,4},{1,3},{3,1},{5,7},{7,5},{8,10},{10,8},{12,... | collective-permute-start | bytes 491528 | tf_op jit(solution)/shard_map/ppermute | solution.py:331
  86.2 0.6 fusion.22
  86.8 1.4 collective-permute-start.17
  89.3 1.6 %collective-permute-done.14.refs_1_ = bf16[80,1024]{1,0:T(8,128)(2,1)S(1)} collective-permute-done((bf16[80,1024]{1,0:T(8,128)(2,1)S(1)}, bf16[80,1024]{1,0:T(8,128)(2,1)S(1)}, u32[]{:S(2)}, u32[]{:S(2)}) %collective-permute-start.14) | collective-permute-done | bytes 163872 | tf_op jit(solution)/shard_map/ppermute | solution.py:331
  90.9 2.3 %collective-permute-start.23 = (bf16[80,1024]{1,0:T(8,128)(2,1)S(1)}, bf16[80,1024]{1,0:T(8,128)(2,1)S(1)}, u32[]{:S(2)}, u32[]{:S(2)}) collective-permute-start(bf16[80,1024]{1,0:T(8,128)(2,1)S(1)} %collective-permute-done.19.refs_3_), channel_id=1, source_target_pairs={{0,2},{2,0},{4,6},{6,4},{1,3},{3,1},{5,7},{7,5},{8,10},{10,8},{12,... | collective-permute-start | bytes 491528 | tf_op jit(solution)/shard_map/ppermute | solution.py:331
  93.2 1.5 collective-permute-start.25
  94.7 10.0 %shard_map.153.refs_8_ = f32[4,2,80]{2,1,0:T(2,128)} custom-call(s32[6]{0:T(128)} %pad_add_fusion.4.spots_ref, s32[1,320]{1,0:T(1,128)} %get-tuple-element.20.wanted_ref, bf16[80,1024]{1,0:T(8,128)(2,1)} %copy-done.2, bf16[80,1024]{1,0:T(8,128)(2,1)} %copy-done.11, bf16[80,1024]{1,0:T(8,128)(2,1)} %copy-done.13, bf16[80,1024]{1,0:T(8,128)(2,1)} %copy-done.16, ...), custom_call_target="tpu_custom_call" | custom-call | flops 3187671040 | bytes 10616832 | tf_op jit(solution)/shard_map/pallas_call | solution.py:289
  105.4 1.5 collective-permute-start.15
  107.5 1.5 collective-permute-start.21
  109.0 0.7 copy-done.23
  109.6 13.5 %shard_map.154.refs_4_ = f32[12,2,80]{2,1,0:T(2,128)} custom-call(s32[14]{0:T(128)} %pad_add_fusion.3.spots_ref, s32[1,640]{1,0:T(1,128)} %slice.92.wanted_ref, bf16[80,1024]{1,0:T(8,128)(2,1)} %copy-done.12, bf16[80,1024]{1,0:T(8,128)(2,1)} %copy-done.14, bf16[80,1024]{1,0:T(8,128)(2,1)} %copy-done.19, bf16[80,1024]{1,0:T(8,128)(2,1)} %copy-done.21, ...), custom_call_target="tpu_custom_call" | custom-call | flops 6375342080 | bytes 11272192 | tf_op jit(solution)/shard_map/pallas_call | solution.py:289
  124.0 10.1 %shard_map.155 = f32[16,2,80]{2,1,0:T(2,128)} custom-call(s32[18]{0:T(128)} %pad_add_fusion.1.spots_ref, s32[1,320]{1,0:T(1,128)} %get-tuple-element.21.wanted_ref, bf16[80,1024]{1,0:T(8,128)(2,1)} %copy-done.20, bf16[80,1024]{1,0:T(8,128)(2,1)} %copy-done.22, bf16[80,1024]{1,0:T(8,128)(2,1)} %copy-done.24, bf16[80,1024]{1,0:T(8,128)(2,1)} %copy-done.25, ...), custom_call_target="tpu_custom_call" | custom-call | flops 3187671040 | bytes 10616832 | tf_op jit(solution)/shard_map/pallas_call | solution.py:289
  134.1 0.7 copy.39
  135.4 4.8 %collective-permute-start.28 = (f32[16,2,80]{2,0,1:T(8,128)S(1)}, f32[16,2,80]{2,0,1:T(8,128)S(1)}, u32[]{:S(2)}, u32[]{:S(2)}) collective-permute-start(f32[16,2,80]{2,0,1:T(8,128)S(1)} %copy.39), channel_id=1, source_target_pairs={{0,16},{8,24},{16,0},{24,8},{1,17},{9,25},{17,1},{25,9},{2,18},{10... | collective-permute-start | bytes 30728 | tf_op jit(solution)/shard_map/ppermute | solution.py:336
  140.2 0.7 fusion.19
  140.9 0.7 slice.98
  142.0 2.0 %collective-permute-done.29 = f32[16,2,80]{2,0,1:T(8,128)S(1)} collective-permute-done((f32[16,2,80]{2,0,1:T(8,128)S(1)}, f32[16,2,80]{2,0,1:T(8,128)S(1)}, u32[]{:S(2)}, u32[]{:S(2)}) %collective-permute-start.29) | collective-permute-done | bytes 10272 | tf_op jit(solution)/shard_map/ppermute | solution.py:336
  144.0 0.7 collective-permute-start.30
  144.9 2.7 %collective-permute-start.32 = (f32[16,2,80]{2,0,1:T(8,128)S(1)}, f32[16,2,80]{2,0,1:T(8,128)S(1)}, u32[]{:S(2)}, u32[]{:S(2)}) collective-permute-start(f32[16,2,80]{2,0,1:T(8,128)S(1)} %pad_maximum_fusion), channel_id=1, source_target_pairs={{0,6},{2,4},{4,2},{6,0},{1,7},{3,5},{5,3},{7,1},{8,14},{10,12},{12... | collective-permute-start | bytes 30728 | tf_op jit(solution)/shard_map/ppermute | solution.py:331
  150.8 1.3 add_reduce_fusion
  (110 shorter events, 9.7 us)
Async XLA Ops:
  0.6 92.6 %collective-permute-start.26 = (bf16[2432,1024]{1,0:T(8,128)(2,1)}, bf16[2432,1024]{1,0:T(8,128)(2,1)}, u32[]{:S(2)}, u32[]{:S(2)}) collective-permute-start(bf16[2432,1024]{1,0:T(8,128)(2,1)} %refs_5_.1), channel_id=1, source_target_pairs={{0,1},{1,0},{2,3},{3,2},{4,5},{5,4},{6,7},{7,6},{8,9},{9,8},{10,11... | collective-permute-start | bytes 14942216 | tf_op jit(solution)/shard_map/ppermute | solution.py:340
  2.9 8.2 %collective-permute-start = (bf16[80,1152]{1,0:T(8,128)(2,1)}, bf16[80,1152]{1,0:T(8,128)(2,1)S(1)}, u32[]{:S(2)}, u32[]{:S(2)}) collective-permute-start(bf16[80,1152]{1,0:T(8,128)(2,1)} %shard_map.149.refs_0_.hidden_ref), channel_id=1, source_target_pairs={{0,2},{2,0},{4,6},{6,4},{1,3},{3,1},{5,7},{7,5},{8,10},{10,8},{12,... | collective-permute-start | bytes 552968 | tf_op jit(solution)/shard_map/ppermute | solution.py:331
  5.4 10.9 %collective-permute-start.1 = (bf16[80,1152]{1,0:T(8,128)(2,1)}, bf16[80,1152]{1,0:T(8,128)(2,1)S(1)}, u32[]{:S(2)}, u32[]{:S(2)}) collective-permute-start(bf16[80,1152]{1,0:T(8,128)(2,1)} %shard_map.149.refs_0_.hidden_ref), channel_id=1, source_target_pairs={{0,4},{2,6},{4,0},{6,2},{1,5},{3,7},{5,1},{7,3},{8,12},{10,14},{12... | collective-permute-start | bytes 552968 | tf_op jit(solution)/shard_map/ppermute | solution.py:331
  6.9 9.4 %collective-permute-start.2 = (bf16[80,1152]{1,0:T(8,128)(2,1)}, bf16[80,1152]{1,0:T(8,128)(2,1)S(1)}, u32[]{:S(2)}, u32[]{:S(2)}) collective-permute-start(bf16[80,1152]{1,0:T(8,128)(2,1)} %shard_map.149.refs_0_.hidden_ref), channel_id=1, source_target_pairs={{0,6},{2,4},{4,2},{6,0},{1,7},{3,5},{5,3},{7,1},{8,14},{10,12},{12... | collective-permute-start | bytes 552968 | tf_op jit(solution)/shard_map/ppermute | solution.py:331
  6.9 10.0 %collective-permute-start.3 = (bf16[80,1152]{1,0:T(8,128)(2,1)}, bf16[80,1152]{1,0:T(8,128)(2,1)S(1)}, u32[]{:S(2)}, u32[]{:S(2)}) collective-permute-start(bf16[80,1152]{1,0:T(8,128)(2,1)} %shard_map.149.refs_0_.hidden_ref), channel_id=1, source_target_pairs={{0,1},{1,0},{2,3},{3,2},{4,5},{5,4},{6,7},{7,6},{8,9},{9,8},{10,11... | collective-permute-start | bytes 552968 | tf_op jit(solution)/shard_map/ppermute | solution.py:340
  11.1 5.8 %collective-permute-start.4 = (bf16[80,1152]{1,0:T(8,128)(2,1)S(1)}, bf16[80,1152]{1,0:T(8,128)(2,1)S(1)}, u32[]{:S(2)}, u32[]{:S(2)}) collective-permute-start(bf16[80,1152]{1,0:T(8,128)(2,1)S(1)} %collective-permute-done.refs_1_), channel_id=1, source_target_pairs={{0,1},{1,0},{2,3},{3,2},{4,5},{5,4},{6,7},{7,6},{8,9},{9,8},{10,11... | collective-permute-start | bytes 552968 | tf_op jit(solution)/shard_map/ppermute | solution.py:340
  16.3 1.4 collective-permute-start.5
  16.3 1.7 %collective-permute-start.6 = (bf16[80,1152]{1,0:T(8,128)(2,1)S(1)}, bf16[80,1152]{1,0:T(8,128)(2,1)S(1)}, u32[]{:S(2)}, u32[]{:S(2)}) collective-permute-start(bf16[80,1152]{1,0:T(8,128)(2,1)S(1)} %collective-permute-done.2.refs_3_), channel_id=1, source_target_pairs={{0,1},{1,0},{2,3},{3,2},{4,5},{5,4},{6,7},{7,6},{8,9},{9,8},{10,11... | collective-permute-start | bytes 552968 | tf_op jit(solution)/shard_map/ppermute | solution.py:340
  16.8 52.6 %copy-start.3 = (f32[1024]{0:T(1024)S(1)}, f32[1024]{0:T(1024)}, u32[]{:S(2)}) copy-start(f32[1024]{0:T(1024)} %param.23) | copy-start | bytes 12292
  16.8 26.4 %copy-start.4 = (s32[40]{0:T(128)S(1)}, s32[40]{0:T(128)}, u32[]{:S(2)}) copy-start(s32[40]{0:T(128)} %param.25) | copy-start | bytes 484
  16.8 57.3 %copy-start.9 = (s32[32]{0:T(128)S(1)}, s32[32]{0:T(128)}, u32[]{:S(2)}) copy-start(s32[32]{0:T(128)} %param.26) | copy-start | bytes 388
  24.5 44.9 %copy-start.1 = (bf16[80,1152]{1,0:T(8,128)(2,1)S(1)}, bf16[80,1152]{1,0:T(8,128)(2,1)}, u32[]{:S(2)}) copy-start(bf16[80,1152]{1,0:T(8,128)(2,1)} %shard_map.149.refs_0_.hidden_ref) | copy-start | bytes 552964
  40.0 3.2 %collective-permute-start.7 = (f32[4,80,1024]{2,1,0:T(8,128)}, f32[4,80,1024]{2,1,0:T(8,128)S(1)}, u32[]{:S(2)}, u32[]{:S(2)}) collective-permute-start(f32[4,80,1024]{2,1,0:T(8,128)} %get-tuple-element.10), channel_id=1, source_target_pairs={{0,1},{1,0},{2,3},{3,2},{4,5},{5,4},{6,7},{7,6},{8,9},{9,8},{10,11... | collective-permute-start | bytes 3932168 | tf_op jit(solution)/shard_map/ppermute | solution.py:340
  45.5 13.3 %all-to-all-start = ((s32[16,1,40]{2,1,0:T(1,128)}), s32[16,1,40]{2,1,0:T(1,128)S(1)}, u32[]{:S(2)}, u32[]{:S(2)}) async-start(s32[16,1,40]{2,1,0:T(1,128)} %bitcast.10), calls=%async_computation | async-start | bytes 16384 | tf_op jit(solution)/shard_map/all_to_all | solution.py:372
  51.4 11.8 %collective-permute-start.10 = (f32[80,1024]{1,0:T(8,128)}, f32[80,1024]{1,0:T(8,128)S(1)}, u32[]{:S(2)}, u32[]{:S(2)}) collective-permute-start(f32[80,1024]{1,0:T(8,128)} %copy-done.8), channel_id=1, source_target_pairs={{0,6},{2,4},{4,2},{6,0},{1,7},{3,5},{5,3},{7,1},{8,14},{10,12},{12... | collective-permute-start | bytes 983048 | tf_op jit(solution)/shard_map/ppermute | solution.py:331
  54.2 15.2 %collective-permute-start.8 = (f32[80,1024]{1,0:T(8,128)}, f32[80,1024]{1,0:T(8,128)S(1)}, u32[]{:S(2)}, u32[]{:S(2)}) collective-permute-start(f32[80,1024]{1,0:T(8,128)} %copy-done.7), channel_id=1, source_target_pairs={{0,2},{2,0},{4,6},{6,4},{1,3},{3,1},{5,7},{7,5},{8,10},{10,8},{12,... | collective-permute-start | bytes 983048 | tf_op jit(solution)/shard_map/ppermute | solution.py:331
  54.8 14.6 %collective-permute-start.9 = (f32[80,1024]{1,0:T(8,128)S(1)}, f32[80,1024]{1,0:T(8,128)S(1)}, u32[]{:S(2)}, u32[]{:S(2)}) collective-permute-start(f32[80,1024]{1,0:T(8,128)S(1)} %get-tuple-element.14), channel_id=1, source_target_pairs={{0,4},{2,6},{4,0},{6,2},{1,5},{3,7},{5,1},{7,3},{8,12},{10,14},{12... | collective-permute-start | bytes 983048 | tf_op jit(solution)/shard_map/ppermute | solution.py:331
  69.6 25.1 %copy-start.2 = (bf16[80,1024]{1,0:T(8,128)(2,1)}, bf16[80,1024]{1,0:T(8,128)(2,1)S(1)}, u32[]{:S(2)}) copy-start(bf16[80,1024]{1,0:T(8,128)(2,1)S(1)} %shard_map.152.refs_0_) | copy-start | bytes 491524
  69.6 9.0 %collective-permute-start.13 = (bf16[80,1024]{1,0:T(8,128)(2,1)S(1)}, bf16[80,1024]{1,0:T(8,128)(2,1)S(1)}, u32[]{:S(2)}, u32[]{:S(2)}) collective-permute-start(bf16[80,1024]{1,0:T(8,128)(2,1)S(1)} %shard_map.152.refs_0_), channel_id=1, source_target_pairs={{0,8},{8,16},{16,24},{24,0},{1,9},{9,17},{17,25},{25,1},{2,10},{10... | collective-permute-start | bytes 491528 | tf_op jit(solution)/shard_map/ppermute | solution.py:336
  71.1 13.5 %collective-permute-start.16 = (bf16[80,1024]{1,0:T(8,128)(2,1)S(1)}, bf16[80,1024]{1,0:T(8,128)(2,1)S(1)}, u32[]{:S(2)}, u32[]{:S(2)}) collective-permute-start(bf16[80,1024]{1,0:T(8,128)(2,1)S(1)} %shard_map.152.refs_0_), channel_id=1, source_target_pairs={{0,16},{8,24},{16,0},{24,8},{1,17},{9,25},{17,1},{25,9},{2,18},{10... | collective-permute-start | bytes 491528 | tf_op jit(solution)/shard_map/ppermute | solution.py:336
  75.6 11.2 %collective-permute-start.19 = (bf16[80,1024]{1,0:T(8,128)(2,1)S(1)}, bf16[80,1024]{1,0:T(8,128)(2,1)S(1)}, u32[]{:S(2)}, u32[]{:S(2)}) collective-permute-start(bf16[80,1024]{1,0:T(8,128)(2,1)S(1)} %shard_map.152.refs_0_), channel_id=1, source_target_pairs={{0,24},{8,0},{16,8},{24,16},{1,25},{9,1},{17,9},{25,17},{2,26},{10... | collective-permute-start | bytes 491528 | tf_op jit(solution)/shard_map/ppermute | solution.py:336
  77.1 11.2 %collective-permute-start.11 = (bf16[80,1024]{1,0:T(8,128)(2,1)S(1)}, bf16[80,1024]{1,0:T(8,128)(2,1)S(1)}, u32[]{:S(2)}, u32[]{:S(2)}) collective-permute-start(bf16[80,1024]{1,0:T(8,128)(2,1)S(1)} %shard_map.152.refs_0_), channel_id=1, source_target_pairs={{0,2},{2,0},{4,6},{6,4},{1,3},{3,1},{5,7},{7,5},{8,10},{10,8},{12,... | collective-permute-start | bytes 491528 | tf_op jit(solution)/shard_map/ppermute | solution.py:331
  78.6 16.1 %copy-start.11 = (bf16[80,1024]{1,0:T(8,128)(2,1)}, bf16[80,1024]{1,0:T(8,128)(2,1)S(1)}, u32[]{:S(2)}) copy-start(bf16[80,1024]{1,0:T(8,128)(2,1)S(1)} %collective-permute-done.13.refs_1_) | copy-start | bytes 491524
  78.6 10.2 %collective-permute-start.24 = (bf16[80,1024]{1,0:T(8,128)(2,1)S(1)}, bf16[80,1024]{1,0:T(8,128)(2,1)S(1)}, u32[]{:S(2)}, u32[]{:S(2)}) collective-permute-start(bf16[80,1024]{1,0:T(8,128)(2,1)S(1)} %shard_map.152.refs_0_), channel_id=1, source_target_pairs={{0,4},{2,6},{4,0},{6,2},{1,5},{3,7},{5,1},{7,3},{8,12},{10,14},{12... | collective-permute-start | bytes 491528 | tf_op jit(solution)/shard_map/ppermute | solution.py:331
  84.6 10.1 %copy-start.13 = (bf16[80,1024]{1,0:T(8,128)(2,1)}, bf16[80,1024]{1,0:T(8,128)(2,1)S(1)}, u32[]{:S(2)}) copy-start(bf16[80,1024]{1,0:T(8,128)(2,1)S(1)} %collective-permute-done.16.refs_2_) | copy-start | bytes 491524
  84.6 6.4 %collective-permute-start.14 = (bf16[80,1024]{1,0:T(8,128)(2,1)S(1)}, bf16[80,1024]{1,0:T(8,128)(2,1)S(1)}, u32[]{:S(2)}, u32[]{:S(2)}) collective-permute-start(bf16[80,1024]{1,0:T(8,128)(2,1)S(1)} %collective-permute-done.13.refs_1_), channel_id=1, source_target_pairs={{0,2},{2,0},{4,6},{6,4},{1,3},{3,1},{5,7},{7,5},{8,10},{10,8},{12,... | collective-permute-start | bytes 491528 | tf_op jit(solution)/shard_map/ppermute | solution.py:331
  86.8 7.9 %copy-start.16 = (bf16[80,1024]{1,0:T(8,128)(2,1)}, bf16[80,1024]{1,0:T(8,128)(2,1)S(1)}, u32[]{:S(2)}) copy-start(bf16[80,1024]{1,0:T(8,128)(2,1)S(1)} %collective-permute-done.19.refs_3_) | copy-start | bytes 491524
  86.8 17.9 %collective-permute-start.17 = (bf16[80,1024]{1,0:T(8,128)(2,1)S(1)}, bf16[80,1024]{1,0:T(8,128)(2,1)S(1)}, u32[]{:S(2)}, u32[]{:S(2)}) collective-permute-start(bf16[80,1024]{1,0:T(8,128)(2,1)S(1)} %collective-permute-done.16.refs_2_), channel_id=1, source_target_pairs={{0,4},{2,6},{4,0},{6,2},{1,5},{3,7},{5,1},{7,3},{8,12},{10,14},{12... | collective-permute-start | bytes 491528 | tf_op jit(solution)/shard_map/ppermute | solution.py:331
  88.3 16.4 %copy-start.12 = (bf16[80,1024]{1,0:T(8,128)(2,1)}, bf16[80,1024]{1,0:T(8,128)(2,1)S(1)}, u32[]{:S(2)}) copy-start(bf16[80,1024]{1,0:T(8,128)(2,1)S(1)} %collective-permute-done.11.refs_0_) | copy-start | bytes 491524
  88.3 18.6 %collective-permute-start.22 = (bf16[80,1024]{1,0:T(8,128)(2,1)S(1)}, bf16[80,1024]{1,0:T(8,128)(2,1)S(1)}, u32[]{:S(2)}, u32[]{:S(2)}) collective-permute-start(bf16[80,1024]{1,0:T(8,128)(2,1)S(1)} %collective-permute-done.16.refs_2_), channel_id=1, source_target_pairs={{0,2},{2,0},{4,6},{6,4},{1,3},{3,1},{5,7},{7,5},{8,10},{10,8},{12,... | collective-permute-start | bytes 491528 | tf_op jit(solution)/shard_map/ppermute | solution.py:331
  88.8 15.9 %copy-start.15 = (bf16[80,1024]{1,0:T(8,128)(2,1)}, bf16[80,1024]{1,0:T(8,128)(2,1)S(1)}, u32[]{:S(2)}) copy-start(bf16[80,1024]{1,0:T(8,128)(2,1)S(1)} %collective-permute-done.24.refs_4_) | copy-start | bytes 491524
  88.8 16.5 %collective-permute-start.20 = (bf16[80,1024]{1,0:T(8,128)(2,1)S(1)}, bf16[80,1024]{1,0:T(8,128)(2,1)S(1)}, u32[]{:S(2)}, u32[]{:S(2)}) collective-permute-start(bf16[80,1024]{1,0:T(8,128)(2,1)S(1)} %collective-permute-done.19.refs_3_), channel_id=1, source_target_pairs={{0,4},{2,6},{4,0},{6,2},{1,5},{3,7},{5,1},{7,3},{8,12},{10,14},{12... | collective-permute-start | bytes 491528 | tf_op jit(solution)/shard_map/ppermute | solution.py:331
  90.9 14.4 %copy-start.14 = (bf16[80,1024]{1,0:T(8,128)(2,1)}, bf16[80,1024]{1,0:T(8,128)(2,1)S(1)}, u32[]{:S(2)}) copy-start(bf16[80,1024]{1,0:T(8,128)(2,1)S(1)} %collective-permute-done.14.refs_1_) | copy-start | bytes 491524
  90.9 16.5 %collective-permute-start.23 = (bf16[80,1024]{1,0:T(8,128)(2,1)S(1)}, bf16[80,1024]{1,0:T(8,128)(2,1)S(1)}, u32[]{:S(2)}, u32[]{:S(2)}) collective-permute-start(bf16[80,1024]{1,0:T(8,128)(2,1)S(1)} %collective-permute-done.19.refs_3_), channel_id=1, source_target_pairs={{0,2},{2,0},{4,6},{6,4},{1,3},{3,1},{5,7},{7,5},{8,10},{10,8},{12,... | collective-permute-start | bytes 491528 | tf_op jit(solution)/shard_map/ppermute | solution.py:331
  93.2 15.7 %collective-permute-start.25 = (bf16[80,1024]{1,0:T(8,128)(2,1)S(1)}, bf16[80,1024]{1,0:T(8,128)(2,1)S(1)}, u32[]{:S(2)}, u32[]{:S(2)}) collective-permute-start(bf16[80,1024]{1,0:T(8,128)(2,1)S(1)} %collective-permute-done.13.refs_1_), channel_id=1, source_target_pairs={{0,4},{2,6},{4,0},{6,2},{1,5},{3,7},{5,1},{7,3},{8,12},{10,14},{12... | collective-permute-start | bytes 491528 | tf_op jit(solution)/shard_map/ppermute | solution.py:331
  104.7 4.2 %copy-start.17 = (bf16[80,1024]{1,0:T(8,128)(2,1)}, bf16[80,1024]{1,0:T(8,128)(2,1)S(1)}, u32[]{:S(2)}) copy-start(bf16[80,1024]{1,0:T(8,128)(2,1)S(1)} %collective-permute-done.17.refs_6_) | copy-start | bytes 491524
  104.7 18.4 %collective-permute-start.12 = (bf16[80,1024]{1,0:T(8,128)(2,1)S(1)}, bf16[80,1024]{1,0:T(8,128)(2,1)S(1)}, u32[]{:S(2)}, u32[]{:S(2)}) collective-permute-start(bf16[80,1024]{1,0:T(8,128)(2,1)S(1)} %collective-permute-done.11.refs_0_), channel_id=1, source_target_pairs={{0,4},{2,6},{4,0},{6,2},{1,5},{3,7},{5,1},{7,3},{8,12},{10,14},{12... | collective-permute-start | bytes 491528 | tf_op jit(solution)/shard_map/ppermute | solution.py:331
  105.4 17.8 %collective-permute-start.15 = (bf16[80,1024]{1,0:T(8,128)(2,1)S(1)}, bf16[80,1024]{1,0:T(8,128)(2,1)S(1)}, u32[]{:S(2)}, u32[]{:S(2)}) collective-permute-start(bf16[80,1024]{1,0:T(8,128)(2,1)S(1)} %collective-permute-done.14.refs_1_), channel_id=1, source_target_pairs={{0,4},{2,6},{4,0},{6,2},{1,5},{3,7},{5,1},{7,3},{8,12},{10,14},{12... | collective-permute-start | bytes 491528 | tf_op jit(solution)/shard_map/ppermute | solution.py:331
  106.9 16.3 %collective-permute-start.18 = (bf16[80,1024]{1,0:T(8,128)(2,1)S(1)}, bf16[80,1024]{1,0:T(8,128)(2,1)S(1)}, u32[]{:S(2)}, u32[]{:S(2)}) collective-permute-start(bf16[80,1024]{1,0:T(8,128)(2,1)S(1)} %collective-permute-done.17.refs_6_), channel_id=1, source_target_pairs={{0,2},{2,0},{4,6},{6,4},{1,3},{3,1},{5,7},{7,5},{8,10},{10,8},{12,... | collective-permute-start | bytes 491528 | tf_op jit(solution)/shard_map/ppermute | solution.py:331
  107.5 15.7 %collective-permute-start.21 = (bf16[80,1024]{1,0:T(8,128)(2,1)S(1)}, bf16[80,1024]{1,0:T(8,128)(2,1)S(1)}, u32[]{:S(2)}, u32[]{:S(2)}) collective-permute-start(bf16[80,1024]{1,0:T(8,128)(2,1)S(1)} %collective-permute-done.20.refs_7_), channel_id=1, source_target_pairs={{0,2},{2,0},{4,6},{6,4},{1,3},{3,1},{5,7},{7,5},{8,10},{10,8},{12,... | collective-permute-start | bytes 491528 | tf_op jit(solution)/shard_map/ppermute | solution.py:331
  124.0 16.3 %copy-start.10 = (s32[32]{0:T(128)S(1)}, s32[32]{0:T(128)}, u32[]{:S(2)}) copy-start(s32[32]{0:T(128)} %param.27) | copy-start | bytes 388
  134.8 6.8 %collective-permute-start.27 = (f32[16,2,80]{2,0,1:T(8,128)S(1)}, f32[16,2,80]{2,0,1:T(8,128)S(1)}, u32[]{:S(2)}, u32[]{:S(2)}) collective-permute-start(f32[16,2,80]{2,0,1:T(8,128)S(1)} %copy.39), channel_id=1, source_target_pairs={{0,8},{8,16},{16,24},{24,0},{1,9},{9,17},{17,25},{25,1},{2,10},{10... | collective-permute-start | bytes 30728 | tf_op jit(solution)/shard_map/ppermute | solution.py:336
  135.4 6.5 %collective-permute-start.28 = (f32[16,2,80]{2,0,1:T(8,128)S(1)}, f32[16,2,80]{2,0,1:T(8,128)S(1)}, u32[]{:S(2)}, u32[]{:S(2)}) collective-permute-start(f32[16,2,80]{2,0,1:T(8,128)S(1)} %copy.39), channel_id=1, source_target_pairs={{0,16},{8,24},{16,0},{24,8},{1,17},{9,25},{17,1},{25,9},{2,18},{10... | collective-permute-start | bytes 30728 | tf_op jit(solution)/shard_map/ppermute | solution.py:336
  140.2 3.7 %collective-permute-start.29 = (f32[16,2,80]{2,0,1:T(8,128)S(1)}, f32[16,2,80]{2,0,1:T(8,128)S(1)}, u32[]{:S(2)}, u32[]{:S(2)}) collective-permute-start(f32[16,2,80]{2,0,1:T(8,128)S(1)} %copy.39), channel_id=1, source_target_pairs={{0,24},{8,0},{16,8},{24,16},{1,25},{9,1},{17,9},{25,17},{2,26},{10... | collective-permute-start | bytes 30728 | tf_op jit(solution)/shard_map/ppermute | solution.py:336
  144.0 5.5 %collective-permute-start.30 = (f32[16,2,80]{2,0,1:T(8,128)S(1)}, f32[16,2,80]{2,0,1:T(8,128)S(1)}, u32[]{:S(2)}, u32[]{:S(2)}) collective-permute-start(f32[16,2,80]{2,0,1:T(8,128)S(1)} %pad_maximum_fusion), channel_id=1, source_target_pairs={{0,2},{2,0},{4,6},{6,4},{1,3},{3,1},{5,7},{7,5},{8,10},{10,8},{12,... | collective-permute-start | bytes 30728 | tf_op jit(solution)/shard_map/ppermute | solution.py:331
  144.7 4.8 %collective-permute-start.31 = (f32[16,2,80]{2,0,1:T(8,128)S(1)}, f32[16,2,80]{2,0,1:T(8,128)S(1)}, u32[]{:S(2)}, u32[]{:S(2)}) collective-permute-start(f32[16,2,80]{2,0,1:T(8,128)S(1)} %pad_maximum_fusion), channel_id=1, source_target_pairs={{0,4},{2,6},{4,0},{6,2},{1,5},{3,7},{5,1},{7,3},{8,12},{10,14},{12... | collective-permute-start | bytes 30728 | tf_op jit(solution)/shard_map/ppermute | solution.py:331
  144.9 4.6 %collective-permute-start.32 = (f32[16,2,80]{2,0,1:T(8,128)S(1)}, f32[16,2,80]{2,0,1:T(8,128)S(1)}, u32[]{:S(2)}, u32[]{:S(2)}) collective-permute-start(f32[16,2,80]{2,0,1:T(8,128)S(1)} %pad_maximum_fusion), channel_id=1, source_target_pairs={{0,6},{2,4},{4,2},{6,0},{1,7},{3,5},{5,3},{7,1},{8,14},{10,12},{12... | collective-permute-start | bytes 30728 | tf_op jit(solution)/shard_map/ppermute | solution.py:331
  149.7 1.2 collective-permute-start.33
  (13 other events, 18.6 us)

commit v5 on v4

--- a/solution.py
+++ b/solution.py
@@ -169,7 +169,7 @@
             ],
         ),
         compiler_params=pltpu.CompilerParams(
-            vmem_limit_bytes=(36 if rows <= 640 else 58) * MIB
+            vmem_limit_bytes=(55 if rows <= 640 else 58) * MIB
         ),
         cost_estimate=pl.CostEstimate(
             flops=2 * every * width * (3 * hidden + 3 * rows),
@@ -179,21 +179,33 @@
     )(place, *blocks, w_gate, w_up, w_down)
 
 
-def pair_kernel(keep_ref, came_ref, targets_ref, goal_ref, *sums):
+def pair_kernel(keep_ref, came_ref, *sums):
     for index, total in enumerate(sums):
         total[...] = keep_ref[index] + came_ref[index]
-    goal_ref[...] = jnp.broadcast_to(targets_ref[...], goal_ref.shape)
-
-
-def pair_sums(keep, came, targets, peers):
+
+
+def pair_sums(keep, came):
     chips, share, width = keep.shape
     part = jax.ShapeDtypeStruct((share, width), jnp.float32)
+    return pl.pallas_call(
+        pair_kernel,
+        out_shape=(part,) * chips,
+        compiler_params=pltpu.CompilerParams(vmem_limit_bytes=24 * MIB),
+    )(keep, came)
+
+
+def begin_kernel(own_ref, came_ref, targets_ref, sum_ref, goal_ref):
+    sum_ref[...] = own_ref[...] + came_ref[...]
+    goal_ref[...] = jnp.broadcast_to(targets_ref[...], goal_ref.shape)
+
+
+def begin_rows(own, came, targets, peers):
     goal = jax.ShapeDtypeStruct((peers, targets.shape[0]), jnp.int32)
     return pl.pallas_call(
-        pair_kernel,
-        out_shape=(goal,) + (part,) * chips,
-        compiler_params=pltpu.CompilerParams(vmem_limit_bytes=24 * MIB),
-    )(keep, came, targets.reshape(1, -1))
+        begin_kernel,
+        out_shape=(jax.ShapeDtypeStruct(own.shape, own.dtype), goal),
+        compiler_params=pltpu.CompilerParams(vmem_limit_bytes=16 * MIB),
+    )(own, came, targets.reshape(1, -1))
 
 
 def norm_kernel(hidden_ref, gain_ref, early_ref, own_ref, *refs):
@@ -214,14 +226,13 @@
     )(hidden, gain.reshape(1, -1), early, own, *others)
 
 
-def head_kernel(count, before, spots_ref, wanted_ref, *refs):
-    blocks, refs = refs[:count], refs[count:]
+def head_kernel(parts, before, spots_ref, wanted_ref, *refs):
+    blocks, refs = refs[:len(parts)], refs[len(parts):]
     earlier, refs = refs[:before], refs[before:]
     head_a, head_b, out_ref, rows_in, peak, total, found, logits_a, logits_b = refs
     step = pl.program_id(0)
     last = pl.num_programs(0) - 1
     tile, columns = logits_a.shape
-    share = out_ref.shape[2]
     base_a, base_b = spots_ref[0], spots_ref[1]
 
     def product(head_ref, logits):
@@ -248,9 +259,9 @@
     @pl.when(step == 0)
     def _():
         start = 0
-        for ref in blocks:
-            rows_in[start:start + ref.shape[0], :] = ref[...]
-            start += ref.shape[0]
+        for ref, (low, high) in zip(blocks, parts):
+            rows_in[start:start + high - low, :] = ref[low:high, :]
+            start += high - low
         peak[...] = jnp.full_like(peak, LOW)
         total[...] = jnp.zeros_like(total)
         found[...] = jnp.zeros_like(found)
@@ -268,27 +279,29 @@
         full = jnp.sum(total[...] * jnp.exp(peak[...] - top), axis=0, keepdims=True)
         lse = top + jnp.log(full)
         hit = jnp.sum(found[...], axis=0, keepdims=True)
-        done = 0
-        for ref in earlier:
-            for index in range(ref.shape[0]):
-                out_ref[spots_ref[2 + done + index]] = ref[index]
-            done += ref.shape[0]
-        for index in range(columns // share):
-            band = slice(index * share, (index + 1) * share)
-            spot = spots_ref[2 + done + index]
-            out_ref[spot, 0:1, :] = lse[:, band]
-            out_ref[spot, 1:2, :] = hit[:, band]
-
-
-def head_stats(spots, wanted, blocks, earlier, head_a, head_b, share):
-    places = spots.shape[0] - 2
-    rows = sum(block.shape[0] for block in blocks)
+        lse = jnp.concatenate([ref[0:1, :] for ref in earlier] + [lse], axis=1)
+        hit = jnp.concatenate([ref[1:2, :] for ref in earlier] + [hit], axis=1)
+        if len(out_ref.shape) == 2:
+            out_ref[0:1, :] = lse
+            out_ref[1:2, :] = hit
+        else:
+            share = out_ref.shape[2]
+            for index in range(out_ref.shape[0]):
+                band = slice(index * share, (index + 1) * share)
+                spot = spots_ref[2 + index]
+                out_ref[spot, 0:1, :] = lse[:, band]
+                out_ref[spot, 1:2, :] = hit[:, band]
+
+
+def head_stats(spots, wanted, blocks, parts, earlier, head_a, head_b, shape):
+    rows = sum(high - low for low, high in parts)
     width = head_a.shape[1]
+    whole = pl.BlockSpec(shape, lambda s, spots: (0,) * len(shape))
     tile = largest_tile(head_a.shape[0], 608, 16)
     steps = head_a.shape[0] // tile
     return pl.pallas_call(
-        functools.partial(head_kernel, len(blocks), len(earlier)),
-        out_shape=jax.ShapeDtypeStruct((places, 2, share), jnp.float32),
+        functools.partial(head_kernel, parts, len(earlier)),
+        out_shape=jax.ShapeDtypeStruct(shape, jnp.float32),
         grid_spec=pltpu.PrefetchScalarGridSpec(
             num_scalar_prefetch=1,
             grid=(steps,),
@@ -296,12 +309,12 @@
                 pl.BlockSpec(block.shape, lambda s, spots: (0, 0), pipeline_mode=pl.Buffered(1))
                 for block in blocks
             ] + [
-                pl.BlockSpec(part.shape, lambda s, spots: (0, 0, 0)) for part in earlier
+                pl.BlockSpec(part.shape, lambda s, spots: (0, 0)) for part in earlier
             ] + [
                 pl.BlockSpec((tile, width), lambda s, spots: (s, 0)),
                 pl.BlockSpec((tile, width), lambda s, spots: (s, 0)),
             ],
-            out_specs=pl.BlockSpec((places, 2, share), lambda s, spots: (0, 0, 0)),
+            out_specs=whole,
             scratch_shapes=[
                 pltpu.VMEM((rows, width), jnp.bfloat16),
                 pltpu.VMEM((8, rows), jnp.float32),
@@ -367,13 +380,14 @@
 
     place = jnp.stack((chip, core)).astype(jnp.int32)
     keep, give = expert_sums(place, plane, w_gate, w_up, w_down, tokens, capacity, width, experts)
-    goal, own, *sends = pair_sums(keep, partner(give), targets, groups * chips)
+    own, *sends = pair_sums(keep, partner(give))
     came = [across(rows, d) for d, rows in zip(offsets, sends)]
+    own, goal = begin_rows(own, came[-1], targets, groups * chips)
     goal = lax.all_to_all(goal, ("grp", "chip"), split_axis=0, concat_axis=0, tiled=True)
     match = spots[:, None] == jnp.arange(groups * chips, dtype=jnp.int32)[None, :]
     goal = jnp.sum(jnp.where(match[:, :, None], goal[None], 0), axis=1)
     wanted = jnp.concatenate((goal, goal), axis=1).reshape(1, -1)
-    normed = norm_rows(send, norm_gain, wanted, own, came)
+    normed = norm_rows(send, norm_gain, wanted, own, came[:-1])
 
     column = [normed] + [along(normed, k) for k in range(1, groups)]
     if chips == 4:
@@ -388,22 +402,32 @@
         blocks = [column] + [across(column, d) for d in offsets]
     base = jnp.stack((device, device + 1 - 2 * core)).astype(jnp.int32) * vocab_rows
     lines = groups * share
-    fixed = jnp.arange(groups * chips, dtype=jnp.int32)
-
-    def stats_of(spots, start, blocks, earlier):
-        end = start + sum(block.shape[0] for block in blocks)
-        spots = jnp.concatenate((base, spots))
+
+    def stats_of(places, start, pieces, earlier, shape):
+        blocks, parts = [block for block, _ in pieces], tuple(part for _, part in pieces)
+        end = start + sum(high - low for low, high in parts)
+        places = jnp.concatenate((base, places))
         return head_stats(
-            spots, wanted[:, start:end], blocks, earlier, vocab_head, other_head, share
+            places, wanted[:, start:end], blocks, parts, earlier, vocab_head, other_head, shape
         )
 
     if chips == 4:
-        first = stats_of(fixed[:groups], 0, column, ())
-        second = stats_of(fixed[:3 * groups], lines, near + far, (first,))
-        stats = stats_of(spots, 3 * lines, cross, (second,))
+        blocks = column + near + far + cross
+        cut = max(256, (3 * lines - share) // 256 * 256)
+        before, after = [], []
+        for index, block in enumerate(blocks):
+            border = min(max(cut - index * share, 0), share)
+            if border > 0:
+                before.append((block, (0, border)))
+            if border < share:
+                after.append((block, (border, share)))
+        first = stats_of(spots, 0, before, (), (2, cut))
+        stats = stats_of(spots, cut, after, (first,), (groups * chips, 2, share))
     else:
+        fixed = jnp.arange(groups, dtype=jnp.int32)
         pieces = [
-            stats_of(fixed[:groups], d * lines, [block], ()) for d, block in enumerate(blocks)
+            stats_of(fixed, d * lines, [(block, (0, lines))], (), (groups, 2, share))
+            for d, block in enumerate(blocks)
         ]
         pieces = jnp.concatenate(pieces, axis=0)
         stats = jnp.zeros_like(pieces).at[spots].set(pieces)

time: 155 us -> 146 us (0.942)
  waiting for transfers between devices: 36 us -> 42.2 us
  local copies, waits for them, and re-layouts: 13 us -> 7.27 us
  starting transfers between devices: 43.9 us -> 39.1 us
  Pallas kernels: 51.8 us -> 48.5 us
    pallas_call x4, Pallas kernels: 34.3 us -> 27.6 us  [the longest x2 26.8 us: head_stats(): pl.pallas_call(functools.partial(head_kernel, parts, len(earlier)), out_s...]
    unnamed x52 -> x58, local copies, waits for them, and re-layouts: 9.43 us -> 3.88 us
    all_to_all x1, waiting for transfers between devices: 3.12 us -> 7.2 us  [local(): lax.all_to_all(goal, ('grp', 'chip'), split_axis=0, concat_axis=0, tiled=...]
    ppermute x21, starting transfers between devices: 26 us -> 22 us  [across(): return lax.ppermute(value, 'chip', [(c, c ^ offset) for c in range(chips)])]
    pallas_call x1, Pallas kernels: 15.5 us -> 19 us  [expert_sums(): pl.pallas_call(functools.partial(expert_kernel, block, slots, width, expe...]
    ppermute x21, waiting for transfers between devices: 21.5 us -> 23.6 us  [across(): return lax.ppermute(value, 'chip', [(c, c ^ offset) for c in range(chips)])]
  transfers between devices with their start and end apart: 35 -> 35, of which waited for: 14 -> 14; matrix products, arithmetic and copies ran while one was open for 4% -> 4% of each run, Pallas kernels for 27% -> 25%
where the time goes in v5:
time: 146 us
  Pallas kernels  48.5 us (33%)
  waiting for transfers between devices  42.2 us (29%)
  starting transfers between devices  39.1 us (27%)
  local copies, waits for them, and re-layouts  7.27 us (5%)
  between operations  4.73 us (3%)
  other arithmetic  3.89 us (3%)
    pallas_call x2, Pallas kernels, head_stats(): pl.pallas_call(functools.partial(head_kernel, parts, len(earlier)), out_s...  26.8 us
    ppermute x21, waiting for transfers between devices, across(): return lax.ppermute(value, 'chip', [(c, c ^ offset) for c in range(chips)])  23.6 us
    ppermute x21, starting transfers between devices, across(): return lax.ppermute(value, 'chip', [(c, c ^ offset) for c in range(chips)])  22 us
    pallas_call x1, Pallas kernels, expert_sums(): pl.pallas_call(functools.partial(expert_kernel, block, slots, width, expe...  19 us
    ppermute x6, starting transfers between devices, along(): lax.ppermute(value, 'grp', [(g, (g + offset) % groups) for g in range(gro...  9.94 us
    ppermute x6, waiting for transfers between devices, along(): lax.ppermute(value, 'grp', [(g, (g + offset) % groups) for g in range(gro...  7.23 us
    all_to_all x1, waiting for transfers between devices, local(): lax.all_to_all(goal, ('grp', 'chip'), split_axis=0, concat_axis=0, tiled=...  7.2 us
    all_to_all x1, starting transfers between devices, local(): lax.all_to_all(goal, ('grp', 'chip'), split_axis=0, concat_axis=0, tiled=...  5.95 us
  transfers between devices with their start and end apart: 35, of which 14 were waited for; matrix products, arithmetic and copies ran while one was open for 4% of the time, Pallas kernels for 25%

profile of v5, /device:TPU:0, one launch (start us, length us, event | category | flops | bytes accessed | tf_op | source)
XLA Modules:
  0.0 145.7 jit_solution(15602262127692205913)
XLA Ops:
  1.1 1.8 %shard_map.149.refs_0_.hidden_ref = bf16[80,1152]{1,0:T(8,128)(2,1)} custom-call(bf16[40,1024]{1,0:T(8,128)(2,1)} %pol_ref.1, bf16[40,1024]{1,0:T(8,128)(2,1)} %ref_ref.1, s32[8,40]{1,0:T(8,128)} %bitcast.104, s32[8,40]{1,0:T(8,128)} %bitcast.105, f32[8,40]{1,0:T(8,128)} %bitcast.106, f32[8,40]{1,0:T(8,128)} %bitcast.107), custom_call_target="tpu_custom_call" | custom-call | tf_op jit(solution)/shard_map/pallas_call | solution.py:47
  2.9 2.5 %collective-permute-start = (bf16[80,1152]{1,0:T(8,128)(2,1)}, bf16[80,1152]{1,0:T(8,128)(2,1)S(1)}, u32[]{:S(2)}, u32[]{:S(2)}) collective-permute-start(bf16[80,1152]{1,0:T(8,128)(2,1)} %shard_map.149.refs_0_.hidden_ref), channel_id=1, source_target_pairs={{0,2},{2,0},{4,6},{6,4},{1,3},{3,1},{5,7},{7,5},{8,10},{10,8},{12,... | collective-permute-start | bytes 552968 | tf_op jit(solution)/shard_map/ppermute | solution.py:344
  5.4 1.5 %collective-permute-start.1 = (bf16[80,1152]{1,0:T(8,128)(2,1)}, bf16[80,1152]{1,0:T(8,128)(2,1)S(1)}, u32[]{:S(2)}, u32[]{:S(2)}) collective-permute-start(bf16[80,1152]{1,0:T(8,128)(2,1)} %shard_map.149.refs_0_.hidden_ref), channel_id=1, source_target_pairs={{0,4},{2,6},{4,0},{6,2},{1,5},{3,7},{5,1},{7,3},{8,12},{10,14},{12... | collective-permute-start | bytes 552968 | tf_op jit(solution)/shard_map/ppermute | solution.py:344
  6.9 4.2 %collective-permute-done.refs_1_ = bf16[80,1152]{1,0:T(8,128)(2,1)S(1)} collective-permute-done((bf16[80,1152]{1,0:T(8,128)(2,1)}, bf16[80,1152]{1,0:T(8,128)(2,1)S(1)}, u32[]{:S(2)}, u32[]{:S(2)}) %collective-permute-start) | collective-permute-done | bytes 184352 | tf_op jit(solution)/shard_map/ppermute | solution.py:344
  11.1 5.2 %collective-permute-done.1.refs_2_ = bf16[80,1152]{1,0:T(8,128)(2,1)S(1)} collective-permute-done((bf16[80,1152]{1,0:T(8,128)(2,1)}, bf16[80,1152]{1,0:T(8,128)(2,1)S(1)}, u32[]{:S(2)}, u32[]{:S(2)}) %collective-permute-start.1) | collective-permute-done | bytes 184352 | tf_op jit(solution)/shard_map/ppermute | solution.py:344
  16.8 0.6 pad_add_fusion.2.place_ref
  18.4 0.7 copy-done.13
  19.1 19.0 %shard_map.150 = (f32[4,80,1024]{2,1,0:T(8,128)}, f32[4,80,1024]{2,1,0:T(8,128)}) custom-call(s32[2]{0:T(128)} %pad_add_fusion.2.place_ref, bf16[80,1152]{1,0:T(8,128)(2,1)} %shard_map.149.refs_0_.hidden_ref, bf16[80,1152]{1,0:T(8,128)(2,1)} %copy-done.7, bf16[80,1152]{1,0:T(8,128)(2,1)} %copy-done.8, bf16[80,1152]{1,0:T(8,128)(2,1)} %copy-done.9, ...), custom_call_target="tpu_custom_call" | custom-call | flops 6442450944 | bytes 22970368 | tf_op jit(solution)/shard_map/pallas_call | solution.py:143
  38.3 3.1 %collective-permute-done.7.came_ref = f32[4,80,1024]{2,1,0:T(8,128)S(1)} collective-permute-done((f32[4,80,1024]{2,1,0:T(8,128)}, f32[4,80,1024]{2,1,0:T(8,128)S(1)}, u32[]{:S(2)}, u32[]{:S(2)}) %collective-permute-start.7) | collective-permute-done | bytes 1310752 | tf_op jit(solution)/shard_map/ppermute | solution.py:353
  41.4 1.3 copy-done
  42.8 1.6 %collective-permute-start.8 = (f32[80,1024]{1,0:T(8,128)S(1)}, f32[80,1024]{1,0:T(8,128)S(1)}, u32[]{:S(2)}, u32[]{:S(2)}) collective-permute-start(f32[80,1024]{1,0:T(8,128)S(1)} %get-tuple-element.13), channel_id=1, source_target_pairs={{0,6},{2,4},{4,2},{6,0},{1,7},{3,5},{5,3},{7,1},{8,14},{10,12},{12... | collective-permute-start | bytes 983048 | tf_op jit(solution)/shard_map/ppermute | solution.py:344
  44.5 0.7 collective-permute-start.10
  45.2 1.3 collective-permute-start.9
  46.5 7.8 %collective-permute-done.8.came_ref = f32[80,1024]{1,0:T(8,128)S(1)} collective-permute-done((f32[80,1024]{1,0:T(8,128)S(1)}, f32[80,1024]{1,0:T(8,128)S(1)}, u32[]{:S(2)}, u32[]{:S(2)}) %collective-permute-start.8) | collective-permute-done | bytes 327712 | tf_op jit(solution)/shard_map/ppermute | solution.py:344
  54.4 0.6 shard_map.152
  55.0 6.0 %all-to-all-start = ((s32[16,1,40]{2,1,0:T(1,128)}), s32[16,1,40]{2,1,0:T(1,128)S(1)}, u32[]{:S(2)}, u32[]{:S(2)}) async-start(s32[16,1,40]{2,1,0:T(1,128)} %bitcast.10), calls=%async_computation | async-start | bytes 16384 | tf_op jit(solution)/shard_map/all_to_all | solution.py:386
  61.0 7.2 %all-to-all-done = s32[16,1,40]{2,1,0:T(1,128)S(1)} async-done(((s32[16,1,40]{2,1,0:T(1,128)}), s32[16,1,40]{2,1,0:T(1,128)S(1)}, u32[]{:S(2)}, u32[]{:S(2)}) %all-to-all-start) | async-done | bytes 2592 | tf_op jit(solution)/shard_map/all_to_all | solution.py:386
  68.7 0.6 collective-permute-start.11
  69.9 2.7 %collective-permute-start.15 = (bf16[80,1024]{1,0:T(8,128)(2,1)S(1)}, bf16[80,1024]{1,0:T(8,128)(2,1)S(1)}, u32[]{:S(2)}, u32[]{:S(2)}) collective-permute-start(bf16[80,1024]{1,0:T(8,128)(2,1)S(1)} %shard_map.153.refs_0_), channel_id=1, source_target_pairs={{0,24},{8,0},{16,8},{24,16},{1,25},{9,1},{17,9},{25,17},{2,26},{10... | collective-permute-start | bytes 491528 | tf_op jit(solution)/shard_map/ppermute | solution.py:349
  72.6 0.6 collective-permute-start.17
  73.2 4.2 %collective-permute-done.11.refs_1_ = bf16[80,1024]{1,0:T(8,128)(2,1)S(1)} collective-permute-done((bf16[80,1024]{1,0:T(8,128)(2,1)S(1)}, bf16[80,1024]{1,0:T(8,128)(2,1)S(1)}, u32[]{:S(2)}, u32[]{:S(2)}) %collective-permute-start.11) | collective-permute-done | bytes 163872 | tf_op jit(solution)/shard_map/ppermute | solution.py:349
  78.0 3.0 %collective-permute-done.13.refs_2_ = bf16[80,1024]{1,0:T(8,128)(2,1)S(1)} collective-permute-done((bf16[80,1024]{1,0:T(8,128)(2,1)S(1)}, bf16[80,1024]{1,0:T(8,128)(2,1)S(1)}, u32[]{:S(2)}, u32[]{:S(2)}) %collective-permute-start.13) | collective-permute-done | bytes 163872 | tf_op jit(solution)/shard_map/ppermute | solution.py:349
  81.0 0.6 collective-permute-start.12
  82.2 1.5 %collective-permute-start.23 = (bf16[80,1024]{1,0:T(8,128)(2,1)S(1)}, bf16[80,1024]{1,0:T(8,128)(2,1)S(1)}, u32[]{:S(2)}, u32[]{:S(2)}) collective-permute-start(bf16[80,1024]{1,0:T(8,128)(2,1)S(1)} %collective-permute-done.13.refs_2_), channel_id=1, source_target_pairs={{0,2},{2,0},{4,6},{6,4},{1,3},{3,1},{5,7},{7,5},{8,10},{10,8},{12,... | collective-permute-start | bytes 491528 | tf_op jit(solution)/shard_map/ppermute | solution.py:344
  83.6 1.5 collective-permute-start.14
  85.1 3.1 %collective-permute-done.12.refs_9_.refs_0_ = bf16[80,1024]{1,0:T(8,128)(2,1)S(1)} collective-permute-done((bf16[80,1024]{1,0:T(8,128)(2,1)S(1)}, bf16[80,1024]{1,0:T(8,128)(2,1)S(1)}, u32[]{:S(2)}, u32[]{:S(2)}) %collective-permute-start.12) | collective-permute-done | bytes 163872 | tf_op jit(solution)/shard_map/ppermute | solution.py:344
  88.6 1.6 %collective-permute-start.16 = (bf16[80,1024]{1,0:T(8,128)(2,1)S(1)}, bf16[80,1024]{1,0:T(8,128)(2,1)S(1)}, u32[]{:S(2)}, u32[]{:S(2)}) collective-permute-start(bf16[80,1024]{1,0:T(8,128)(2,1)S(1)} %collective-permute-done.15.refs_3_), channel_id=1, source_target_pairs={{0,4},{2,6},{4,0},{6,2},{1,5},{3,7},{5,1},{7,3},{8,12},{10,14},{12... | collective-permute-start | bytes 491528 | tf_op jit(solution)/shard_map/ppermute | solution.py:344
  91.1 0.6 slice.80.wanted_ref
  92.7 0.8 collective-permute-done.24.refs_7_
  93.5 1.0 collective-permute-start.20
  95.0 0.7 collective-permute-done.16.refs_2_
  95.7 1.6 %collective-permute-start.22 = (bf16[80,1024]{1,0:T(8,128)(2,1)S(1)}, bf16[80,1024]{1,0:T(8,128)(2,1)S(1)}, u32[]{:S(2)}, u32[]{:S(2)}) collective-permute-start(bf16[80,1024]{1,0:T(8,128)(2,1)S(1)} %collective-permute-done.16.refs_2_), channel_id=1, source_target_pairs={{0,2},{2,0},{4,6},{6,4},{1,3},{3,1},{5,7},{7,5},{8,10},{10,8},{12,... | collective-permute-start | bytes 491528 | tf_op jit(solution)/shard_map/ppermute | solution.py:344
  97.4 14.4 %shard_map.154.refs_7_ = f32[2,768]{1,0:T(2,128)} custom-call(s32[18]{0:T(128)} %pad_add_fusion.1.spots_ref, s32[1,768]{1,0:T(1,128)} %slice.80.wanted_ref, bf16[80,1024]{1,0:T(8,128)(2,1)} %copy-done.2, bf16[80,1024]{1,0:T(8,128)(2,1)} %copy-done.14, bf16[80,1024]{1,0:T(8,128)(2,1)} %copy-done.15, bf16[80,1024]{1,0:T(8,128)(2,1)} %copy-done.18, ...), custom_call_target="tpu_custom_call" | custom-call | flops 7650410496 | bytes 11534336 | tf_op jit(solution)/shard_map/pallas_call | solution.py:302
  111.9 0.6 copy-done.25
  112.7 0.7 copy-done.28
  113.3 12.4 %shard_map.155 = f32[16,2,80]{2,1,0:T(2,128)} custom-call(s32[18]{0:T(128)} %pad_add_fusion.1.spots_ref, s32[1,512]{1,0:T(1,128)} %slice.79.wanted_ref, bf16[80,1024]{1,0:T(8,128)(2,1)} %copy-done.16, bf16[80,1024]{1,0:T(8,128)(2,1)} %copy-done.21, bf16[80,1024]{1,0:T(8,128)(2,1)} %copy-done.23, bf16[80,1024]{1,0:T(8,128)(2,1)} %copy-done.25, ...), custom_call_target="tpu_custom_call" | custom-call | flops 5100273664 | bytes 11010048 | tf_op jit(solution)/shard_map/pallas_call | solution.py:302
  125.8 0.7 copy.39
  126.5 2.1 %collective-permute-start.27 = (f32[16,2,80]{2,0,1:T(8,128)S(1)}, f32[16,2,80]{2,0,1:T(8,128)S(1)}, u32[]{:S(2)}, u32[]{:S(2)}) collective-permute-start(f32[16,2,80]{2,0,1:T(8,128)S(1)} %copy.39), channel_id=1, source_target_pairs={{0,8},{8,16},{16,24},{24,0},{1,9},{9,17},{17,25},{25,1},{2,10},{10... | collective-permute-start | bytes 30728 | tf_op jit(solution)/shard_map/ppermute | solution.py:349
  128.6 1.3 collective-permute-start.28
  129.9 2.6 %collective-permute-start.29 = (f32[16,2,80]{2,0,1:T(8,128)S(1)}, f32[16,2,80]{2,0,1:T(8,128)S(1)}, u32[]{:S(2)}, u32[]{:S(2)}) collective-permute-start(f32[16,2,80]{2,0,1:T(8,128)S(1)} %copy.39), channel_id=1, source_target_pairs={{0,24},{8,0},{16,8},{24,16},{1,25},{9,1},{17,9},{25,17},{2,26},{10... | collective-permute-start | bytes 30728 | tf_op jit(solution)/shard_map/ppermute | solution.py:349
  132.5 0.7 fusion.19
  133.2 0.7 slice.85
  134.0 1.3 collective-permute-start.30
  135.3 1.4 collective-permute-start.31
  136.7 0.9 collective-permute-start.32
  139.6 1.8 %collective-permute-done.32 = f32[16,2,80]{2,0,1:T(8,128)S(1)} collective-permute-done((f32[16,2,80]{2,0,1:T(8,128)S(1)}, f32[16,2,80]{2,0,1:T(8,128)S(1)}, u32[]{:S(2)}, u32[]{:S(2)}) %collective-permute-start.32) | collective-permute-done | bytes 10272 | tf_op jit(solution)/shard_map/ppermute | solution.py:344
  142.0 0.6 collective-permute-done.33
  142.6 1.3 add_reduce_fusion
  (112 shorter events, 8.4 us)
Async XLA Ops:
  0.6 96.7 %collective-permute-start.26 = (bf16[2432,1024]{1,0:T(8,128)(2,1)}, bf16[2432,1024]{1,0:T(8,128)(2,1)}, u32[]{:S(2)}, u32[]{:S(2)}) collective-permute-start(bf16[2432,1024]{1,0:T(8,128)(2,1)} %refs_8_.3), channel_id=1, source_target_pairs={{0,1},{1,0},{2,3},{3,2},{4,5},{5,4},{6,7},{7,6},{8,9},{9,8},{10,11... | collective-permute-start | bytes 14942216 | tf_op jit(solution)/shard_map/ppermute | solution.py:353
  2.9 8.2 %collective-permute-start = (bf16[80,1152]{1,0:T(8,128)(2,1)}, bf16[80,1152]{1,0:T(8,128)(2,1)S(1)}, u32[]{:S(2)}, u32[]{:S(2)}) collective-permute-start(bf16[80,1152]{1,0:T(8,128)(2,1)} %shard_map.149.refs_0_.hidden_ref), channel_id=1, source_target_pairs={{0,2},{2,0},{4,6},{6,4},{1,3},{3,1},{5,7},{7,5},{8,10},{10,8},{12,... | collective-permute-start | bytes 552968 | tf_op jit(solution)/shard_map/ppermute | solution.py:344
  5.4 10.9 %collective-permute-start.1 = (bf16[80,1152]{1,0:T(8,128)(2,1)}, bf16[80,1152]{1,0:T(8,128)(2,1)S(1)}, u32[]{:S(2)}, u32[]{:S(2)}) collective-permute-start(bf16[80,1152]{1,0:T(8,128)(2,1)} %shard_map.149.refs_0_.hidden_ref), channel_id=1, source_target_pairs={{0,4},{2,6},{4,0},{6,2},{1,5},{3,7},{5,1},{7,3},{8,12},{10,14},{12... | collective-permute-start | bytes 552968 | tf_op jit(solution)/shard_map/ppermute | solution.py:344
  6.9 9.4 %collective-permute-start.2 = (bf16[80,1152]{1,0:T(8,128)(2,1)}, bf16[80,1152]{1,0:T(8,128)(2,1)S(1)}, u32[]{:S(2)}, u32[]{:S(2)}) collective-permute-start(bf16[80,1152]{1,0:T(8,128)(2,1)} %shard_map.149.refs_0_.hidden_ref), channel_id=1, source_target_pairs={{0,6},{2,4},{4,2},{6,0},{1,7},{3,5},{5,3},{7,1},{8,14},{10,12},{12... | collective-permute-start | bytes 552968 | tf_op jit(solution)/shard_map/ppermute | solution.py:344
  6.9 10.5 %collective-permute-start.3 = (bf16[80,1152]{1,0:T(8,128)(2,1)}, bf16[80,1152]{1,0:T(8,128)(2,1)S(1)}, u32[]{:S(2)}, u32[]{:S(2)}) collective-permute-start(bf16[80,1152]{1,0:T(8,128)(2,1)} %shard_map.149.refs_0_.hidden_ref), channel_id=1, source_target_pairs={{0,1},{1,0},{2,3},{3,2},{4,5},{5,4},{6,7},{7,6},{8,9},{9,8},{10,11... | collective-permute-start | bytes 552968 | tf_op jit(solution)/shard_map/ppermute | solution.py:353
  11.1 6.4 %collective-permute-start.4 = (bf16[80,1152]{1,0:T(8,128)(2,1)S(1)}, bf16[80,1152]{1,0:T(8,128)(2,1)S(1)}, u32[]{:S(2)}, u32[]{:S(2)}) collective-permute-start(bf16[80,1152]{1,0:T(8,128)(2,1)S(1)} %collective-permute-done.refs_1_), channel_id=1, source_target_pairs={{0,1},{1,0},{2,3},{3,2},{4,5},{5,4},{6,7},{7,6},{8,9},{9,8},{10,11... | collective-permute-start | bytes 552968 | tf_op jit(solution)/shard_map/ppermute | solution.py:353
  16.3 1.4 collective-permute-start.5
  16.4 1.7 %collective-permute-start.6 = (bf16[80,1152]{1,0:T(8,128)(2,1)S(1)}, bf16[80,1152]{1,0:T(8,128)(2,1)S(1)}, u32[]{:S(2)}, u32[]{:S(2)}) collective-permute-start(bf16[80,1152]{1,0:T(8,128)(2,1)S(1)} %collective-permute-done.2.refs_3_), channel_id=1, source_target_pairs={{0,1},{1,0},{2,3},{3,2},{4,5},{5,4},{6,7},{7,6},{8,9},{9,8},{10,11... | collective-permute-start | bytes 552968 | tf_op jit(solution)/shard_map/ppermute | solution.py:353
  17.5 36.9 %copy-start.4 = (s32[40]{0:T(128)S(1)}, s32[40]{0:T(128)}, u32[]{:S(2)}) copy-start(s32[40]{0:T(128)} %param.25) | copy-start | bytes 484
  17.5 51.1 %copy-start.1 = (bf16[80,1152]{1,0:T(8,128)(2,1)S(1)}, bf16[80,1152]{1,0:T(8,128)(2,1)}, u32[]{:S(2)}) copy-start(bf16[80,1152]{1,0:T(8,128)(2,1)} %shard_map.149.refs_0_.hidden_ref) | copy-start | bytes 552964
  17.5 51.1 %copy-start.3 = (f32[1024]{0:T(1024)S(1)}, f32[1024]{0:T(1024)}, u32[]{:S(2)}) copy-start(f32[1024]{0:T(1024)} %param.23) | copy-start | bytes 12292
  17.5 72.8 %copy-start.5 = (s32[32]{0:T(128)S(1)}, s32[32]{0:T(128)}, u32[]{:S(2)}) copy-start(s32[32]{0:T(128)} %param.26) | copy-start | bytes 388
  38.1 3.2 %collective-permute-start.7 = (f32[4,80,1024]{2,1,0:T(8,128)}, f32[4,80,1024]{2,1,0:T(8,128)S(1)}, u32[]{:S(2)}, u32[]{:S(2)}) collective-permute-start(f32[4,80,1024]{2,1,0:T(8,128)} %get-tuple-element.11), channel_id=1, source_target_pairs={{0,1},{1,0},{2,3},{3,2},{4,5},{5,4},{6,7},{7,6},{8,9},{9,8},{10,11... | collective-permute-start | bytes 3932168 | tf_op jit(solution)/shard_map/ppermute | solution.py:353
  42.8 11.6 %collective-permute-start.8 = (f32[80,1024]{1,0:T(8,128)S(1)}, f32[80,1024]{1,0:T(8,128)S(1)}, u32[]{:S(2)}, u32[]{:S(2)}) collective-permute-start(f32[80,1024]{1,0:T(8,128)S(1)} %get-tuple-element.13), channel_id=1, source_target_pairs={{0,6},{2,4},{4,2},{6,0},{1,7},{3,5},{5,3},{7,1},{8,14},{10,12},{12... | collective-permute-start | bytes 983048 | tf_op jit(solution)/shard_map/ppermute | solution.py:344
  44.5 24.0 %collective-permute-start.10 = (f32[80,1024]{1,0:T(8,128)S(1)}, f32[80,1024]{1,0:T(8,128)S(1)}, u32[]{:S(2)}, u32[]{:S(2)}) collective-permute-start(f32[80,1024]{1,0:T(8,128)S(1)} %get-tuple-element.17), channel_id=1, source_target_pairs={{0,4},{2,6},{4,0},{6,2},{1,5},{3,7},{5,1},{7,3},{8,12},{10,14},{12... | collective-permute-start | bytes 983048 | tf_op jit(solution)/shard_map/ppermute | solution.py:344
  45.2 23.3 %collective-permute-start.9 = (f32[80,1024]{1,0:T(8,128)S(1)}, f32[80,1024]{1,0:T(8,128)S(1)}, u32[]{:S(2)}, u32[]{:S(2)}) collective-permute-start(f32[80,1024]{1,0:T(8,128)S(1)} %get-tuple-element.16), channel_id=1, source_target_pairs={{0,2},{2,0},{4,6},{6,4},{1,3},{3,1},{5,7},{7,5},{8,10},{10,8},{12,... | collective-permute-start | bytes 983048 | tf_op jit(solution)/shard_map/ppermute | solution.py:344
  55.0 13.2 %all-to-all-start = ((s32[16,1,40]{2,1,0:T(1,128)}), s32[16,1,40]{2,1,0:T(1,128)S(1)}, u32[]{:S(2)}, u32[]{:S(2)}) async-start(s32[16,1,40]{2,1,0:T(1,128)} %bitcast.10), calls=%async_computation | async-start | bytes 16384 | tf_op jit(solution)/shard_map/all_to_all | solution.py:386
  68.7 28.6 %copy-start.2 = (bf16[80,1024]{1,0:T(8,128)(2,1)}, bf16[80,1024]{1,0:T(8,128)(2,1)S(1)}, u32[]{:S(2)}) copy-start(bf16[80,1024]{1,0:T(8,128)(2,1)S(1)} %shard_map.153.refs_0_) | copy-start | bytes 491524
  68.7 8.7 %collective-permute-start.11 = (bf16[80,1024]{1,0:T(8,128)(2,1)S(1)}, bf16[80,1024]{1,0:T(8,128)(2,1)S(1)}, u32[]{:S(2)}, u32[]{:S(2)}) collective-permute-start(bf16[80,1024]{1,0:T(8,128)(2,1)S(1)} %shard_map.153.refs_0_), channel_id=1, source_target_pairs={{0,8},{8,16},{16,24},{24,0},{1,9},{9,17},{17,25},{25,1},{2,10},{10... | collective-permute-start | bytes 491528 | tf_op jit(solution)/shard_map/ppermute | solution.py:349
  69.4 11.7 %collective-permute-start.13 = (bf16[80,1024]{1,0:T(8,128)(2,1)S(1)}, bf16[80,1024]{1,0:T(8,128)(2,1)S(1)}, u32[]{:S(2)}, u32[]{:S(2)}) collective-permute-start(bf16[80,1024]{1,0:T(8,128)(2,1)S(1)} %shard_map.153.refs_0_), channel_id=1, source_target_pairs={{0,16},{8,24},{16,0},{24,8},{1,17},{9,25},{17,1},{25,9},{2,18},{10... | collective-permute-start | bytes 491528 | tf_op jit(solution)/shard_map/ppermute | solution.py:349
  69.9 11.7 %collective-permute-start.15 = (bf16[80,1024]{1,0:T(8,128)(2,1)S(1)}, bf16[80,1024]{1,0:T(8,128)(2,1)S(1)}, u32[]{:S(2)}, u32[]{:S(2)}) collective-permute-start(bf16[80,1024]{1,0:T(8,128)(2,1)S(1)} %shard_map.153.refs_0_), channel_id=1, source_target_pairs={{0,24},{8,0},{16,8},{24,16},{1,25},{9,1},{17,9},{25,17},{2,26},{10... | collective-permute-start | bytes 491528 | tf_op jit(solution)/shard_map/ppermute | solution.py:349
  72.6 9.6 %collective-permute-start.17 = (bf16[80,1024]{1,0:T(8,128)(2,1)S(1)}, bf16[80,1024]{1,0:T(8,128)(2,1)S(1)}, u32[]{:S(2)}, u32[]{:S(2)}) collective-permute-start(bf16[80,1024]{1,0:T(8,128)(2,1)S(1)} %shard_map.153.refs_0_), channel_id=1, source_target_pairs={{0,2},{2,0},{4,6},{6,4},{1,3},{3,1},{5,7},{7,5},{8,10},{10,8},{12,... | collective-permute-start | bytes 491528 | tf_op jit(solution)/shard_map/ppermute | solution.py:344
  77.4 19.9 %copy-start.14 = (bf16[80,1024]{1,0:T(8,128)(2,1)}, bf16[80,1024]{1,0:T(8,128)(2,1)S(1)}, u32[]{:S(2)}) copy-start(bf16[80,1024]{1,0:T(8,128)(2,1)S(1)} %collective-permute-done.11.refs_1_) | copy-start | bytes 491524
  77.4 6.2 %collective-permute-start.25 = (bf16[80,1024]{1,0:T(8,128)(2,1)S(1)}, bf16[80,1024]{1,0:T(8,128)(2,1)S(1)}, u32[]{:S(2)}, u32[]{:S(2)}) collective-permute-start(bf16[80,1024]{1,0:T(8,128)(2,1)S(1)} %shard_map.153.refs_0_), channel_id=1, source_target_pairs={{0,4},{2,6},{4,0},{6,2},{1,5},{3,7},{5,1},{7,3},{8,12},{10,14},{12... | collective-permute-start | bytes 491528 | tf_op jit(solution)/shard_map/ppermute | solution.py:344
  81.0 16.3 %copy-start.15 = (bf16[80,1024]{1,0:T(8,128)(2,1)}, bf16[80,1024]{1,0:T(8,128)(2,1)S(1)}, u32[]{:S(2)}) copy-start(bf16[80,1024]{1,0:T(8,128)(2,1)S(1)} %collective-permute-done.13.refs_2_) | copy-start | bytes 491524
  81.0 7.2 %collective-permute-start.12 = (bf16[80,1024]{1,0:T(8,128)(2,1)S(1)}, bf16[80,1024]{1,0:T(8,128)(2,1)S(1)}, u32[]{:S(2)}, u32[]{:S(2)}) collective-permute-start(bf16[80,1024]{1,0:T(8,128)(2,1)S(1)} %collective-permute-done.11.refs_1_), channel_id=1, source_target_pairs={{0,4},{2,6},{4,0},{6,2},{1,5},{3,7},{5,1},{7,3},{8,12},{10,14},{12... | collective-permute-start | bytes 491528 | tf_op jit(solution)/shard_map/ppermute | solution.py:344
  81.6 15.8 %copy-start.18 = (bf16[80,1024]{1,0:T(8,128)(2,1)}, bf16[80,1024]{1,0:T(8,128)(2,1)S(1)}, u32[]{:S(2)}) copy-start(bf16[80,1024]{1,0:T(8,128)(2,1)S(1)} %collective-permute-done.15.refs_3_) | copy-start | bytes 491524
  81.6 7.0 %collective-permute-start.19 = (bf16[80,1024]{1,0:T(8,128)(2,1)S(1)}, bf16[80,1024]{1,0:T(8,128)(2,1)S(1)}, u32[]{:S(2)}, u32[]{:S(2)}) collective-permute-start(bf16[80,1024]{1,0:T(8,128)(2,1)S(1)} %collective-permute-done.11.refs_1_), channel_id=1, source_target_pairs={{0,2},{2,0},{4,6},{6,4},{1,3},{3,1},{5,7},{7,5},{8,10},{10,8},{12,... | collective-permute-start | bytes 491528 | tf_op jit(solution)/shard_map/ppermute | solution.py:344
  82.2 15.2 %copy-start.17 = (bf16[80,1024]{1,0:T(8,128)(2,1)}, bf16[80,1024]{1,0:T(8,128)(2,1)S(1)}, u32[]{:S(2)}) copy-start(bf16[80,1024]{1,0:T(8,128)(2,1)S(1)} %collective-permute-done.17.refs_4_) | copy-start | bytes 491524
  82.2 10.1 %collective-permute-start.23 = (bf16[80,1024]{1,0:T(8,128)(2,1)S(1)}, bf16[80,1024]{1,0:T(8,128)(2,1)S(1)}, u32[]{:S(2)}, u32[]{:S(2)}) collective-permute-start(bf16[80,1024]{1,0:T(8,128)(2,1)S(1)} %collective-permute-done.13.refs_2_), channel_id=1, source_target_pairs={{0,2},{2,0},{4,6},{6,4},{1,3},{3,1},{5,7},{7,5},{8,10},{10,8},{12,... | collective-permute-start | bytes 491528 | tf_op jit(solution)/shard_map/ppermute | solution.py:344
  83.6 13.7 %copy-start.19 = (bf16[80,1024]{1,0:T(8,128)(2,1)}, bf16[80,1024]{1,0:T(8,128)(2,1)S(1)}, u32[]{:S(2)}) copy-start(bf16[80,1024]{1,0:T(8,128)(2,1)S(1)} %collective-permute-done.25.refs_8_) | copy-start | bytes 491524
  83.6 10.8 %collective-permute-start.14 = (bf16[80,1024]{1,0:T(8,128)(2,1)S(1)}, bf16[80,1024]{1,0:T(8,128)(2,1)S(1)}, u32[]{:S(2)}, u32[]{:S(2)}) collective-permute-start(bf16[80,1024]{1,0:T(8,128)(2,1)S(1)} %collective-permute-done.13.refs_2_), channel_id=1, source_target_pairs={{0,4},{2,6},{4,0},{6,2},{1,5},{3,7},{5,1},{7,3},{8,12},{10,14},{12... | collective-permute-start | bytes 491528 | tf_op jit(solution)/shard_map/ppermute | solution.py:344
  88.2 5.3 %collective-permute-start.24 = (bf16[80,1024]{1,0:T(8,128)(2,1)S(1)}, bf16[80,1024]{1,0:T(8,128)(2,1)S(1)}, u32[]{:S(2)}, u32[]{:S(2)}) collective-permute-start(bf16[80,1024]{1,0:T(8,128)(2,1)S(1)} %collective-permute-done.15.refs_3_), channel_id=1, source_target_pairs={{0,2},{2,0},{4,6},{6,4},{1,3},{3,1},{5,7},{7,5},{8,10},{10,8},{12,... | collective-permute-start | bytes 491528 | tf_op jit(solution)/shard_map/ppermute | solution.py:344
  88.6 7.1 %collective-permute-start.16 = (bf16[80,1024]{1,0:T(8,128)(2,1)S(1)}, bf16[80,1024]{1,0:T(8,128)(2,1)S(1)}, u32[]{:S(2)}, u32[]{:S(2)}) collective-permute-start(bf16[80,1024]{1,0:T(8,128)(2,1)S(1)} %collective-permute-done.15.refs_3_), channel_id=1, source_target_pairs={{0,4},{2,6},{4,0},{6,2},{1,5},{3,7},{5,1},{7,3},{8,12},{10,14},{12... | collective-permute-start | bytes 491528 | tf_op jit(solution)/shard_map/ppermute | solution.py:344
  92.3 19.6 %collective-permute-start.18 = (bf16[80,1024]{1,0:T(8,128)(2,1)S(1)}, bf16[80,1024]{1,0:T(8,128)(2,1)S(1)}, u32[]{:S(2)}, u32[]{:S(2)}) collective-permute-start(bf16[80,1024]{1,0:T(8,128)(2,1)S(1)} %collective-permute-done.17.refs_4_), channel_id=1, source_target_pairs={{0,4},{2,6},{4,0},{6,2},{1,5},{3,7},{5,1},{7,3},{8,12},{10,14},{12... | collective-permute-start | bytes 491528 | tf_op jit(solution)/shard_map/ppermute | solution.py:344
  93.5 18.4 %collective-permute-start.20 = (bf16[80,1024]{1,0:T(8,128)(2,1)S(1)}, bf16[80,1024]{1,0:T(8,128)(2,1)S(1)}, u32[]{:S(2)}, u32[]{:S(2)}) collective-permute-start(bf16[80,1024]{1,0:T(8,128)(2,1)S(1)} %collective-permute-done.19.refs_5_), channel_id=1, source_target_pairs={{0,4},{2,6},{4,0},{6,2},{1,5},{3,7},{5,1},{7,3},{8,12},{10,14},{12... | collective-permute-start | bytes 491528 | tf_op jit(solution)/shard_map/ppermute | solution.py:344
  94.5 17.4 %copy-start.21 = (bf16[80,1024]{1,0:T(8,128)(2,1)}, bf16[80,1024]{1,0:T(8,128)(2,1)S(1)}, u32[]{:S(2)}) copy-start(bf16[80,1024]{1,0:T(8,128)(2,1)S(1)} %collective-permute-done.14.refs_1_) | copy-start | bytes 491524
  94.5 17.4 %collective-permute-start.21 = (bf16[80,1024]{1,0:T(8,128)(2,1)S(1)}, bf16[80,1024]{1,0:T(8,128)(2,1)S(1)}, u32[]{:S(2)}, u32[]{:S(2)}) collective-permute-start(bf16[80,1024]{1,0:T(8,128)(2,1)S(1)} %collective-permute-done.14.refs_1_), channel_id=1, source_target_pairs={{0,2},{2,0},{4,6},{6,4},{1,3},{3,1},{5,7},{7,5},{8,10},{10,8},{12,... | collective-permute-start | bytes 491528 | tf_op jit(solution)/shard_map/ppermute | solution.py:344
  95.7 16.1 %copy-start.23 = (bf16[80,1024]{1,0:T(8,128)(2,1)}, bf16[80,1024]{1,0:T(8,128)(2,1)S(1)}, u32[]{:S(2)}) copy-start(bf16[80,1024]{1,0:T(8,128)(2,1)S(1)} %collective-permute-done.16.refs_2_) | copy-start | bytes 491524
  95.7 16.2 %collective-permute-start.22 = (bf16[80,1024]{1,0:T(8,128)(2,1)S(1)}, bf16[80,1024]{1,0:T(8,128)(2,1)S(1)}, u32[]{:S(2)}, u32[]{:S(2)}) collective-permute-start(bf16[80,1024]{1,0:T(8,128)(2,1)S(1)} %collective-permute-done.16.refs_2_), channel_id=1, source_target_pairs={{0,2},{2,0},{4,6},{6,4},{1,3},{3,1},{5,7},{7,5},{8,10},{10,8},{12,... | collective-permute-start | bytes 491528 | tf_op jit(solution)/shard_map/ppermute | solution.py:344
  111.8 20.7 %copy-start.6 = (s32[32]{0:T(128)S(1)}, s32[32]{0:T(128)}, u32[]{:S(2)}) copy-start(s32[32]{0:T(128)} %param.27) | copy-start | bytes 388
  126.5 7.5 %collective-permute-start.27 = (f32[16,2,80]{2,0,1:T(8,128)S(1)}, f32[16,2,80]{2,0,1:T(8,128)S(1)}, u32[]{:S(2)}, u32[]{:S(2)}) collective-permute-start(f32[16,2,80]{2,0,1:T(8,128)S(1)} %copy.39), channel_id=1, source_target_pairs={{0,8},{8,16},{16,24},{24,0},{1,9},{9,17},{17,25},{25,1},{2,10},{10... | collective-permute-start | bytes 30728 | tf_op jit(solution)/shard_map/ppermute | solution.py:349
  128.6 5.4 %collective-permute-start.28 = (f32[16,2,80]{2,0,1:T(8,128)S(1)}, f32[16,2,80]{2,0,1:T(8,128)S(1)}, u32[]{:S(2)}, u32[]{:S(2)}) collective-permute-start(f32[16,2,80]{2,0,1:T(8,128)S(1)} %copy.39), channel_id=1, source_target_pairs={{0,16},{8,24},{16,0},{24,8},{1,17},{9,25},{17,1},{25,9},{2,18},{10... | collective-permute-start | bytes 30728 | tf_op jit(solution)/shard_map/ppermute | solution.py:349
  129.9 4.1 %collective-permute-start.29 = (f32[16,2,80]{2,0,1:T(8,128)S(1)}, f32[16,2,80]{2,0,1:T(8,128)S(1)}, u32[]{:S(2)}, u32[]{:S(2)}) collective-permute-start(f32[16,2,80]{2,0,1:T(8,128)S(1)} %copy.39), channel_id=1, source_target_pairs={{0,24},{8,0},{16,8},{24,16},{1,25},{9,1},{17,9},{25,17},{2,26},{10... | collective-permute-start | bytes 30728 | tf_op jit(solution)/shard_map/ppermute | solution.py:349
  134.0 5.5 %collective-permute-start.30 = (f32[16,2,80]{2,0,1:T(8,128)S(1)}, f32[16,2,80]{2,0,1:T(8,128)S(1)}, u32[]{:S(2)}, u32[]{:S(2)}) collective-permute-start(f32[16,2,80]{2,0,1:T(8,128)S(1)} %pad_maximum_fusion), channel_id=1, source_target_pairs={{0,2},{2,0},{4,6},{6,4},{1,3},{3,1},{5,7},{7,5},{8,10},{10,8},{12,... | collective-permute-start | bytes 30728 | tf_op jit(solution)/shard_map/ppermute | solution.py:344
  135.3 4.3 %collective-permute-start.31 = (f32[16,2,80]{2,0,1:T(8,128)S(1)}, f32[16,2,80]{2,0,1:T(8,128)S(1)}, u32[]{:S(2)}, u32[]{:S(2)}) collective-permute-start(f32[16,2,80]{2,0,1:T(8,128)S(1)} %pad_maximum_fusion), channel_id=1, source_target_pairs={{0,4},{2,6},{4,0},{6,2},{1,5},{3,7},{5,1},{7,3},{8,12},{10,14},{12... | collective-permute-start | bytes 30728 | tf_op jit(solution)/shard_map/ppermute | solution.py:344
  136.7 4.6 %collective-permute-start.32 = (f32[16,2,80]{2,0,1:T(8,128)S(1)}, f32[16,2,80]{2,0,1:T(8,128)S(1)}, u32[]{:S(2)}, u32[]{:S(2)}) collective-permute-start(f32[16,2,80]{2,0,1:T(8,128)S(1)} %pad_maximum_fusion), channel_id=1, source_target_pairs={{0,6},{2,4},{4,2},{6,0},{1,7},{3,5},{5,3},{7,1},{8,14},{10,12},{12... | collective-permute-start | bytes 30728 | tf_op jit(solution)/shard_map/ppermute | solution.py:344
  141.4 1.2 collective-permute-start.33
  (16 other events, 44.3 us)

commit v6 on v5

--- a/solution.py
+++ b/solution.py
@@ -52,11 +52,12 @@
     )(pol_hidden, ref_hidden, pol_routes.T, ref_routes.T, pol_gates.T, ref_gates.T)
 
 
-def expert_kernel(block, slots, width, experts, chips, place_ref, *refs):
+def expert_kernel(block, slots, width, experts, chips, place_ref, early_ref, *refs):
+    del early_ref
     count = 2 * chips
     blocks, refs = refs[:count], refs[count:]
     gate_ref, up_ref, down_ref, keep_ref, give_ref = refs[:5]
-    rows_in, table, pick, weight, picked, made = refs[5:]
+    rows_in, table, pick, weight, picked, made, gate_buf, up_buf, down_buf, arrived = refs[5:]
     step = pl.program_id(0)
     last = pl.num_programs(0) - 1
     rows = rows_in.shape[0]
@@ -64,8 +65,18 @@
     local_experts = pick.shape[0] // slots
     chip, core = place_ref[0], place_ref[1]
 
+    def weight_copies(e):
+        pairs = ((gate_ref, gate_buf), (up_ref, up_buf), (down_ref, down_buf))
+        return [
+            pltpu.make_async_copy(source.at[e], buffer.at[e], arrived.at[index, e])
+            for index, (source, buffer) in enumerate(pairs)
+        ]
+
     @pl.when(step == 0)
     def _():
+        for e in range(local_experts):
+            for copy in weight_copies(e):
+                copy.start()
         for index, ref in enumerate(blocks):
             owner = 2 * (chip ^ (index % chips)) + (core ^ (index // chips))
             rows_in[pl.ds(pl.multiple_of(owner * share, 16), share), :] = ref[...]
@@ -97,10 +108,12 @@
 
     band = pl.ds(pl.multiple_of(step * slots, slots), slots)
     mine = picked[band, :]
-    gate_act = jnp.dot(mine, gate_ref[0], preferred_element_type=jnp.float32)
-    up_act = jnp.dot(mine, up_ref[0], preferred_element_type=jnp.float32)
+    for copy in weight_copies(step):
+        copy.wait()
+    gate_act = jnp.dot(mine, gate_buf[step], preferred_element_type=jnp.float32)
+    up_act = jnp.dot(mine, up_buf[step], preferred_element_type=jnp.float32)
     inner = (gate_act / (1.0 + jnp.exp(-gate_act)) * up_act).astype(jnp.bfloat16)
-    output = jnp.dot(inner, down_ref[0], preferred_element_type=jnp.float32).astype(jnp.bfloat16)
+    output = jnp.dot(inner, down_buf[step], preferred_element_type=jnp.float32).astype(jnp.bfloat16)
     scaled = output.astype(jnp.float32) * weight[band, :]
     high = scaled.astype(jnp.bfloat16)
     made[band, :width] = high
@@ -129,7 +142,7 @@
                     give_ref[c ^ chip] = target
 
 
-def expert_sums(place, blocks, w_gate, w_up, w_down, block, capacity, width, experts):
+def expert_sums(place, early, blocks, w_gate, w_up, w_down, block, capacity, width, experts):
     count = len(blocks)
     share, wide = blocks[0].shape
     rows = count * share
@@ -146,10 +159,8 @@
         grid_spec=pltpu.PrefetchScalarGridSpec(
             num_scalar_prefetch=1,
             grid=(local_experts,),
-            in_specs=[whole] * count + [
-                pl.BlockSpec((1, width, hidden), lambda e, place: (e, 0, 0)),
-                pl.BlockSpec((1, width, hidden), lambda e, place: (e, 0, 0)),
-                pl.BlockSpec((1, hidden, width), lambda e, place: (e, 0, 0)),
+            in_specs=[pl.BlockSpec(memory_space=pl.ANY)] + [whole] * count + [
+                pl.BlockSpec(memory_space=pl.ANY) for _ in range(3)
             ],
             out_specs=(
                 pl.BlockSpec(
@@ -166,6 +177,10 @@
                 pltpu.VMEM((every, 1), jnp.float32),
                 pltpu.VMEM((every, width), jnp.bfloat16),
                 pltpu.VMEM((every, 2 * width), jnp.bfloat16),
+                pltpu.VMEM(w_gate.shape, jnp.bfloat16),
+                pltpu.VMEM(w_up.shape, jnp.bfloat16),
+                pltpu.VMEM(w_down.shape, jnp.bfloat16),
+                pltpu.SemaphoreType.DMA((3, local_experts)),
             ],
         ),
         compiler_params=pltpu.CompilerParams(
@@ -176,54 +191,51 @@
             bytes_accessed=w_gate.size * 6 + rows * wide * 2 + rows * width * 4,
             transcendentals=every * hidden,
         ),
-    )(place, *blocks, w_gate, w_up, w_down)
-
-
-def pair_kernel(keep_ref, came_ref, *sums):
-    for index, total in enumerate(sums):
-        total[...] = keep_ref[index] + came_ref[index]
-
-
-def pair_sums(keep, came):
+    )(place, early, *blocks, w_gate, w_up, w_down)
+
+
+def pair_kernel(keep_ref, came_ref, goal_ref, own_ref, *sends):
+    own_ref[...] = keep_ref[0] + came_ref[0]
+    share, lines = keep_ref.shape[1], goal_ref.shape[1]
+    for index, send in enumerate(sends):
+        send[:share] = keep_ref[index + 1] + came_ref[index + 1]
+        send[share:] = jnp.zeros((send.shape[0] - share, send.shape[1]), jnp.float32)
+        send[share:share + 1, :lines] = goal_ref[...]
+
+
+def pair_sums(keep, came, goal):
     chips, share, width = keep.shape
-    part = jax.ShapeDtypeStruct((share, width), jnp.float32)
+    own = jax.ShapeDtypeStruct((share, width), jnp.float32)
+    send = jax.ShapeDtypeStruct((share + 8, width), jnp.float32)
     return pl.pallas_call(
         pair_kernel,
-        out_shape=(part,) * chips,
+        out_shape=(own,) + (send,) * (chips - 1),
         compiler_params=pltpu.CompilerParams(vmem_limit_bytes=24 * MIB),
-    )(keep, came)
-
-
-def begin_kernel(own_ref, came_ref, targets_ref, sum_ref, goal_ref):
-    sum_ref[...] = own_ref[...] + came_ref[...]
-    goal_ref[...] = jnp.broadcast_to(targets_ref[...], goal_ref.shape)
-
-
-def begin_rows(own, came, targets, peers):
-    goal = jax.ShapeDtypeStruct((peers, targets.shape[0]), jnp.int32)
-    return pl.pallas_call(
-        begin_kernel,
-        out_shape=(jax.ShapeDtypeStruct(own.shape, own.dtype), goal),
-        compiler_params=pltpu.CompilerParams(vmem_limit_bytes=16 * MIB),
-    )(own, came, targets.reshape(1, -1))
-
-
-def norm_kernel(hidden_ref, gain_ref, early_ref, own_ref, *refs):
-    del early_ref
-    width = own_ref.shape[1]
+    )(keep, came, goal)
+
+
+def norm_kernel(hidden_ref, gain_ref, goal_ref, own_ref, *refs):
+    came, normed_ref, wanted_ref = refs[:-2], refs[-2], refs[-1]
+    share, width = own_ref.shape
+    lines = goal_ref.shape[1]
     mixed = hidden_ref[:, :width].astype(jnp.float32) + own_ref[...]
-    for ref in refs[:-1]:
-        mixed += ref[...]
+    wanted_ref[0:1, :] = goal_ref[...].astype(jnp.int32)
+    for index, ref in enumerate(came):
+        mixed += ref[:share]
+        wanted_ref[index + 1:index + 2, :] = ref[share:share + 1, :lines].astype(jnp.int32)
     scale = lax.rsqrt(jnp.mean(mixed * mixed, axis=1, keepdims=True) + 1e-06)
-    refs[-1][...] = (mixed * scale * gain_ref[...]).astype(jnp.bfloat16)
-
-
-def norm_rows(hidden, gain, early, own, others):
+    normed_ref[...] = (mixed * scale * gain_ref[...]).astype(jnp.bfloat16)
+
+
+def norm_rows(hidden, gain, goal, own, came):
     return pl.pallas_call(
         norm_kernel,
-        out_shape=jax.ShapeDtypeStruct(own.shape, jnp.bfloat16),
+        out_shape=(
+            jax.ShapeDtypeStruct(own.shape, jnp.bfloat16),
+            jax.ShapeDtypeStruct((len(came) + 1, goal.shape[1]), jnp.int32),
+        ),
         compiler_params=pltpu.CompilerParams(vmem_limit_bytes=16 * MIB),
-    )(hidden, gain.reshape(1, -1), early, own, *others)
+    )(hidden, gain.reshape(1, -1), goal, own, *came)
 
 
 def head_kernel(parts, before, spots_ref, wanted_ref, *refs):
@@ -376,18 +388,19 @@
     home = (group - jnp.arange(groups, dtype=jnp.int32)) % groups
     spots = home[None, :] * chips + (chip ^ jnp.arange(chips, dtype=jnp.int32))[:, None]
     spots = spots.reshape(-1)
+    goal = targets.astype(jnp.float32).reshape(1, tokens)
+    goal = jnp.concatenate((goal, goal), axis=1)
+    goal = jnp.concatenate([goal] + [along(goal, k) for k in range(1, groups)], axis=1)
     other_head = partner(vocab_head)
 
     place = jnp.stack((chip, core)).astype(jnp.int32)
-    keep, give = expert_sums(place, plane, w_gate, w_up, w_down, tokens, capacity, width, experts)
-    own, *sends = pair_sums(keep, partner(give))
+    keep, give = expert_sums(
+        place, goal, plane, w_gate, w_up, w_down, tokens, capacity, width, experts
+    )
+    own, *sends = pair_sums(keep, partner(give), goal)
     came = [across(rows, d) for d, rows in zip(offsets, sends)]
-    own, goal = begin_rows(own, came[-1], targets, groups * chips)
-    goal = lax.all_to_all(goal, ("grp", "chip"), split_axis=0, concat_axis=0, tiled=True)
-    match = spots[:, None] == jnp.arange(groups * chips, dtype=jnp.int32)[None, :]
-    goal = jnp.sum(jnp.where(match[:, :, None], goal[None], 0), axis=1)
-    wanted = jnp.concatenate((goal, goal), axis=1).reshape(1, -1)
-    normed = norm_rows(send, norm_gain, wanted, own, came[:-1])
+    normed, wanted = norm_rows(send, norm_gain, goal, own, came)
+    wanted = wanted.reshape(1, -1)
 
     column = [normed] + [along(normed, k) for k in range(1, groups)]
     if chips == 4:

time: 146 us -> 145 us (level)
  Pallas kernels: 48.5 us -> 44.3 us
  starting transfers between devices: 39.1 us -> 40.9 us
    ppermute x6 -> x9, waiting for transfers between devices: 7.23 us -> 16.6 us  [along(): lax.ppermute(value, 'grp', [(g, (g + offset) % groups) for g in range(gro...]
    all_to_all x1 -> x0, waiting for transfers between devices: 7.2 us -> none  [local(): lax.all_to_all(goal, ('grp', 'chip'), split_axis=0, concat_axis=0, tiled=...]
    all_to_all x1 -> x0, starting transfers between devices: 5.95 us -> none  [local(): lax.all_to_all(goal, ('grp', 'chip'), split_axis=0, concat_axis=0, tiled=...]
    ppermute x6 -> x9, starting transfers between devices: 9.94 us -> 15.4 us  [along(): lax.ppermute(value, 'grp', [(g, (g + offset) % groups) for g in range(gro...]
    pallas_call x1, Pallas kernels: 19 us -> 15.4 us  [expert_sums(): pl.pallas_call(functools.partial(expert_kernel, block, slots, width, expe...]
    ppermute x21, starting transfers between devices: 22 us -> 23.8 us  [across(): return lax.ppermute(value, 'chip', [(c, c ^ offset) for c in range(chips)])]
    ppermute x21, waiting for transfers between devices: 23.6 us -> 22.1 us  [across(): return lax.ppermute(value, 'chip', [(c, c ^ offset) for c in range(chips)])]
  transfers between devices with their start and end apart: 35 -> 37, of which waited for: 14 -> 14; matrix products, arithmetic and copies ran while one was open for 4% -> 4% of each run, Pallas kernels for 25% -> 22%
where the time goes in v6:
time: 145 us
  Pallas kernels  44.3 us (31%)
  waiting for transfers between devices  42.4 us (29%)
  starting transfers between devices  40.9 us (28%)
  local copies, waits for them, and re-layouts  8.22 us (6%)
  between operations  4.64 us (3%)
  other arithmetic  4.3 us (3%)
    pallas_call x2, Pallas kernels, head_stats(): pl.pallas_call(functools.partial(head_kernel, parts, len(earlier)), out_s...  26.8 us
    ppermute x21, starting transfers between devices, across(): return lax.ppermute(value, 'chip', [(c, c ^ offset) for c in range(chips)])  23.8 us
    ppermute x21, waiting for transfers between devices, across(): return lax.ppermute(value, 'chip', [(c, c ^ offset) for c in range(chips)])  22.1 us
    ppermute x9, waiting for transfers between devices, along(): lax.ppermute(value, 'grp', [(g, (g + offset) % groups) for g in range(gro...  16.6 us
    ppermute x9, starting transfers between devices, along(): lax.ppermute(value, 'grp', [(g, (g + offset) % groups) for g in range(gro...  15.4 us
    pallas_call x1, Pallas kernels, expert_sums(): pl.pallas_call(functools.partial(expert_kernel, block, slots, width, expe...  15.4 us
    unnamed x58, local copies, waits for them, and re-layouts  4.2 us
    ppermute x7, waiting for transfers between devices, partner(): return lax.ppermute(value, 'core', ((0, 1), (1, 0)))  3.8 us
  transfers between devices with their start and end apart: 37, of which 14 were waited for; matrix products, arithmetic and copies ran while one was open for 4% of the time, Pallas kernels for 22%

profile of v6, /device:TPU:0, one launch (start us, length us, event | category | flops | bytes accessed | tf_op | source)
XLA Modules:
  0.0 144.8 jit_solution(7261744662396230245)
XLA Ops:
  1.1 1.8 %shard_map.149.refs_0_.hidden_ref = bf16[80,1152]{1,0:T(8,128)(2,1)} custom-call(bf16[40,1024]{1,0:T(8,128)(2,1)} %pol_ref.1, bf16[40,1024]{1,0:T(8,128)(2,1)} %ref_ref.1, s32[8,40]{1,0:T(8,128)} %bitcast.99, s32[8,40]{1,0:T(8,128)} %bitcast.100, f32[8,40]{1,0:T(8,128)} %bitcast.101, f32[8,40]{1,0:T(8,128)} %bitcast.102), custom_call_target="tpu_custom_call" | custom-call | tf_op jit(solution)/shard_map/pallas_call | solution.py:47
  2.9 2.5 %collective-permute-start.3 = (bf16[80,1152]{1,0:T(8,128)(2,1)}, bf16[80,1152]{1,0:T(8,128)(2,1)S(1)}, u32[]{:S(2)}, u32[]{:S(2)}) collective-permute-start(bf16[80,1152]{1,0:T(8,128)(2,1)} %shard_map.149.refs_0_.hidden_ref), channel_id=1, source_target_pairs={{0,2},{2,0},{4,6},{6,4},{1,3},{3,1},{5,7},{7,5},{8,10},{10,8},{12,... | collective-permute-start | bytes 552968 | tf_op jit(solution)/shard_map/ppermute | solution.py:356
  5.4 1.5 %collective-permute-start.4 = (bf16[80,1152]{1,0:T(8,128)(2,1)}, bf16[80,1152]{1,0:T(8,128)(2,1)S(1)}, u32[]{:S(2)}, u32[]{:S(2)}) collective-permute-start(bf16[80,1152]{1,0:T(8,128)(2,1)} %shard_map.149.refs_0_.hidden_ref), channel_id=1, source_target_pairs={{0,4},{2,6},{4,0},{6,2},{1,5},{3,7},{5,1},{7,3},{8,12},{10,14},{12... | collective-permute-start | bytes 552968 | tf_op jit(solution)/shard_map/ppermute | solution.py:356
  6.9 0.7 convert_bitcast_fusion
  7.7 2.1 %collective-permute-start = (f32[1,80]{1,0:T(1,128)S(1)}, f32[1,80]{1,0:T(1,128)S(1)}, u32[]{:S(2)}, u32[]{:S(2)}) collective-permute-start(f32[1,80]{1,0:T(1,128)S(1)} %pad_maximum_fusion.1), channel_id=1, source_target_pairs={{0,8},{8,16},{16,24},{24,0},{1,9},{9,17},{17,25},{25,1},{2,10},{10... | collective-permute-start | bytes 968 | tf_op jit(solution)/shard_map/ppermute | solution.py:361
  9.7 3.5 %collective-permute-done = f32[1,80]{1,0:T(1,128)S(1)} collective-permute-done((f32[1,80]{1,0:T(1,128)S(1)}, f32[1,80]{1,0:T(1,128)S(1)}, u32[]{:S(2)}, u32[]{:S(2)}) %collective-permute-start) | collective-permute-done | bytes 352 | tf_op jit(solution)/shard_map/ppermute | solution.py:361
  13.3 1.0 collective-permute-start.1
  14.3 3.4 %collective-permute-done.1 = f32[1,80]{1,0:T(1,128)S(1)} collective-permute-done((f32[1,80]{1,0:T(1,128)S(1)}, f32[1,80]{1,0:T(1,128)S(1)}, u32[]{:S(2)}, u32[]{:S(2)}) %collective-permute-start.1) | collective-permute-done | bytes 352 | tf_op jit(solution)/shard_map/ppermute | solution.py:361
  17.7 2.0 %collective-permute-start.2 = (f32[1,80]{1,0:T(1,128)S(1)}, f32[1,80]{1,0:T(1,128)S(1)}, u32[]{:S(2)}, u32[]{:S(2)}) collective-permute-start(f32[1,80]{1,0:T(1,128)S(1)} %pad_maximum_fusion.1), channel_id=1, source_target_pairs={{0,24},{8,0},{16,8},{24,16},{1,25},{9,1},{17,9},{25,17},{2,26},{10... | collective-permute-start | bytes 968 | tf_op jit(solution)/shard_map/ppermute | solution.py:361
  19.7 1.5 %collective-permute-done.2 = f32[1,80]{1,0:T(1,128)S(1)} collective-permute-done((f32[1,80]{1,0:T(1,128)S(1)}, f32[1,80]{1,0:T(1,128)S(1)}, u32[]{:S(2)}, u32[]{:S(2)}) %collective-permute-start.2) | collective-permute-done | bytes 352 | tf_op jit(solution)/shard_map/ppermute | solution.py:361
  22.3 0.6 pad_add_fusion.1.place_ref
  22.9 0.6 concatenate.13.early_ref.goal_ref
  24.4 0.7 copy-done.13
  25.0 15.4 %shard_map.150 = (f32[4,80,1024]{2,1,0:T(8,128)}, f32[4,80,1024]{2,1,0:T(8,128)}) custom-call(s32[2]{0:T(128)} %pad_add_fusion.1.place_ref, f32[1,320]{1,0:T(1,128)} %concatenate.13.early_ref.goal_ref, bf16[80,1152]{1,0:T(8,128)(2,1)} %shard_map.149.refs_0_.hidden_ref, bf16[80,1152]{1,0:T(8,128)(2,1)} %copy-done.7, bf16[80,1152]{1,0:T(8,128)(2,1)} %copy-done.8, ...), custom_call_target="tpu_custom_call" | custom-call | flops 6442450944 | bytes 22970368 | tf_op jit(solution)/shard_map/pallas_call | solution.py:156
  40.6 3.2 %collective-permute-done.10.came_ref = f32[4,80,1024]{2,1,0:T(8,128)S(1)} collective-permute-done((f32[4,80,1024]{2,1,0:T(8,128)}, f32[4,80,1024]{2,1,0:T(8,128)S(1)}, u32[]{:S(2)}, u32[]{:S(2)}) %collective-permute-start.10) | collective-permute-done | bytes 1310752 | tf_op jit(solution)/shard_map/ppermute | solution.py:365
  43.7 1.3 copy-done
  45.2 1.8 %collective-permute-start.11 = (f32[88,1024]{1,0:T(8,128)S(1)}, f32[88,1024]{1,0:T(8,128)S(1)}, u32[]{:S(2)}, u32[]{:S(2)}) collective-permute-start(f32[88,1024]{1,0:T(8,128)S(1)} %get-tuple-element.13), channel_id=1, source_target_pairs={{0,2},{2,0},{4,6},{6,4},{1,3},{3,1},{5,7},{7,5},{8,10},{10,8},{12,... | collective-permute-start | bytes 1081352 | tf_op jit(solution)/shard_map/ppermute | solution.py:356
  46.9 1.5 %collective-permute-start.12 = (f32[88,1024]{1,0:T(8,128)S(1)}, f32[88,1024]{1,0:T(8,128)S(1)}, u32[]{:S(2)}, u32[]{:S(2)}) collective-permute-start(f32[88,1024]{1,0:T(8,128)S(1)} %get-tuple-element.14), channel_id=1, source_target_pairs={{0,4},{2,6},{4,0},{6,2},{1,5},{3,7},{5,1},{7,3},{8,12},{10,14},{12... | collective-permute-start | bytes 1081352 | tf_op jit(solution)/shard_map/ppermute | solution.py:356
  48.7 7.8 %collective-permute-done.11.refs_0_ = f32[88,1024]{1,0:T(8,128)S(1)} collective-permute-done((f32[88,1024]{1,0:T(8,128)S(1)}, f32[88,1024]{1,0:T(8,128)S(1)}, u32[]{:S(2)}, u32[]{:S(2)}) %collective-permute-start.11) | collective-permute-done | bytes 360480 | tf_op jit(solution)/shard_map/ppermute | solution.py:356
  56.5 8.4 %collective-permute-done.12.refs_1_ = f32[88,1024]{1,0:T(8,128)S(1)} collective-permute-done((f32[88,1024]{1,0:T(8,128)S(1)}, f32[88,1024]{1,0:T(8,128)S(1)}, u32[]{:S(2)}, u32[]{:S(2)}) %collective-permute-start.12) | collective-permute-done | bytes 360480 | tf_op jit(solution)/shard_map/ppermute | solution.py:356
  65.1 4.2 %collective-permute-start.16 = (bf16[80,1024]{1,0:T(8,128)(2,1)S(1)}, bf16[80,1024]{1,0:T(8,128)(2,1)S(1)}, u32[]{:S(2)}, u32[]{:S(2)}) collective-permute-start(bf16[80,1024]{1,0:T(8,128)(2,1)S(1)} %get-tuple-element.17.refs_0_), channel_id=1, source_target_pairs={{0,16},{8,24},{16,0},{24,8},{1,17},{9,25},{17,1},{25,9},{2,18},{10... | collective-permute-start | bytes 491528 | tf_op jit(solution)/shard_map/ppermute | solution.py:361
  69.3 1.3 collective-permute-start.20
  70.6 3.5 %collective-permute-done.14.refs_1_ = bf16[80,1024]{1,0:T(8,128)(2,1)S(1)} collective-permute-done((bf16[80,1024]{1,0:T(8,128)(2,1)S(1)}, bf16[80,1024]{1,0:T(8,128)(2,1)S(1)}, u32[]{:S(2)}, u32[]{:S(2)}) %collective-permute-start.14) | collective-permute-done | bytes 163872 | tf_op jit(solution)/shard_map/ppermute | solution.py:361
  74.1 1.5 %collective-permute-start.28 = (bf16[80,1024]{1,0:T(8,128)(2,1)S(1)}, bf16[80,1024]{1,0:T(8,128)(2,1)S(1)}, u32[]{:S(2)}, u32[]{:S(2)}) collective-permute-start(bf16[80,1024]{1,0:T(8,128)(2,1)S(1)} %get-tuple-element.17.refs_0_), channel_id=1, source_target_pairs={{0,4},{2,6},{4,0},{6,2},{1,5},{3,7},{5,1},{7,3},{8,12},{10,14},{12... | collective-permute-start | bytes 491528 | tf_op jit(solution)/shard_map/ppermute | solution.py:356
  75.6 3.6 %collective-permute-done.16.refs_2_ = bf16[80,1024]{1,0:T(8,128)(2,1)S(1)} collective-permute-done((bf16[80,1024]{1,0:T(8,128)(2,1)S(1)}, bf16[80,1024]{1,0:T(8,128)(2,1)S(1)}, u32[]{:S(2)}, u32[]{:S(2)}) %collective-permute-start.16) | collective-permute-done | bytes 163872 | tf_op jit(solution)/shard_map/ppermute | solution.py:361
  79.3 1.4 collective-permute-start.15
  81.4 1.4 collective-permute-start.26
  83.4 2.6 %collective-permute-done.15.refs_9_.refs_0_ = bf16[80,1024]{1,0:T(8,128)(2,1)S(1)} collective-permute-done((bf16[80,1024]{1,0:T(8,128)(2,1)S(1)}, bf16[80,1024]{1,0:T(8,128)(2,1)S(1)}, u32[]{:S(2)}, u32[]{:S(2)}) %collective-permute-start.15) | collective-permute-done | bytes 163872 | tf_op jit(solution)/shard_map/ppermute | solution.py:356
  86.0 1.8 %collective-permute-start.27 = (bf16[80,1024]{1,0:T(8,128)(2,1)S(1)}, bf16[80,1024]{1,0:T(8,128)(2,1)S(1)}, u32[]{:S(2)}, u32[]{:S(2)}) collective-permute-start(bf16[80,1024]{1,0:T(8,128)(2,1)S(1)} %collective-permute-done.18.refs_3_), channel_id=1, source_target_pairs={{0,2},{2,0},{4,6},{6,4},{1,3},{3,1},{5,7},{7,5},{8,10},{10,8},{12,... | collective-permute-start | bytes 491528 | tf_op jit(solution)/shard_map/ppermute | solution.py:356
  90.7 0.6 collective-permute-done.26.refs_6_
  91.3 0.8 collective-permute-start.21
  92.1 1.3 collective-permute-done.27.refs_7_
  94.1 1.5 %collective-permute-start.24 = (bf16[80,1024]{1,0:T(8,128)(2,1)S(1)}, bf16[80,1024]{1,0:T(8,128)(2,1)S(1)}, u32[]{:S(2)}, u32[]{:S(2)}) collective-permute-start(bf16[80,1024]{1,0:T(8,128)(2,1)S(1)} %collective-permute-done.17.refs_1_), channel_id=1, source_target_pairs={{0,2},{2,0},{4,6},{6,4},{1,3},{3,1},{5,7},{7,5},{8,10},{10,8},{12,... | collective-permute-start | bytes 491528 | tf_op jit(solution)/shard_map/ppermute | solution.py:356
  96.2 14.4 %shard_map.153.refs_7_ = f32[2,768]{1,0:T(2,128)} custom-call(s32[18]{0:T(128)} %pad_add_fusion.spots_ref, s32[1,768]{1,0:T(1,128)} %slice.80.wanted_ref, bf16[80,1024]{1,0:T(8,128)(2,1)} %copy-done.4, bf16[80,1024]{1,0:T(8,128)(2,1)} %copy-done.14, bf16[80,1024]{1,0:T(8,128)(2,1)} %copy-done.15, bf16[80,1024]{1,0:T(8,128)(2,1)} %copy-done.16, ...), custom_call_target="tpu_custom_call" | custom-call | flops 7650410496 | bytes 11534336 | tf_op jit(solution)/shard_map/pallas_call | solution.py:314
  111.4 0.7 copy-done.28
  112.1 12.4 %shard_map.154 = f32[16,2,80]{2,1,0:T(2,128)} custom-call(s32[18]{0:T(128)} %pad_add_fusion.spots_ref, s32[1,512]{1,0:T(1,128)} %slice.79.wanted_ref, bf16[80,1024]{1,0:T(8,128)(2,1)} %copy-done.17, bf16[80,1024]{1,0:T(8,128)(2,1)} %copy-done.21, bf16[80,1024]{1,0:T(8,128)(2,1)} %copy-done.23, bf16[80,1024]{1,0:T(8,128)(2,1)} %copy-done.25, ...), custom_call_target="tpu_custom_call" | custom-call | flops 5100273664 | bytes 11010048 | tf_op jit(solution)/shard_map/pallas_call | solution.py:314
  124.5 0.7 copy.23
  125.3 3.7 %collective-permute-start.30 = (f32[16,2,80]{2,0,1:T(8,128)S(1)}, f32[16,2,80]{2,0,1:T(8,128)S(1)}, u32[]{:S(2)}, u32[]{:S(2)}) collective-permute-start(f32[16,2,80]{2,0,1:T(8,128)S(1)} %copy.23), channel_id=1, source_target_pairs={{0,8},{8,16},{16,24},{24,0},{1,9},{9,17},{17,25},{25,1},{2,10},{10... | collective-permute-start | bytes 30728 | tf_op jit(solution)/shard_map/ppermute | solution.py:361
  129.0 2.4 %collective-permute-start.32 = (f32[16,2,80]{2,0,1:T(8,128)S(1)}, f32[16,2,80]{2,0,1:T(8,128)S(1)}, u32[]{:S(2)}, u32[]{:S(2)}) collective-permute-start(f32[16,2,80]{2,0,1:T(8,128)S(1)} %copy.23), channel_id=1, source_target_pairs={{0,24},{8,0},{16,8},{24,16},{1,25},{9,1},{17,9},{25,17},{2,26},{10... | collective-permute-start | bytes 30728 | tf_op jit(solution)/shard_map/ppermute | solution.py:361
  131.4 0.6 fusion.19
  132.0 0.7 slice.85
  132.7 0.9 collective-permute-done.31
  133.7 0.6 collective-permute-start.33
  134.3 1.5 %collective-permute-start.34 = (f32[16,2,80]{2,0,1:T(8,128)S(1)}, f32[16,2,80]{2,0,1:T(8,128)S(1)}, u32[]{:S(2)}, u32[]{:S(2)}) collective-permute-start(f32[16,2,80]{2,0,1:T(8,128)S(1)} %pad_maximum_fusion), channel_id=1, source_target_pairs={{0,4},{2,6},{4,0},{6,2},{1,5},{3,7},{5,1},{7,3},{8,12},{10,14},{12... | collective-permute-start | bytes 30728 | tf_op jit(solution)/shard_map/ppermute | solution.py:356
  135.8 1.4 collective-permute-start.35
  139.1 1.3 collective-permute-done.35
  141.1 0.6 collective-permute-done.36
  141.8 1.2 add_reduce_fusion
  (115 shorter events, 10.0 us)
Async XLA Ops:
  0.6 95.5 %collective-permute-start.29 = (bf16[2432,1024]{1,0:T(8,128)(2,1)}, bf16[2432,1024]{1,0:T(8,128)(2,1)}, u32[]{:S(2)}, u32[]{:S(2)}) collective-permute-start(bf16[2432,1024]{1,0:T(8,128)(2,1)} %refs_8_.3), channel_id=1, source_target_pairs={{0,1},{1,0},{2,3},{3,2},{4,5},{5,4},{6,7},{7,6},{8,9},{9,8},{10,11... | collective-permute-start | bytes 14942216 | tf_op jit(solution)/shard_map/ppermute | solution.py:365
  2.9 18.3 %collective-permute-start.3 = (bf16[80,1152]{1,0:T(8,128)(2,1)}, bf16[80,1152]{1,0:T(8,128)(2,1)S(1)}, u32[]{:S(2)}, u32[]{:S(2)}) collective-permute-start(bf16[80,1152]{1,0:T(8,128)(2,1)} %shard_map.149.refs_0_.hidden_ref), channel_id=1, source_target_pairs={{0,2},{2,0},{4,6},{6,4},{1,3},{3,1},{5,7},{7,5},{8,10},{10,8},{12,... | collective-permute-start | bytes 552968 | tf_op jit(solution)/shard_map/ppermute | solution.py:356
  5.4 16.4 %collective-permute-start.4 = (bf16[80,1152]{1,0:T(8,128)(2,1)}, bf16[80,1152]{1,0:T(8,128)(2,1)S(1)}, u32[]{:S(2)}, u32[]{:S(2)}) collective-permute-start(bf16[80,1152]{1,0:T(8,128)(2,1)} %shard_map.149.refs_0_.hidden_ref), channel_id=1, source_target_pairs={{0,4},{2,6},{4,0},{6,2},{1,5},{3,7},{5,1},{7,3},{8,12},{10,14},{12... | collective-permute-start | bytes 552968 | tf_op jit(solution)/shard_map/ppermute | solution.py:356
  6.9 14.9 %collective-permute-start.5 = (bf16[80,1152]{1,0:T(8,128)(2,1)}, bf16[80,1152]{1,0:T(8,128)(2,1)S(1)}, u32[]{:S(2)}, u32[]{:S(2)}) collective-permute-start(bf16[80,1152]{1,0:T(8,128)(2,1)} %shard_map.149.refs_0_.hidden_ref), channel_id=1, source_target_pairs={{0,6},{2,4},{4,2},{6,0},{1,7},{3,5},{5,3},{7,1},{8,14},{10,12},{12... | collective-permute-start | bytes 552968 | tf_op jit(solution)/shard_map/ppermute | solution.py:356
  7.7 5.6 %collective-permute-start = (f32[1,80]{1,0:T(1,128)S(1)}, f32[1,80]{1,0:T(1,128)S(1)}, u32[]{:S(2)}, u32[]{:S(2)}) collective-permute-start(f32[1,80]{1,0:T(1,128)S(1)} %pad_maximum_fusion.1), channel_id=1, source_target_pairs={{0,8},{8,16},{16,24},{24,0},{1,9},{9,17},{17,25},{25,1},{2,10},{10... | collective-permute-start | bytes 968 | tf_op jit(solution)/shard_map/ppermute | solution.py:361
  13.3 4.4 %collective-permute-start.1 = (f32[1,80]{1,0:T(1,128)S(1)}, f32[1,80]{1,0:T(1,128)S(1)}, u32[]{:S(2)}, u32[]{:S(2)}) collective-permute-start(f32[1,80]{1,0:T(1,128)S(1)} %pad_maximum_fusion.1), channel_id=1, source_target_pairs={{0,16},{8,24},{16,0},{24,8},{1,17},{9,25},{17,1},{25,9},{2,18},{10... | collective-permute-start | bytes 968 | tf_op jit(solution)/shard_map/ppermute | solution.py:361
  17.7 3.5 %collective-permute-start.2 = (f32[1,80]{1,0:T(1,128)S(1)}, f32[1,80]{1,0:T(1,128)S(1)}, u32[]{:S(2)}, u32[]{:S(2)}) collective-permute-start(f32[1,80]{1,0:T(1,128)S(1)} %pad_maximum_fusion.1), channel_id=1, source_target_pairs={{0,24},{8,0},{16,8},{24,16},{1,25},{9,1},{17,9},{25,17},{2,26},{10... | collective-permute-start | bytes 968 | tf_op jit(solution)/shard_map/ppermute | solution.py:361
  21.3 2.3 %collective-permute-start.6 = (bf16[80,1152]{1,0:T(8,128)(2,1)}, bf16[80,1152]{1,0:T(8,128)(2,1)S(1)}, u32[]{:S(2)}, u32[]{:S(2)}) collective-permute-start(bf16[80,1152]{1,0:T(8,128)(2,1)} %shard_map.149.refs_0_.hidden_ref), channel_id=1, source_target_pairs={{0,1},{1,0},{2,3},{3,2},{4,5},{5,4},{6,7},{7,6},{8,9},{9,8},{10,11... | collective-permute-start | bytes 552968 | tf_op jit(solution)/shard_map/ppermute | solution.py:365
  21.3 2.3 %collective-permute-start.7 = (bf16[80,1152]{1,0:T(8,128)(2,1)S(1)}, bf16[80,1152]{1,0:T(8,128)(2,1)S(1)}, u32[]{:S(2)}, u32[]{:S(2)}) collective-permute-start(bf16[80,1152]{1,0:T(8,128)(2,1)S(1)} %collective-permute-done.3.refs_1_), channel_id=1, source_target_pairs={{0,1},{1,0},{2,3},{3,2},{4,5},{5,4},{6,7},{7,6},{8,9},{9,8},{10,11... | collective-permute-start | bytes 552968 | tf_op jit(solution)/shard_map/ppermute | solution.py:365
  21.8 1.8 %collective-permute-start.8 = (bf16[80,1152]{1,0:T(8,128)(2,1)S(1)}, bf16[80,1152]{1,0:T(8,128)(2,1)S(1)}, u32[]{:S(2)}, u32[]{:S(2)}) collective-permute-start(bf16[80,1152]{1,0:T(8,128)(2,1)S(1)} %collective-permute-done.4.refs_2_), channel_id=1, source_target_pairs={{0,1},{1,0},{2,3},{3,2},{4,5},{5,4},{6,7},{7,6},{8,9},{9,8},{10,11... | collective-permute-start | bytes 552968 | tf_op jit(solution)/shard_map/ppermute | solution.py:365
  21.9 1.7 %collective-permute-start.9 = (bf16[80,1152]{1,0:T(8,128)(2,1)S(1)}, bf16[80,1152]{1,0:T(8,128)(2,1)S(1)}, u32[]{:S(2)}, u32[]{:S(2)}) collective-permute-start(bf16[80,1152]{1,0:T(8,128)(2,1)S(1)} %collective-permute-done.5.refs_3_), channel_id=1, source_target_pairs={{0,1},{1,0},{2,3},{3,2},{4,5},{5,4},{6,7},{7,6},{8,9},{9,8},{10,11... | collective-permute-start | bytes 552968 | tf_op jit(solution)/shard_map/ppermute | solution.py:365
  23.5 20.2 %copy-start.2 = (f32[1,320]{1,0:T(1,128)S(1)}, f32[1,320]{1,0:T(1,128)}, u32[]{:S(2)}) copy-start(f32[1,320]{1,0:T(1,128)} %concatenate.13.early_ref.goal_ref) | copy-start | bytes 3844
  23.5 41.3 %copy-start.1 = (bf16[80,1152]{1,0:T(8,128)(2,1)S(1)}, bf16[80,1152]{1,0:T(8,128)(2,1)}, u32[]{:S(2)}) copy-start(bf16[80,1152]{1,0:T(8,128)(2,1)} %shard_map.149.refs_0_.hidden_ref) | copy-start | bytes 552964
  23.5 41.3 %copy-start.3 = (f32[1024]{0:T(1024)S(1)}, f32[1024]{0:T(1024)}, u32[]{:S(2)}) copy-start(f32[1024]{0:T(1024)} %param.23) | copy-start | bytes 12292
  23.5 65.0 %copy-start.5 = (s32[32]{0:T(128)S(1)}, s32[32]{0:T(128)}, u32[]{:S(2)}) copy-start(s32[32]{0:T(128)} %param.26) | copy-start | bytes 388
  40.4 3.3 %collective-permute-start.10 = (f32[4,80,1024]{2,1,0:T(8,128)}, f32[4,80,1024]{2,1,0:T(8,128)S(1)}, u32[]{:S(2)}, u32[]{:S(2)}) collective-permute-start(f32[4,80,1024]{2,1,0:T(8,128)} %get-tuple-element.11), channel_id=1, source_target_pairs={{0,1},{1,0},{2,3},{3,2},{4,5},{5,4},{6,7},{7,6},{8,9},{9,8},{10,11... | collective-permute-start | bytes 3932168 | tf_op jit(solution)/shard_map/ppermute | solution.py:365
  45.2 11.3 %collective-permute-start.11 = (f32[88,1024]{1,0:T(8,128)S(1)}, f32[88,1024]{1,0:T(8,128)S(1)}, u32[]{:S(2)}, u32[]{:S(2)}) collective-permute-start(f32[88,1024]{1,0:T(8,128)S(1)} %get-tuple-element.13), channel_id=1, source_target_pairs={{0,2},{2,0},{4,6},{6,4},{1,3},{3,1},{5,7},{7,5},{8,10},{10,8},{12,... | collective-permute-start | bytes 1081352 | tf_op jit(solution)/shard_map/ppermute | solution.py:356
  46.9 17.9 %collective-permute-start.12 = (f32[88,1024]{1,0:T(8,128)S(1)}, f32[88,1024]{1,0:T(8,128)S(1)}, u32[]{:S(2)}, u32[]{:S(2)}) collective-permute-start(f32[88,1024]{1,0:T(8,128)S(1)} %get-tuple-element.14), channel_id=1, source_target_pairs={{0,4},{2,6},{4,0},{6,2},{1,5},{3,7},{5,1},{7,3},{8,12},{10,14},{12... | collective-permute-start | bytes 1081352 | tf_op jit(solution)/shard_map/ppermute | solution.py:356
  48.5 16.4 %collective-permute-start.13 = (f32[88,1024]{1,0:T(8,128)S(1)}, f32[88,1024]{1,0:T(8,128)S(1)}, u32[]{:S(2)}, u32[]{:S(2)}) collective-permute-start(f32[88,1024]{1,0:T(8,128)S(1)} %get-tuple-element.15), channel_id=1, source_target_pairs={{0,6},{2,4},{4,2},{6,0},{1,7},{3,5},{5,3},{7,1},{8,14},{10,12},{12... | collective-permute-start | bytes 1081352 | tf_op jit(solution)/shard_map/ppermute | solution.py:356
  65.0 31.1 %copy-start.4 = (bf16[80,1024]{1,0:T(8,128)(2,1)}, bf16[80,1024]{1,0:T(8,128)(2,1)S(1)}, u32[]{:S(2)}) copy-start(bf16[80,1024]{1,0:T(8,128)(2,1)S(1)} %get-tuple-element.17.refs_0_) | copy-start | bytes 491524
  65.0 9.0 %collective-permute-start.14 = (bf16[80,1024]{1,0:T(8,128)(2,1)S(1)}, bf16[80,1024]{1,0:T(8,128)(2,1)S(1)}, u32[]{:S(2)}, u32[]{:S(2)}) collective-permute-start(bf16[80,1024]{1,0:T(8,128)(2,1)S(1)} %get-tuple-element.17.refs_0_), channel_id=1, source_target_pairs={{0,8},{8,16},{16,24},{24,0},{1,9},{9,17},{17,25},{25,1},{2,10},{10... | collective-permute-start | bytes 491528 | tf_op jit(solution)/shard_map/ppermute | solution.py:361
  65.1 14.2 %collective-permute-start.16 = (bf16[80,1024]{1,0:T(8,128)(2,1)S(1)}, bf16[80,1024]{1,0:T(8,128)(2,1)S(1)}, u32[]{:S(2)}, u32[]{:S(2)}) collective-permute-start(bf16[80,1024]{1,0:T(8,128)(2,1)S(1)} %get-tuple-element.17.refs_0_), channel_id=1, source_target_pairs={{0,16},{8,24},{16,0},{24,8},{1,17},{9,25},{17,1},{25,9},{2,18},{10... | collective-permute-start | bytes 491528 | tf_op jit(solution)/shard_map/ppermute | solution.py:361
  69.3 11.4 %collective-permute-start.18 = (bf16[80,1024]{1,0:T(8,128)(2,1)S(1)}, bf16[80,1024]{1,0:T(8,128)(2,1)S(1)}, u32[]{:S(2)}, u32[]{:S(2)}) collective-permute-start(bf16[80,1024]{1,0:T(8,128)(2,1)S(1)} %get-tuple-element.17.refs_0_), channel_id=1, source_target_pairs={{0,24},{8,0},{16,8},{24,16},{1,25},{9,1},{17,9},{25,17},{2,26},{10... | collective-permute-start | bytes 491528 | tf_op jit(solution)/shard_map/ppermute | solution.py:361
  69.3 12.1 %collective-permute-start.20 = (bf16[80,1024]{1,0:T(8,128)(2,1)S(1)}, bf16[80,1024]{1,0:T(8,128)(2,1)S(1)}, u32[]{:S(2)}, u32[]{:S(2)}) collective-permute-start(bf16[80,1024]{1,0:T(8,128)(2,1)S(1)} %get-tuple-element.17.refs_0_), channel_id=1, source_target_pairs={{0,2},{2,0},{4,6},{6,4},{1,3},{3,1},{5,7},{7,5},{8,10},{10,8},{12,... | collective-permute-start | bytes 491528 | tf_op jit(solution)/shard_map/ppermute | solution.py:356
  74.1 22.0 %copy-start.14 = (bf16[80,1024]{1,0:T(8,128)(2,1)}, bf16[80,1024]{1,0:T(8,128)(2,1)S(1)}, u32[]{:S(2)}) copy-start(bf16[80,1024]{1,0:T(8,128)(2,1)S(1)} %collective-permute-done.14.refs_1_) | copy-start | bytes 491524
  74.1 8.7 %collective-permute-start.28 = (bf16[80,1024]{1,0:T(8,128)(2,1)S(1)}, bf16[80,1024]{1,0:T(8,128)(2,1)S(1)}, u32[]{:S(2)}, u32[]{:S(2)}) collective-permute-start(bf16[80,1024]{1,0:T(8,128)(2,1)S(1)} %get-tuple-element.17.refs_0_), channel_id=1, source_target_pairs={{0,4},{2,6},{4,0},{6,2},{1,5},{3,7},{5,1},{7,3},{8,12},{10,14},{12... | collective-permute-start | bytes 491528 | tf_op jit(solution)/shard_map/ppermute | solution.py:356
  79.3 16.9 %copy-start.15 = (bf16[80,1024]{1,0:T(8,128)(2,1)}, bf16[80,1024]{1,0:T(8,128)(2,1)S(1)}, u32[]{:S(2)}) copy-start(bf16[80,1024]{1,0:T(8,128)(2,1)S(1)} %collective-permute-done.16.refs_2_) | copy-start | bytes 491524
  79.3 6.8 %collective-permute-start.15 = (bf16[80,1024]{1,0:T(8,128)(2,1)S(1)}, bf16[80,1024]{1,0:T(8,128)(2,1)S(1)}, u32[]{:S(2)}, u32[]{:S(2)}) collective-permute-start(bf16[80,1024]{1,0:T(8,128)(2,1)S(1)} %collective-permute-done.14.refs_1_), channel_id=1, source_target_pairs={{0,4},{2,6},{4,0},{6,2},{1,5},{3,7},{5,1},{7,3},{8,12},{10,14},{12... | collective-permute-start | bytes 491528 | tf_op jit(solution)/shard_map/ppermute | solution.py:356
  80.7 15.4 %copy-start.16 = (bf16[80,1024]{1,0:T(8,128)(2,1)}, bf16[80,1024]{1,0:T(8,128)(2,1)S(1)}, u32[]{:S(2)}) copy-start(bf16[80,1024]{1,0:T(8,128)(2,1)S(1)} %collective-permute-done.18.refs_3_) | copy-start | bytes 491524
  80.7 7.1 %collective-permute-start.22 = (bf16[80,1024]{1,0:T(8,128)(2,1)S(1)}, bf16[80,1024]{1,0:T(8,128)(2,1)S(1)}, u32[]{:S(2)}, u32[]{:S(2)}) collective-permute-start(bf16[80,1024]{1,0:T(8,128)(2,1)S(1)} %collective-permute-done.14.refs_1_), channel_id=1, source_target_pairs={{0,2},{2,0},{4,6},{6,4},{1,3},{3,1},{5,7},{7,5},{8,10},{10,8},{12,... | collective-permute-start | bytes 491528 | tf_op jit(solution)/shard_map/ppermute | solution.py:356
  81.4 10.0 %collective-permute-start.26 = (bf16[80,1024]{1,0:T(8,128)(2,1)S(1)}, bf16[80,1024]{1,0:T(8,128)(2,1)S(1)}, u32[]{:S(2)}, u32[]{:S(2)}) collective-permute-start(bf16[80,1024]{1,0:T(8,128)(2,1)S(1)} %collective-permute-done.16.refs_2_), channel_id=1, source_target_pairs={{0,2},{2,0},{4,6},{6,4},{1,3},{3,1},{5,7},{7,5},{8,10},{10,8},{12,... | collective-permute-start | bytes 491528 | tf_op jit(solution)/shard_map/ppermute | solution.py:356
  82.8 11.3 %collective-permute-start.17 = (bf16[80,1024]{1,0:T(8,128)(2,1)S(1)}, bf16[80,1024]{1,0:T(8,128)(2,1)S(1)}, u32[]{:S(2)}, u32[]{:S(2)}) collective-permute-start(bf16[80,1024]{1,0:T(8,128)(2,1)S(1)} %collective-permute-done.16.refs_2_), channel_id=1, source_target_pairs={{0,4},{2,6},{4,0},{6,2},{1,5},{3,7},{5,1},{7,3},{8,12},{10,14},{12... | collective-permute-start | bytes 491528 | tf_op jit(solution)/shard_map/ppermute | solution.py:356
  86.0 7.4 %collective-permute-start.27 = (bf16[80,1024]{1,0:T(8,128)(2,1)S(1)}, bf16[80,1024]{1,0:T(8,128)(2,1)S(1)}, u32[]{:S(2)}, u32[]{:S(2)}) collective-permute-start(bf16[80,1024]{1,0:T(8,128)(2,1)S(1)} %collective-permute-done.18.refs_3_), channel_id=1, source_target_pairs={{0,2},{2,0},{4,6},{6,4},{1,3},{3,1},{5,7},{7,5},{8,10},{10,8},{12,... | collective-permute-start | bytes 491528 | tf_op jit(solution)/shard_map/ppermute | solution.py:356
  87.8 7.7 %collective-permute-start.19 = (bf16[80,1024]{1,0:T(8,128)(2,1)S(1)}, bf16[80,1024]{1,0:T(8,128)(2,1)S(1)}, u32[]{:S(2)}, u32[]{:S(2)}) collective-permute-start(bf16[80,1024]{1,0:T(8,128)(2,1)S(1)} %collective-permute-done.18.refs_3_), channel_id=1, source_target_pairs={{0,4},{2,6},{4,0},{6,2},{1,5},{3,7},{5,1},{7,3},{8,12},{10,14},{12... | collective-permute-start | bytes 491528 | tf_op jit(solution)/shard_map/ppermute | solution.py:356
  91.3 19.3 %collective-permute-start.21 = (bf16[80,1024]{1,0:T(8,128)(2,1)S(1)}, bf16[80,1024]{1,0:T(8,128)(2,1)S(1)}, u32[]{:S(2)}, u32[]{:S(2)}) collective-permute-start(bf16[80,1024]{1,0:T(8,128)(2,1)S(1)} %collective-permute-done.20.refs_4_), channel_id=1, source_target_pairs={{0,4},{2,6},{4,0},{6,2},{1,5},{3,7},{5,1},{7,3},{8,12},{10,14},{12... | collective-permute-start | bytes 491528 | tf_op jit(solution)/shard_map/ppermute | solution.py:356
  93.5 17.2 %collective-permute-start.23 = (bf16[80,1024]{1,0:T(8,128)(2,1)S(1)}, bf16[80,1024]{1,0:T(8,128)(2,1)S(1)}, u32[]{:S(2)}, u32[]{:S(2)}) collective-permute-start(bf16[80,1024]{1,0:T(8,128)(2,1)S(1)} %collective-permute-done.22.refs_5_), channel_id=1, source_target_pairs={{0,4},{2,6},{4,0},{6,2},{1,5},{3,7},{5,1},{7,3},{8,12},{10,14},{12... | collective-permute-start | bytes 491528 | tf_op jit(solution)/shard_map/ppermute | solution.py:356
  94.1 16.5 %copy-start.21 = (bf16[80,1024]{1,0:T(8,128)(2,1)}, bf16[80,1024]{1,0:T(8,128)(2,1)S(1)}, u32[]{:S(2)}) copy-start(bf16[80,1024]{1,0:T(8,128)(2,1)S(1)} %collective-permute-done.17.refs_1_) | copy-start | bytes 491524
  94.1 16.6 %collective-permute-start.24 = (bf16[80,1024]{1,0:T(8,128)(2,1)S(1)}, bf16[80,1024]{1,0:T(8,128)(2,1)S(1)}, u32[]{:S(2)}, u32[]{:S(2)}) collective-permute-start(bf16[80,1024]{1,0:T(8,128)(2,1)S(1)} %collective-permute-done.17.refs_1_), channel_id=1, source_target_pairs={{0,2},{2,0},{4,6},{6,4},{1,3},{3,1},{5,7},{7,5},{8,10},{10,8},{12,... | collective-permute-start | bytes 491528 | tf_op jit(solution)/shard_map/ppermute | solution.py:356
  95.5 15.1 %copy-start.23 = (bf16[80,1024]{1,0:T(8,128)(2,1)}, bf16[80,1024]{1,0:T(8,128)(2,1)S(1)}, u32[]{:S(2)}) copy-start(bf16[80,1024]{1,0:T(8,128)(2,1)S(1)} %collective-permute-done.19.refs_2_) | copy-start | bytes 491524
  95.5 15.1 %collective-permute-start.25 = (bf16[80,1024]{1,0:T(8,128)(2,1)S(1)}, bf16[80,1024]{1,0:T(8,128)(2,1)S(1)}, u32[]{:S(2)}, u32[]{:S(2)}) collective-permute-start(bf16[80,1024]{1,0:T(8,128)(2,1)S(1)} %collective-permute-done.19.refs_2_), channel_id=1, source_target_pairs={{0,2},{2,0},{4,6},{6,4},{1,3},{3,1},{5,7},{7,5},{8,10},{10,8},{12,... | collective-permute-start | bytes 491528 | tf_op jit(solution)/shard_map/ppermute | solution.py:356
  110.6 20.8 %copy-start.6 = (s32[32]{0:T(128)S(1)}, s32[32]{0:T(128)}, u32[]{:S(2)}) copy-start(s32[32]{0:T(128)} %param.27) | copy-start | bytes 388
  125.3 7.5 %collective-permute-start.30 = (f32[16,2,80]{2,0,1:T(8,128)S(1)}, f32[16,2,80]{2,0,1:T(8,128)S(1)}, u32[]{:S(2)}, u32[]{:S(2)}) collective-permute-start(f32[16,2,80]{2,0,1:T(8,128)S(1)} %copy.23), channel_id=1, source_target_pairs={{0,8},{8,16},{16,24},{24,0},{1,9},{9,17},{17,25},{25,1},{2,10},{10... | collective-permute-start | bytes 30728 | tf_op jit(solution)/shard_map/ppermute | solution.py:361
  129.0 4.6 %collective-permute-start.31 = (f32[16,2,80]{2,0,1:T(8,128)S(1)}, f32[16,2,80]{2,0,1:T(8,128)S(1)}, u32[]{:S(2)}, u32[]{:S(2)}) collective-permute-start(f32[16,2,80]{2,0,1:T(8,128)S(1)} %copy.23), channel_id=1, source_target_pairs={{0,16},{8,24},{16,0},{24,8},{1,17},{9,25},{17,1},{25,9},{2,18},{10... | collective-permute-start | bytes 30728 | tf_op jit(solution)/shard_map/ppermute | solution.py:361
  129.0 4.6 %collective-permute-start.32 = (f32[16,2,80]{2,0,1:T(8,128)S(1)}, f32[16,2,80]{2,0,1:T(8,128)S(1)}, u32[]{:S(2)}, u32[]{:S(2)}) collective-permute-start(f32[16,2,80]{2,0,1:T(8,128)S(1)} %copy.23), channel_id=1, source_target_pairs={{0,24},{8,0},{16,8},{24,16},{1,25},{9,1},{17,9},{25,17},{2,26},{10... | collective-permute-start | bytes 30728 | tf_op jit(solution)/shard_map/ppermute | solution.py:361
  133.7 5.4 %collective-permute-start.33 = (f32[16,2,80]{2,0,1:T(8,128)S(1)}, f32[16,2,80]{2,0,1:T(8,128)S(1)}, u32[]{:S(2)}, u32[]{:S(2)}) collective-permute-start(f32[16,2,80]{2,0,1:T(8,128)S(1)} %pad_maximum_fusion), channel_id=1, source_target_pairs={{0,2},{2,0},{4,6},{6,4},{1,3},{3,1},{5,7},{7,5},{8,10},{10,8},{12,... | collective-permute-start | bytes 30728 | tf_op jit(solution)/shard_map/ppermute | solution.py:356
  134.3 4.8 %collective-permute-start.34 = (f32[16,2,80]{2,0,1:T(8,128)S(1)}, f32[16,2,80]{2,0,1:T(8,128)S(1)}, u32[]{:S(2)}, u32[]{:S(2)}) collective-permute-start(f32[16,2,80]{2,0,1:T(8,128)S(1)} %pad_maximum_fusion), channel_id=1, source_target_pairs={{0,4},{2,6},{4,0},{6,2},{1,5},{3,7},{5,1},{7,3},{8,12},{10,14},{12... | collective-permute-start | bytes 30728 | tf_op jit(solution)/shard_map/ppermute | solution.py:356
  135.8 4.6 %collective-permute-start.35 = (f32[16,2,80]{2,0,1:T(8,128)S(1)}, f32[16,2,80]{2,0,1:T(8,128)S(1)}, u32[]{:S(2)}, u32[]{:S(2)}) collective-permute-start(f32[16,2,80]{2,0,1:T(8,128)S(1)} %pad_maximum_fusion), channel_id=1, source_target_pairs={{0,6},{2,4},{4,2},{6,0},{1,7},{3,5},{5,3},{7,1},{8,14},{10,12},{12... | collective-permute-start | bytes 30728 | tf_op jit(solution)/shard_map/ppermute | solution.py:356
  140.6 1.2 collective-permute-start.36
  (18 other events, 67.2 us)

commit v7 on v6

--- a/solution.py
+++ b/solution.py
@@ -184,7 +184,7 @@
             ],
         ),
         compiler_params=pltpu.CompilerParams(
-            vmem_limit_bytes=(55 if rows <= 640 else 58) * MIB
+            vmem_limit_bytes=60 * MIB
         ),
         cost_estimate=pl.CostEstimate(
             flops=2 * every * width * (3 * hidden + 3 * rows),
@@ -336,7 +336,7 @@
                 pltpu.VMEM((tile, rows), jnp.float32),
             ],
         ),
-        compiler_params=pltpu.CompilerParams(vmem_limit_bytes=58 * MIB),
+        compiler_params=pltpu.CompilerParams(vmem_limit_bytes=60 * MIB),
         cost_estimate=pl.CostEstimate(
             flops=4 * rows * width * head_a.shape[0],
             bytes_accessed=head_a.size * 4 + rows * width * 2,
@@ -390,7 +390,10 @@
     spots = spots.reshape(-1)
     goal = targets.astype(jnp.float32).reshape(1, tokens)
     goal = jnp.concatenate((goal, goal), axis=1)
-    goal = jnp.concatenate([goal] + [along(goal, k) for k in range(1, groups)], axis=1)
+    goal = jnp.broadcast_to(goal, (groups, share))
+    goal = lax.all_to_all(goal, "grp", split_axis=0, concat_axis=0, tiled=True)
+    match = home[:, None] == jnp.arange(groups, dtype=jnp.int32)[None, :]
+    goal = jnp.sum(jnp.where(match[:, :, None], goal[None], 0.0), axis=1).reshape(1, -1)
     other_head = partner(vocab_head)
 
     place = jnp.stack((chip, core)).astype(jnp.int32)

time: 145 us -> 142 us (0.979)
  waiting for transfers between devices: 42.4 us -> 37.9 us
    ppermute x9 -> x6, waiting for transfers between devices: 16.6 us -> 9.05 us  [along(): lax.ppermute(value, 'grp', [(g, (g + offset) % groups) for g in range(gro...]
    ppermute x9 -> x6, starting transfers between devices: 15.4 us -> 9 us  [along(): lax.ppermute(value, 'grp', [(g, (g + offset) % groups) for g in range(gro...]
    all_to_all x0 -> x1, starting transfers between devices: none -> 5.34 us  [local(): goal = lax.all_to_all(goal, 'grp', split_axis=0, concat_axis=0, tiled=True)]
    all_to_all x0 -> x1, waiting for transfers between devices: none -> 1.76 us  [local(): goal = lax.all_to_all(goal, 'grp', split_axis=0, concat_axis=0, tiled=True)]
    ppermute x21, starting transfers between devices: 23.8 us -> 25.3 us  [across(): return lax.ppermute(value, 'chip', [(c, c ^ offset) for c in range(chips)])]
  transfers between devices with their start and end apart: 37 -> 35, of which waited for: 14 -> 13; matrix products, arithmetic and copies ran while one was open for 4% -> 5% of each run, Pallas kernels for 22% -> 23%
where the time goes in v7:
time: 142 us; the launch traced here: 141 us
  Pallas kernels  44.3 us (31%)
  starting transfers between devices  41 us (29%)
  waiting for transfers between devices  37.9 us (27%)
  local copies, waits for them, and re-layouts  8.81 us (6%)
  between operations  4.7 us (3%)
  other arithmetic  4.53 us (3%)
    pallas_call x2, Pallas kernels, head_stats(): pl.pallas_call(functools.partial(head_kernel, parts, len(earlier)), out_s...  26.8 us
    ppermute x21, starting transfers between devices, across(): return lax.ppermute(value, 'chip', [(c, c ^ offset) for c in range(chips)])  25.3 us
    ppermute x21, waiting for transfers between devices, across(): return lax.ppermute(value, 'chip', [(c, c ^ offset) for c in range(chips)])  23.2 us
    pallas_call x1, Pallas kernels, expert_sums(): pl.pallas_call(functools.partial(expert_kernel, block, slots, width, expe...  15.4 us
    ppermute x6, waiting for transfers between devices, along(): lax.ppermute(value, 'grp', [(g, (g + offset) % groups) for g in range(gro...  9.05 us
    ppermute x6, starting transfers between devices, along(): lax.ppermute(value, 'grp', [(g, (g + offset) % groups) for g in range(gro...  9 us
    all_to_all x1, starting transfers between devices, local(): goal = lax.all_to_all(goal, 'grp', split_axis=0, concat_axis=0, tiled=True)  5.34 us
    unnamed x58, local copies, waits for them, and re-layouts  4.2 us
  transfers between devices with their start and end apart: 35, of which 13 were waited for; matrix products, arithmetic and copies ran while one was open for 5% of the time, Pallas kernels for 23%

profile of v7, /device:TPU:0, one launch (start us, length us, event | category | flops | bytes accessed | tf_op | source)
XLA Modules:
  0.0 141.2 jit_solution(4753292098846565923)
XLA Ops:
  1.1 1.8 %shard_map.149.refs_0_.hidden_ref = bf16[80,1152]{1,0:T(8,128)(2,1)} custom-call(bf16[40,1024]{1,0:T(8,128)(2,1)} %pol_ref.1, bf16[40,1024]{1,0:T(8,128)(2,1)} %ref_ref.1, s32[8,40]{1,0:T(8,128)} %bitcast.103, s32[8,40]{1,0:T(8,128)} %bitcast.104, f32[8,40]{1,0:T(8,128)} %bitcast.105, f32[8,40]{1,0:T(8,128)} %bitcast.106), custom_call_target="tpu_custom_call" | custom-call | tf_op jit(solution)/shard_map/pallas_call | solution.py:47
  2.9 2.5 %collective-permute-start = (bf16[80,1152]{1,0:T(8,128)(2,1)}, bf16[80,1152]{1,0:T(8,128)(2,1)S(1)}, u32[]{:S(2)}, u32[]{:S(2)}) collective-permute-start(bf16[80,1152]{1,0:T(8,128)(2,1)} %shard_map.149.refs_0_.hidden_ref), channel_id=1, source_target_pairs={{0,2},{2,0},{4,6},{6,4},{1,3},{3,1},{5,7},{7,5},{8,10},{10,8},{12,... | collective-permute-start | bytes 552968 | tf_op jit(solution)/shard_map/ppermute | solution.py:356
  5.4 1.5 %collective-permute-start.1 = (bf16[80,1152]{1,0:T(8,128)(2,1)}, bf16[80,1152]{1,0:T(8,128)(2,1)S(1)}, u32[]{:S(2)}, u32[]{:S(2)}) collective-permute-start(bf16[80,1152]{1,0:T(8,128)(2,1)} %shard_map.149.refs_0_.hidden_ref), channel_id=1, source_target_pairs={{0,4},{2,6},{4,0},{6,2},{1,5},{3,7},{5,1},{7,3},{8,12},{10,14},{12... | collective-permute-start | bytes 552968 | tf_op jit(solution)/shard_map/ppermute | solution.py:356
  6.9 0.7 convert_bitcast_fusion
  8.3 5.3 %all-to-all-start = ((f32[4,1,80]{2,1,0:T(1,128)}), f32[4,1,80]{2,1,0:T(1,128)S(1)}, u32[]{:S(2)}, u32[]{:S(2)}) async-start(f32[4,1,80]{2,1,0:T(1,128)} %broadcast_in_dim.46), calls=%async_computation | async-start | bytes 4096 | tf_op jit(solution)/shard_map/all_to_all | solution.py:394
  14.0 2.4 %collective-permute-done.1.refs_2_ = bf16[80,1152]{1,0:T(8,128)(2,1)S(1)} collective-permute-done((bf16[80,1152]{1,0:T(8,128)(2,1)}, bf16[80,1152]{1,0:T(8,128)(2,1)S(1)}, u32[]{:S(2)}, u32[]{:S(2)}) %collective-permute-start.1) | collective-permute-done | bytes 184352 | tf_op jit(solution)/shard_map/ppermute | solution.py:356
  17.4 1.8 %all-to-all-done = f32[4,1,80]{2,1,0:T(1,128)S(1)} async-done(((f32[4,1,80]{2,1,0:T(1,128)}), f32[4,1,80]{2,1,0:T(1,128)S(1)}, u32[]{:S(2)}, u32[]{:S(2)}) %all-to-all-start) | async-done | bytes 1312 | tf_op jit(solution)/shard_map/all_to_all | solution.py:394
  19.3 0.6 reshape.135.early_ref.goal_ref
  20.7 0.7 copy-done.13
  21.4 15.4 %shard_map.150 = (f32[4,80,1024]{2,1,0:T(8,128)}, f32[4,80,1024]{2,1,0:T(8,128)}) custom-call(s32[2]{0:T(128)} %pad_add_fusion.1.place_ref, f32[1,320]{1,0:T(1,128)} %reshape.135.early_ref.goal_ref, bf16[80,1152]{1,0:T(8,128)(2,1)} %shard_map.149.refs_0_.hidden_ref, bf16[80,1152]{1,0:T(8,128)(2,1)} %copy-done.7, bf16[80,1152]{1,0:T(8,128)(2,1)} %copy-done.8, ...), custom_call_target="tpu_custom_call" | custom-call | flops 6442450944 | bytes 22970368 | tf_op jit(solution)/shard_map/pallas_call | solution.py:156
  36.8 3.2 %collective-permute-done.7.came_ref = f32[4,80,1024]{2,1,0:T(8,128)S(1)} collective-permute-done((f32[4,80,1024]{2,1,0:T(8,128)}, f32[4,80,1024]{2,1,0:T(8,128)S(1)}, u32[]{:S(2)}, u32[]{:S(2)}) %collective-permute-start.7) | collective-permute-done | bytes 1310752 | tf_op jit(solution)/shard_map/ppermute | solution.py:365
  40.1 1.3 copy-done
  41.5 2.5 %collective-permute-start.10 = (f32[88,1024]{1,0:T(8,128)S(1)}, f32[88,1024]{1,0:T(8,128)S(1)}, u32[]{:S(2)}, u32[]{:S(2)}) collective-permute-start(f32[88,1024]{1,0:T(8,128)S(1)} %get-tuple-element.15), channel_id=1, source_target_pairs={{0,6},{2,4},{4,2},{6,0},{1,7},{3,5},{5,3},{7,1},{8,14},{10,12},{12... | collective-permute-start | bytes 1081352 | tf_op jit(solution)/shard_map/ppermute | solution.py:356
  45.1 8.7 %collective-permute-done.10.refs_2_ = f32[88,1024]{1,0:T(8,128)S(1)} collective-permute-done((f32[88,1024]{1,0:T(8,128)S(1)}, f32[88,1024]{1,0:T(8,128)S(1)}, u32[]{:S(2)}, u32[]{:S(2)}) %collective-permute-start.10) | collective-permute-done | bytes 360480 | tf_op jit(solution)/shard_map/ppermute | solution.py:356
  53.8 7.0 %collective-permute-done.8.refs_0_ = f32[88,1024]{1,0:T(8,128)S(1)} collective-permute-done((f32[88,1024]{1,0:T(8,128)S(1)}, f32[88,1024]{1,0:T(8,128)S(1)}, u32[]{:S(2)}, u32[]{:S(2)}) %collective-permute-start.8) | collective-permute-done | bytes 360480 | tf_op jit(solution)/shard_map/ppermute | solution.py:356
  61.0 0.6 collective-permute-start.11
  61.6 1.8 %collective-permute-start.13 = (bf16[80,1024]{1,0:T(8,128)(2,1)S(1)}, bf16[80,1024]{1,0:T(8,128)(2,1)S(1)}, u32[]{:S(2)}, u32[]{:S(2)}) collective-permute-start(bf16[80,1024]{1,0:T(8,128)(2,1)S(1)} %get-tuple-element.17.refs_0_), channel_id=1, source_target_pairs={{0,16},{8,24},{16,0},{24,8},{1,17},{9,25},{17,1},{25,9},{2,18},{10... | collective-permute-start | bytes 491528 | tf_op jit(solution)/shard_map/ppermute | solution.py:361
  63.4 1.4 %collective-permute-start.15 = (bf16[80,1024]{1,0:T(8,128)(2,1)S(1)}, bf16[80,1024]{1,0:T(8,128)(2,1)S(1)}, u32[]{:S(2)}, u32[]{:S(2)}) collective-permute-start(bf16[80,1024]{1,0:T(8,128)(2,1)S(1)} %get-tuple-element.17.refs_0_), channel_id=1, source_target_pairs={{0,24},{8,0},{16,8},{24,16},{1,25},{9,1},{17,9},{25,17},{2,26},{10... | collective-permute-start | bytes 491528 | tf_op jit(solution)/shard_map/ppermute | solution.py:361
  64.9 1.5 %collective-permute-start.17 = (bf16[80,1024]{1,0:T(8,128)(2,1)S(1)}, bf16[80,1024]{1,0:T(8,128)(2,1)S(1)}, u32[]{:S(2)}, u32[]{:S(2)}) collective-permute-start(bf16[80,1024]{1,0:T(8,128)(2,1)S(1)} %get-tuple-element.17.refs_0_), channel_id=1, source_target_pairs={{0,2},{2,0},{4,6},{6,4},{1,3},{3,1},{5,7},{7,5},{8,10},{10,8},{12,... | collective-permute-start | bytes 491528 | tf_op jit(solution)/shard_map/ppermute | solution.py:356
  66.4 3.6 %collective-permute-done.11.refs_1_ = bf16[80,1024]{1,0:T(8,128)(2,1)S(1)} collective-permute-done((bf16[80,1024]{1,0:T(8,128)(2,1)S(1)}, bf16[80,1024]{1,0:T(8,128)(2,1)S(1)}, u32[]{:S(2)}, u32[]{:S(2)}) %collective-permute-start.11) | collective-permute-done | bytes 163872 | tf_op jit(solution)/shard_map/ppermute | solution.py:361
  70.0 1.4 %collective-permute-start.25 = (bf16[80,1024]{1,0:T(8,128)(2,1)S(1)}, bf16[80,1024]{1,0:T(8,128)(2,1)S(1)}, u32[]{:S(2)}, u32[]{:S(2)}) collective-permute-start(bf16[80,1024]{1,0:T(8,128)(2,1)S(1)} %get-tuple-element.17.refs_0_), channel_id=1, source_target_pairs={{0,4},{2,6},{4,0},{6,2},{1,5},{3,7},{5,1},{7,3},{8,12},{10,14},{12... | collective-permute-start | bytes 491528 | tf_op jit(solution)/shard_map/ppermute | solution.py:356
  71.4 4.6 %collective-permute-done.13.refs_2_ = bf16[80,1024]{1,0:T(8,128)(2,1)S(1)} collective-permute-done((bf16[80,1024]{1,0:T(8,128)(2,1)S(1)}, bf16[80,1024]{1,0:T(8,128)(2,1)S(1)}, u32[]{:S(2)}, u32[]{:S(2)}) %collective-permute-start.13) | collective-permute-done | bytes 163872 | tf_op jit(solution)/shard_map/ppermute | solution.py:361
  76.0 1.5 %collective-permute-start.12 = (bf16[80,1024]{1,0:T(8,128)(2,1)S(1)}, bf16[80,1024]{1,0:T(8,128)(2,1)S(1)}, u32[]{:S(2)}, u32[]{:S(2)}) collective-permute-start(bf16[80,1024]{1,0:T(8,128)(2,1)S(1)} %collective-permute-done.11.refs_1_), channel_id=1, source_target_pairs={{0,4},{2,6},{4,0},{6,2},{1,5},{3,7},{5,1},{7,3},{8,12},{10,14},{12... | collective-permute-start | bytes 491528 | tf_op jit(solution)/shard_map/ppermute | solution.py:356
  77.6 1.5 %collective-permute-start.19 = (bf16[80,1024]{1,0:T(8,128)(2,1)S(1)}, bf16[80,1024]{1,0:T(8,128)(2,1)S(1)}, u32[]{:S(2)}, u32[]{:S(2)}) collective-permute-start(bf16[80,1024]{1,0:T(8,128)(2,1)S(1)} %collective-permute-done.11.refs_1_), channel_id=1, source_target_pairs={{0,2},{2,0},{4,6},{6,4},{1,3},{3,1},{5,7},{7,5},{8,10},{10,8},{12,... | collective-permute-start | bytes 491528 | tf_op jit(solution)/shard_map/ppermute | solution.py:356
  80.2 2.5 %collective-permute-done.12.refs_9_.refs_0_ = bf16[80,1024]{1,0:T(8,128)(2,1)S(1)} collective-permute-done((bf16[80,1024]{1,0:T(8,128)(2,1)S(1)}, bf16[80,1024]{1,0:T(8,128)(2,1)S(1)}, u32[]{:S(2)}, u32[]{:S(2)}) %collective-permute-start.12) | collective-permute-done | bytes 163872 | tf_op jit(solution)/shard_map/ppermute | solution.py:356
  82.7 1.5 %collective-permute-start.24 = (bf16[80,1024]{1,0:T(8,128)(2,1)S(1)}, bf16[80,1024]{1,0:T(8,128)(2,1)S(1)}, u32[]{:S(2)}, u32[]{:S(2)}) collective-permute-start(bf16[80,1024]{1,0:T(8,128)(2,1)S(1)} %collective-permute-done.15.refs_3_), channel_id=1, source_target_pairs={{0,2},{2,0},{4,6},{6,4},{1,3},{3,1},{5,7},{7,5},{8,10},{10,8},{12,... | collective-permute-start | bytes 491528 | tf_op jit(solution)/shard_map/ppermute | solution.py:356
  84.7 1.4 collective-permute-start.16
  88.3 0.7 collective-permute-start.18
  89.1 1.3 collective-permute-start.20
  90.4 1.0 collective-permute-start.21
  91.4 1.3 collective-permute-start.22
  92.8 14.4 %shard_map.153.refs_7_ = f32[2,768]{1,0:T(2,128)} custom-call(s32[18]{0:T(128)} %pad_add_fusion.spots_ref, s32[1,768]{1,0:T(1,128)} %slice.80.wanted_ref, bf16[80,1024]{1,0:T(8,128)(2,1)} %copy-done.4, bf16[80,1024]{1,0:T(8,128)(2,1)} %copy-done.14, bf16[80,1024]{1,0:T(8,128)(2,1)} %copy-done.15, bf16[80,1024]{1,0:T(8,128)(2,1)} %copy-done.16, ...), custom_call_target="tpu_custom_call" | custom-call | flops 7650410496 | bytes 11534336 | tf_op jit(solution)/shard_map/pallas_call | solution.py:314
  107.3 0.6 copy-done.25
  108.0 0.7 copy-done.28
  108.7 12.4 %shard_map.154 = f32[16,2,80]{2,1,0:T(2,128)} custom-call(s32[18]{0:T(128)} %pad_add_fusion.spots_ref, s32[1,512]{1,0:T(1,128)} %slice.79.wanted_ref, bf16[80,1024]{1,0:T(8,128)(2,1)} %copy-done.17, bf16[80,1024]{1,0:T(8,128)(2,1)} %copy-done.21, bf16[80,1024]{1,0:T(8,128)(2,1)} %copy-done.23, bf16[80,1024]{1,0:T(8,128)(2,1)} %copy-done.25, ...), custom_call_target="tpu_custom_call" | custom-call | flops 5100273664 | bytes 11010048 | tf_op jit(solution)/shard_map/pallas_call | solution.py:314
  121.1 0.7 copy.37
  121.8 2.8 %collective-permute-start.27 = (f32[16,2,80]{2,0,1:T(8,128)S(1)}, f32[16,2,80]{2,0,1:T(8,128)S(1)}, u32[]{:S(2)}, u32[]{:S(2)}) collective-permute-start(f32[16,2,80]{2,0,1:T(8,128)S(1)} %copy.37), channel_id=1, source_target_pairs={{0,8},{8,16},{16,24},{24,0},{1,9},{9,17},{17,25},{25,1},{2,10},{10... | collective-permute-start | bytes 30728 | tf_op jit(solution)/shard_map/ppermute | solution.py:361
  124.6 0.7 collective-permute-start.28
  125.3 1.6 %collective-permute-start.29 = (f32[16,2,80]{2,0,1:T(8,128)S(1)}, f32[16,2,80]{2,0,1:T(8,128)S(1)}, u32[]{:S(2)}, u32[]{:S(2)}) collective-permute-start(f32[16,2,80]{2,0,1:T(8,128)S(1)} %copy.37), channel_id=1, source_target_pairs={{0,24},{8,0},{16,8},{24,16},{1,25},{9,1},{17,9},{25,17},{2,26},{10... | collective-permute-start | bytes 30728 | tf_op jit(solution)/shard_map/ppermute | solution.py:361
  126.9 0.7 fusion.19
  127.6 0.7 slice.85
  128.4 0.9 collective-permute-done.28
  129.3 1.6 %collective-permute-start.30 = (f32[16,2,80]{2,0,1:T(8,128)S(1)}, f32[16,2,80]{2,0,1:T(8,128)S(1)}, u32[]{:S(2)}, u32[]{:S(2)}) collective-permute-start(f32[16,2,80]{2,0,1:T(8,128)S(1)} %pad_maximum_fusion), channel_id=1, source_target_pairs={{0,2},{2,0},{4,6},{6,4},{1,3},{3,1},{5,7},{7,5},{8,10},{10,8},{12,... | collective-permute-start | bytes 30728 | tf_op jit(solution)/shard_map/ppermute | solution.py:356
  130.8 1.3 collective-permute-start.31
  132.2 0.7 collective-permute-start.32
  134.8 2.0 %collective-permute-done.32 = f32[16,2,80]{2,0,1:T(8,128)S(1)} collective-permute-done((f32[16,2,80]{2,0,1:T(8,128)S(1)}, f32[16,2,80]{2,0,1:T(8,128)S(1)}, u32[]{:S(2)}, u32[]{:S(2)}) %collective-permute-start.32) | collective-permute-done | bytes 10272 | tf_op jit(solution)/shard_map/ppermute | solution.py:356
  137.5 0.6 collective-permute-done.33
  138.1 1.3 add_reduce_fusion
  (115 shorter events, 9.7 us)
Async XLA Ops:
  0.6 92.1 %collective-permute-start.26 = (bf16[2432,1024]{1,0:T(8,128)(2,1)}, bf16[2432,1024]{1,0:T(8,128)(2,1)}, u32[]{:S(2)}, u32[]{:S(2)}) collective-permute-start(bf16[2432,1024]{1,0:T(8,128)(2,1)} %refs_8_.3), channel_id=1, source_target_pairs={{0,1},{1,0},{2,3},{3,2},{4,5},{5,4},{6,7},{7,6},{8,9},{9,8},{10,11... | collective-permute-start | bytes 14942216 | tf_op jit(solution)/shard_map/ppermute | solution.py:365
  2.9 10.8 %collective-permute-start = (bf16[80,1152]{1,0:T(8,128)(2,1)}, bf16[80,1152]{1,0:T(8,128)(2,1)S(1)}, u32[]{:S(2)}, u32[]{:S(2)}) collective-permute-start(bf16[80,1152]{1,0:T(8,128)(2,1)} %shard_map.149.refs_0_.hidden_ref), channel_id=1, source_target_pairs={{0,2},{2,0},{4,6},{6,4},{1,3},{3,1},{5,7},{7,5},{8,10},{10,8},{12,... | collective-permute-start | bytes 552968 | tf_op jit(solution)/shard_map/ppermute | solution.py:356
  5.4 10.9 %collective-permute-start.1 = (bf16[80,1152]{1,0:T(8,128)(2,1)}, bf16[80,1152]{1,0:T(8,128)(2,1)S(1)}, u32[]{:S(2)}, u32[]{:S(2)}) collective-permute-start(bf16[80,1152]{1,0:T(8,128)(2,1)} %shard_map.149.refs_0_.hidden_ref), channel_id=1, source_target_pairs={{0,4},{2,6},{4,0},{6,2},{1,5},{3,7},{5,1},{7,3},{8,12},{10,14},{12... | collective-permute-start | bytes 552968 | tf_op jit(solution)/shard_map/ppermute | solution.py:356
  6.9 9.4 %collective-permute-start.2 = (bf16[80,1152]{1,0:T(8,128)(2,1)}, bf16[80,1152]{1,0:T(8,128)(2,1)S(1)}, u32[]{:S(2)}, u32[]{:S(2)}) collective-permute-start(bf16[80,1152]{1,0:T(8,128)(2,1)} %shard_map.149.refs_0_.hidden_ref), channel_id=1, source_target_pairs={{0,6},{2,4},{4,2},{6,0},{1,7},{3,5},{5,3},{7,1},{8,14},{10,12},{12... | collective-permute-start | bytes 552968 | tf_op jit(solution)/shard_map/ppermute | solution.py:356
  6.9 13.0 %collective-permute-start.3 = (bf16[80,1152]{1,0:T(8,128)(2,1)}, bf16[80,1152]{1,0:T(8,128)(2,1)S(1)}, u32[]{:S(2)}, u32[]{:S(2)}) collective-permute-start(bf16[80,1152]{1,0:T(8,128)(2,1)} %shard_map.149.refs_0_.hidden_ref), channel_id=1, source_target_pairs={{0,1},{1,0},{2,3},{3,2},{4,5},{5,4},{6,7},{7,6},{8,9},{9,8},{10,11... | collective-permute-start | bytes 552968 | tf_op jit(solution)/shard_map/ppermute | solution.py:365
  8.3 10.9 %all-to-all-start = ((f32[4,1,80]{2,1,0:T(1,128)}), f32[4,1,80]{2,1,0:T(1,128)S(1)}, u32[]{:S(2)}, u32[]{:S(2)}) async-start(f32[4,1,80]{2,1,0:T(1,128)} %broadcast_in_dim.46), calls=%async_computation | async-start | bytes 4096 | tf_op jit(solution)/shard_map/all_to_all | solution.py:394
  13.7 6.2 %collective-permute-start.4 = (bf16[80,1152]{1,0:T(8,128)(2,1)S(1)}, bf16[80,1152]{1,0:T(8,128)(2,1)S(1)}, u32[]{:S(2)}, u32[]{:S(2)}) collective-permute-start(bf16[80,1152]{1,0:T(8,128)(2,1)S(1)} %collective-permute-done.refs_1_), channel_id=1, source_target_pairs={{0,1},{1,0},{2,3},{3,2},{4,5},{5,4},{6,7},{7,6},{8,9},{9,8},{10,11... | collective-permute-start | bytes 552968 | tf_op jit(solution)/shard_map/ppermute | solution.py:365
  16.3 3.6 %collective-permute-start.5 = (bf16[80,1152]{1,0:T(8,128)(2,1)S(1)}, bf16[80,1152]{1,0:T(8,128)(2,1)S(1)}, u32[]{:S(2)}, u32[]{:S(2)}) collective-permute-start(bf16[80,1152]{1,0:T(8,128)(2,1)S(1)} %collective-permute-done.1.refs_2_), channel_id=1, source_target_pairs={{0,1},{1,0},{2,3},{3,2},{4,5},{5,4},{6,7},{7,6},{8,9},{9,8},{10,11... | collective-permute-start | bytes 552968 | tf_op jit(solution)/shard_map/ppermute | solution.py:365
  16.4 3.6 %collective-permute-start.6 = (bf16[80,1152]{1,0:T(8,128)(2,1)S(1)}, bf16[80,1152]{1,0:T(8,128)(2,1)S(1)}, u32[]{:S(2)}, u32[]{:S(2)}) collective-permute-start(bf16[80,1152]{1,0:T(8,128)(2,1)S(1)} %collective-permute-done.2.refs_3_), channel_id=1, source_target_pairs={{0,1},{1,0},{2,3},{3,2},{4,5},{5,4},{6,7},{7,6},{8,9},{9,8},{10,11... | collective-permute-start | bytes 552968 | tf_op jit(solution)/shard_map/ppermute | solution.py:365
  19.9 20.2 %copy-start.2 = (f32[1,320]{1,0:T(1,128)S(1)}, f32[1,320]{1,0:T(1,128)}, u32[]{:S(2)}) copy-start(f32[1,320]{1,0:T(1,128)} %reshape.135.early_ref.goal_ref) | copy-start | bytes 3844
  19.9 40.9 %copy-start.1 = (bf16[80,1152]{1,0:T(8,128)(2,1)S(1)}, bf16[80,1152]{1,0:T(8,128)(2,1)}, u32[]{:S(2)}) copy-start(bf16[80,1152]{1,0:T(8,128)(2,1)} %shard_map.149.refs_0_.hidden_ref) | copy-start | bytes 552964
  19.9 40.9 %copy-start.3 = (f32[1024]{0:T(1024)S(1)}, f32[1024]{0:T(1024)}, u32[]{:S(2)}) copy-start(f32[1024]{0:T(1024)} %param.23) | copy-start | bytes 12292
  19.9 66.3 %copy-start.5 = (s32[32]{0:T(128)S(1)}, s32[32]{0:T(128)}, u32[]{:S(2)}) copy-start(s32[32]{0:T(128)} %param.26) | copy-start | bytes 388
  36.8 3.3 %collective-permute-start.7 = (f32[4,80,1024]{2,1,0:T(8,128)}, f32[4,80,1024]{2,1,0:T(8,128)S(1)}, u32[]{:S(2)}, u32[]{:S(2)}) collective-permute-start(f32[4,80,1024]{2,1,0:T(8,128)} %get-tuple-element.11), channel_id=1, source_target_pairs={{0,1},{1,0},{2,3},{3,2},{4,5},{5,4},{6,7},{7,6},{8,9},{9,8},{10,11... | collective-permute-start | bytes 3932168 | tf_op jit(solution)/shard_map/ppermute | solution.py:365
  41.5 12.3 %collective-permute-start.10 = (f32[88,1024]{1,0:T(8,128)S(1)}, f32[88,1024]{1,0:T(8,128)S(1)}, u32[]{:S(2)}, u32[]{:S(2)}) collective-permute-start(f32[88,1024]{1,0:T(8,128)S(1)} %get-tuple-element.15), channel_id=1, source_target_pairs={{0,6},{2,4},{4,2},{6,0},{1,7},{3,5},{5,3},{7,1},{8,14},{10,12},{12... | collective-permute-start | bytes 1081352 | tf_op jit(solution)/shard_map/ppermute | solution.py:356
  44.0 16.7 %collective-permute-start.8 = (f32[88,1024]{1,0:T(8,128)S(1)}, f32[88,1024]{1,0:T(8,128)S(1)}, u32[]{:S(2)}, u32[]{:S(2)}) collective-permute-start(f32[88,1024]{1,0:T(8,128)S(1)} %get-tuple-element.13), channel_id=1, source_target_pairs={{0,2},{2,0},{4,6},{6,4},{1,3},{3,1},{5,7},{7,5},{8,10},{10,8},{12,... | collective-permute-start | bytes 1081352 | tf_op jit(solution)/shard_map/ppermute | solution.py:356
  44.6 16.2 %collective-permute-start.9 = (f32[88,1024]{1,0:T(8,128)S(1)}, f32[88,1024]{1,0:T(8,128)S(1)}, u32[]{:S(2)}, u32[]{:S(2)}) collective-permute-start(f32[88,1024]{1,0:T(8,128)S(1)} %get-tuple-element.14), channel_id=1, source_target_pairs={{0,4},{2,6},{4,0},{6,2},{1,5},{3,7},{5,1},{7,3},{8,12},{10,14},{12... | collective-permute-start | bytes 1081352 | tf_op jit(solution)/shard_map/ppermute | solution.py:356
  61.0 31.7 %copy-start.4 = (bf16[80,1024]{1,0:T(8,128)(2,1)}, bf16[80,1024]{1,0:T(8,128)(2,1)S(1)}, u32[]{:S(2)}) copy-start(bf16[80,1024]{1,0:T(8,128)(2,1)S(1)} %get-tuple-element.17.refs_0_) | copy-start | bytes 491524
  61.0 9.0 %collective-permute-start.11 = (bf16[80,1024]{1,0:T(8,128)(2,1)S(1)}, bf16[80,1024]{1,0:T(8,128)(2,1)S(1)}, u32[]{:S(2)}, u32[]{:S(2)}) collective-permute-start(bf16[80,1024]{1,0:T(8,128)(2,1)S(1)} %get-tuple-element.17.refs_0_), channel_id=1, source_target_pairs={{0,8},{8,16},{16,24},{24,0},{1,9},{9,17},{17,25},{25,1},{2,10},{10... | collective-permute-start | bytes 491528 | tf_op jit(solution)/shard_map/ppermute | solution.py:361
  61.6 14.4 %collective-permute-start.13 = (bf16[80,1024]{1,0:T(8,128)(2,1)S(1)}, bf16[80,1024]{1,0:T(8,128)(2,1)S(1)}, u32[]{:S(2)}, u32[]{:S(2)}) collective-permute-start(bf16[80,1024]{1,0:T(8,128)(2,1)S(1)} %get-tuple-element.17.refs_0_), channel_id=1, source_target_pairs={{0,16},{8,24},{16,0},{24,8},{1,17},{9,25},{17,1},{25,9},{2,18},{10... | collective-permute-start | bytes 491528 | tf_op jit(solution)/shard_map/ppermute | solution.py:361
  63.4 14.1 %collective-permute-start.15 = (bf16[80,1024]{1,0:T(8,128)(2,1)S(1)}, bf16[80,1024]{1,0:T(8,128)(2,1)S(1)}, u32[]{:S(2)}, u32[]{:S(2)}) collective-permute-start(bf16[80,1024]{1,0:T(8,128)(2,1)S(1)} %get-tuple-element.17.refs_0_), channel_id=1, source_target_pairs={{0,24},{8,0},{16,8},{24,16},{1,25},{9,1},{17,9},{25,17},{2,26},{10... | collective-permute-start | bytes 491528 | tf_op jit(solution)/shard_map/ppermute | solution.py:361
  64.9 14.3 %collective-permute-start.17 = (bf16[80,1024]{1,0:T(8,128)(2,1)S(1)}, bf16[80,1024]{1,0:T(8,128)(2,1)S(1)}, u32[]{:S(2)}, u32[]{:S(2)}) collective-permute-start(bf16[80,1024]{1,0:T(8,128)(2,1)S(1)} %get-tuple-element.17.refs_0_), channel_id=1, source_target_pairs={{0,2},{2,0},{4,6},{6,4},{1,3},{3,1},{5,7},{7,5},{8,10},{10,8},{12,... | collective-permute-start | bytes 491528 | tf_op jit(solution)/shard_map/ppermute | solution.py:356
  70.0 22.7 %copy-start.14 = (bf16[80,1024]{1,0:T(8,128)(2,1)}, bf16[80,1024]{1,0:T(8,128)(2,1)S(1)}, u32[]{:S(2)}) copy-start(bf16[80,1024]{1,0:T(8,128)(2,1)S(1)} %collective-permute-done.11.refs_1_) | copy-start | bytes 491524
  70.0 9.7 %collective-permute-start.25 = (bf16[80,1024]{1,0:T(8,128)(2,1)S(1)}, bf16[80,1024]{1,0:T(8,128)(2,1)S(1)}, u32[]{:S(2)}, u32[]{:S(2)}) collective-permute-start(bf16[80,1024]{1,0:T(8,128)(2,1)S(1)} %get-tuple-element.17.refs_0_), channel_id=1, source_target_pairs={{0,4},{2,6},{4,0},{6,2},{1,5},{3,7},{5,1},{7,3},{8,12},{10,14},{12... | collective-permute-start | bytes 491528 | tf_op jit(solution)/shard_map/ppermute | solution.py:356
  76.0 16.7 %copy-start.15 = (bf16[80,1024]{1,0:T(8,128)(2,1)}, bf16[80,1024]{1,0:T(8,128)(2,1)S(1)}, u32[]{:S(2)}) copy-start(bf16[80,1024]{1,0:T(8,128)(2,1)S(1)} %collective-permute-done.13.refs_2_) | copy-start | bytes 491524
  76.0 6.7 %collective-permute-start.12 = (bf16[80,1024]{1,0:T(8,128)(2,1)S(1)}, bf16[80,1024]{1,0:T(8,128)(2,1)S(1)}, u32[]{:S(2)}, u32[]{:S(2)}) collective-permute-start(bf16[80,1024]{1,0:T(8,128)(2,1)S(1)} %collective-permute-done.11.refs_1_), channel_id=1, source_target_pairs={{0,4},{2,6},{4,0},{6,2},{1,5},{3,7},{5,1},{7,3},{8,12},{10,14},{12... | collective-permute-start | bytes 491528 | tf_op jit(solution)/shard_map/ppermute | solution.py:356
  77.6 15.2 %copy-start.16 = (bf16[80,1024]{1,0:T(8,128)(2,1)}, bf16[80,1024]{1,0:T(8,128)(2,1)S(1)}, u32[]{:S(2)}) copy-start(bf16[80,1024]{1,0:T(8,128)(2,1)S(1)} %collective-permute-done.15.refs_3_) | copy-start | bytes 491524
  77.6 7.1 %collective-permute-start.19 = (bf16[80,1024]{1,0:T(8,128)(2,1)S(1)}, bf16[80,1024]{1,0:T(8,128)(2,1)S(1)}, u32[]{:S(2)}, u32[]{:S(2)}) collective-permute-start(bf16[80,1024]{1,0:T(8,128)(2,1)S(1)} %collective-permute-done.11.refs_1_), channel_id=1, source_target_pairs={{0,2},{2,0},{4,6},{6,4},{1,3},{3,1},{5,7},{7,5},{8,10},{10,8},{12,... | collective-permute-start | bytes 491528 | tf_op jit(solution)/shard_map/ppermute | solution.py:356
  79.1 13.6 %copy-start.18 = (bf16[80,1024]{1,0:T(8,128)(2,1)}, bf16[80,1024]{1,0:T(8,128)(2,1)S(1)}, u32[]{:S(2)}) copy-start(bf16[80,1024]{1,0:T(8,128)(2,1)S(1)} %collective-permute-done.17.refs_4_) | copy-start | bytes 491524
  79.1 9.2 %collective-permute-start.23 = (bf16[80,1024]{1,0:T(8,128)(2,1)S(1)}, bf16[80,1024]{1,0:T(8,128)(2,1)S(1)}, u32[]{:S(2)}, u32[]{:S(2)}) collective-permute-start(bf16[80,1024]{1,0:T(8,128)(2,1)S(1)} %collective-permute-done.13.refs_2_), channel_id=1, source_target_pairs={{0,2},{2,0},{4,6},{6,4},{1,3},{3,1},{5,7},{7,5},{8,10},{10,8},{12,... | collective-permute-start | bytes 491528 | tf_op jit(solution)/shard_map/ppermute | solution.py:356
  79.7 13.1 %copy-start.19 = (bf16[80,1024]{1,0:T(8,128)(2,1)}, bf16[80,1024]{1,0:T(8,128)(2,1)S(1)}, u32[]{:S(2)}) copy-start(bf16[80,1024]{1,0:T(8,128)(2,1)S(1)} %collective-permute-done.25.refs_8_) | copy-start | bytes 491524
  79.7 10.7 %collective-permute-start.14 = (bf16[80,1024]{1,0:T(8,128)(2,1)S(1)}, bf16[80,1024]{1,0:T(8,128)(2,1)S(1)}, u32[]{:S(2)}, u32[]{:S(2)}) collective-permute-start(bf16[80,1024]{1,0:T(8,128)(2,1)S(1)} %collective-permute-done.13.refs_2_), channel_id=1, source_target_pairs={{0,4},{2,6},{4,0},{6,2},{1,5},{3,7},{5,1},{7,3},{8,12},{10,14},{12... | collective-permute-start | bytes 491528 | tf_op jit(solution)/shard_map/ppermute | solution.py:356
  82.7 6.3 %collective-permute-start.24 = (bf16[80,1024]{1,0:T(8,128)(2,1)S(1)}, bf16[80,1024]{1,0:T(8,128)(2,1)S(1)}, u32[]{:S(2)}, u32[]{:S(2)}) collective-permute-start(bf16[80,1024]{1,0:T(8,128)(2,1)S(1)} %collective-permute-done.15.refs_3_), channel_id=1, source_target_pairs={{0,2},{2,0},{4,6},{6,4},{1,3},{3,1},{5,7},{7,5},{8,10},{10,8},{12,... | collective-permute-start | bytes 491528 | tf_op jit(solution)/shard_map/ppermute | solution.py:356
  84.7 6.7 %collective-permute-start.16 = (bf16[80,1024]{1,0:T(8,128)(2,1)S(1)}, bf16[80,1024]{1,0:T(8,128)(2,1)S(1)}, u32[]{:S(2)}, u32[]{:S(2)}) collective-permute-start(bf16[80,1024]{1,0:T(8,128)(2,1)S(1)} %collective-permute-done.15.refs_3_), channel_id=1, source_target_pairs={{0,4},{2,6},{4,0},{6,2},{1,5},{3,7},{5,1},{7,3},{8,12},{10,14},{12... | collective-permute-start | bytes 491528 | tf_op jit(solution)/shard_map/ppermute | solution.py:356
  88.3 18.9 %collective-permute-start.18 = (bf16[80,1024]{1,0:T(8,128)(2,1)S(1)}, bf16[80,1024]{1,0:T(8,128)(2,1)S(1)}, u32[]{:S(2)}, u32[]{:S(2)}) collective-permute-start(bf16[80,1024]{1,0:T(8,128)(2,1)S(1)} %collective-permute-done.17.refs_4_), channel_id=1, source_target_pairs={{0,4},{2,6},{4,0},{6,2},{1,5},{3,7},{5,1},{7,3},{8,12},{10,14},{12... | collective-permute-start | bytes 491528 | tf_op jit(solution)/shard_map/ppermute | solution.py:356
  89.1 18.2 %collective-permute-start.20 = (bf16[80,1024]{1,0:T(8,128)(2,1)S(1)}, bf16[80,1024]{1,0:T(8,128)(2,1)S(1)}, u32[]{:S(2)}, u32[]{:S(2)}) collective-permute-start(bf16[80,1024]{1,0:T(8,128)(2,1)S(1)} %collective-permute-done.19.refs_5_), channel_id=1, source_target_pairs={{0,4},{2,6},{4,0},{6,2},{1,5},{3,7},{5,1},{7,3},{8,12},{10,14},{12... | collective-permute-start | bytes 491528 | tf_op jit(solution)/shard_map/ppermute | solution.py:356
  90.4 16.8 %copy-start.21 = (bf16[80,1024]{1,0:T(8,128)(2,1)}, bf16[80,1024]{1,0:T(8,128)(2,1)S(1)}, u32[]{:S(2)}) copy-start(bf16[80,1024]{1,0:T(8,128)(2,1)S(1)} %collective-permute-done.14.refs_1_) | copy-start | bytes 491524
  90.4 16.9 %collective-permute-start.21 = (bf16[80,1024]{1,0:T(8,128)(2,1)S(1)}, bf16[80,1024]{1,0:T(8,128)(2,1)S(1)}, u32[]{:S(2)}, u32[]{:S(2)}) collective-permute-start(bf16[80,1024]{1,0:T(8,128)(2,1)S(1)} %collective-permute-done.14.refs_1_), channel_id=1, source_target_pairs={{0,2},{2,0},{4,6},{6,4},{1,3},{3,1},{5,7},{7,5},{8,10},{10,8},{12,... | collective-permute-start | bytes 491528 | tf_op jit(solution)/shard_map/ppermute | solution.py:356
  91.4 15.8 %copy-start.23 = (bf16[80,1024]{1,0:T(8,128)(2,1)}, bf16[80,1024]{1,0:T(8,128)(2,1)S(1)}, u32[]{:S(2)}) copy-start(bf16[80,1024]{1,0:T(8,128)(2,1)S(1)} %collective-permute-done.16.refs_2_) | copy-start | bytes 491524
  91.4 15.9 %collective-permute-start.22 = (bf16[80,1024]{1,0:T(8,128)(2,1)S(1)}, bf16[80,1024]{1,0:T(8,128)(2,1)S(1)}, u32[]{:S(2)}, u32[]{:S(2)}) collective-permute-start(bf16[80,1024]{1,0:T(8,128)(2,1)S(1)} %collective-permute-done.16.refs_2_), channel_id=1, source_target_pairs={{0,2},{2,0},{4,6},{6,4},{1,3},{3,1},{5,7},{7,5},{8,10},{10,8},{12,... | collective-permute-start | bytes 491528 | tf_op jit(solution)/shard_map/ppermute | solution.py:356
  107.2 19.8 %copy-start.6 = (s32[32]{0:T(128)S(1)}, s32[32]{0:T(128)}, u32[]{:S(2)}) copy-start(s32[32]{0:T(128)} %param.27) | copy-start | bytes 388
  121.8 6.5 %collective-permute-start.27 = (f32[16,2,80]{2,0,1:T(8,128)S(1)}, f32[16,2,80]{2,0,1:T(8,128)S(1)}, u32[]{:S(2)}, u32[]{:S(2)}) collective-permute-start(f32[16,2,80]{2,0,1:T(8,128)S(1)} %copy.37), channel_id=1, source_target_pairs={{0,8},{8,16},{16,24},{24,0},{1,9},{9,17},{17,25},{25,1},{2,10},{10... | collective-permute-start | bytes 30728 | tf_op jit(solution)/shard_map/ppermute | solution.py:361
  124.6 4.6 %collective-permute-start.28 = (f32[16,2,80]{2,0,1:T(8,128)S(1)}, f32[16,2,80]{2,0,1:T(8,128)S(1)}, u32[]{:S(2)}, u32[]{:S(2)}) collective-permute-start(f32[16,2,80]{2,0,1:T(8,128)S(1)} %copy.37), channel_id=1, source_target_pairs={{0,16},{8,24},{16,0},{24,8},{1,17},{9,25},{17,1},{25,9},{2,18},{10... | collective-permute-start | bytes 30728 | tf_op jit(solution)/shard_map/ppermute | solution.py:361
  125.3 3.9 %collective-permute-start.29 = (f32[16,2,80]{2,0,1:T(8,128)S(1)}, f32[16,2,80]{2,0,1:T(8,128)S(1)}, u32[]{:S(2)}, u32[]{:S(2)}) collective-permute-start(f32[16,2,80]{2,0,1:T(8,128)S(1)} %copy.37), channel_id=1, source_target_pairs={{0,24},{8,0},{16,8},{24,16},{1,25},{9,1},{17,9},{25,17},{2,26},{10... | collective-permute-start | bytes 30728 | tf_op jit(solution)/shard_map/ppermute | solution.py:361
  129.3 5.5 %collective-permute-start.30 = (f32[16,2,80]{2,0,1:T(8,128)S(1)}, f32[16,2,80]{2,0,1:T(8,128)S(1)}, u32[]{:S(2)}, u32[]{:S(2)}) collective-permute-start(f32[16,2,80]{2,0,1:T(8,128)S(1)} %pad_maximum_fusion), channel_id=1, source_target_pairs={{0,2},{2,0},{4,6},{6,4},{1,3},{3,1},{5,7},{7,5},{8,10},{10,8},{12,... | collective-permute-start | bytes 30728 | tf_op jit(solution)/shard_map/ppermute | solution.py:356
  130.8 3.9 %collective-permute-start.31 = (f32[16,2,80]{2,0,1:T(8,128)S(1)}, f32[16,2,80]{2,0,1:T(8,128)S(1)}, u32[]{:S(2)}, u32[]{:S(2)}) collective-permute-start(f32[16,2,80]{2,0,1:T(8,128)S(1)} %pad_maximum_fusion), channel_id=1, source_target_pairs={{0,4},{2,6},{4,0},{6,2},{1,5},{3,7},{5,1},{7,3},{8,12},{10,14},{12... | collective-permute-start | bytes 30728 | tf_op jit(solution)/shard_map/ppermute | solution.py:356
  132.2 4.6 %collective-permute-start.32 = (f32[16,2,80]{2,0,1:T(8,128)S(1)}, f32[16,2,80]{2,0,1:T(8,128)S(1)}, u32[]{:S(2)}, u32[]{:S(2)}) collective-permute-start(f32[16,2,80]{2,0,1:T(8,128)S(1)} %pad_maximum_fusion), channel_id=1, source_target_pairs={{0,6},{2,4},{4,2},{6,0},{1,7},{3,5},{5,3},{7,1},{8,14},{10,12},{12... | collective-permute-start | bytes 30728 | tf_op jit(solution)/shard_map/ppermute | solution.py:356
  136.9 1.2 collective-permute-start.33
  (16 other events, 46.8 us)

commit v8 on v7

--- a/solution.py
+++ b/solution.py
@@ -238,6 +238,83 @@
     )(hidden, gain.reshape(1, -1), goal, own, *came)
 
 
+def split_kernel(keep_ref, came_ref, goal_ref, own_ref, mid_x, mid_y, send_x, send_y):
+    share, width = own_ref.shape
+    half, lines = width // 2, goal_ref.shape[1]
+    left, right = slice(0, half), slice(half, width)
+
+    def total(d, side):
+        return keep_ref[d, :, side] + came_ref[d, :, side]
+
+    own_ref[...] = keep_ref[0] + came_ref[0]
+    mid_x[...] = total(1, right)
+    mid_y[...] = total(2, left)
+    for send, near, side in ((send_x, 1, left), (send_y, 2, right)):
+        send[:share] = total(near, side)
+        send[share:2 * share] = total(3, side)
+        send[2 * share:] = jnp.zeros((8, half), jnp.float32)
+        send[2 * share:2 * share + 1, :lines] = goal_ref[...]
+
+
+def split_sums(keep, came, goal):
+    _, share, width = keep.shape
+    own = jax.ShapeDtypeStruct((share, width), jnp.float32)
+    middle = jax.ShapeDtypeStruct((share, width // 2), jnp.float32)
+    send = jax.ShapeDtypeStruct((2 * share + 8, width // 2), jnp.float32)
+    return pl.pallas_call(
+        split_kernel,
+        out_shape=(own, middle, middle, send, send),
+        compiler_params=pltpu.CompilerParams(vmem_limit_bytes=24 * MIB),
+    )(keep, came, goal)
+
+
+def middle_kernel(mid_x, mid_y, from_x, from_y, next_x, next_y):
+    share = mid_x.shape[0]
+    next_x[...] = mid_x[...] + from_y[share:2 * share]
+    next_y[:share] = mid_y[...] + from_x[share:2 * share]
+    next_y[share:] = from_x[2 * share:]
+
+
+def middle_sums(mid_x, mid_y, from_x, from_y):
+    share, half = mid_x.shape
+    return pl.pallas_call(
+        middle_kernel,
+        out_shape=(
+            jax.ShapeDtypeStruct((share, half), jnp.float32),
+            jax.ShapeDtypeStruct((share + 8, half), jnp.float32),
+        ),
+        compiler_params=pltpu.CompilerParams(vmem_limit_bytes=16 * MIB),
+    )(mid_x, mid_y, from_x, from_y)
+
+
+def join_kernel(
+    hidden_ref, gain_ref, goal_ref, own_ref, from_x, from_y, last_x, last_y, normed_ref, wanted_ref
+):
+    share, width = own_ref.shape
+    lines = goal_ref.shape[1]
+    came = jnp.concatenate(
+        (from_x[:share] + last_y[:share], from_y[:share] + last_x[...]), axis=1
+    )
+    mixed = hidden_ref[:, :width].astype(jnp.float32) + own_ref[...] + came
+    scale = lax.rsqrt(jnp.mean(mixed * mixed, axis=1, keepdims=True) + 1e-06)
+    normed_ref[...] = (mixed * scale * gain_ref[...]).astype(jnp.bfloat16)
+    wanted_ref[0:1, :] = goal_ref[...].astype(jnp.int32)
+    wanted_ref[1:2, :] = from_x[2 * share:2 * share + 1, :lines].astype(jnp.int32)
+    wanted_ref[2:3, :] = from_y[2 * share:2 * share + 1, :lines].astype(jnp.int32)
+    wanted_ref[3:4, :] = last_y[share:share + 1, :lines].astype(jnp.int32)
+
+
+def join_rows(hidden, gain, goal, own, *parts):
+    return pl.pallas_call(
+        join_kernel,
+        out_shape=(
+            jax.ShapeDtypeStruct(own.shape, jnp.bfloat16),
+            jax.ShapeDtypeStruct((4, goal.shape[1]), jnp.int32),
+        ),
+        compiler_params=pltpu.CompilerParams(vmem_limit_bytes=16 * MIB),
+    )(hidden, gain.reshape(1, -1), goal, own, *parts)
+
+
 def head_kernel(parts, before, spots_ref, wanted_ref, *refs):
     blocks, refs = refs[:len(parts)], refs[len(parts):]
     earlier, refs = refs[:before], refs[before:]
@@ -400,9 +477,18 @@
     keep, give = expert_sums(
         place, goal, plane, w_gate, w_up, w_down, tokens, capacity, width, experts
     )
-    own, *sends = pair_sums(keep, partner(give), goal)
-    came = [across(rows, d) for d, rows in zip(offsets, sends)]
-    normed, wanted = norm_rows(send, norm_gain, goal, own, came)
+    if chips == 4 and groups * share <= width // 2:
+        own, mid_x, mid_y, send_x, send_y = split_sums(keep, partner(give), goal)
+        from_x, from_y = across(send_x, 1), across(send_y, 2)
+        next_x, next_y = middle_sums(mid_x, mid_y, from_x, from_y)
+        last_x, last_y = across(next_x, 1), across(next_y, 2)
+        normed, wanted = join_rows(
+            send, norm_gain, goal, own, from_x, from_y, last_x, last_y
+        )
+    else:
+        own, *sends = pair_sums(keep, partner(give), goal)
+        came = [across(rows, d) for d, rows in zip(offsets, sends)]
+        normed, wanted = norm_rows(send, norm_gain, goal, own, came)
     wanted = wanted.reshape(1, -1)
 
     column = [normed] + [along(normed, k) for k in range(1, groups)]

time: 142 us -> 138 us (0.972)
  waiting for transfers between devices: 37.9 us -> 35.1 us
    ppermute x21 -> x22, starting transfers between devices: 25.3 us -> 23.1 us  [across(): return lax.ppermute(value, 'chip', [(c, c ^ offset) for c in range(chips)])]
    ppermute x21 -> x22, waiting for transfers between devices: 23.2 us -> 21.4 us  [across(): return lax.ppermute(value, 'chip', [(c, c ^ offset) for c in range(chips)])]
  transfers between devices with their start and end apart: 35 -> 36, of which waited for: 13 -> 14; matrix products, arithmetic and copies ran while one was open for 5% -> 5% of each run, Pallas kernels for 23% -> 23%
where the time goes in v8:
time: 138 us
  Pallas kernels  44.3 us (32%)
  starting transfers between devices  40.2 us (29%)
  waiting for transfers between devices  35.1 us (25%)
  local copies, waits for them, and re-layouts  8.87 us (6%)
  between operations  4.72 us (3%)
  other arithmetic  4.56 us (3%)
    pallas_call x2, Pallas kernels, head_stats(): pl.pallas_call(functools.partial(head_kernel, parts, len(earlier)), out_s...  26.8 us
    ppermute x22, starting transfers between devices, across(): return lax.ppermute(value, 'chip', [(c, c ^ offset) for c in range(chips)])  23.1 us
    ppermute x22, waiting for transfers between devices, across(): return lax.ppermute(value, 'chip', [(c, c ^ offset) for c in range(chips)])  21.4 us
    pallas_call x1, Pallas kernels, expert_sums(): pl.pallas_call(functools.partial(expert_kernel, block, slots, width, expe...  15.4 us
    ppermute x6, starting transfers between devices, along(): lax.ppermute(value, 'grp', [(g, (g + offset) % groups) for g in range(gro...  10.3 us
    ppermute x6, waiting for transfers between devices, along(): lax.ppermute(value, 'grp', [(g, (g + offset) % groups) for g in range(gro...  8.11 us
    all_to_all x1, starting transfers between devices, local(): goal = lax.all_to_all(goal, 'grp', split_axis=0, concat_axis=0, tiled=True)  5.34 us
    unnamed x58, local copies, waits for them, and re-layouts  4.21 us
  transfers between devices with their start and end apart: 36, of which 14 were waited for; matrix products, arithmetic and copies ran while one was open for 5% of the time, Pallas kernels for 23%

profile of v8, /device:TPU:0, one launch (start us, length us, event | category | flops | bytes accessed | tf_op | source)
XLA Modules:
  0.0 137.7 jit_solution(13701472976189938330)
XLA Ops:
  1.1 1.8 %shard_map.149.refs_0_.hidden_ref = bf16[80,1152]{1,0:T(8,128)(2,1)} custom-call(bf16[40,1024]{1,0:T(8,128)(2,1)} %pol_ref.1, bf16[40,1024]{1,0:T(8,128)(2,1)} %ref_ref.1, s32[8,40]{1,0:T(8,128)} %bitcast.103, s32[8,40]{1,0:T(8,128)} %bitcast.104, f32[8,40]{1,0:T(8,128)} %bitcast.105, f32[8,40]{1,0:T(8,128)} %bitcast.106), custom_call_target="tpu_custom_call" | custom-call | tf_op jit(solution)/shard_map/pallas_call | solution.py:47
  2.9 2.5 %collective-permute-start = (bf16[80,1152]{1,0:T(8,128)(2,1)}, bf16[80,1152]{1,0:T(8,128)(2,1)S(1)}, u32[]{:S(2)}, u32[]{:S(2)}) collective-permute-start(bf16[80,1152]{1,0:T(8,128)(2,1)} %shard_map.149.refs_0_.hidden_ref), channel_id=1, source_target_pairs={{0,2},{2,0},{4,6},{6,4},{1,3},{3,1},{5,7},{7,5},{8,10},{10,8},{12,... | collective-permute-start | bytes 552968 | tf_op jit(solution)/shard_map/ppermute | solution.py:433
  5.4 1.5 %collective-permute-start.1 = (bf16[80,1152]{1,0:T(8,128)(2,1)}, bf16[80,1152]{1,0:T(8,128)(2,1)S(1)}, u32[]{:S(2)}, u32[]{:S(2)}) collective-permute-start(bf16[80,1152]{1,0:T(8,128)(2,1)} %shard_map.149.refs_0_.hidden_ref), channel_id=1, source_target_pairs={{0,4},{2,6},{4,0},{6,2},{1,5},{3,7},{5,1},{7,3},{8,12},{10,14},{12... | collective-permute-start | bytes 552968 | tf_op jit(solution)/shard_map/ppermute | solution.py:433
  6.9 0.7 convert_bitcast_fusion
  8.3 5.3 %all-to-all-start = ((f32[4,1,80]{2,1,0:T(1,128)}), f32[4,1,80]{2,1,0:T(1,128)S(1)}, u32[]{:S(2)}, u32[]{:S(2)}) async-start(f32[4,1,80]{2,1,0:T(1,128)} %broadcast_in_dim.46), calls=%async_computation | async-start | bytes 4096 | tf_op jit(solution)/shard_map/all_to_all | solution.py:471
  14.0 2.4 %collective-permute-done.1.refs_2_ = bf16[80,1152]{1,0:T(8,128)(2,1)S(1)} collective-permute-done((bf16[80,1152]{1,0:T(8,128)(2,1)}, bf16[80,1152]{1,0:T(8,128)(2,1)S(1)}, u32[]{:S(2)}, u32[]{:S(2)}) %collective-permute-start.1) | collective-permute-done | bytes 184352 | tf_op jit(solution)/shard_map/ppermute | solution.py:433
  16.8 0.6 pad_add_fusion.1.place_ref
  17.5 1.7 %all-to-all-done = f32[4,1,80]{2,1,0:T(1,128)S(1)} async-done(((f32[4,1,80]{2,1,0:T(1,128)}), f32[4,1,80]{2,1,0:T(1,128)S(1)}, u32[]{:S(2)}, u32[]{:S(2)}) %all-to-all-start) | async-done | bytes 1312 | tf_op jit(solution)/shard_map/all_to_all | solution.py:471
  19.2 0.7 reshape.135.early_ref.goal_ref
  20.8 0.7 copy-done.13
  21.4 15.4 %shard_map.150 = (f32[4,80,1024]{2,1,0:T(8,128)}, f32[4,80,1024]{2,1,0:T(8,128)}) custom-call(s32[2]{0:T(128)} %pad_add_fusion.1.place_ref, f32[1,320]{1,0:T(1,128)} %reshape.135.early_ref.goal_ref, bf16[80,1152]{1,0:T(8,128)(2,1)} %shard_map.149.refs_0_.hidden_ref, bf16[80,1152]{1,0:T(8,128)(2,1)} %copy-done.7, bf16[80,1152]{1,0:T(8,128)(2,1)} %copy-done.8, ...), custom_call_target="tpu_custom_call" | custom-call | flops 6442450944 | bytes 22970368 | tf_op jit(solution)/shard_map/pallas_call | solution.py:156
  36.9 3.2 %collective-permute-done.7.came_ref = f32[4,80,1024]{2,1,0:T(8,128)S(1)} collective-permute-done((f32[4,80,1024]{2,1,0:T(8,128)}, f32[4,80,1024]{2,1,0:T(8,128)S(1)}, u32[]{:S(2)}, u32[]{:S(2)}) %collective-permute-start.7) | collective-permute-done | bytes 1310752 | tf_op jit(solution)/shard_map/ppermute | solution.py:442
  40.1 1.3 copy-done
  41.6 1.6 %collective-permute-start.8 = (f32[168,512]{1,0:T(8,128)S(1)}, f32[168,512]{1,0:T(8,128)S(1)}, u32[]{:S(2)}, u32[]{:S(2)}) collective-permute-start(f32[168,512]{1,0:T(8,128)S(1)} %get-tuple-element.16), channel_id=1, source_target_pairs={{0,2},{2,0},{4,6},{6,4},{1,3},{3,1},{5,7},{7,5},{8,10},{10,8},{12,... | collective-permute-start | bytes 1032200 | tf_op jit(solution)/shard_map/ppermute | solution.py:433
  43.1 1.5 %collective-permute-start.9 = (f32[168,512]{1,0:T(8,128)S(1)}, f32[168,512]{1,0:T(8,128)S(1)}, u32[]{:S(2)}, u32[]{:S(2)}) collective-permute-start(f32[168,512]{1,0:T(8,128)S(1)} %get-tuple-element.17), channel_id=1, source_target_pairs={{0,4},{2,6},{4,0},{6,2},{1,5},{3,7},{5,1},{7,3},{8,12},{10,14},{12... | collective-permute-start | bytes 1032200 | tf_op jit(solution)/shard_map/ppermute | solution.py:433
  44.7 7.1 %collective-permute-done.8.from_x = f32[168,512]{1,0:T(8,128)S(1)} collective-permute-done((f32[168,512]{1,0:T(8,128)S(1)}, f32[168,512]{1,0:T(8,128)S(1)}, u32[]{:S(2)}, u32[]{:S(2)}) %collective-permute-start.8) | collective-permute-done | bytes 344096 | tf_op jit(solution)/shard_map/ppermute | solution.py:433
  51.8 1.2 collective-permute-done.9.from_y
  53.0 1.6 %collective-permute-start.11 = (f32[88,512]{1,0:T(8,128)S(1)}, f32[88,512]{1,0:T(8,128)S(1)}, u32[]{:S(2)}, u32[]{:S(2)}) collective-permute-start(f32[88,512]{1,0:T(8,128)S(1)} %get-tuple-element.21), channel_id=1, source_target_pairs={{0,4},{2,6},{4,0},{6,2},{1,5},{3,7},{5,1},{7,3},{8,12},{10,14},{12... | collective-permute-start | bytes 540680 | tf_op jit(solution)/shard_map/ppermute | solution.py:433
  55.1 4.8 %collective-permute-done.10.last_x = f32[80,512]{1,0:T(8,128)S(1)} collective-permute-done((f32[80,512]{1,0:T(8,128)S(1)}, f32[80,512]{1,0:T(8,128)S(1)}, u32[]{:S(2)}, u32[]{:S(2)}) %collective-permute-start.10) | collective-permute-done | bytes 163872 | tf_op jit(solution)/shard_map/ppermute | solution.py:433
  60.1 0.6 collective-permute-start.12
  60.7 0.9 collective-permute-start.14
  61.7 2.3 %collective-permute-start.16 = (bf16[80,1024]{1,0:T(8,128)(2,1)S(1)}, bf16[80,1024]{1,0:T(8,128)(2,1)S(1)}, u32[]{:S(2)}, u32[]{:S(2)}) collective-permute-start(bf16[80,1024]{1,0:T(8,128)(2,1)S(1)} %get-tuple-element.23.refs_0_), channel_id=1, source_target_pairs={{0,24},{8,0},{16,8},{24,16},{1,25},{9,1},{17,9},{25,17},{2,26},{10... | collective-permute-start | bytes 491528 | tf_op jit(solution)/shard_map/ppermute | solution.py:438
  64.6 4.6 %collective-permute-done.12.refs_1_ = bf16[80,1024]{1,0:T(8,128)(2,1)S(1)} collective-permute-done((bf16[80,1024]{1,0:T(8,128)(2,1)S(1)}, bf16[80,1024]{1,0:T(8,128)(2,1)S(1)}, u32[]{:S(2)}, u32[]{:S(2)}) %collective-permute-start.12) | collective-permute-done | bytes 163872 | tf_op jit(solution)/shard_map/ppermute | solution.py:438
  69.7 3.5 %collective-permute-done.14.refs_2_ = bf16[80,1024]{1,0:T(8,128)(2,1)S(1)} collective-permute-done((bf16[80,1024]{1,0:T(8,128)(2,1)S(1)}, bf16[80,1024]{1,0:T(8,128)(2,1)S(1)}, u32[]{:S(2)}, u32[]{:S(2)}) %collective-permute-start.14) | collective-permute-done | bytes 163872 | tf_op jit(solution)/shard_map/ppermute | solution.py:438
  73.4 0.9 collective-permute-start.20
  74.3 1.1 collective-permute-start.24
  75.5 1.8 %collective-permute-start.15 = (bf16[80,1024]{1,0:T(8,128)(2,1)S(1)}, bf16[80,1024]{1,0:T(8,128)(2,1)S(1)}, u32[]{:S(2)}, u32[]{:S(2)}) collective-permute-start(bf16[80,1024]{1,0:T(8,128)(2,1)S(1)} %collective-permute-done.14.refs_2_), channel_id=1, source_target_pairs={{0,4},{2,6},{4,0},{6,2},{1,5},{3,7},{5,1},{7,3},{8,12},{10,14},{12... | collective-permute-start | bytes 491528 | tf_op jit(solution)/shard_map/ppermute | solution.py:433
  77.3 3.0 %collective-permute-done.13.refs_9_.refs_0_ = bf16[80,1024]{1,0:T(8,128)(2,1)S(1)} collective-permute-done((bf16[80,1024]{1,0:T(8,128)(2,1)S(1)}, bf16[80,1024]{1,0:T(8,128)(2,1)S(1)}, u32[]{:S(2)}, u32[]{:S(2)}) %collective-permute-start.13) | collective-permute-done | bytes 163872 | tf_op jit(solution)/shard_map/ppermute | solution.py:433
  80.5 1.8 %collective-permute-start.17 = (bf16[80,1024]{1,0:T(8,128)(2,1)S(1)}, bf16[80,1024]{1,0:T(8,128)(2,1)S(1)}, u32[]{:S(2)}, u32[]{:S(2)}) collective-permute-start(bf16[80,1024]{1,0:T(8,128)(2,1)S(1)} %collective-permute-done.16.refs_3_), channel_id=1, source_target_pairs={{0,4},{2,6},{4,0},{6,2},{1,5},{3,7},{5,1},{7,3},{8,12},{10,14},{12... | collective-permute-start | bytes 491528 | tf_op jit(solution)/shard_map/ppermute | solution.py:433
  84.8 0.8 collective-permute-done.25.refs_7_
  85.6 1.0 collective-permute-start.21
  87.6 1.5 %collective-permute-start.23 = (bf16[80,1024]{1,0:T(8,128)(2,1)S(1)}, bf16[80,1024]{1,0:T(8,128)(2,1)S(1)}, u32[]{:S(2)}, u32[]{:S(2)}) collective-permute-start(bf16[80,1024]{1,0:T(8,128)(2,1)S(1)} %collective-permute-done.17.refs_2_), channel_id=1, source_target_pairs={{0,2},{2,0},{4,6},{6,4},{1,3},{3,1},{5,7},{7,5},{8,10},{10,8},{12,... | collective-permute-start | bytes 491528 | tf_op jit(solution)/shard_map/ppermute | solution.py:433
  89.3 14.4 %shard_map.154.refs_7_ = f32[2,768]{1,0:T(2,128)} custom-call(s32[18]{0:T(128)} %pad_add_fusion.spots_ref, s32[1,768]{1,0:T(1,128)} %slice.80.wanted_ref, bf16[80,1024]{1,0:T(8,128)(2,1)} %copy-done.4, bf16[80,1024]{1,0:T(8,128)(2,1)} %copy-done.14, bf16[80,1024]{1,0:T(8,128)(2,1)} %copy-done.15, bf16[80,1024]{1,0:T(8,128)(2,1)} %copy-done.16, ...), custom_call_target="tpu_custom_call" | custom-call | flops 7650410496 | bytes 11534336 | tf_op jit(solution)/shard_map/pallas_call | solution.py:391
  103.7 0.6 copy-done.25
  104.5 0.7 copy-done.28
  105.2 12.4 %shard_map.155 = f32[16,2,80]{2,1,0:T(2,128)} custom-call(s32[18]{0:T(128)} %pad_add_fusion.spots_ref, s32[1,512]{1,0:T(1,128)} %slice.79.wanted_ref, bf16[80,1024]{1,0:T(8,128)(2,1)} %copy-done.17, bf16[80,1024]{1,0:T(8,128)(2,1)} %copy-done.21, bf16[80,1024]{1,0:T(8,128)(2,1)} %copy-done.23, bf16[80,1024]{1,0:T(8,128)(2,1)} %copy-done.25, ...), custom_call_target="tpu_custom_call" | custom-call | flops 5100273664 | bytes 11010048 | tf_op jit(solution)/shard_map/pallas_call | solution.py:391
  117.6 0.7 copy.37
  118.3 2.0 %collective-permute-start.28 = (f32[16,2,80]{2,0,1:T(8,128)S(1)}, f32[16,2,80]{2,0,1:T(8,128)S(1)}, u32[]{:S(2)}, u32[]{:S(2)}) collective-permute-start(f32[16,2,80]{2,0,1:T(8,128)S(1)} %copy.37), channel_id=1, source_target_pairs={{0,8},{8,16},{16,24},{24,0},{1,9},{9,17},{17,25},{25,1},{2,10},{10... | collective-permute-start | bytes 30728 | tf_op jit(solution)/shard_map/ppermute | solution.py:438
  120.3 1.9 %collective-permute-start.29 = (f32[16,2,80]{2,0,1:T(8,128)S(1)}, f32[16,2,80]{2,0,1:T(8,128)S(1)}, u32[]{:S(2)}, u32[]{:S(2)}) collective-permute-start(f32[16,2,80]{2,0,1:T(8,128)S(1)} %copy.37), channel_id=1, source_target_pairs={{0,16},{8,24},{16,0},{24,8},{1,17},{9,25},{17,1},{25,9},{2,18},{10... | collective-permute-start | bytes 30728 | tf_op jit(solution)/shard_map/ppermute | solution.py:438
  122.2 2.5 %collective-permute-start.30 = (f32[16,2,80]{2,0,1:T(8,128)S(1)}, f32[16,2,80]{2,0,1:T(8,128)S(1)}, u32[]{:S(2)}, u32[]{:S(2)}) collective-permute-start(f32[16,2,80]{2,0,1:T(8,128)S(1)} %copy.37), channel_id=1, source_target_pairs={{0,24},{8,0},{16,8},{24,16},{1,25},{9,1},{17,9},{25,17},{2,26},{10... | collective-permute-start | bytes 30728 | tf_op jit(solution)/shard_map/ppermute | solution.py:438
  124.8 0.7 fusion.19
  125.4 0.7 slice.85
  126.2 1.1 collective-permute-start.31
  127.3 1.4 collective-permute-start.32
  128.7 1.1 collective-permute-start.33
  131.8 1.6 %collective-permute-done.33 = f32[16,2,80]{2,0,1:T(8,128)S(1)} collective-permute-done((f32[16,2,80]{2,0,1:T(8,128)S(1)}, f32[16,2,80]{2,0,1:T(8,128)S(1)}, u32[]{:S(2)}, u32[]{:S(2)}) %collective-permute-start.33) | collective-permute-done | bytes 10272 | tf_op jit(solution)/shard_map/ppermute | solution.py:433
  134.0 0.6 collective-permute-done.34
  134.6 1.3 add_reduce_fusion
  (118 shorter events, 9.9 us)
Async XLA Ops:
  0.6 88.5 %collective-permute-start.27 = (bf16[2432,1024]{1,0:T(8,128)(2,1)}, bf16[2432,1024]{1,0:T(8,128)(2,1)}, u32[]{:S(2)}, u32[]{:S(2)}) collective-permute-start(bf16[2432,1024]{1,0:T(8,128)(2,1)} %refs_8_.3), channel_id=1, source_target_pairs={{0,1},{1,0},{2,3},{3,2},{4,5},{5,4},{6,7},{7,6},{8,9},{9,8},{10,11... | collective-permute-start | bytes 14942216 | tf_op jit(solution)/shard_map/ppermute | solution.py:442
  2.9 10.8 %collective-permute-start = (bf16[80,1152]{1,0:T(8,128)(2,1)}, bf16[80,1152]{1,0:T(8,128)(2,1)S(1)}, u32[]{:S(2)}, u32[]{:S(2)}) collective-permute-start(bf16[80,1152]{1,0:T(8,128)(2,1)} %shard_map.149.refs_0_.hidden_ref), channel_id=1, source_target_pairs={{0,2},{2,0},{4,6},{6,4},{1,3},{3,1},{5,7},{7,5},{8,10},{10,8},{12,... | collective-permute-start | bytes 552968 | tf_op jit(solution)/shard_map/ppermute | solution.py:433
  5.4 10.9 %collective-permute-start.1 = (bf16[80,1152]{1,0:T(8,128)(2,1)}, bf16[80,1152]{1,0:T(8,128)(2,1)S(1)}, u32[]{:S(2)}, u32[]{:S(2)}) collective-permute-start(bf16[80,1152]{1,0:T(8,128)(2,1)} %shard_map.149.refs_0_.hidden_ref), channel_id=1, source_target_pairs={{0,4},{2,6},{4,0},{6,2},{1,5},{3,7},{5,1},{7,3},{8,12},{10,14},{12... | collective-permute-start | bytes 552968 | tf_op jit(solution)/shard_map/ppermute | solution.py:433
  6.9 9.4 %collective-permute-start.2 = (bf16[80,1152]{1,0:T(8,128)(2,1)}, bf16[80,1152]{1,0:T(8,128)(2,1)S(1)}, u32[]{:S(2)}, u32[]{:S(2)}) collective-permute-start(bf16[80,1152]{1,0:T(8,128)(2,1)} %shard_map.149.refs_0_.hidden_ref), channel_id=1, source_target_pairs={{0,6},{2,4},{4,2},{6,0},{1,7},{3,5},{5,3},{7,1},{8,14},{10,12},{12... | collective-permute-start | bytes 552968 | tf_op jit(solution)/shard_map/ppermute | solution.py:433
  6.9 13.0 %collective-permute-start.3 = (bf16[80,1152]{1,0:T(8,128)(2,1)}, bf16[80,1152]{1,0:T(8,128)(2,1)S(1)}, u32[]{:S(2)}, u32[]{:S(2)}) collective-permute-start(bf16[80,1152]{1,0:T(8,128)(2,1)} %shard_map.149.refs_0_.hidden_ref), channel_id=1, source_target_pairs={{0,1},{1,0},{2,3},{3,2},{4,5},{5,4},{6,7},{7,6},{8,9},{9,8},{10,11... | collective-permute-start | bytes 552968 | tf_op jit(solution)/shard_map/ppermute | solution.py:442
  8.3 10.9 %all-to-all-start = ((f32[4,1,80]{2,1,0:T(1,128)}), f32[4,1,80]{2,1,0:T(1,128)S(1)}, u32[]{:S(2)}, u32[]{:S(2)}) async-start(f32[4,1,80]{2,1,0:T(1,128)} %broadcast_in_dim.46), calls=%async_computation | async-start | bytes 4096 | tf_op jit(solution)/shard_map/all_to_all | solution.py:471
  13.7 6.2 %collective-permute-start.4 = (bf16[80,1152]{1,0:T(8,128)(2,1)S(1)}, bf16[80,1152]{1,0:T(8,128)(2,1)S(1)}, u32[]{:S(2)}, u32[]{:S(2)}) collective-permute-start(bf16[80,1152]{1,0:T(8,128)(2,1)S(1)} %collective-permute-done.refs_1_), channel_id=1, source_target_pairs={{0,1},{1,0},{2,3},{3,2},{4,5},{5,4},{6,7},{7,6},{8,9},{9,8},{10,11... | collective-permute-start | bytes 552968 | tf_op jit(solution)/shard_map/ppermute | solution.py:442
  16.3 3.6 %collective-permute-start.5 = (bf16[80,1152]{1,0:T(8,128)(2,1)S(1)}, bf16[80,1152]{1,0:T(8,128)(2,1)S(1)}, u32[]{:S(2)}, u32[]{:S(2)}) collective-permute-start(bf16[80,1152]{1,0:T(8,128)(2,1)S(1)} %collective-permute-done.1.refs_2_), channel_id=1, source_target_pairs={{0,1},{1,0},{2,3},{3,2},{4,5},{5,4},{6,7},{7,6},{8,9},{9,8},{10,11... | collective-permute-start | bytes 552968 | tf_op jit(solution)/shard_map/ppermute | solution.py:442
  16.3 3.6 %collective-permute-start.6 = (bf16[80,1152]{1,0:T(8,128)(2,1)S(1)}, bf16[80,1152]{1,0:T(8,128)(2,1)S(1)}, u32[]{:S(2)}, u32[]{:S(2)}) collective-permute-start(bf16[80,1152]{1,0:T(8,128)(2,1)S(1)} %collective-permute-done.2.refs_3_), channel_id=1, source_target_pairs={{0,1},{1,0},{2,3},{3,2},{4,5},{5,4},{6,7},{7,6},{8,9},{9,8},{10,11... | collective-permute-start | bytes 552968 | tf_op jit(solution)/shard_map/ppermute | solution.py:442
  19.9 20.2 %copy-start.2 = (f32[1,320]{1,0:T(1,128)S(1)}, f32[1,320]{1,0:T(1,128)}, u32[]{:S(2)}) copy-start(f32[1,320]{1,0:T(1,128)} %reshape.135.early_ref.goal_ref) | copy-start | bytes 3844
  19.9 40.0 %copy-start.1 = (bf16[80,1152]{1,0:T(8,128)(2,1)S(1)}, bf16[80,1152]{1,0:T(8,128)(2,1)}, u32[]{:S(2)}) copy-start(bf16[80,1152]{1,0:T(8,128)(2,1)} %shard_map.149.refs_0_.hidden_ref) | copy-start | bytes 552964
  19.9 40.0 %copy-start.3 = (f32[1024]{0:T(1024)S(1)}, f32[1024]{0:T(1024)}, u32[]{:S(2)}) copy-start(f32[1024]{0:T(1024)} %param.23) | copy-start | bytes 12292
  36.8 45.7 %copy-start.5 = (s32[32]{0:T(128)S(1)}, s32[32]{0:T(128)}, u32[]{:S(2)}) copy-start(s32[32]{0:T(128)} %param.26) | copy-start | bytes 388
  36.8 3.3 %collective-permute-start.7 = (f32[4,80,1024]{2,1,0:T(8,128)}, f32[4,80,1024]{2,1,0:T(8,128)S(1)}, u32[]{:S(2)}, u32[]{:S(2)}) collective-permute-start(f32[4,80,1024]{2,1,0:T(8,128)} %get-tuple-element.14), channel_id=1, source_target_pairs={{0,1},{1,0},{2,3},{3,2},{4,5},{5,4},{6,7},{7,6},{8,9},{9,8},{10,11... | collective-permute-start | bytes 3932168 | tf_op jit(solution)/shard_map/ppermute | solution.py:442
  41.6 10.2 %collective-permute-start.8 = (f32[168,512]{1,0:T(8,128)S(1)}, f32[168,512]{1,0:T(8,128)S(1)}, u32[]{:S(2)}, u32[]{:S(2)}) collective-permute-start(f32[168,512]{1,0:T(8,128)S(1)} %get-tuple-element.16), channel_id=1, source_target_pairs={{0,2},{2,0},{4,6},{6,4},{1,3},{3,1},{5,7},{7,5},{8,10},{10,8},{12,... | collective-permute-start | bytes 1032200 | tf_op jit(solution)/shard_map/ppermute | solution.py:433
  43.1 9.8 %collective-permute-start.9 = (f32[168,512]{1,0:T(8,128)S(1)}, f32[168,512]{1,0:T(8,128)S(1)}, u32[]{:S(2)}, u32[]{:S(2)}) collective-permute-start(f32[168,512]{1,0:T(8,128)S(1)} %get-tuple-element.17), channel_id=1, source_target_pairs={{0,4},{2,6},{4,0},{6,2},{1,5},{3,7},{5,1},{7,3},{8,12},{10,14},{12... | collective-permute-start | bytes 1032200 | tf_op jit(solution)/shard_map/ppermute | solution.py:433
  53.0 6.9 %collective-permute-start.11 = (f32[88,512]{1,0:T(8,128)S(1)}, f32[88,512]{1,0:T(8,128)S(1)}, u32[]{:S(2)}, u32[]{:S(2)}) collective-permute-start(f32[88,512]{1,0:T(8,128)S(1)} %get-tuple-element.21), channel_id=1, source_target_pairs={{0,4},{2,6},{4,0},{6,2},{1,5},{3,7},{5,1},{7,3},{8,12},{10,14},{12... | collective-permute-start | bytes 540680 | tf_op jit(solution)/shard_map/ppermute | solution.py:433
  54.6 5.3 %collective-permute-start.10 = (f32[80,512]{1,0:T(8,128)S(1)}, f32[80,512]{1,0:T(8,128)S(1)}, u32[]{:S(2)}, u32[]{:S(2)}) collective-permute-start(f32[80,512]{1,0:T(8,128)S(1)} %get-tuple-element.20), channel_id=1, source_target_pairs={{0,2},{2,0},{4,6},{6,4},{1,3},{3,1},{5,7},{7,5},{8,10},{10,8},{12,... | collective-permute-start | bytes 491528 | tf_op jit(solution)/shard_map/ppermute | solution.py:433
  60.1 29.1 %copy-start.4 = (bf16[80,1024]{1,0:T(8,128)(2,1)}, bf16[80,1024]{1,0:T(8,128)(2,1)S(1)}, u32[]{:S(2)}) copy-start(bf16[80,1024]{1,0:T(8,128)(2,1)S(1)} %get-tuple-element.23.refs_0_) | copy-start | bytes 491524
  60.1 9.0 %collective-permute-start.12 = (bf16[80,1024]{1,0:T(8,128)(2,1)S(1)}, bf16[80,1024]{1,0:T(8,128)(2,1)S(1)}, u32[]{:S(2)}, u32[]{:S(2)}) collective-permute-start(bf16[80,1024]{1,0:T(8,128)(2,1)S(1)} %get-tuple-element.23.refs_0_), channel_id=1, source_target_pairs={{0,8},{8,16},{16,24},{24,0},{1,9},{9,17},{17,25},{25,1},{2,10},{10... | collective-permute-start | bytes 491528 | tf_op jit(solution)/shard_map/ppermute | solution.py:438
  60.7 12.4 %collective-permute-start.14 = (bf16[80,1024]{1,0:T(8,128)(2,1)S(1)}, bf16[80,1024]{1,0:T(8,128)(2,1)S(1)}, u32[]{:S(2)}, u32[]{:S(2)}) collective-permute-start(bf16[80,1024]{1,0:T(8,128)(2,1)S(1)} %get-tuple-element.23.refs_0_), channel_id=1, source_target_pairs={{0,16},{8,24},{16,0},{24,8},{1,17},{9,25},{17,1},{25,9},{2,18},{10... | collective-permute-start | bytes 491528 | tf_op jit(solution)/shard_map/ppermute | solution.py:438
  61.7 11.7 %collective-permute-start.16 = (bf16[80,1024]{1,0:T(8,128)(2,1)S(1)}, bf16[80,1024]{1,0:T(8,128)(2,1)S(1)}, u32[]{:S(2)}, u32[]{:S(2)}) collective-permute-start(bf16[80,1024]{1,0:T(8,128)(2,1)S(1)} %get-tuple-element.23.refs_0_), channel_id=1, source_target_pairs={{0,24},{8,0},{16,8},{24,16},{1,25},{9,1},{17,9},{25,17},{2,26},{10... | collective-permute-start | bytes 491528 | tf_op jit(solution)/shard_map/ppermute | solution.py:438
  64.0 10.3 %collective-permute-start.18 = (bf16[80,1024]{1,0:T(8,128)(2,1)S(1)}, bf16[80,1024]{1,0:T(8,128)(2,1)S(1)}, u32[]{:S(2)}, u32[]{:S(2)}) collective-permute-start(bf16[80,1024]{1,0:T(8,128)(2,1)S(1)} %get-tuple-element.23.refs_0_), channel_id=1, source_target_pairs={{0,2},{2,0},{4,6},{6,4},{1,3},{3,1},{5,7},{7,5},{8,10},{10,8},{12,... | collective-permute-start | bytes 491528 | tf_op jit(solution)/shard_map/ppermute | solution.py:433
  69.1 20.0 %copy-start.14 = (bf16[80,1024]{1,0:T(8,128)(2,1)}, bf16[80,1024]{1,0:T(8,128)(2,1)S(1)}, u32[]{:S(2)}) copy-start(bf16[80,1024]{1,0:T(8,128)(2,1)S(1)} %collective-permute-done.12.refs_1_) | copy-start | bytes 491524
  69.1 6.3 %collective-permute-start.26 = (bf16[80,1024]{1,0:T(8,128)(2,1)S(1)}, bf16[80,1024]{1,0:T(8,128)(2,1)S(1)}, u32[]{:S(2)}, u32[]{:S(2)}) collective-permute-start(bf16[80,1024]{1,0:T(8,128)(2,1)S(1)} %get-tuple-element.23.refs_0_), channel_id=1, source_target_pairs={{0,4},{2,6},{4,0},{6,2},{1,5},{3,7},{5,1},{7,3},{8,12},{10,14},{12... | collective-permute-start | bytes 491528 | tf_op jit(solution)/shard_map/ppermute | solution.py:433
  73.1 16.0 %copy-start.15 = (bf16[80,1024]{1,0:T(8,128)(2,1)}, bf16[80,1024]{1,0:T(8,128)(2,1)S(1)}, u32[]{:S(2)}) copy-start(bf16[80,1024]{1,0:T(8,128)(2,1)S(1)} %collective-permute-done.14.refs_2_) | copy-start | bytes 491524
  73.1 7.1 %collective-permute-start.13 = (bf16[80,1024]{1,0:T(8,128)(2,1)S(1)}, bf16[80,1024]{1,0:T(8,128)(2,1)S(1)}, u32[]{:S(2)}, u32[]{:S(2)}) collective-permute-start(bf16[80,1024]{1,0:T(8,128)(2,1)S(1)} %collective-permute-done.12.refs_1_), channel_id=1, source_target_pairs={{0,4},{2,6},{4,0},{6,2},{1,5},{3,7},{5,1},{7,3},{8,12},{10,14},{12... | collective-permute-start | bytes 491528 | tf_op jit(solution)/shard_map/ppermute | solution.py:433
  73.4 15.8 %copy-start.16 = (bf16[80,1024]{1,0:T(8,128)(2,1)}, bf16[80,1024]{1,0:T(8,128)(2,1)S(1)}, u32[]{:S(2)}) copy-start(bf16[80,1024]{1,0:T(8,128)(2,1)S(1)} %collective-permute-done.16.refs_3_) | copy-start | bytes 491524
  73.4 7.1 %collective-permute-start.20 = (bf16[80,1024]{1,0:T(8,128)(2,1)S(1)}, bf16[80,1024]{1,0:T(8,128)(2,1)S(1)}, u32[]{:S(2)}, u32[]{:S(2)}) collective-permute-start(bf16[80,1024]{1,0:T(8,128)(2,1)S(1)} %collective-permute-done.12.refs_1_), channel_id=1, source_target_pairs={{0,2},{2,0},{4,6},{6,4},{1,3},{3,1},{5,7},{7,5},{8,10},{10,8},{12,... | collective-permute-start | bytes 491528 | tf_op jit(solution)/shard_map/ppermute | solution.py:433
  74.3 14.9 %copy-start.18 = (bf16[80,1024]{1,0:T(8,128)(2,1)}, bf16[80,1024]{1,0:T(8,128)(2,1)S(1)}, u32[]{:S(2)}) copy-start(bf16[80,1024]{1,0:T(8,128)(2,1)S(1)} %collective-permute-done.18.refs_4_) | copy-start | bytes 491524
  74.3 10.3 %collective-permute-start.24 = (bf16[80,1024]{1,0:T(8,128)(2,1)S(1)}, bf16[80,1024]{1,0:T(8,128)(2,1)S(1)}, u32[]{:S(2)}, u32[]{:S(2)}) collective-permute-start(bf16[80,1024]{1,0:T(8,128)(2,1)S(1)} %collective-permute-done.14.refs_2_), channel_id=1, source_target_pairs={{0,2},{2,0},{4,6},{6,4},{1,3},{3,1},{5,7},{7,5},{8,10},{10,8},{12,... | collective-permute-start | bytes 491528 | tf_op jit(solution)/shard_map/ppermute | solution.py:433
  75.5 11.2 %collective-permute-start.15 = (bf16[80,1024]{1,0:T(8,128)(2,1)S(1)}, bf16[80,1024]{1,0:T(8,128)(2,1)S(1)}, u32[]{:S(2)}, u32[]{:S(2)}) collective-permute-start(bf16[80,1024]{1,0:T(8,128)(2,1)S(1)} %collective-permute-done.14.refs_2_), channel_id=1, source_target_pairs={{0,4},{2,6},{4,0},{6,2},{1,5},{3,7},{5,1},{7,3},{8,12},{10,14},{12... | collective-permute-start | bytes 491528 | tf_op jit(solution)/shard_map/ppermute | solution.py:433
  80.3 5.3 %collective-permute-start.25 = (bf16[80,1024]{1,0:T(8,128)(2,1)S(1)}, bf16[80,1024]{1,0:T(8,128)(2,1)S(1)}, u32[]{:S(2)}, u32[]{:S(2)}) collective-permute-start(bf16[80,1024]{1,0:T(8,128)(2,1)S(1)} %collective-permute-done.16.refs_3_), channel_id=1, source_target_pairs={{0,2},{2,0},{4,6},{6,4},{1,3},{3,1},{5,7},{7,5},{8,10},{10,8},{12,... | collective-permute-start | bytes 491528 | tf_op jit(solution)/shard_map/ppermute | solution.py:433
  80.5 7.1 %collective-permute-start.17 = (bf16[80,1024]{1,0:T(8,128)(2,1)S(1)}, bf16[80,1024]{1,0:T(8,128)(2,1)S(1)}, u32[]{:S(2)}, u32[]{:S(2)}) collective-permute-start(bf16[80,1024]{1,0:T(8,128)(2,1)S(1)} %collective-permute-done.16.refs_3_), channel_id=1, source_target_pairs={{0,4},{2,6},{4,0},{6,2},{1,5},{3,7},{5,1},{7,3},{8,12},{10,14},{12... | collective-permute-start | bytes 491528 | tf_op jit(solution)/shard_map/ppermute | solution.py:433
  84.6 19.1 %collective-permute-start.19 = (bf16[80,1024]{1,0:T(8,128)(2,1)S(1)}, bf16[80,1024]{1,0:T(8,128)(2,1)S(1)}, u32[]{:S(2)}, u32[]{:S(2)}) collective-permute-start(bf16[80,1024]{1,0:T(8,128)(2,1)S(1)} %collective-permute-done.18.refs_4_), channel_id=1, source_target_pairs={{0,4},{2,6},{4,0},{6,2},{1,5},{3,7},{5,1},{7,3},{8,12},{10,14},{12... | collective-permute-start | bytes 491528 | tf_op jit(solution)/shard_map/ppermute | solution.py:433
  85.6 18.1 %collective-permute-start.21 = (bf16[80,1024]{1,0:T(8,128)(2,1)S(1)}, bf16[80,1024]{1,0:T(8,128)(2,1)S(1)}, u32[]{:S(2)}, u32[]{:S(2)}) collective-permute-start(bf16[80,1024]{1,0:T(8,128)(2,1)S(1)} %collective-permute-done.20.refs_5_), channel_id=1, source_target_pairs={{0,4},{2,6},{4,0},{6,2},{1,5},{3,7},{5,1},{7,3},{8,12},{10,14},{12... | collective-permute-start | bytes 491528 | tf_op jit(solution)/shard_map/ppermute | solution.py:433
  86.6 17.0 %copy-start.21 = (bf16[80,1024]{1,0:T(8,128)(2,1)}, bf16[80,1024]{1,0:T(8,128)(2,1)S(1)}, u32[]{:S(2)}) copy-start(bf16[80,1024]{1,0:T(8,128)(2,1)S(1)} %collective-permute-done.15.refs_1_) | copy-start | bytes 491524
  86.6 17.1 %collective-permute-start.22 = (bf16[80,1024]{1,0:T(8,128)(2,1)S(1)}, bf16[80,1024]{1,0:T(8,128)(2,1)S(1)}, u32[]{:S(2)}, u32[]{:S(2)}) collective-permute-start(bf16[80,1024]{1,0:T(8,128)(2,1)S(1)} %collective-permute-done.15.refs_1_), channel_id=1, source_target_pairs={{0,2},{2,0},{4,6},{6,4},{1,3},{3,1},{5,7},{7,5},{8,10},{10,8},{12,... | collective-permute-start | bytes 491528 | tf_op jit(solution)/shard_map/ppermute | solution.py:433
  87.6 16.0 %copy-start.23 = (bf16[80,1024]{1,0:T(8,128)(2,1)}, bf16[80,1024]{1,0:T(8,128)(2,1)S(1)}, u32[]{:S(2)}) copy-start(bf16[80,1024]{1,0:T(8,128)(2,1)S(1)} %collective-permute-done.17.refs_2_) | copy-start | bytes 491524
  87.6 16.1 %collective-permute-start.23 = (bf16[80,1024]{1,0:T(8,128)(2,1)S(1)}, bf16[80,1024]{1,0:T(8,128)(2,1)S(1)}, u32[]{:S(2)}, u32[]{:S(2)}) collective-permute-start(bf16[80,1024]{1,0:T(8,128)(2,1)S(1)} %collective-permute-done.17.refs_2_), channel_id=1, source_target_pairs={{0,2},{2,0},{4,6},{6,4},{1,3},{3,1},{5,7},{7,5},{8,10},{10,8},{12,... | collective-permute-start | bytes 491528 | tf_op jit(solution)/shard_map/ppermute | solution.py:433
  103.7 21.1 %copy-start.6 = (s32[32]{0:T(128)S(1)}, s32[32]{0:T(128)}, u32[]{:S(2)}) copy-start(s32[32]{0:T(128)} %param.27) | copy-start | bytes 388
  118.3 7.8 %collective-permute-start.28 = (f32[16,2,80]{2,0,1:T(8,128)S(1)}, f32[16,2,80]{2,0,1:T(8,128)S(1)}, u32[]{:S(2)}, u32[]{:S(2)}) collective-permute-start(f32[16,2,80]{2,0,1:T(8,128)S(1)} %copy.37), channel_id=1, source_target_pairs={{0,8},{8,16},{16,24},{24,0},{1,9},{9,17},{17,25},{25,1},{2,10},{10... | collective-permute-start | bytes 30728 | tf_op jit(solution)/shard_map/ppermute | solution.py:438
  120.3 5.8 %collective-permute-start.29 = (f32[16,2,80]{2,0,1:T(8,128)S(1)}, f32[16,2,80]{2,0,1:T(8,128)S(1)}, u32[]{:S(2)}, u32[]{:S(2)}) collective-permute-start(f32[16,2,80]{2,0,1:T(8,128)S(1)} %copy.37), channel_id=1, source_target_pairs={{0,16},{8,24},{16,0},{24,8},{1,17},{9,25},{17,1},{25,9},{2,18},{10... | collective-permute-start | bytes 30728 | tf_op jit(solution)/shard_map/ppermute | solution.py:438
  122.2 4.0 %collective-permute-start.30 = (f32[16,2,80]{2,0,1:T(8,128)S(1)}, f32[16,2,80]{2,0,1:T(8,128)S(1)}, u32[]{:S(2)}, u32[]{:S(2)}) collective-permute-start(f32[16,2,80]{2,0,1:T(8,128)S(1)} %copy.37), channel_id=1, source_target_pairs={{0,24},{8,0},{16,8},{24,16},{1,25},{9,1},{17,9},{25,17},{2,26},{10... | collective-permute-start | bytes 30728 | tf_op jit(solution)/shard_map/ppermute | solution.py:438
  126.2 5.5 %collective-permute-start.31 = (f32[16,2,80]{2,0,1:T(8,128)S(1)}, f32[16,2,80]{2,0,1:T(8,128)S(1)}, u32[]{:S(2)}, u32[]{:S(2)}) collective-permute-start(f32[16,2,80]{2,0,1:T(8,128)S(1)} %pad_maximum_fusion), channel_id=1, source_target_pairs={{0,2},{2,0},{4,6},{6,4},{1,3},{3,1},{5,7},{7,5},{8,10},{10,8},{12,... | collective-permute-start | bytes 30728 | tf_op jit(solution)/shard_map/ppermute | solution.py:433
  127.3 4.4 %collective-permute-start.32 = (f32[16,2,80]{2,0,1:T(8,128)S(1)}, f32[16,2,80]{2,0,1:T(8,128)S(1)}, u32[]{:S(2)}, u32[]{:S(2)}) collective-permute-start(f32[16,2,80]{2,0,1:T(8,128)S(1)} %pad_maximum_fusion), channel_id=1, source_target_pairs={{0,4},{2,6},{4,0},{6,2},{1,5},{3,7},{5,1},{7,3},{8,12},{10,14},{12... | collective-permute-start | bytes 30728 | tf_op jit(solution)/shard_map/ppermute | solution.py:433
  128.7 4.6 %collective-permute-start.33 = (f32[16,2,80]{2,0,1:T(8,128)S(1)}, f32[16,2,80]{2,0,1:T(8,128)S(1)}, u32[]{:S(2)}, u32[]{:S(2)}) collective-permute-start(f32[16,2,80]{2,0,1:T(8,128)S(1)} %pad_maximum_fusion), channel_id=1, source_target_pairs={{0,6},{2,4},{4,2},{6,0},{1,7},{3,5},{5,3},{7,1},{8,14},{10,12},{12... | collective-permute-start | bytes 30728 | tf_op jit(solution)/shard_map/ppermute | solution.py:433
  133.5 1.2 collective-permute-start.34
  (17 other events, 60.4 us)

commit v9 on v8

--- a/solution.py
+++ b/solution.py
@@ -515,16 +515,8 @@
 
     if chips == 4:
         blocks = column + near + far + cross
-        cut = max(256, (3 * lines - share) // 256 * 256)
-        before, after = [], []
-        for index, block in enumerate(blocks):
-            border = min(max(cut - index * share, 0), share)
-            if border > 0:
-                before.append((block, (0, border)))
-            if border < share:
-                after.append((block, (border, share)))
-        first = stats_of(spots, 0, before, (), (2, cut))
-        stats = stats_of(spots, cut, after, (first,), (groups * chips, 2, share))
+        pieces = [(block, (0, share)) for block in blocks]
+        stats = stats_of(spots, 0, pieces, (), (groups * chips, 2, share))
     else:
         fixed = jnp.arange(groups, dtype=jnp.int32)
         pieces = [

time: 138 us -> 134 us (0.971)
  Pallas kernels: 44.3 us -> 37.2 us
  waiting for transfers between devices: 35.1 us -> 38.3 us
  local copies, waits for them, and re-layouts: 8.87 us -> 7.42 us
    pallas_call x2 -> x1, Pallas kernels: 26.8 us -> 19.8 us  [head_stats(): pl.pallas_call(functools.partial(head_kernel, parts, len(earlier)), out_s...]
    ppermute x22, waiting for transfers between devices: 21.4 us -> 24.6 us  [across(): return lax.ppermute(value, 'chip', [(c, c ^ offset) for c in range(chips)])]
  transfers between devices with their start and end apart: 36 -> 36, of which waited for: 14 -> 15; matrix products, arithmetic and copies ran while one was open for 5% -> 5% of each run, Pallas kernels for 23% -> 13%
where the time goes in v9:
time: 134 us
  starting transfers between devices  41.2 us (31%)
  waiting for transfers between devices  38.3 us (29%)
  Pallas kernels  37.2 us (28%)
  local copies, waits for them, and re-layouts  7.42 us (6%)
  between operations  4.76 us (4%)
  other arithmetic  4.65 us (3%)
    ppermute x22, waiting for transfers between devices, across(): return lax.ppermute(value, 'chip', [(c, c ^ offset) for c in range(chips)])  24.6 us
    ppermute x22, starting transfers between devices, across(): return lax.ppermute(value, 'chip', [(c, c ^ offset) for c in range(chips)])  23.6 us
    pallas_call x1, Pallas kernels, head_stats(): pl.pallas_call(functools.partial(head_kernel, parts, len(earlier)), out_s...  19.8 us
    pallas_call x1, Pallas kernels, expert_sums(): pl.pallas_call(functools.partial(expert_kernel, block, slots, width, expe...  15.4 us
    ppermute x6, starting transfers between devices, along(): lax.ppermute(value, 'grp', [(g, (g + offset) % groups) for g in range(gro...  10.9 us
    ppermute x6, waiting for transfers between devices, along(): lax.ppermute(value, 'grp', [(g, (g + offset) % groups) for g in range(gro...  8.14 us
    all_to_all x1, starting transfers between devices, local(): goal = lax.all_to_all(goal, 'grp', split_axis=0, concat_axis=0, tiled=True)  5.34 us
    ppermute x7, waiting for transfers between devices, partner(): return lax.ppermute(value, 'core', ((0, 1), (1, 0)))  3.88 us
  transfers between devices with their start and end apart: 36, of which 15 were waited for; matrix products, arithmetic and copies ran while one was open for 5% of the time, Pallas kernels for 13%

profile of v9, /device:TPU:0, one launch (start us, length us, event | category | flops | bytes accessed | tf_op | source)
XLA Modules:
  0.0 133.5 jit_solution(6119644113150415975)
XLA Ops:
  1.1 1.8 %shard_map.149.refs_0_.hidden_ref = bf16[80,1152]{1,0:T(8,128)(2,1)} custom-call(bf16[40,1024]{1,0:T(8,128)(2,1)} %pol_ref.1, bf16[40,1024]{1,0:T(8,128)(2,1)} %ref_ref.1, s32[8,40]{1,0:T(8,128)} %bitcast.103, s32[8,40]{1,0:T(8,128)} %bitcast.104, f32[8,40]{1,0:T(8,128)} %bitcast.105, f32[8,40]{1,0:T(8,128)} %bitcast.106), custom_call_target="tpu_custom_call" | custom-call | tf_op jit(solution)/shard_map/pallas_call | solution.py:47
  2.9 2.5 %collective-permute-start = (bf16[80,1152]{1,0:T(8,128)(2,1)}, bf16[80,1152]{1,0:T(8,128)(2,1)S(1)}, u32[]{:S(2)}, u32[]{:S(2)}) collective-permute-start(bf16[80,1152]{1,0:T(8,128)(2,1)} %shard_map.149.refs_0_.hidden_ref), channel_id=1, source_target_pairs={{0,2},{2,0},{4,6},{6,4},{1,3},{3,1},{5,7},{7,5},{8,10},{10,8},{12,... | collective-permute-start | bytes 552968 | tf_op jit(solution)/shard_map/ppermute | solution.py:433
  5.4 1.5 %collective-permute-start.1 = (bf16[80,1152]{1,0:T(8,128)(2,1)}, bf16[80,1152]{1,0:T(8,128)(2,1)S(1)}, u32[]{:S(2)}, u32[]{:S(2)}) collective-permute-start(bf16[80,1152]{1,0:T(8,128)(2,1)} %shard_map.149.refs_0_.hidden_ref), channel_id=1, source_target_pairs={{0,4},{2,6},{4,0},{6,2},{1,5},{3,7},{5,1},{7,3},{8,12},{10,14},{12... | collective-permute-start | bytes 552968 | tf_op jit(solution)/shard_map/ppermute | solution.py:433
  6.9 0.7 convert_bitcast_fusion
  7.7 0.6 broadcast_in_dim.46
  8.3 5.3 %all-to-all-start = ((f32[4,1,80]{2,1,0:T(1,128)}), f32[4,1,80]{2,1,0:T(1,128)S(1)}, u32[]{:S(2)}, u32[]{:S(2)}) async-start(f32[4,1,80]{2,1,0:T(1,128)} %broadcast_in_dim.46), calls=%async_computation | async-start | bytes 4096 | tf_op jit(solution)/shard_map/all_to_all | solution.py:471
  14.0 2.4 %collective-permute-done.1.refs_2_ = bf16[80,1152]{1,0:T(8,128)(2,1)S(1)} collective-permute-done((bf16[80,1152]{1,0:T(8,128)(2,1)}, bf16[80,1152]{1,0:T(8,128)(2,1)S(1)}, u32[]{:S(2)}, u32[]{:S(2)}) %collective-permute-start.1) | collective-permute-done | bytes 184352 | tf_op jit(solution)/shard_map/ppermute | solution.py:433
  16.8 0.6 pad_add_fusion.1.place_ref
  17.5 1.7 %all-to-all-done = f32[4,1,80]{2,1,0:T(1,128)S(1)} async-done(((f32[4,1,80]{2,1,0:T(1,128)}), f32[4,1,80]{2,1,0:T(1,128)S(1)}, u32[]{:S(2)}, u32[]{:S(2)}) %all-to-all-start) | async-done | bytes 1312 | tf_op jit(solution)/shard_map/all_to_all | solution.py:471
  19.2 0.7 reshape.135.early_ref.goal_ref
  20.8 0.7 copy-done.13
  21.4 15.4 %shard_map.150 = (f32[4,80,1024]{2,1,0:T(8,128)}, f32[4,80,1024]{2,1,0:T(8,128)}) custom-call(s32[2]{0:T(128)} %pad_add_fusion.1.place_ref, f32[1,320]{1,0:T(1,128)} %reshape.135.early_ref.goal_ref, bf16[80,1152]{1,0:T(8,128)(2,1)} %shard_map.149.refs_0_.hidden_ref, bf16[80,1152]{1,0:T(8,128)(2,1)} %copy-done.7, bf16[80,1152]{1,0:T(8,128)(2,1)} %copy-done.8, ...), custom_call_target="tpu_custom_call" | custom-call | flops 6442450944 | bytes 22970368 | tf_op jit(solution)/shard_map/pallas_call | solution.py:156
  36.9 3.2 %collective-permute-done.7.came_ref = f32[4,80,1024]{2,1,0:T(8,128)S(1)} collective-permute-done((f32[4,80,1024]{2,1,0:T(8,128)}, f32[4,80,1024]{2,1,0:T(8,128)S(1)}, u32[]{:S(2)}, u32[]{:S(2)}) %collective-permute-start.7) | collective-permute-done | bytes 1310752 | tf_op jit(solution)/shard_map/ppermute | solution.py:442
  40.1 1.3 copy-done
  41.6 1.6 %collective-permute-start.8 = (f32[168,512]{1,0:T(8,128)S(1)}, f32[168,512]{1,0:T(8,128)S(1)}, u32[]{:S(2)}, u32[]{:S(2)}) collective-permute-start(f32[168,512]{1,0:T(8,128)S(1)} %get-tuple-element.16), channel_id=1, source_target_pairs={{0,2},{2,0},{4,6},{6,4},{1,3},{3,1},{5,7},{7,5},{8,10},{10,8},{12,... | collective-permute-start | bytes 1032200 | tf_op jit(solution)/shard_map/ppermute | solution.py:433
  43.1 1.5 %collective-permute-start.9 = (f32[168,512]{1,0:T(8,128)S(1)}, f32[168,512]{1,0:T(8,128)S(1)}, u32[]{:S(2)}, u32[]{:S(2)}) collective-permute-start(f32[168,512]{1,0:T(8,128)S(1)} %get-tuple-element.17), channel_id=1, source_target_pairs={{0,4},{2,6},{4,0},{6,2},{1,5},{3,7},{5,1},{7,3},{8,12},{10,14},{12... | collective-permute-start | bytes 1032200 | tf_op jit(solution)/shard_map/ppermute | solution.py:433
  44.7 7.1 %collective-permute-done.8.from_x = f32[168,512]{1,0:T(8,128)S(1)} collective-permute-done((f32[168,512]{1,0:T(8,128)S(1)}, f32[168,512]{1,0:T(8,128)S(1)}, u32[]{:S(2)}, u32[]{:S(2)}) %collective-permute-start.8) | collective-permute-done | bytes 344096 | tf_op jit(solution)/shard_map/ppermute | solution.py:433
  51.8 1.2 collective-permute-done.9.from_y
  53.0 1.6 %collective-permute-start.11 = (f32[88,512]{1,0:T(8,128)S(1)}, f32[88,512]{1,0:T(8,128)S(1)}, u32[]{:S(2)}, u32[]{:S(2)}) collective-permute-start(f32[88,512]{1,0:T(8,128)S(1)} %get-tuple-element.21), channel_id=1, source_target_pairs={{0,4},{2,6},{4,0},{6,2},{1,5},{3,7},{5,1},{7,3},{8,12},{10,14},{12... | collective-permute-start | bytes 540680 | tf_op jit(solution)/shard_map/ppermute | solution.py:433
  55.1 4.8 %collective-permute-done.10.last_x = f32[80,512]{1,0:T(8,128)S(1)} collective-permute-done((f32[80,512]{1,0:T(8,128)S(1)}, f32[80,512]{1,0:T(8,128)S(1)}, u32[]{:S(2)}, u32[]{:S(2)}) %collective-permute-start.10) | collective-permute-done | bytes 163872 | tf_op jit(solution)/shard_map/ppermute | solution.py:433
  60.1 0.6 collective-permute-start.12
  60.7 0.9 collective-permute-start.13
  61.7 2.3 %collective-permute-start.14 = (bf16[80,1024]{1,0:T(8,128)(2,1)S(1)}, bf16[80,1024]{1,0:T(8,128)(2,1)S(1)}, u32[]{:S(2)}, u32[]{:S(2)}) collective-permute-start(bf16[80,1024]{1,0:T(8,128)(2,1)S(1)} %get-tuple-element.23.refs_0_), channel_id=1, source_target_pairs={{0,24},{8,0},{16,8},{24,16},{1,25},{9,1},{17,9},{25,17},{2,26},{10... | collective-permute-start | bytes 491528 | tf_op jit(solution)/shard_map/ppermute | solution.py:438
  64.5 4.6 %collective-permute-done.12.refs_1_ = bf16[80,1024]{1,0:T(8,128)(2,1)S(1)} collective-permute-done((bf16[80,1024]{1,0:T(8,128)(2,1)S(1)}, bf16[80,1024]{1,0:T(8,128)(2,1)S(1)}, u32[]{:S(2)}, u32[]{:S(2)}) %collective-permute-start.12) | collective-permute-done | bytes 163872 | tf_op jit(solution)/shard_map/ppermute | solution.py:438
  69.7 3.5 %collective-permute-done.13.refs_2_ = bf16[80,1024]{1,0:T(8,128)(2,1)S(1)} collective-permute-done((bf16[80,1024]{1,0:T(8,128)(2,1)S(1)}, bf16[80,1024]{1,0:T(8,128)(2,1)S(1)}, u32[]{:S(2)}, u32[]{:S(2)}) %collective-permute-start.13) | collective-permute-done | bytes 163872 | tf_op jit(solution)/shard_map/ppermute | solution.py:438
  73.1 0.6 collective-permute-start.16
  74.3 1.2 collective-permute-start.17
  75.5 1.8 %collective-permute-start.22 = (bf16[80,1024]{1,0:T(8,128)(2,1)S(1)}, bf16[80,1024]{1,0:T(8,128)(2,1)S(1)}, u32[]{:S(2)}, u32[]{:S(2)}) collective-permute-start(bf16[80,1024]{1,0:T(8,128)(2,1)S(1)} %collective-permute-done.14.refs_3_), channel_id=1, source_target_pairs={{0,4},{2,6},{4,0},{6,2},{1,5},{3,7},{5,1},{7,3},{8,12},{10,14},{12... | collective-permute-start | bytes 491528 | tf_op jit(solution)/shard_map/ppermute | solution.py:433
  77.3 3.0 %collective-permute-done.16.refs_5_ = bf16[80,1024]{1,0:T(8,128)(2,1)S(1)} collective-permute-done((bf16[80,1024]{1,0:T(8,128)(2,1)S(1)}, bf16[80,1024]{1,0:T(8,128)(2,1)S(1)}, u32[]{:S(2)}, u32[]{:S(2)}) %collective-permute-start.16) | collective-permute-done | bytes 163872 | tf_op jit(solution)/shard_map/ppermute | solution.py:433
  80.3 0.6 collective-permute-start.18
  81.4 3.0 %collective-permute-done.22.refs_11_ = bf16[80,1024]{1,0:T(8,128)(2,1)S(1)} collective-permute-done((bf16[80,1024]{1,0:T(8,128)(2,1)S(1)}, bf16[80,1024]{1,0:T(8,128)(2,1)S(1)}, u32[]{:S(2)}, u32[]{:S(2)}) %collective-permute-start.22) | collective-permute-done | bytes 163872 | tf_op jit(solution)/shard_map/ppermute | solution.py:433
  84.9 1.6 %collective-permute-start.24 = (bf16[80,1024]{1,0:T(8,128)(2,1)S(1)}, bf16[80,1024]{1,0:T(8,128)(2,1)S(1)}, u32[]{:S(2)}, u32[]{:S(2)}) collective-permute-start(bf16[80,1024]{1,0:T(8,128)(2,1)S(1)} %collective-permute-done.16.refs_5_), channel_id=1, source_target_pairs={{0,4},{2,6},{4,0},{6,2},{1,5},{3,7},{5,1},{7,3},{8,12},{10,14},{12... | collective-permute-start | bytes 491528 | tf_op jit(solution)/shard_map/ppermute | solution.py:433
  86.4 1.2 collective-permute-start.25
  88.0 1.4 %collective-permute-start.26 = (bf16[80,1024]{1,0:T(8,128)(2,1)S(1)}, bf16[80,1024]{1,0:T(8,128)(2,1)S(1)}, u32[]{:S(2)}, u32[]{:S(2)}) collective-permute-start(bf16[80,1024]{1,0:T(8,128)(2,1)S(1)} %collective-permute-done.22.refs_11_), channel_id=1, source_target_pairs={{0,2},{2,0},{4,6},{6,4},{1,3},{3,1},{5,7},{7,5},{8,10},{10,8},{12,... | collective-permute-start | bytes 491528 | tf_op jit(solution)/shard_map/ppermute | solution.py:433
  90.5 0.7 reshape.136.wanted_ref
  91.2 1.0 collective-permute-done.24.refs_13_
  92.2 1.3 collective-permute-done.26.refs_15_
  94.2 19.8 %shard_map.154 = f32[16,2,80]{2,1,0:T(2,128)} custom-call(s32[18]{0:T(128)} %pad_add_fusion.spots_ref, s32[1,1280]{1,0:T(1,128)} %reshape.136.wanted_ref, bf16[80,1024]{1,0:T(8,128)(2,1)} %copy-done.4, bf16[80,1024]{1,0:T(8,128)(2,1)} %copy-done.14, bf16[80,1024]{1,0:T(8,128)(2,1)} %copy-done.15, bf16[80,1024]{1,0:T(8,128)(2,1)} %copy-done.16, ...), custom_call_target="tpu_custom_call" | custom-call | flops 12750684160 | bytes 12582912 | tf_op jit(solution)/shard_map/pallas_call | solution.py:391
  114.0 0.7 copy.37
  114.7 2.7 %collective-permute-start.28 = (f32[16,2,80]{2,0,1:T(8,128)S(1)}, f32[16,2,80]{2,0,1:T(8,128)S(1)}, u32[]{:S(2)}, u32[]{:S(2)}) collective-permute-start(f32[16,2,80]{2,0,1:T(8,128)S(1)} %copy.37), channel_id=1, source_target_pairs={{0,8},{8,16},{16,24},{24,0},{1,9},{9,17},{17,25},{25,1},{2,10},{10... | collective-permute-start | bytes 30728 | tf_op jit(solution)/shard_map/ppermute | solution.py:438
  117.4 2.0 %collective-permute-start.29 = (f32[16,2,80]{2,0,1:T(8,128)S(1)}, f32[16,2,80]{2,0,1:T(8,128)S(1)}, u32[]{:S(2)}, u32[]{:S(2)}) collective-permute-start(f32[16,2,80]{2,0,1:T(8,128)S(1)} %copy.37), channel_id=1, source_target_pairs={{0,16},{8,24},{16,0},{24,8},{1,17},{9,25},{17,1},{25,9},{2,18},{10... | collective-permute-start | bytes 30728 | tf_op jit(solution)/shard_map/ppermute | solution.py:438
  119.4 2.3 %collective-permute-start.30 = (f32[16,2,80]{2,0,1:T(8,128)S(1)}, f32[16,2,80]{2,0,1:T(8,128)S(1)}, u32[]{:S(2)}, u32[]{:S(2)}) collective-permute-start(f32[16,2,80]{2,0,1:T(8,128)S(1)} %copy.37), channel_id=1, source_target_pairs={{0,24},{8,0},{16,8},{24,16},{1,25},{9,1},{17,9},{25,17},{2,26},{10... | collective-permute-start | bytes 30728 | tf_op jit(solution)/shard_map/ppermute | solution.py:438
  121.7 0.7 fusion.19
  122.4 0.7 slice.75
  123.2 0.8 collective-permute-start.31
  124.5 2.3 %collective-permute-start.33 = (f32[16,2,80]{2,0,1:T(8,128)S(1)}, f32[16,2,80]{2,0,1:T(8,128)S(1)}, u32[]{:S(2)}, u32[]{:S(2)}) collective-permute-start(f32[16,2,80]{2,0,1:T(8,128)S(1)} %pad_maximum_fusion), channel_id=1, source_target_pairs={{0,6},{2,4},{4,2},{6,0},{1,7},{3,5},{5,3},{7,1},{8,14},{10,12},{12... | collective-permute-start | bytes 30728 | tf_op jit(solution)/shard_map/ppermute | solution.py:433
  129.8 0.6 collective-permute-done.34
  130.4 1.4 %add_reduce_fusion = f32[]{:T(128)} fusion(f32[16,40]{1,0:T(8,128)S(1)} %collective-permute-done.34, s32[16]{0:T(128)S(1)} %get-tuple-element.30, s32[]{:T(128)} %get-tuple-element.25, s32[]{:T(128)S(6)} %sub.89, s32[16]{0:T(128)S(1)} %get-tuple-element.31, f32[16,80]{1,0:T(8,128)S(1)} %fusion.1), kind=kLoop, calls=%fused_computation.29 | loop fusion | flops 8319 | bytes 7820 | tf_op jit(solution)/shard_map/reduce_sum | solution.py:547
  (115 shorter events, 9.2 us)
Async XLA Ops:
  0.6 92.9 %collective-permute-start.27 = (bf16[2432,1024]{1,0:T(8,128)(2,1)}, bf16[2432,1024]{1,0:T(8,128)(2,1)}, u32[]{:S(2)}, u32[]{:S(2)}) collective-permute-start(bf16[2432,1024]{1,0:T(8,128)(2,1)} %refs_16_.1), channel_id=1, source_target_pairs={{0,1},{1,0},{2,3},{3,2},{4,5},{5,4},{6,7},{7,6},{8,9},{9,8},{10,11... | collective-permute-start | bytes 14942216 | tf_op jit(solution)/shard_map/ppermute | solution.py:442
  2.9 10.8 %collective-permute-start = (bf16[80,1152]{1,0:T(8,128)(2,1)}, bf16[80,1152]{1,0:T(8,128)(2,1)S(1)}, u32[]{:S(2)}, u32[]{:S(2)}) collective-permute-start(bf16[80,1152]{1,0:T(8,128)(2,1)} %shard_map.149.refs_0_.hidden_ref), channel_id=1, source_target_pairs={{0,2},{2,0},{4,6},{6,4},{1,3},{3,1},{5,7},{7,5},{8,10},{10,8},{12,... | collective-permute-start | bytes 552968 | tf_op jit(solution)/shard_map/ppermute | solution.py:433
  5.4 10.9 %collective-permute-start.1 = (bf16[80,1152]{1,0:T(8,128)(2,1)}, bf16[80,1152]{1,0:T(8,128)(2,1)S(1)}, u32[]{:S(2)}, u32[]{:S(2)}) collective-permute-start(bf16[80,1152]{1,0:T(8,128)(2,1)} %shard_map.149.refs_0_.hidden_ref), channel_id=1, source_target_pairs={{0,4},{2,6},{4,0},{6,2},{1,5},{3,7},{5,1},{7,3},{8,12},{10,14},{12... | collective-permute-start | bytes 552968 | tf_op jit(solution)/shard_map/ppermute | solution.py:433
  6.9 9.4 %collective-permute-start.2 = (bf16[80,1152]{1,0:T(8,128)(2,1)}, bf16[80,1152]{1,0:T(8,128)(2,1)S(1)}, u32[]{:S(2)}, u32[]{:S(2)}) collective-permute-start(bf16[80,1152]{1,0:T(8,128)(2,1)} %shard_map.149.refs_0_.hidden_ref), channel_id=1, source_target_pairs={{0,6},{2,4},{4,2},{6,0},{1,7},{3,5},{5,3},{7,1},{8,14},{10,12},{12... | collective-permute-start | bytes 552968 | tf_op jit(solution)/shard_map/ppermute | solution.py:433
  6.9 13.0 %collective-permute-start.3 = (bf16[80,1152]{1,0:T(8,128)(2,1)}, bf16[80,1152]{1,0:T(8,128)(2,1)S(1)}, u32[]{:S(2)}, u32[]{:S(2)}) collective-permute-start(bf16[80,1152]{1,0:T(8,128)(2,1)} %shard_map.149.refs_0_.hidden_ref), channel_id=1, source_target_pairs={{0,1},{1,0},{2,3},{3,2},{4,5},{5,4},{6,7},{7,6},{8,9},{9,8},{10,11... | collective-permute-start | bytes 552968 | tf_op jit(solution)/shard_map/ppermute | solution.py:442
  8.3 10.9 %all-to-all-start = ((f32[4,1,80]{2,1,0:T(1,128)}), f32[4,1,80]{2,1,0:T(1,128)S(1)}, u32[]{:S(2)}, u32[]{:S(2)}) async-start(f32[4,1,80]{2,1,0:T(1,128)} %broadcast_in_dim.46), calls=%async_computation | async-start | bytes 4096 | tf_op jit(solution)/shard_map/all_to_all | solution.py:471
  13.7 6.2 %collective-permute-start.4 = (bf16[80,1152]{1,0:T(8,128)(2,1)S(1)}, bf16[80,1152]{1,0:T(8,128)(2,1)S(1)}, u32[]{:S(2)}, u32[]{:S(2)}) collective-permute-start(bf16[80,1152]{1,0:T(8,128)(2,1)S(1)} %collective-permute-done.refs_1_), channel_id=1, source_target_pairs={{0,1},{1,0},{2,3},{3,2},{4,5},{5,4},{6,7},{7,6},{8,9},{9,8},{10,11... | collective-permute-start | bytes 552968 | tf_op jit(solution)/shard_map/ppermute | solution.py:442
  16.3 3.6 %collective-permute-start.5 = (bf16[80,1152]{1,0:T(8,128)(2,1)S(1)}, bf16[80,1152]{1,0:T(8,128)(2,1)S(1)}, u32[]{:S(2)}, u32[]{:S(2)}) collective-permute-start(bf16[80,1152]{1,0:T(8,128)(2,1)S(1)} %collective-permute-done.1.refs_2_), channel_id=1, source_target_pairs={{0,1},{1,0},{2,3},{3,2},{4,5},{5,4},{6,7},{7,6},{8,9},{9,8},{10,11... | collective-permute-start | bytes 552968 | tf_op jit(solution)/shard_map/ppermute | solution.py:442
  16.3 3.6 %collective-permute-start.6 = (bf16[80,1152]{1,0:T(8,128)(2,1)S(1)}, bf16[80,1152]{1,0:T(8,128)(2,1)S(1)}, u32[]{:S(2)}, u32[]{:S(2)}) collective-permute-start(bf16[80,1152]{1,0:T(8,128)(2,1)S(1)} %collective-permute-done.2.refs_3_), channel_id=1, source_target_pairs={{0,1},{1,0},{2,3},{3,2},{4,5},{5,4},{6,7},{7,6},{8,9},{9,8},{10,11... | collective-permute-start | bytes 552968 | tf_op jit(solution)/shard_map/ppermute | solution.py:442
  19.9 20.2 %copy-start.2 = (f32[1,320]{1,0:T(1,128)S(1)}, f32[1,320]{1,0:T(1,128)}, u32[]{:S(2)}) copy-start(f32[1,320]{1,0:T(1,128)} %reshape.135.early_ref.goal_ref) | copy-start | bytes 3844
  19.9 40.0 %copy-start.1 = (bf16[80,1152]{1,0:T(8,128)(2,1)S(1)}, bf16[80,1152]{1,0:T(8,128)(2,1)}, u32[]{:S(2)}) copy-start(bf16[80,1152]{1,0:T(8,128)(2,1)} %shard_map.149.refs_0_.hidden_ref) | copy-start | bytes 552964
  19.9 40.0 %copy-start.3 = (f32[1024]{0:T(1024)S(1)}, f32[1024]{0:T(1024)}, u32[]{:S(2)}) copy-start(f32[1024]{0:T(1024)} %param.23) | copy-start | bytes 12292
  36.8 52.8 %copy-start.5 = (s32[32]{0:T(128)S(1)}, s32[32]{0:T(128)}, u32[]{:S(2)}) copy-start(s32[32]{0:T(128)} %param.26) | copy-start | bytes 388
  36.8 3.3 %collective-permute-start.7 = (f32[4,80,1024]{2,1,0:T(8,128)}, f32[4,80,1024]{2,1,0:T(8,128)S(1)}, u32[]{:S(2)}, u32[]{:S(2)}) collective-permute-start(f32[4,80,1024]{2,1,0:T(8,128)} %get-tuple-element.14), channel_id=1, source_target_pairs={{0,1},{1,0},{2,3},{3,2},{4,5},{5,4},{6,7},{7,6},{8,9},{9,8},{10,11... | collective-permute-start | bytes 3932168 | tf_op jit(solution)/shard_map/ppermute | solution.py:442
  41.6 10.2 %collective-permute-start.8 = (f32[168,512]{1,0:T(8,128)S(1)}, f32[168,512]{1,0:T(8,128)S(1)}, u32[]{:S(2)}, u32[]{:S(2)}) collective-permute-start(f32[168,512]{1,0:T(8,128)S(1)} %get-tuple-element.16), channel_id=1, source_target_pairs={{0,2},{2,0},{4,6},{6,4},{1,3},{3,1},{5,7},{7,5},{8,10},{10,8},{12,... | collective-permute-start | bytes 1032200 | tf_op jit(solution)/shard_map/ppermute | solution.py:433
  43.1 9.8 %collective-permute-start.9 = (f32[168,512]{1,0:T(8,128)S(1)}, f32[168,512]{1,0:T(8,128)S(1)}, u32[]{:S(2)}, u32[]{:S(2)}) collective-permute-start(f32[168,512]{1,0:T(8,128)S(1)} %get-tuple-element.17), channel_id=1, source_target_pairs={{0,4},{2,6},{4,0},{6,2},{1,5},{3,7},{5,1},{7,3},{8,12},{10,14},{12... | collective-permute-start | bytes 1032200 | tf_op jit(solution)/shard_map/ppermute | solution.py:433
  53.0 6.9 %collective-permute-start.11 = (f32[88,512]{1,0:T(8,128)S(1)}, f32[88,512]{1,0:T(8,128)S(1)}, u32[]{:S(2)}, u32[]{:S(2)}) collective-permute-start(f32[88,512]{1,0:T(8,128)S(1)} %get-tuple-element.21), channel_id=1, source_target_pairs={{0,4},{2,6},{4,0},{6,2},{1,5},{3,7},{5,1},{7,3},{8,12},{10,14},{12... | collective-permute-start | bytes 540680 | tf_op jit(solution)/shard_map/ppermute | solution.py:433
  54.6 5.3 %collective-permute-start.10 = (f32[80,512]{1,0:T(8,128)S(1)}, f32[80,512]{1,0:T(8,128)S(1)}, u32[]{:S(2)}, u32[]{:S(2)}) collective-permute-start(f32[80,512]{1,0:T(8,128)S(1)} %get-tuple-element.20), channel_id=1, source_target_pairs={{0,2},{2,0},{4,6},{6,4},{1,3},{3,1},{5,7},{7,5},{8,10},{10,8},{12,... | collective-permute-start | bytes 491528 | tf_op jit(solution)/shard_map/ppermute | solution.py:433
  60.1 33.4 %copy-start.4 = (bf16[80,1024]{1,0:T(8,128)(2,1)}, bf16[80,1024]{1,0:T(8,128)(2,1)S(1)}, u32[]{:S(2)}) copy-start(bf16[80,1024]{1,0:T(8,128)(2,1)S(1)} %get-tuple-element.23.refs_0_) | copy-start | bytes 491524
  60.1 9.0 %collective-permute-start.12 = (bf16[80,1024]{1,0:T(8,128)(2,1)S(1)}, bf16[80,1024]{1,0:T(8,128)(2,1)S(1)}, u32[]{:S(2)}, u32[]{:S(2)}) collective-permute-start(bf16[80,1024]{1,0:T(8,128)(2,1)S(1)} %get-tuple-element.23.refs_0_), channel_id=1, source_target_pairs={{0,8},{8,16},{16,24},{24,0},{1,9},{9,17},{17,25},{25,1},{2,10},{10... | collective-permute-start | bytes 491528 | tf_op jit(solution)/shard_map/ppermute | solution.py:438
  60.7 12.4 %collective-permute-start.13 = (bf16[80,1024]{1,0:T(8,128)(2,1)S(1)}, bf16[80,1024]{1,0:T(8,128)(2,1)S(1)}, u32[]{:S(2)}, u32[]{:S(2)}) collective-permute-start(bf16[80,1024]{1,0:T(8,128)(2,1)S(1)} %get-tuple-element.23.refs_0_), channel_id=1, source_target_pairs={{0,16},{8,24},{16,0},{24,8},{1,17},{9,25},{17,1},{25,9},{2,18},{10... | collective-permute-start | bytes 491528 | tf_op jit(solution)/shard_map/ppermute | solution.py:438
  61.7 12.1 %collective-permute-start.14 = (bf16[80,1024]{1,0:T(8,128)(2,1)S(1)}, bf16[80,1024]{1,0:T(8,128)(2,1)S(1)}, u32[]{:S(2)}, u32[]{:S(2)}) collective-permute-start(bf16[80,1024]{1,0:T(8,128)(2,1)S(1)} %get-tuple-element.23.refs_0_), channel_id=1, source_target_pairs={{0,24},{8,0},{16,8},{24,16},{1,25},{9,1},{17,9},{25,17},{2,26},{10... | collective-permute-start | bytes 491528 | tf_op jit(solution)/shard_map/ppermute | solution.py:438
  64.0 10.3 %collective-permute-start.15 = (bf16[80,1024]{1,0:T(8,128)(2,1)S(1)}, bf16[80,1024]{1,0:T(8,128)(2,1)S(1)}, u32[]{:S(2)}, u32[]{:S(2)}) collective-permute-start(bf16[80,1024]{1,0:T(8,128)(2,1)S(1)} %get-tuple-element.23.refs_0_), channel_id=1, source_target_pairs={{0,2},{2,0},{4,6},{6,4},{1,3},{3,1},{5,7},{7,5},{8,10},{10,8},{12,... | collective-permute-start | bytes 491528 | tf_op jit(solution)/shard_map/ppermute | solution.py:433
  69.1 24.4 %copy-start.14 = (bf16[80,1024]{1,0:T(8,128)(2,1)}, bf16[80,1024]{1,0:T(8,128)(2,1)S(1)}, u32[]{:S(2)}) copy-start(bf16[80,1024]{1,0:T(8,128)(2,1)S(1)} %collective-permute-done.12.refs_1_) | copy-start | bytes 491524
  69.1 6.3 %collective-permute-start.19 = (bf16[80,1024]{1,0:T(8,128)(2,1)S(1)}, bf16[80,1024]{1,0:T(8,128)(2,1)S(1)}, u32[]{:S(2)}, u32[]{:S(2)}) collective-permute-start(bf16[80,1024]{1,0:T(8,128)(2,1)S(1)} %get-tuple-element.23.refs_0_), channel_id=1, source_target_pairs={{0,4},{2,6},{4,0},{6,2},{1,5},{3,7},{5,1},{7,3},{8,12},{10,14},{12... | collective-permute-start | bytes 491528 | tf_op jit(solution)/shard_map/ppermute | solution.py:433
  73.1 20.4 %copy-start.15 = (bf16[80,1024]{1,0:T(8,128)(2,1)}, bf16[80,1024]{1,0:T(8,128)(2,1)S(1)}, u32[]{:S(2)}) copy-start(bf16[80,1024]{1,0:T(8,128)(2,1)S(1)} %collective-permute-done.13.refs_2_) | copy-start | bytes 491524
  73.1 7.1 %collective-permute-start.16 = (bf16[80,1024]{1,0:T(8,128)(2,1)S(1)}, bf16[80,1024]{1,0:T(8,128)(2,1)S(1)}, u32[]{:S(2)}, u32[]{:S(2)}) collective-permute-start(bf16[80,1024]{1,0:T(8,128)(2,1)S(1)} %collective-permute-done.12.refs_1_), channel_id=1, source_target_pairs={{0,2},{2,0},{4,6},{6,4},{1,3},{3,1},{5,7},{7,5},{8,10},{10,8},{12,... | collective-permute-start | bytes 491528 | tf_op jit(solution)/shard_map/ppermute | solution.py:433
  73.8 19.8 %copy-start.16 = (bf16[80,1024]{1,0:T(8,128)(2,1)}, bf16[80,1024]{1,0:T(8,128)(2,1)S(1)}, u32[]{:S(2)}) copy-start(bf16[80,1024]{1,0:T(8,128)(2,1)S(1)} %collective-permute-done.14.refs_3_) | copy-start | bytes 491524
  73.8 7.1 %collective-permute-start.21 = (bf16[80,1024]{1,0:T(8,128)(2,1)S(1)}, bf16[80,1024]{1,0:T(8,128)(2,1)S(1)}, u32[]{:S(2)}, u32[]{:S(2)}) collective-permute-start(bf16[80,1024]{1,0:T(8,128)(2,1)S(1)} %collective-permute-done.13.refs_2_), channel_id=1, source_target_pairs={{0,4},{2,6},{4,0},{6,2},{1,5},{3,7},{5,1},{7,3},{8,12},{10,14},{12... | collective-permute-start | bytes 491528 | tf_op jit(solution)/shard_map/ppermute | solution.py:433
  74.3 19.3 %copy-start.17 = (bf16[80,1024]{1,0:T(8,128)(2,1)}, bf16[80,1024]{1,0:T(8,128)(2,1)S(1)}, u32[]{:S(2)}) copy-start(bf16[80,1024]{1,0:T(8,128)(2,1)S(1)} %collective-permute-done.15.refs_4_) | copy-start | bytes 491524
  74.3 10.6 %collective-permute-start.17 = (bf16[80,1024]{1,0:T(8,128)(2,1)S(1)}, bf16[80,1024]{1,0:T(8,128)(2,1)S(1)}, u32[]{:S(2)}, u32[]{:S(2)}) collective-permute-start(bf16[80,1024]{1,0:T(8,128)(2,1)S(1)} %collective-permute-done.13.refs_2_), channel_id=1, source_target_pairs={{0,2},{2,0},{4,6},{6,4},{1,3},{3,1},{5,7},{7,5},{8,10},{10,8},{12,... | collective-permute-start | bytes 491528 | tf_op jit(solution)/shard_map/ppermute | solution.py:433
  75.5 18.1 %copy-start.18 = (bf16[80,1024]{1,0:T(8,128)(2,1)}, bf16[80,1024]{1,0:T(8,128)(2,1)S(1)}, u32[]{:S(2)}) copy-start(bf16[80,1024]{1,0:T(8,128)(2,1)S(1)} %collective-permute-done.19.refs_8_) | copy-start | bytes 491524
  75.5 8.9 %collective-permute-start.22 = (bf16[80,1024]{1,0:T(8,128)(2,1)S(1)}, bf16[80,1024]{1,0:T(8,128)(2,1)S(1)}, u32[]{:S(2)}, u32[]{:S(2)}) collective-permute-start(bf16[80,1024]{1,0:T(8,128)(2,1)S(1)} %collective-permute-done.14.refs_3_), channel_id=1, source_target_pairs={{0,4},{2,6},{4,0},{6,2},{1,5},{3,7},{5,1},{7,3},{8,12},{10,14},{12... | collective-permute-start | bytes 491528 | tf_op jit(solution)/shard_map/ppermute | solution.py:433
  80.3 13.3 %copy-start.19 = (bf16[80,1024]{1,0:T(8,128)(2,1)}, bf16[80,1024]{1,0:T(8,128)(2,1)S(1)}, u32[]{:S(2)}) copy-start(bf16[80,1024]{1,0:T(8,128)(2,1)S(1)} %collective-permute-done.16.refs_5_) | copy-start | bytes 491524
  80.3 6.2 %collective-permute-start.18 = (bf16[80,1024]{1,0:T(8,128)(2,1)S(1)}, bf16[80,1024]{1,0:T(8,128)(2,1)S(1)}, u32[]{:S(2)}, u32[]{:S(2)}) collective-permute-start(bf16[80,1024]{1,0:T(8,128)(2,1)S(1)} %collective-permute-done.14.refs_3_), channel_id=1, source_target_pairs={{0,2},{2,0},{4,6},{6,4},{1,3},{3,1},{5,7},{7,5},{8,10},{10,8},{12,... | collective-permute-start | bytes 491528 | tf_op jit(solution)/shard_map/ppermute | solution.py:433
  80.9 7.1 %collective-permute-start.20 = (bf16[80,1024]{1,0:T(8,128)(2,1)S(1)}, bf16[80,1024]{1,0:T(8,128)(2,1)S(1)}, u32[]{:S(2)}, u32[]{:S(2)}) collective-permute-start(bf16[80,1024]{1,0:T(8,128)(2,1)S(1)} %collective-permute-done.12.refs_1_), channel_id=1, source_target_pairs={{0,4},{2,6},{4,0},{6,2},{1,5},{3,7},{5,1},{7,3},{8,12},{10,14},{12... | collective-permute-start | bytes 491528 | tf_op jit(solution)/shard_map/ppermute | solution.py:433
  84.4 6.7 %collective-permute-start.23 = (bf16[80,1024]{1,0:T(8,128)(2,1)S(1)}, bf16[80,1024]{1,0:T(8,128)(2,1)S(1)}, u32[]{:S(2)}, u32[]{:S(2)}) collective-permute-start(bf16[80,1024]{1,0:T(8,128)(2,1)S(1)} %collective-permute-done.15.refs_4_), channel_id=1, source_target_pairs={{0,4},{2,6},{4,0},{6,2},{1,5},{3,7},{5,1},{7,3},{8,12},{10,14},{12... | collective-permute-start | bytes 491528 | tf_op jit(solution)/shard_map/ppermute | solution.py:433
  84.9 7.3 %collective-permute-start.24 = (bf16[80,1024]{1,0:T(8,128)(2,1)S(1)}, bf16[80,1024]{1,0:T(8,128)(2,1)S(1)}, u32[]{:S(2)}, u32[]{:S(2)}) collective-permute-start(bf16[80,1024]{1,0:T(8,128)(2,1)S(1)} %collective-permute-done.16.refs_5_), channel_id=1, source_target_pairs={{0,4},{2,6},{4,0},{6,2},{1,5},{3,7},{5,1},{7,3},{8,12},{10,14},{12... | collective-permute-start | bytes 491528 | tf_op jit(solution)/shard_map/ppermute | solution.py:433
  86.4 5.8 %collective-permute-start.25 = (bf16[80,1024]{1,0:T(8,128)(2,1)S(1)}, bf16[80,1024]{1,0:T(8,128)(2,1)S(1)}, u32[]{:S(2)}, u32[]{:S(2)}) collective-permute-start(bf16[80,1024]{1,0:T(8,128)(2,1)S(1)} %collective-permute-done.21.refs_10_), channel_id=1, source_target_pairs={{0,2},{2,0},{4,6},{6,4},{1,3},{3,1},{5,7},{7,5},{8,10},{10,8},{12,... | collective-permute-start | bytes 491528 | tf_op jit(solution)/shard_map/ppermute | solution.py:433
  88.0 5.5 %collective-permute-start.26 = (bf16[80,1024]{1,0:T(8,128)(2,1)S(1)}, bf16[80,1024]{1,0:T(8,128)(2,1)S(1)}, u32[]{:S(2)}, u32[]{:S(2)}) collective-permute-start(bf16[80,1024]{1,0:T(8,128)(2,1)S(1)} %collective-permute-done.22.refs_11_), channel_id=1, source_target_pairs={{0,2},{2,0},{4,6},{6,4},{1,3},{3,1},{5,7},{7,5},{8,10},{10,8},{12,... | collective-permute-start | bytes 491528 | tf_op jit(solution)/shard_map/ppermute | solution.py:433
  91.2 30.6 %copy-start.6 = (s32[32]{0:T(128)S(1)}, s32[32]{0:T(128)}, u32[]{:S(2)}) copy-start(s32[32]{0:T(128)} %param.27) | copy-start | bytes 388
  114.7 8.5 %collective-permute-start.28 = (f32[16,2,80]{2,0,1:T(8,128)S(1)}, f32[16,2,80]{2,0,1:T(8,128)S(1)}, u32[]{:S(2)}, u32[]{:S(2)}) collective-permute-start(f32[16,2,80]{2,0,1:T(8,128)S(1)} %copy.37), channel_id=1, source_target_pairs={{0,8},{8,16},{16,24},{24,0},{1,9},{9,17},{17,25},{25,1},{2,10},{10... | collective-permute-start | bytes 30728 | tf_op jit(solution)/shard_map/ppermute | solution.py:438
  117.4 5.8 %collective-permute-start.29 = (f32[16,2,80]{2,0,1:T(8,128)S(1)}, f32[16,2,80]{2,0,1:T(8,128)S(1)}, u32[]{:S(2)}, u32[]{:S(2)}) collective-permute-start(f32[16,2,80]{2,0,1:T(8,128)S(1)} %copy.37), channel_id=1, source_target_pairs={{0,16},{8,24},{16,0},{24,8},{1,17},{9,25},{17,1},{25,9},{2,18},{10... | collective-permute-start | bytes 30728 | tf_op jit(solution)/shard_map/ppermute | solution.py:438
  119.4 3.8 %collective-permute-start.30 = (f32[16,2,80]{2,0,1:T(8,128)S(1)}, f32[16,2,80]{2,0,1:T(8,128)S(1)}, u32[]{:S(2)}, u32[]{:S(2)}) collective-permute-start(f32[16,2,80]{2,0,1:T(8,128)S(1)} %copy.37), channel_id=1, source_target_pairs={{0,24},{8,0},{16,8},{24,16},{1,25},{9,1},{17,9},{25,17},{2,26},{10... | collective-permute-start | bytes 30728 | tf_op jit(solution)/shard_map/ppermute | solution.py:438
  123.2 5.5 %collective-permute-start.31 = (f32[16,2,80]{2,0,1:T(8,128)S(1)}, f32[16,2,80]{2,0,1:T(8,128)S(1)}, u32[]{:S(2)}, u32[]{:S(2)}) collective-permute-start(f32[16,2,80]{2,0,1:T(8,128)S(1)} %pad_maximum_fusion), channel_id=1, source_target_pairs={{0,2},{2,0},{4,6},{6,4},{1,3},{3,1},{5,7},{7,5},{8,10},{10,8},{12,... | collective-permute-start | bytes 30728 | tf_op jit(solution)/shard_map/ppermute | solution.py:433
  124.1 4.7 %collective-permute-start.32 = (f32[16,2,80]{2,0,1:T(8,128)S(1)}, f32[16,2,80]{2,0,1:T(8,128)S(1)}, u32[]{:S(2)}, u32[]{:S(2)}) collective-permute-start(f32[16,2,80]{2,0,1:T(8,128)S(1)} %pad_maximum_fusion), channel_id=1, source_target_pairs={{0,4},{2,6},{4,0},{6,2},{1,5},{3,7},{5,1},{7,3},{8,12},{10,14},{12... | collective-permute-start | bytes 30728 | tf_op jit(solution)/shard_map/ppermute | solution.py:433
  124.5 4.6 %collective-permute-start.33 = (f32[16,2,80]{2,0,1:T(8,128)S(1)}, f32[16,2,80]{2,0,1:T(8,128)S(1)}, u32[]{:S(2)}, u32[]{:S(2)}) collective-permute-start(f32[16,2,80]{2,0,1:T(8,128)S(1)} %pad_maximum_fusion), channel_id=1, source_target_pairs={{0,6},{2,4},{4,2},{6,0},{1,7},{3,5},{5,3},{7,1},{8,14},{10,12},{12... | collective-permute-start | bytes 30728 | tf_op jit(solution)/shard_map/ppermute | solution.py:433
  129.2 1.2 collective-permute-start.34
  (17 other events, 67.4 us)
